TPU v7x, 32 devices: a whole 2x2x4 slice. The times are simulated.
32 devices in a mesh: teach: 4 (over y, x), stud: 2 (over core), mdl: 4 (over z).
Axes of the slice: x: 2, y: 2, z: 4, core: 2. Of those that a mesh axis runs over, the one named last changes fastest.
Arguments:
- states: bfloat16 [1024, 512], P(('teach', 'stud')), may hold values from -6 to 6
- task_ids: int32 [1024, 1], P(('teach', 'stud')), may hold values from 0 to 3; in each aligned block of 128 rows (0 to 127, 128 to 255, ...) at most 48 rows name the same one
- student_batch: int32 [1024, 1], P(('teach', 'stud')), may hold values from 0 to 7; in each aligned block of 128 rows (0 to 127, 128 to 255, ...) at most 32 rows name the same one
- teach_in: bfloat16 [4, 512, 1024], P('teach', None, 'mdl'), may hold values from -0.25 to 0.25
- teach_out: bfloat16 [4, 1024, 512], P('teach', 'mdl'), may hold values from -0.1875 to 0.1875
- student_up: bfloat16 [512, 1024], P(None, 'mdl'), may hold values from -0.25 to 0.25
- student_down: bfloat16 [512, 1024], P(None, 'mdl'), may hold values from -0.1875 to 0.1875
Outputs:
- grad_up: float32 [512, 1024], P(('teach', 'stud'), 'mdl')
- grad_down: float32 [512, 1024], P(('teach', 'stud'), 'mdl')
Inputs may be any that keep to these rules, and one draw needn't show every extreme that they name: `task_ids`: teacher t lives at index t // 1 of teach. Among one device's 128 states no teacher is named more than 48 times, and in every draw some teacher is named exactly 48 times there; every teacher is named somewhere. `student_batch`: batch b belongs to teach index b // 2 and stud index b % 2. Among one device's 128 states no batch is named more than 32 times, some batch exactly 32 times; every batch holds one state or more.
All inputs are finite; a program needn't handle non-finite values.
Results may differ from a plain program's by a relative error of at most 0.0023.
Values may be sent and summed in bfloat16 or wider, within the bound.
No kernel may reach another device: no remote copies, remote signals or barrier semaphores. Data moves between devices by JAX's collectives and lax.ppermute only.
A program may use at most 64 MiB of HBM per device.

v0:
```python
import jax
import jax.numpy as jnp
from jax import lax
from jax.sharding import PartitionSpec as P


def silu_slope(value):
    sig = jax.nn.sigmoid(value)
    return sig * (1.0 + value * (1.0 - sig))


def slot_table(labels_of, groups, capacity):
    onehot = (labels_of[:, None] == jnp.arange(groups, dtype=jnp.int32)[None, :]).astype(jnp.int32)
    before = jnp.sum((jnp.cumsum(onehot, axis=0) - onehot) * onehot, axis=1)
    slot_index = labels_of * capacity + before
    return (slot_index[None, :] == jnp.arange(groups * capacity, dtype=jnp.int32)[:, None]).astype(
        jnp.float32
    )


def on_device(states, task_ids, student_batch, teach_in, teach_out, student_up, student_down):
    row_count = states.shape[0]
    width = states.shape[1]
    owners = lax.axis_size("teach")
    local_teachers = teach_in.shape[0]
    teachers = owners * local_teachers
    batches = lax.axis_size(("teach", "stud"))
    teach_room = 3 * row_count // (2 * teachers)
    action_width = teach_out.shape[2]
    dispatch = slot_table(task_ids[:, 0], teachers, teach_room)
    outgoing = jnp.dot(
        dispatch.astype(jnp.bfloat16), states, preferred_element_type=jnp.float32
    ).astype(jnp.bfloat16)
    outgoing = outgoing.reshape(owners, local_teachers, teach_room, width)
    hidden = jnp.einsum(
        "ntcd,tdh->ntch",
        lax.all_to_all(outgoing, "teach", split_axis=0, concat_axis=0, tiled=True),
        teach_in,
        preferred_element_type=jnp.float32,
    )
    hidden = jax.nn.silu(hidden).astype(jnp.bfloat16)
    partial_labels = jnp.einsum(
        "ntch,tha->ntca", hidden, teach_out, preferred_element_type=jnp.float32
    )
    partial_labels = lax.psum(partial_labels, "mdl")
    returned = lax.all_to_all(partial_labels, "teach", split_axis=0, concat_axis=0, tiled=True)
    targets = jnp.dot(
        dispatch.T,
        returned.reshape(-1, action_width),
        precision=lax.Precision.HIGHEST,
        preferred_element_type=jnp.float32,
    )
    batch_list = student_batch[:, 0]
    member = (batch_list[:, None] == jnp.arange(batches, dtype=jnp.int32)[None, :]).astype(
        jnp.float32
    )
    counts = lax.psum(jnp.sum(member, axis=0), ("teach", "stud"))
    weight = jnp.dot(
        member, 2.0 / counts, precision=lax.Precision.HIGHEST, preferred_element_type=jnp.float32
    )
    pre = jnp.dot(states, student_up, preferred_element_type=jnp.float32)
    act = jax.nn.silu(pre).astype(jnp.bfloat16)
    partial_pred = jnp.einsum("rh,ah->ra", act, student_down, preferred_element_type=jnp.float32)
    error = lax.psum(partial_pred, "mdl") - targets
    scaled = (error * weight[:, None]).astype(jnp.bfloat16)
    grad_down = jnp.einsum("ra,rh->ah", scaled, act, preferred_element_type=jnp.float32)
    back = jnp.dot(scaled, student_down, preferred_element_type=jnp.float32)
    pre_grad = (back * silu_slope(pre)).astype(jnp.bfloat16)
    grad_up = jnp.einsum("rd,rh->dh", states, pre_grad, preferred_element_type=jnp.float32)
    share_up, share_down = (
        lax.psum_scatter(grad_up, ("teach", "stud"), scatter_dimension=0, tiled=True),
        lax.psum_scatter(grad_down, ("teach", "stud"), scatter_dimension=0, tiled=True),
    )
    return (share_up, share_down)


def solution(mesh):
    in_specs = (
        P(("teach", "stud"), None),
        P(("teach", "stud"), None),
        P(("teach", "stud"), None),
        P("teach", None, "mdl"),
        P("teach", "mdl", None),
        P(None, "mdl"),
        P(None, "mdl"),
    )
    out_specs = (P(("teach", "stud"), "mdl"), P(("teach", "stud"), "mdl"))
    return jax.shard_map(
        on_device, mesh=mesh, in_specs=in_specs, out_specs=out_specs, check_vma=False
    )
```

profile of v0, /device:TPU:0, one launch (start us, length us, event | category | flops | bytes accessed | tf_op | source)
XLA Modules:
  0.0 159.4 jit_solution(13348237406113118501)
XLA Ops:
  7.2 0.0 copy-start
  7.2 0.0 copy-start.4
  7.2 0.7 copy-done.4
  7.9 0.1 fusion.24
  8.0 0.2 reduce_window_sum.11
  8.1 0.2 select_reduce_fusion
  8.3 0.5 copy-done.1
  8.8 0.9 convolution_convert_fusion
  9.6 5.3 %all-to-all-start = ((bf16[4,1,48,512]{3,2,1,0:T(8,128)(2,1)}), bf16[4,1,48,512]{3,2,1,0:T(8,128)(2,1)S(1)}, u32[]{:S(2)}, u32[]{:S(2)}) async-start(bf16[4,1,48,512]{3,2,1,0:T(8,128)(2,1)} %bitcast.2), calls=%async_computation | async-start | bytes 393216 | tf_op jit(solution)/shard_map/all_to_all | solution.py:37
  14.9 0.2 fusion.35
  15.1 0.0 copy-start.5
  15.2 0.0 copy-start.6
  15.2 0.9 fusion.34
  16.1 4.0 %all-to-all-done = bf16[4,1,48,512]{3,2,1,0:T(8,128)(2,1)S(1)} async-done(((bf16[4,1,48,512]{3,2,1,0:T(8,128)(2,1)}), bf16[4,1,48,512]{3,2,1,0:T(8,128)(2,1)S(1)}, u32[]{:S(2)}, u32[]{:S(2)}) %all-to-all-start) | async-done | bytes 196640 | tf_op jit(solution)/shard_map/all_to_all | solution.py:37
  20.1 1.2 convolution_bitcast_fusion.1
  21.3 0.0 all-reduce.3.cloned.1.call-update
  21.3 40.8 %all-reduce.3.cloned.1.call-done = (f32[128,512]{1,0:T(8,128)}, f32[4,1,48,512]{3,2,0,1:T(8,128)}) async-done(((f32[128,512]{1,0:T(8,128)}, f32[4,1,48,512]{3,2,0,1:T(8,128)}), (f32[128,512]{1,0:T(8,128)}, f32[4,1,48,512]{3,2,0,1:T(8,128)})) %all-reduce.3.cloned.1.call-update) | async-done | bytes 655376 | tf_op jit(solution)/shard_map/psum | solution.py:64
  62.1 3.8 %all-to-all-start.1 = ((f32[4,1,48,512]{3,2,1,0:T(8,128)}), f32[4,1,48,512]{3,2,1,0:T(8,128)S(1)}, u32[]{:S(2)}, u32[]{:S(2)}) async-start(f32[4,1,48,512]{3,2,1,0:T(8,128)} %bitcast.71), calls=%async_computation.1 | async-start | bytes 786432 | tf_op jit(solution)/shard_map/all_to_all | solution.py:46
  65.9 0.7 copy-done.7
  66.6 0.1 convert_reduce_fusion
  66.7 13.6 %psum.23 = f32[8]{0:T(128)S(1)} all-reduce(f32[8]{0:T(128)S(1)} %convert_reduce_fusion), channel_id=1, replica_groups=mesh['teach'=4,'stud'=2,'mdl'=4] {'teach','stud'}, use_global_device_ids=true, to_apply=%region_5.6 | all-reduce | flops 8 | bytes 64 | tf_op jit(solution)/shard_map/psum | solution.py:57
  80.3 0.1 convolution_bitcast_fusion.3
  80.5 0.0 all-to-all-done.1
  80.5 0.4 fusion.1
  80.8 0.5 convolution_bitcast_fusion
  81.3 1.0 copy.16
  82.3 0.0 reduce-scatter.7.cloned.1.call-update
  82.3 0.0 reduce-scatter.5.cloned.1.call-start
  82.4 1.1 fusion.33
  83.5 0.0 reduce-scatter.5.cloned.1.call-update
  83.5 31.3 %reduce-scatter.7.cloned.1.call-done = f32[64,256]{1,0:T(8,128)} async-done(((f32[512,256]{1,0:T(8,128)}), f32[64,256]{1,0:T(8,128)}) %reduce-scatter.7.cloned.1.call-update) | async-done | bytes 65552
  114.7 38.2 %reduce-scatter.5.cloned.1.call-done = f32[64,256]{1,0:T(8,128)} async-done(((f32[512,256]{1,0:T(8,128)}), f32[64,256]{1,0:T(8,128)}) %reduce-scatter.5.cloned.1.call-update) | async-done | bytes 65552 | tf_op jit(solution)/shard_map/reduce_scatter | solution.py:72
  (12 shorter events, 0.0 us)
Async XLA Ops:
  7.2 8.0 %copy-start = (bf16[512,256]{1,0:T(8,128)(2,1)S(1)}, bf16[512,256]{1,0:T(8,128)(2,1)}, u32[]{:S(2)}) copy-start(bf16[512,256]{1,0:T(8,128)(2,1)} %param.13) | copy-start | bytes 786436
  7.2 0.7 copy-start.4
  7.9 0.9 copy-start.1
  9.6 5.3 %copy-start.2 = (bf16[512,256]{1,0:T(8,128)(2,1)S(1)}, bf16[512,256]{1,0:T(8,128)(2,1)}, u32[]{:S(2)}) copy-start(bf16[512,256]{1,0:T(8,128)(2,1)} %param.12) | copy-start | bytes 786436
  9.6 10.5 %all-to-all-start = ((bf16[4,1,48,512]{3,2,1,0:T(8,128)(2,1)}), bf16[4,1,48,512]{3,2,1,0:T(8,128)(2,1)S(1)}, u32[]{:S(2)}, u32[]{:S(2)}) async-start(bf16[4,1,48,512]{3,2,1,0:T(8,128)(2,1)} %bitcast.2), calls=%async_computation | async-start | bytes 393216 | tf_op jit(solution)/shard_map/all_to_all | solution.py:37
  14.9 47.2 %all-reduce.3.cloned.1.call-start = ((), (), s32[]{:S(2)}) async-start(), calls=%async_computation.6 | async-start | bytes 1310720 | tf_op jit(solution)/shard_map/psum | solution.py:64
  15.1 5.0 %copy-start.5 = (bf16[1,256,512]{2,1,0:T(8,128)(2,1)S(1)}, bf16[1,256,512]{2,1,0:T(8,128)(2,1)}, u32[]{:S(2)}) copy-start(bf16[1,256,512]{2,1,0:T(8,128)(2,1)} %param.11) | copy-start | bytes 786436
  15.2 5.0 %copy-start.6 = (bf16[1,512,256]{2,1,0:T(8,128)(2,1)S(1)}, bf16[1,512,256]{2,1,0:T(8,128)(2,1)}, u32[]{:S(2)}) copy-start(bf16[1,512,256]{2,1,0:T(8,128)(2,1)} %param.10) | copy-start | bytes 786436
  62.1 18.3 %copy-start.3 = (f32[128,512]{1,0:T(8,128)S(1)}, f32[128,512]{1,0:T(8,128)}, u32[]{:S(2)}) copy-start(f32[128,512]{1,0:T(8,128)} %get-tuple-element.8) | copy-start | bytes 786436
  62.1 18.3 %all-to-all-start.1 = ((f32[4,1,48,512]{3,2,1,0:T(8,128)}), f32[4,1,48,512]{3,2,1,0:T(8,128)S(1)}, u32[]{:S(2)}, u32[]{:S(2)}) async-start(f32[4,1,48,512]{3,2,1,0:T(8,128)} %bitcast.71), calls=%async_computation.1 | async-start | bytes 786432 | tf_op jit(solution)/shard_map/all_to_all | solution.py:46
  65.9 0.7 copy-start.7
  65.9 48.8 %reduce-scatter.7.cloned.1.call-start = ((), (), s32[]{:S(2)}) async-start(), calls=%async_computation.5 | async-start | bytes 589824
  82.3 70.6 %reduce-scatter.5.cloned.1.call-start = ((), (), s32[]{:S(2)}) async-start(), calls=%async_computation.4 | async-start | bytes 589824 | tf_op jit(solution)/shard_map/reduce_scatter | solution.py:72
Sparse Core Ops, SparseCore 0:
  21.5 40.6 all-reduce.2
  82.5 32.2 reduce-scatter.6
  118.7 34.1 reduce-scatter.4
where the time goes:
time: 160 us; the launch traced here: 159 us
  waiting for transfers between devices  114 us (71%)
  between operations  13.8 us (9%)
  blocking collectives  13.6 us (8%)
  starting transfers between devices  9.11 us (6%)
  matrix products  5.19 us (3%)
  local copies, waits for them, and re-layouts  2.82 us (2%)
    psum x1, waiting for transfers between devices, on_device(): error = lax.psum(partial_pred, 'mdl') - targets  40.8 us
    reduce_scatter x1, waiting for transfers between devices, on_device(): lax.psum_scatter(grad_down, ('teach', 'stud'), scatter_dimension=0, tiled...  38.2 us
    unnamed x4, waiting for transfers between devices  31.3 us
    psum x1, blocking collectives, on_device(): counts = lax.psum(jnp.sum(member, axis=0), ('teach', 'stud'))  13.6 us
    all_to_all x1, starting transfers between devices, on_device(): lax.all_to_all(outgoing, 'teach', split_axis=0, concat_axis=0, tiled=True)  5.29 us
    all_to_all x1, waiting for transfers between devices, on_device(): lax.all_to_all(outgoing, 'teach', split_axis=0, concat_axis=0, tiled=True)  4.03 us
    all_to_all x1, starting transfers between devices, on_device(): lax.all_to_all(partial_labels, 'teach', split_axis=0, concat_axis=0, tile...  3.77 us
  transfers between devices with their start and end apart: 5, of which 4 were waited for; matrix products, arithmetic and copies ran while one was open for 2% of the time, Pallas kernels for 0%

commit v1 on v0

v1 whole, which is shorter than its diff:
```python
import jax
import jax.numpy as jnp
from jax import lax
from jax.sharding import PartitionSpec as P

LANES = 128


def silu_slope(value):
    sig = jax.nn.sigmoid(value)
    return sig * (1.0 + value * (1.0 - sig))


def partner_table(size, step):
    if size & (size - 1) == 0:
        return [(i, i ^ step) for i in range(size)]
    return [(i, (i + step) % size) for i in range(size)]


def partner_to(axis, step):
    size, me = lax.axis_size(axis), lax.axis_index(axis)
    return me ^ step if size & (size - 1) == 0 else (me + step) % size


def partner_from(axis, step):
    size, me = lax.axis_size(axis), lax.axis_index(axis)
    return me ^ step if size & (size - 1) == 0 else (me + size - step) % size


def send(block, axis, step):
    return lax.ppermute(block, axis, partner_table(lax.axis_size(axis), step))


def on_device(states, task_ids, student_batch, teach_in, teach_out, student_up, student_down):
    row_count, width = states.shape
    owners, studs, parts = lax.axis_size("teach"), lax.axis_size("stud"), lax.axis_size("mdl")
    local_teachers = teach_in.shape[0]
    teachers = owners * local_teachers
    batches = owners * studs
    room = 3 * row_count // (2 * teachers)
    extra = -(-batches // LANES) * LANES
    task_list, batch_list = task_ids[:, 0], student_batch[:, 0]
    named = (task_list[:, None] == jnp.arange(teachers, dtype=jnp.int32)[None, :]).astype(jnp.float32)
    earlier = (jnp.arange(row_count)[:, None] > jnp.arange(row_count)[None, :]).astype(jnp.float32)
    before = jnp.sum(jnp.dot(earlier, named) * named, axis=1).astype(jnp.int32)
    block_of = jnp.array([partner_to("teach", k) for k in range(owners)])
    step_of = jnp.sum(
        (block_of[None, :] == (task_list // local_teachers)[:, None]) * jnp.arange(owners)[None, :], axis=1
    )
    slot = (step_of * local_teachers + task_list % local_teachers) * room + before
    dispatch = (slot[None, :] == jnp.arange(teachers * room, dtype=jnp.int32)[:, None]).astype(jnp.bfloat16)
    member = (batch_list[:, None] == jnp.arange(extra, dtype=jnp.int32)[None, :]).astype(jnp.bfloat16)
    own_counts = jnp.sum(member.astype(jnp.float32), axis=0)
    outgoing = jnp.dot(dispatch, states, preferred_element_type=jnp.float32).astype(jnp.bfloat16)
    tags = jnp.dot(dispatch, member, preferred_element_type=jnp.float32)
    head = (jnp.arange(teachers * room) % (local_teachers * room) == 0).astype(jnp.float32)
    tags = (tags + head[:, None] * (2.0 * own_counts)[None, :]).astype(jnp.bfloat16)
    outgoing = jnp.concatenate([outgoing, tags], axis=1).reshape(owners, local_teachers * room, width + extra)
    arrived = [outgoing[0]] + [send(outgoing[k], "teach", k) for k in range(1, owners)]
    slots = local_teachers * room * owners
    rows = jnp.stack(arrived)
    tags = rows[:, :, width:].astype(jnp.float32)
    doubled = jnp.floor(tags[:, :1] * 0.5)
    counts = jnp.sum(doubled[:, 0], axis=0)
    tags = jnp.concatenate([tags[:, :1] - 2.0 * doubled, tags[:, 1:]], axis=1).reshape(slots, extra)
    others = [send(counts[None, :], "stud", k) for k in range(1, studs)]
    counts = counts + sum(o[0] for o in others)
    rows = rows[:, :, :width].reshape(owners, local_teachers, room, width)
    hidden = jnp.einsum("ntcd,tdh->ntch", rows, teach_in, preferred_element_type=jnp.float32)
    hidden = jax.nn.silu(hidden).astype(jnp.bfloat16)
    labels = jnp.einsum("ntch,tha->ntca", hidden, teach_out, preferred_element_type=jnp.float32)
    rows = rows.reshape(slots, width)
    pre = jnp.dot(rows, student_up, preferred_element_type=jnp.float32)
    act = jax.nn.silu(pre).astype(jnp.bfloat16)
    pred = jnp.einsum("rh,ah->ra", act, student_down, preferred_element_type=jnp.float32)
    error = (pred - labels.reshape(pred.shape)).reshape(parts, slots // parts, -1)
    mine = lax.axis_index("mdl")
    total = lax.dynamic_index_in_dim(error, mine, 0, False)
    for k in range(1, parts):
        total = total + send(
            lax.dynamic_index_in_dim(error, partner_to("mdl", k), 0, False), "mdl", k
        )
    weight = jnp.sum(tags * jnp.where(counts > 0, 2.0 / counts, 0.0)[None, :], axis=1)
    weight = lax.dynamic_index_in_dim(weight.reshape(parts, -1), mine, 0, False)
    scaled = (total * weight[:, None]).astype(jnp.bfloat16)
    full = jnp.zeros((parts,) + scaled.shape, scaled.dtype)
    full = lax.dynamic_update_index_in_dim(full, scaled, mine, 0)
    for k in range(1, parts):
        full = lax.dynamic_update_index_in_dim(full, send(scaled, "mdl", k), partner_from("mdl", k), 0)
    scaled = full.reshape(slots, -1)
    grad_down = jnp.einsum("ra,rh->ah", scaled, act, preferred_element_type=jnp.float32)
    back = jnp.dot(scaled, student_down, preferred_element_type=jnp.float32)
    pre_grad = (back * silu_slope(pre)).astype(jnp.bfloat16)
    grad_up = jnp.einsum("rd,rh->dh", rows, pre_grad, preferred_element_type=jnp.float32)

    def share(grad):
        height = grad.shape[0] // (owners * studs)
        grad = grad.reshape(owners, studs, height, -1)
        half = lax.dynamic_index_in_dim(grad, lax.axis_index("stud"), 1, False)
        for k in range(1, studs):
            half = half + send(lax.dynamic_index_in_dim(grad, partner_to("stud", k), 1, False), "stud", k)
        part = lax.dynamic_index_in_dim(half, lax.axis_index("teach"), 0, False)
        for k in range(1, owners):
            block = lax.dynamic_index_in_dim(half, partner_to("teach", k), 0, False)
            part = part + send(block.astype(jnp.bfloat16), "teach", k).astype(jnp.float32)
        return part

    return share(grad_up), share(grad_down)


def solution(mesh):
    in_specs = (
        P(("teach", "stud"), None),
        P(("teach", "stud"), None),
        P(("teach", "stud"), None),
        P("teach", None, "mdl"),
        P("teach", "mdl", None),
        P(None, "mdl"),
        P(None, "mdl"),
    )
    out_specs = (P(("teach", "stud"), "mdl"), P(("teach", "stud"), "mdl"))
    return jax.shard_map(
        on_device, mesh=mesh, in_specs=in_specs, out_specs=out_specs, check_vma=False
    )
```

time: 160 us -> 48.3 us (0.30)
  waiting for transfers between devices: 114 us -> 18.1 us
  blocking collectives: 13.6 us -> 0 us
  between operations: 13.8 us -> 0.91 us
  starting transfers between devices: 9.11 us -> 21.4 us
  matrix products: 5.19 us -> 3.08 us
    psum x1 -> x0, waiting for transfers between devices: 40.8 us -> none  [on_device(): error = lax.psum(partial_pred, 'mdl') - targets]
    reduce_scatter x1 -> x0, waiting for transfers between devices: 38.2 us -> none  [on_device(): lax.psum_scatter(grad_down, ('teach', 'stud'), scatter_dimension=0, tiled...]
    unnamed x4 -> x0, waiting for transfers between devices: 31.3 us -> none
    ppermute x0 -> x18, starting transfers between devices: none -> 21.4 us  [send(): return lax.ppermute(block, axis, partner_table(lax.axis_size(axis), step))]
    ppermute x0 -> x18, waiting for transfers between devices: none -> 18.1 us  [send(): return lax.ppermute(block, axis, partner_table(lax.axis_size(axis), step))]
    psum x1 -> x0, blocking collectives: 13.6 us -> none  [on_device(): counts = lax.psum(jnp.sum(member, axis=0), ('teach', 'stud'))]
    all_to_all x2 -> x0, starting transfers between devices: 9.06 us -> none  [the longest x1 5.29 us: on_device(): lax.all_to_all(outgoing, 'teach', split_axis=0, concat_axis=0, tiled=True)]
    all_to_all x2 -> x0, waiting for transfers between devices: 4.04 us -> none  [the longest x1 4.03 us: on_device(): lax.all_to_all(outgoing, 'teach', split_axis=0, concat_axis=0, tiled=True)]
  transfers between devices with their start and end apart: 5 -> 18, of which waited for: 4 -> 11; matrix products, arithmetic and copies ran while one was open for 2% -> 5% of each run, Pallas kernels for 0% -> 0%
where the time goes in v1:
time: 48.3 us; the launch traced here: 48.1 us
  starting transfers between devices  21.4 us (44%)
  waiting for transfers between devices  18.1 us (37%)
  matrix products  3.08 us (6%)
  local copies, waits for them, and re-layouts  2.69 us (6%)
  other arithmetic  1.97 us (4%)
  between operations  0.91 us (2%)
    ppermute x18, starting transfers between devices, send(): return lax.ppermute(block, axis, partner_table(lax.axis_size(axis), step))  21.4 us
    ppermute x18, waiting for transfers between devices, send(): return lax.ppermute(block, axis, partner_table(lax.axis_size(axis), step))  18.1 us
    unnamed x12, local copies, waits for them, and re-layouts  2.24 us
    add x2, other arithmetic, share(): part + send(block.astype(jnp.bfloat16), 'teach', k).astype(jnp.float32)  1.29 us
    dot_general x1, matrix products, on_device(): jnp.dot(dispatch, states, preferred_element_type=jnp.float32)  1.1 us
  transfers between devices with their start and end apart: 18, of which 11 were waited for; matrix products, arithmetic and copies ran while one was open for 5% of the time, Pallas kernels for 0%

profile of v1, /device:TPU:0, one launch (start us, length us, event | category | flops | bytes accessed | tf_op | source)
XLA Modules:
  0.0 48.1 jit_solution(9242125665163047027)
XLA Ops:
  0.7 0.7 %copy-done.4 = s32[128,1]{0,1:T(1,128)S(1)} copy-done((s32[128,1]{0,1:T(1,128)S(1)}, s32[128,1]{0,1:T(1,128)}, u32[]{:S(2)}) %copy-start.4) | copy-done | bytes 536
  1.7 0.7 %copy-done.5 = s32[128,1]{0,1:T(1,128)S(1)} copy-done((s32[128,1]{0,1:T(1,128)S(1)}, s32[128,1]{0,1:T(1,128)}, u32[]{:S(2)}) %copy-start.5) | copy-done | bytes 536
  2.5 1.1 %convolution_convert_fusion = bf16[192,512]{1,0:T(8,128)(2,1)S(1)} fusion(bf16[128,512]{1,0:T(8,128)(2,1)} %param.7, s32[128]{0:T(128)S(1)} %convert_add_fusion), kind=kOutput, calls=%fused_computation.1 | convolution fusion | flops 25288704 | bytes 328192 | tf_op jit(solution)/shard_map/dot_general | solution.py:54
  3.8 4.0 %collective-permute-start.2 = (bf16[48,640]{1,0:T(8,128)(2,1)S(1)}, bf16[48,640]{1,0:T(8,128)(2,1)S(1)}, u32[]{:S(2)}, u32[]{:S(2)}) collective-permute-start(bf16[48,640]{1,0:T(8,128)(2,1)S(1)} %get-tuple-element.17), channel_id=1, source_target_pairs={{0,24},{8,16},{16,8},{24,0},{1,25},{9,17},{17,9},{25,1},{2,26},{10... | collective-permute-start | bytes 184328 | tf_op jit(solution)/shard_map/ppermute | solution.py:31
  7.8 0.5 %collective-permute-start.1 = (bf16[48,640]{1,0:T(8,128)(2,1)S(1)}, bf16[48,640]{1,0:T(8,128)(2,1)S(1)}, u32[]{:S(2)}, u32[]{:S(2)}) collective-permute-start(bf16[48,640]{1,0:T(8,128)(2,1)S(1)} %get-tuple-element.18), channel_id=1, source_target_pairs={{0,16},{8,24},{16,0},{24,8},{1,17},{9,25},{17,1},{25,9},{2,18},{10... | collective-permute-start | bytes 184328 | tf_op jit(solution)/shard_map/ppermute | solution.py:31
  8.4 1.6 %collective-permute-done.2 = bf16[48,640]{1,0:T(8,128)(2,1)S(1)} collective-permute-done((bf16[48,640]{1,0:T(8,128)(2,1)S(1)}, bf16[48,640]{1,0:T(8,128)(2,1)S(1)}, u32[]{:S(2)}, u32[]{:S(2)}) %collective-permute-start.2) | collective-permute-done | bytes 61472 | tf_op jit(solution)/shard_map/ppermute | solution.py:31
  10.0 2.0 %collective-permute-done.1 = bf16[48,640]{1,0:T(8,128)(2,1)S(1)} collective-permute-done((bf16[48,640]{1,0:T(8,128)(2,1)S(1)}, bf16[48,640]{1,0:T(8,128)(2,1)S(1)}, u32[]{:S(2)}, u32[]{:S(2)}) %collective-permute-start.1) | collective-permute-done | bytes 61472 | tf_op jit(solution)/shard_map/ppermute | solution.py:31
  12.0 0.5 %collective-permute-done = bf16[48,640]{1,0:T(8,128)(2,1)S(1)} collective-permute-done((bf16[48,640]{1,0:T(8,128)(2,1)S(1)}, bf16[48,640]{1,0:T(8,128)(2,1)S(1)}, u32[]{:S(2)}, u32[]{:S(2)}) %collective-permute-start) | collective-permute-done | bytes 61472 | tf_op jit(solution)/shard_map/ppermute | solution.py:31
  12.7 0.8 %copy-done.3 = bf16[1,512,256]{2,1,0:T(8,128)(2,1)S(1)} copy-done((bf16[1,512,256]{2,1,0:T(8,128)(2,1)S(1)}, bf16[1,512,256]{2,1,0:T(8,128)(2,1)}, u32[]{:S(2)}) %copy-start.3) | copy-done | bytes 262168
  13.6 0.4 fusion.5
  14.6 3.7 %collective-permute-start.5 = (f32[48,512]{1,0:T(8,128)S(1)}, f32[48,512]{1,0:T(8,128)S(1)}, u32[]{:S(2)}, u32[]{:S(2)}) collective-permute-start(f32[48,512]{1,0:T(8,128)S(1)} %get-tuple-element.7), channel_id=1, source_target_pairs={{0,3},{1,2},{2,1},{3,0},{4,7},{5,6},{6,5},{7,4},{8,11},{9,10},{10,... | collective-permute-start | bytes 294920 | tf_op jit(solution)/shard_map/ppermute | solution.py:31
  18.3 0.8 %collective-permute-start.3 = (f32[48,512]{1,0:T(8,128)S(1)}, f32[48,512]{1,0:T(8,128)S(1)}, u32[]{:S(2)}, u32[]{:S(2)}) collective-permute-start(f32[48,512]{1,0:T(8,128)S(1)} %get-tuple-element.6), channel_id=1, source_target_pairs={{0,1},{1,0},{2,3},{3,2},{4,5},{5,4},{6,7},{7,6},{8,9},{9,8},{10,11... | collective-permute-start | bytes 294920 | tf_op jit(solution)/shard_map/ppermute | solution.py:31
  19.2 2.9 %collective-permute-done.5 = f32[48,512]{1,0:T(8,128)S(1)} collective-permute-done((f32[48,512]{1,0:T(8,128)S(1)}, f32[48,512]{1,0:T(8,128)S(1)}, u32[]{:S(2)}, u32[]{:S(2)}) %collective-permute-start.5) | collective-permute-done | bytes 98336 | tf_op jit(solution)/shard_map/ppermute | solution.py:31
  22.1 4.2 %collective-permute-done.4 = f32[48,512]{1,0:T(8,128)S(1)} collective-permute-done((f32[48,512]{1,0:T(8,128)S(1)}, f32[48,512]{1,0:T(8,128)S(1)}, u32[]{:S(2)}, u32[]{:S(2)}) %collective-permute-start.4) | collective-permute-done | bytes 98336 | tf_op jit(solution)/shard_map/ppermute | solution.py:31
  26.4 0.6 %collective-permute-start.7 = (bf16[48,512]{1,0:T(8,128)(2,1)S(1)}, bf16[48,512]{1,0:T(8,128)(2,1)S(1)}, u32[]{:S(2)}, u32[]{:S(2)}) collective-permute-start(bf16[48,512]{1,0:T(8,128)(2,1)S(1)} %get-tuple-element.3), channel_id=1, source_target_pairs={{0,1},{1,0},{2,3},{3,2},{4,5},{5,4},{6,7},{7,6},{8,9},{9,8},{10,11... | collective-permute-start | bytes 147464 | tf_op jit(solution)/shard_map/ppermute | solution.py:31
  27.2 2.6 %collective-permute-start.8 = (bf16[48,512]{1,0:T(8,128)(2,1)S(1)}, bf16[48,512]{1,0:T(8,128)(2,1)S(1)}, u32[]{:S(2)}, u32[]{:S(2)}) collective-permute-start(bf16[48,512]{1,0:T(8,128)(2,1)S(1)} %get-tuple-element.3), channel_id=1, source_target_pairs={{0,2},{1,3},{2,0},{3,1},{4,6},{5,7},{6,4},{7,5},{8,10},{9,11},{10,... | collective-permute-start | bytes 147464 | tf_op jit(solution)/shard_map/ppermute | solution.py:31
  29.8 1.3 %collective-permute-start.9 = (bf16[48,512]{1,0:T(8,128)(2,1)S(1)}, bf16[48,512]{1,0:T(8,128)(2,1)S(1)}, u32[]{:S(2)}, u32[]{:S(2)}) collective-permute-start(bf16[48,512]{1,0:T(8,128)(2,1)S(1)} %get-tuple-element.3), channel_id=1, source_target_pairs={{0,3},{1,2},{2,1},{3,0},{4,7},{5,6},{6,5},{7,4},{8,11},{9,10},{10,... | collective-permute-start | bytes 147464 | tf_op jit(solution)/shard_map/ppermute | solution.py:31
  31.1 2.2 %collective-permute-done.8 = bf16[48,512]{1,0:T(8,128)(2,1)S(1)} collective-permute-done((bf16[48,512]{1,0:T(8,128)(2,1)S(1)}, bf16[48,512]{1,0:T(8,128)(2,1)S(1)}, u32[]{:S(2)}, u32[]{:S(2)}) %collective-permute-start.8) | collective-permute-done | bytes 49184 | tf_op jit(solution)/shard_map/ppermute | solution.py:31
  33.3 2.4 %collective-permute-done.9 = bf16[48,512]{1,0:T(8,128)(2,1)S(1)} collective-permute-done((bf16[48,512]{1,0:T(8,128)(2,1)S(1)}, bf16[48,512]{1,0:T(8,128)(2,1)S(1)}, u32[]{:S(2)}, u32[]{:S(2)}) %collective-permute-start.9) | collective-permute-done | bytes 49184 | tf_op jit(solution)/shard_map/ppermute | solution.py:31
  35.7 0.5 %fusion.4 = f32[4,2,64,256]{3,2,1,0:T(8,128)S(1)} fusion(bf16[4,2,64,192]{3,2,1,0:T(8,128)(2,1)S(1)} %bitcast.155, bf16[192,512]{1,0:T(8,128)(2,1)S(1)} %bitcast.143, bf16[512,256]{1,0:T(8,128)(2,1)S(1)} %copy-done, f32[192,256]{1,0:T(8,128)S(1)} %fusion.57), kind=kOutput, calls=%fused_computation.10 | convolution fusion | flops 101105664 | bytes 1376256 | tf_op jit(solution)/shard_map/rd,rh->dh/dot_general | solution.py:94
  36.7 0.6 %collective-permute-start.14 = (f32[4,64,256]{2,1,0:T(8,128)S(1)}, f32[4,64,256]{2,1,0:T(8,128)S(1)}, u32[]{:S(2)}, u32[]{:S(2)}) collective-permute-start(f32[4,64,256]{2,1,0:T(8,128)S(1)} %dynamic-slice_bitcast_fusion), channel_id=1, source_target_pairs={{0,4},{4,0},{1,5},{5,1},{2,6},{6,2},{3,7},{7,3},{8,12},{12,8},{9,1... | collective-permute-start | bytes 786440 | tf_op jit(solution)/shard_map/ppermute | solution.py:31
  37.3 0.5 %collective-permute-done.10 = f32[4,64,256]{2,1,0:T(8,128)S(1)} collective-permute-done((f32[4,64,256]{2,1,0:T(8,128)S(1)}, f32[4,64,256]{2,1,0:T(8,128)S(1)}, u32[]{:S(2)}, u32[]{:S(2)}) %collective-permute-start.10) | collective-permute-done | bytes 262176 | tf_op jit(solution)/shard_map/ppermute | solution.py:31
  37.9 1.5 %collective-permute-start.13 = (bf16[64,256]{1,0:T(8,128)(2,1)S(1)}, bf16[64,256]{1,0:T(8,128)(2,1)S(1)}, u32[]{:S(2)}, u32[]{:S(2)}) collective-permute-start(bf16[64,256]{1,0:T(8,128)(2,1)S(1)} %get-tuple-element.13), channel_id=1, source_target_pairs={{0,24},{8,16},{16,8},{24,0},{1,25},{9,17},{17,9},{25,1},{2,26},{10... | collective-permute-start | bytes 98312 | tf_op jit(solution)/shard_map/ppermute | solution.py:31
  39.4 0.5 %collective-permute-start.12 = (bf16[64,256]{1,0:T(8,128)(2,1)S(1)}, bf16[64,256]{1,0:T(8,128)(2,1)S(1)}, u32[]{:S(2)}, u32[]{:S(2)}) collective-permute-start(bf16[64,256]{1,0:T(8,128)(2,1)S(1)} %get-tuple-element.14), channel_id=1, source_target_pairs={{0,16},{8,24},{16,0},{24,8},{1,17},{9,25},{17,1},{25,9},{2,18},{10... | collective-permute-start | bytes 98312 | tf_op jit(solution)/shard_map/ppermute | solution.py:31
  39.9 1.5 %collective-permute-start.11 = (bf16[64,256]{1,0:T(8,128)(2,1)S(1)}, bf16[64,256]{1,0:T(8,128)(2,1)S(1)}, u32[]{:S(2)}, u32[]{:S(2)}) collective-permute-start(bf16[64,256]{1,0:T(8,128)(2,1)S(1)} %get-tuple-element.12), channel_id=1, source_target_pairs={{0,8},{8,0},{16,24},{24,16},{1,9},{9,1},{17,25},{25,17},{2,10},{10... | collective-permute-start | bytes 98312 | tf_op jit(solution)/shard_map/ppermute | solution.py:31
  41.5 1.5 %collective-permute-start.17 = (bf16[64,256]{1,0:T(8,128)(2,1)S(1)}, bf16[64,256]{1,0:T(8,128)(2,1)S(1)}, u32[]{:S(2)}, u32[]{:S(2)}) collective-permute-start(bf16[64,256]{1,0:T(8,128)(2,1)S(1)} %get-tuple-element.10), channel_id=1, source_target_pairs={{0,24},{8,16},{16,8},{24,0},{1,25},{9,17},{17,9},{25,1},{2,26},{10... | collective-permute-start | bytes 98312 | tf_op jit(solution)/shard_map/ppermute | solution.py:31
  43.1 0.5 %collective-permute-start.16 = (bf16[64,256]{1,0:T(8,128)(2,1)S(1)}, bf16[64,256]{1,0:T(8,128)(2,1)S(1)}, u32[]{:S(2)}, u32[]{:S(2)}) collective-permute-start(bf16[64,256]{1,0:T(8,128)(2,1)S(1)} %get-tuple-element.11), channel_id=1, source_target_pairs={{0,16},{8,24},{16,0},{24,8},{1,17},{9,25},{17,1},{25,9},{2,18},{10... | collective-permute-start | bytes 98312 | tf_op jit(solution)/shard_map/ppermute | solution.py:31
  43.6 1.5 %collective-permute-start.15 = (bf16[64,256]{1,0:T(8,128)(2,1)S(1)}, bf16[64,256]{1,0:T(8,128)(2,1)S(1)}, u32[]{:S(2)}, u32[]{:S(2)}) collective-permute-start(bf16[64,256]{1,0:T(8,128)(2,1)S(1)} %get-tuple-element.9), channel_id=1, source_target_pairs={{0,8},{8,0},{16,24},{24,16},{1,9},{9,1},{17,25},{25,17},{2,10},{10... | collective-permute-start | bytes 98312 | tf_op jit(solution)/shard_map/ppermute | solution.py:31
  45.1 0.6 %fusion.31 = f32[64,256]{1,0:T(8,128)} fusion(bf16[64,256]{1,0:T(8,128)(2,1)S(1)} %collective-permute-done.13, bf16[64,256]{1,0:T(8,128)(2,1)S(1)} %collective-permute-done.12, bf16[64,256]{1,0:T(8,128)(2,1)S(1)} %collective-permute-done.11, f32[4,64,256]{2,1,0:T(8,128)S(1)} %bitcast_add_fusion.1, s32[]{:T(128)S(6)} %select_n.79), kind=kLoop, calls=%fused_computation.53 | loop fusion | flops 98304 | bytes 229380 | tf_op jit(solution)/shard_map/add | solution.py:105
  45.7 0.8 %collective-permute-done.17 = bf16[64,256]{1,0:T(8,128)(2,1)S(1)} collective-permute-done((bf16[64,256]{1,0:T(8,128)(2,1)S(1)}, bf16[64,256]{1,0:T(8,128)(2,1)S(1)}, u32[]{:S(2)}, u32[]{:S(2)}) %collective-permute-start.17) | collective-permute-done | bytes 32800 | tf_op jit(solution)/shard_map/ppermute | solution.py:31
  47.0 0.5 %collective-permute-done.15 = bf16[64,256]{1,0:T(8,128)(2,1)S(1)} collective-permute-done((bf16[64,256]{1,0:T(8,128)(2,1)S(1)}, bf16[64,256]{1,0:T(8,128)(2,1)S(1)}, u32[]{:S(2)}, u32[]{:S(2)}) %collective-permute-start.15) | collective-permute-done | bytes 32800 | tf_op jit(solution)/shard_map/ppermute | solution.py:31
  47.5 0.6 %fusion.29 = f32[64,256]{1,0:T(8,128)} fusion(bf16[64,256]{1,0:T(8,128)(2,1)S(1)} %collective-permute-done.17, bf16[64,256]{1,0:T(8,128)(2,1)S(1)} %collective-permute-done.16, bf16[64,256]{1,0:T(8,128)(2,1)S(1)} %collective-permute-done.15, f32[4,64,256]{2,1,0:T(8,128)S(1)} %bitcast_add_fusion, s32[]{:T(128)S(6)} %select_n.79), kind=kLoop, calls=%fused_computation.50 | loop fusion | flops 98304 | bytes 229380 | tf_op jit(solution)/shard_map/add | solution.py:105
  (55 shorter events, 3.0 us)
Async XLA Ops:
  0.6 13.6 %copy-start = (bf16[512,256]{1,0:T(8,128)(2,1)S(1)}, bf16[512,256]{1,0:T(8,128)(2,1)}, u32[]{:S(2)}) copy-start(bf16[512,256]{1,0:T(8,128)(2,1)} %param.13) | copy-start | bytes 786436
  0.7 0.7 %copy-start.4 = (s32[128,1]{0,1:T(1,128)S(1)}, s32[128,1]{0,1:T(1,128)}, u32[]{:S(2)}) copy-start(s32[128,1]{0,1:T(1,128)} %param.8) | copy-start | bytes 1540
  1.7 0.7 %copy-start.5 = (s32[128,1]{0,1:T(1,128)S(1)}, s32[128,1]{0,1:T(1,128)}, u32[]{:S(2)}) copy-start(s32[128,1]{0,1:T(1,128)} %param.9) | copy-start | bytes 1540
  3.8 6.2 %collective-permute-start.2 = (bf16[48,640]{1,0:T(8,128)(2,1)S(1)}, bf16[48,640]{1,0:T(8,128)(2,1)S(1)}, u32[]{:S(2)}, u32[]{:S(2)}) collective-permute-start(bf16[48,640]{1,0:T(8,128)(2,1)S(1)} %get-tuple-element.17), channel_id=1, source_target_pairs={{0,24},{8,16},{16,8},{24,0},{1,25},{9,17},{17,9},{25,1},{2,26},{10... | collective-permute-start | bytes 184328 | tf_op jit(solution)/shard_map/ppermute | solution.py:31
  7.8 4.2 %collective-permute-start.1 = (bf16[48,640]{1,0:T(8,128)(2,1)S(1)}, bf16[48,640]{1,0:T(8,128)(2,1)S(1)}, u32[]{:S(2)}, u32[]{:S(2)}) collective-permute-start(bf16[48,640]{1,0:T(8,128)(2,1)S(1)} %get-tuple-element.18), channel_id=1, source_target_pairs={{0,16},{8,24},{16,0},{24,8},{1,17},{9,25},{17,1},{25,9},{2,18},{10... | collective-permute-start | bytes 184328 | tf_op jit(solution)/shard_map/ppermute | solution.py:31
  8.3 4.2 %collective-permute-start = (bf16[48,640]{1,0:T(8,128)(2,1)S(1)}, bf16[48,640]{1,0:T(8,128)(2,1)S(1)}, u32[]{:S(2)}, u32[]{:S(2)}) collective-permute-start(bf16[48,640]{1,0:T(8,128)(2,1)S(1)} %get-tuple-element.16), channel_id=1, source_target_pairs={{0,8},{8,0},{16,24},{24,16},{1,9},{9,1},{17,25},{25,17},{2,10},{10... | collective-permute-start | bytes 184328 | tf_op jit(solution)/shard_map/ppermute | solution.py:31
  12.6 1.0 %copy-start.3 = (bf16[1,512,256]{2,1,0:T(8,128)(2,1)S(1)}, bf16[1,512,256]{2,1,0:T(8,128)(2,1)}, u32[]{:S(2)}) copy-start(bf16[1,512,256]{2,1,0:T(8,128)(2,1)} %param.10) | copy-start | bytes 786436
  12.6 1.0 %copy-start.2 = (bf16[1,256,512]{2,1,0:T(8,128)(2,1)S(1)}, bf16[1,256,512]{2,1,0:T(8,128)(2,1)}, u32[]{:S(2)}) copy-start(bf16[1,256,512]{2,1,0:T(8,128)(2,1)} %param.11) | copy-start | bytes 786436
  12.7 1.4 %copy-start.1 = (bf16[512,256]{1,0:T(8,128)(2,1)S(1)}, bf16[512,256]{1,0:T(8,128)(2,1)}, u32[]{:S(2)}) copy-start(bf16[512,256]{1,0:T(8,128)(2,1)} %param.12) | copy-start | bytes 786436
  12.7 6.4 %collective-permute-start.6 = (f32[1,128]{1,0:T(1,128)S(1)}, f32[1,128]{1,0:T(1,128)S(1)}, u32[]{:S(2)}, u32[]{:S(2)}) collective-permute-start(f32[1,128]{1,0:T(1,128)S(1)} %bitcast.157), channel_id=1, source_target_pairs={{0,4},{4,0},{1,5},{5,1},{2,6},{6,2},{3,7},{7,3},{8,12},{12,8},{9,1... | collective-permute-start | bytes 1544 | tf_op jit(solution)/shard_map/ppermute | solution.py:31
  14.6 7.5 %collective-permute-start.5 = (f32[48,512]{1,0:T(8,128)S(1)}, f32[48,512]{1,0:T(8,128)S(1)}, u32[]{:S(2)}, u32[]{:S(2)}) collective-permute-start(f32[48,512]{1,0:T(8,128)S(1)} %get-tuple-element.7), channel_id=1, source_target_pairs={{0,3},{1,2},{2,1},{3,0},{4,7},{5,6},{6,5},{7,4},{8,11},{9,10},{10,... | collective-permute-start | bytes 294920 | tf_op jit(solution)/shard_map/ppermute | solution.py:31
  18.3 8.1 %collective-permute-start.4 = (f32[48,512]{1,0:T(8,128)S(1)}, f32[48,512]{1,0:T(8,128)S(1)}, u32[]{:S(2)}, u32[]{:S(2)}) collective-permute-start(f32[48,512]{1,0:T(8,128)S(1)} %get-tuple-element.8), channel_id=1, source_target_pairs={{0,2},{1,3},{2,0},{3,1},{4,6},{5,7},{6,4},{7,5},{8,10},{9,11},{10,... | collective-permute-start | bytes 294920 | tf_op jit(solution)/shard_map/ppermute | solution.py:31
  18.3 8.1 %collective-permute-start.3 = (f32[48,512]{1,0:T(8,128)S(1)}, f32[48,512]{1,0:T(8,128)S(1)}, u32[]{:S(2)}, u32[]{:S(2)}) collective-permute-start(f32[48,512]{1,0:T(8,128)S(1)} %get-tuple-element.6), channel_id=1, source_target_pairs={{0,1},{1,0},{2,3},{3,2},{4,5},{5,4},{6,7},{7,6},{8,9},{9,8},{10,11... | collective-permute-start | bytes 294920 | tf_op jit(solution)/shard_map/ppermute | solution.py:31
  26.4 4.7 %collective-permute-start.7 = (bf16[48,512]{1,0:T(8,128)(2,1)S(1)}, bf16[48,512]{1,0:T(8,128)(2,1)S(1)}, u32[]{:S(2)}, u32[]{:S(2)}) collective-permute-start(bf16[48,512]{1,0:T(8,128)(2,1)S(1)} %get-tuple-element.3), channel_id=1, source_target_pairs={{0,1},{1,0},{2,3},{3,2},{4,5},{5,4},{6,7},{7,6},{8,9},{9,8},{10,11... | collective-permute-start | bytes 147464 | tf_op jit(solution)/shard_map/ppermute | solution.py:31
  27.2 6.1 %collective-permute-start.8 = (bf16[48,512]{1,0:T(8,128)(2,1)S(1)}, bf16[48,512]{1,0:T(8,128)(2,1)S(1)}, u32[]{:S(2)}, u32[]{:S(2)}) collective-permute-start(bf16[48,512]{1,0:T(8,128)(2,1)S(1)} %get-tuple-element.3), channel_id=1, source_target_pairs={{0,2},{1,3},{2,0},{3,1},{4,6},{5,7},{6,4},{7,5},{8,10},{9,11},{10,... | collective-permute-start | bytes 147464 | tf_op jit(solution)/shard_map/ppermute | solution.py:31
  29.8 5.9 %collective-permute-start.9 = (bf16[48,512]{1,0:T(8,128)(2,1)S(1)}, bf16[48,512]{1,0:T(8,128)(2,1)S(1)}, u32[]{:S(2)}, u32[]{:S(2)}) collective-permute-start(bf16[48,512]{1,0:T(8,128)(2,1)S(1)} %get-tuple-element.3), channel_id=1, source_target_pairs={{0,3},{1,2},{2,1},{3,0},{4,7},{5,6},{6,5},{7,4},{8,11},{9,10},{10,... | collective-permute-start | bytes 147464 | tf_op jit(solution)/shard_map/ppermute | solution.py:31
  36.2 1.6 %collective-permute-start.10 = (f32[4,64,256]{2,1,0:T(8,128)S(1)}, f32[4,64,256]{2,1,0:T(8,128)S(1)}, u32[]{:S(2)}, u32[]{:S(2)}) collective-permute-start(f32[4,64,256]{2,1,0:T(8,128)S(1)} %dynamic-slice_bitcast_fusion.1), channel_id=1, source_target_pairs={{0,4},{4,0},{1,5},{5,1},{2,6},{6,2},{3,7},{7,3},{8,12},{12,8},{9,1... | collective-permute-start | bytes 786440 | tf_op jit(solution)/shard_map/ppermute | solution.py:31
  36.7 4.7 %collective-permute-start.14 = (f32[4,64,256]{2,1,0:T(8,128)S(1)}, f32[4,64,256]{2,1,0:T(8,128)S(1)}, u32[]{:S(2)}, u32[]{:S(2)}) collective-permute-start(f32[4,64,256]{2,1,0:T(8,128)S(1)} %dynamic-slice_bitcast_fusion), channel_id=1, source_target_pairs={{0,4},{4,0},{1,5},{5,1},{2,6},{6,2},{3,7},{7,3},{8,12},{12,8},{9,1... | collective-permute-start | bytes 786440 | tf_op jit(solution)/shard_map/ppermute | solution.py:31
  37.9 5.7 %collective-permute-start.13 = (bf16[64,256]{1,0:T(8,128)(2,1)S(1)}, bf16[64,256]{1,0:T(8,128)(2,1)S(1)}, u32[]{:S(2)}, u32[]{:S(2)}) collective-permute-start(bf16[64,256]{1,0:T(8,128)(2,1)S(1)} %get-tuple-element.13), channel_id=1, source_target_pairs={{0,24},{8,16},{16,8},{24,0},{1,25},{9,17},{17,9},{25,1},{2,26},{10... | collective-permute-start | bytes 98312 | tf_op jit(solution)/shard_map/ppermute | solution.py:31
  39.4 5.6 %collective-permute-start.12 = (bf16[64,256]{1,0:T(8,128)(2,1)S(1)}, bf16[64,256]{1,0:T(8,128)(2,1)S(1)}, u32[]{:S(2)}, u32[]{:S(2)}) collective-permute-start(bf16[64,256]{1,0:T(8,128)(2,1)S(1)} %get-tuple-element.14), channel_id=1, source_target_pairs={{0,16},{8,24},{16,0},{24,8},{1,17},{9,25},{17,1},{25,9},{2,18},{10... | collective-permute-start | bytes 98312 | tf_op jit(solution)/shard_map/ppermute | solution.py:31
  39.9 5.1 %collective-permute-start.11 = (bf16[64,256]{1,0:T(8,128)(2,1)S(1)}, bf16[64,256]{1,0:T(8,128)(2,1)S(1)}, u32[]{:S(2)}, u32[]{:S(2)}) collective-permute-start(bf16[64,256]{1,0:T(8,128)(2,1)S(1)} %get-tuple-element.12), channel_id=1, source_target_pairs={{0,8},{8,0},{16,24},{24,16},{1,9},{9,1},{17,25},{25,17},{2,10},{10... | collective-permute-start | bytes 98312 | tf_op jit(solution)/shard_map/ppermute | solution.py:31
  41.5 5.0 %collective-permute-start.17 = (bf16[64,256]{1,0:T(8,128)(2,1)S(1)}, bf16[64,256]{1,0:T(8,128)(2,1)S(1)}, u32[]{:S(2)}, u32[]{:S(2)}) collective-permute-start(bf16[64,256]{1,0:T(8,128)(2,1)S(1)} %get-tuple-element.10), channel_id=1, source_target_pairs={{0,24},{8,16},{16,8},{24,0},{1,25},{9,17},{17,9},{25,1},{2,26},{10... | collective-permute-start | bytes 98312 | tf_op jit(solution)/shard_map/ppermute | solution.py:31
  43.1 3.9 %collective-permute-start.16 = (bf16[64,256]{1,0:T(8,128)(2,1)S(1)}, bf16[64,256]{1,0:T(8,128)(2,1)S(1)}, u32[]{:S(2)}, u32[]{:S(2)}) collective-permute-start(bf16[64,256]{1,0:T(8,128)(2,1)S(1)} %get-tuple-element.11), channel_id=1, source_target_pairs={{0,16},{8,24},{16,0},{24,8},{1,17},{9,25},{17,1},{25,9},{2,18},{10... | collective-permute-start | bytes 98312 | tf_op jit(solution)/shard_map/ppermute | solution.py:31
  43.6 3.9 %collective-permute-start.15 = (bf16[64,256]{1,0:T(8,128)(2,1)S(1)}, bf16[64,256]{1,0:T(8,128)(2,1)S(1)}, u32[]{:S(2)}, u32[]{:S(2)}) collective-permute-start(bf16[64,256]{1,0:T(8,128)(2,1)S(1)} %get-tuple-element.9), channel_id=1, source_target_pairs={{0,8},{8,0},{16,24},{24,16},{1,9},{9,1},{17,25},{25,17},{2,10},{10... | collective-permute-start | bytes 98312 | tf_op jit(solution)/shard_map/ppermute | solution.py:31

commit v2 on v0

v2 whole, which is shorter than its diff:
```python
import functools

import jax
import jax.numpy as jnp
from jax import lax
from jax.experimental import pallas as pl
from jax.experimental.pallas import tpu as pltpu
from jax.sharding import PartitionSpec as P

LANES = 128
ROW_TILE = 16
VMEM = pl.BlockSpec(memory_space=pltpu.VMEM)


def up_to(value, step):
    return -(-value // step) * step


def is_power(size):
    return size & (size - 1) == 0


def partner_to(size, me, step):
    return me ^ step if is_power(size) else (me + step) % size


def partner_from(size, me, step):
    return me ^ step if is_power(size) else (me + size - step) % size


def send(block, axis, step):
    size = lax.axis_size(axis)
    return lax.ppermute(block, axis, [(i, partner_to(size, i, step)) for i in range(size)])


def call(body, outs, operands, flops):
    moved = sum(a.size * a.dtype.itemsize for a in operands) + sum(
        o.size * o.dtype.itemsize for o in outs
    )
    return pl.pallas_call(
        body,
        out_shape=outs,
        in_specs=[VMEM] * len(operands),
        out_specs=[VMEM] * len(outs),
        cost_estimate=pl.CostEstimate(flops=flops, bytes_accessed=moved, transcendentals=0),
        compiler_params=pltpu.CompilerParams(vmem_limit_bytes=24 * 1024 * 1024),
    )(*operands)


def dot(left, right, contract=((1,), (0,))):
    return lax.dot_general(left, right, (contract, ((), ())), preferred_element_type=jnp.float32)


def dispatch_body(owners, local, room, extra, states, task, batch, *outs):
    rows, width = states.shape
    me = lax.axis_index("teach")
    task_list, batch_list = task[...], batch[...]
    group = up_to(owners * local, ROW_TILE)
    named = lax.broadcasted_iota(jnp.int32, (group, rows), 0) == task_list
    earlier = lax.broadcasted_iota(jnp.int32, (rows, rows), 0) < lax.broadcasted_iota(
        jnp.int32, (rows, rows), 1
    )
    named = named.astype(jnp.float32)
    before = dot(named.astype(jnp.bfloat16), earlier.astype(jnp.float32).astype(jnp.bfloat16))
    before = jnp.sum(before * named, axis=0, keepdims=True).astype(jnp.int32)
    owner = task_list // local if local > 1 else task_list
    step = owner ^ me if is_power(owners) else (owner - me + owners) % owners
    place = step * local + task_list % local if local > 1 else step
    slot = place * room + before
    index = lax.broadcasted_iota(jnp.int32, (owners * local * room, rows), 0)
    chosen = (index == slot).astype(jnp.float32)
    head = (index % (local * room) == 0).astype(jnp.float32)
    member = (lax.broadcasted_iota(jnp.int32, (extra, rows), 0) == batch_list).astype(jnp.float32)
    moved = dot(chosen.astype(jnp.bfloat16), states[...]).astype(jnp.bfloat16)
    tags = dot(
        (chosen + 2.0 * head).astype(jnp.bfloat16), member.astype(jnp.bfloat16), ((1,), (1,))
    ).astype(jnp.bfloat16)
    for k, out in enumerate(outs):
        span = slice(k * local * room, (k + 1) * local * room)
        out[:, :width] = moved[span]
        out[:, width:] = tags[span]


def forward_body(owners, local, room, parts, *refs):
    blocks, refs = refs[:owners], refs[owners:]
    teach_in, teach_out, student_up, student_down = refs[:4]
    rows_out, act_out, slope_out, tags_out, counts_out, own = refs[4:10]
    sends, error = refs[10:-1], refs[-1]
    width = student_up.shape[0]
    full = [block[...] for block in blocks]
    counts = None
    for block in full:
        mine = jnp.floor(block[:1, width:].astype(jnp.float32) * 0.5)
        counts = mine if counts is None else counts + mine
    counts_out[...] = counts
    for l in range(local):
        span = slice(l * owners * room, (l + 1) * owners * room)
        for k, block in enumerate(full):
            start = l * owners * room + k * room
            rows_out[start : start + room] = block[l * room : (l + 1) * room, :width]
            tag = block[l * room : (l + 1) * room, width:].astype(jnp.float32)
            if l == 0:
                head = lax.broadcasted_iota(jnp.int32, tag.shape, 0) == 0
                tag = jnp.where(head, tag - 2.0 * jnp.floor(tag * 0.5), tag)
            tags_out[start : start + room] = tag
        rows = rows_out[span]
        hidden = dot(rows, teach_in[l])
        hidden = (hidden / (1.0 + jnp.exp(-hidden))).astype(jnp.bfloat16)
        labels = dot(hidden, teach_out[l])
        pre = dot(rows, student_up[...])
        sig = 1.0 / (1.0 + jnp.exp(-pre))
        act = (pre * sig).astype(jnp.bfloat16)
        act_out[span] = act
        slope_out[span] = sig * (1.0 + pre * (1.0 - sig))
        error[span] = dot(act, student_down[...], ((1,), (1,))) - labels
    me = lax.axis_index("mdl")
    height = own.shape[0]
    own[...] = error[pl.ds(pl.multiple_of(me * height, 8), height)]
    for k, out in enumerate(sends):
        there = partner_to(parts, me, k + 1)
        out[...] = error[pl.ds(pl.multiple_of(there * height, 8), height)]


def backward_body(parts, *refs):
    chunks, refs = refs[:parts], refs[parts:]
    rows, act, slope, student_down, grad_up, grad_down, scaled = refs
    me = lax.axis_index("mdl")
    height = chunks[0].shape[0]
    for k, chunk in enumerate(chunks):
        there = partner_from(parts, me, k)
        scaled[pl.ds(pl.multiple_of(there * height, 8), height)] = chunk[...].astype(jnp.float32)
    full = scaled[...].astype(jnp.bfloat16)
    grad_down[...] = dot(full, act[...], ((0,), (0,)))
    pre_grad = (dot(full, student_down[...]) * slope[...]).astype(jnp.bfloat16)
    grad_up[...] = dot(rows[...], pre_grad, ((0,), (0,)))


def on_device(states, task_ids, student_batch, teach_in, teach_out, student_up, student_down):
    row_count, width = states.shape
    owners, studs, parts = lax.axis_size("teach"), lax.axis_size("stud"), lax.axis_size("mdl")
    local, _, hidden = teach_in.shape
    actions = teach_out.shape[2]
    units = student_up.shape[1]
    teachers, batches = owners * local, owners * studs
    room = up_to(3 * row_count // (2 * teachers), ROW_TILE)
    extra = up_to(batches, LANES)
    slots = teachers * room
    height = slots // parts
    f32, bf16 = jnp.float32, jnp.bfloat16
    block = jax.ShapeDtypeStruct((local * room, width + extra), bf16)
    blocks = call(
        functools.partial(dispatch_body, owners, local, room, extra),
        [block] * owners,
        (states, task_ids.reshape(1, row_count), student_batch.reshape(1, row_count)),
        2 * slots * row_count * width,
    )
    blocks = [blocks[0]] + [send(blocks[k], "teach", k) for k in range(1, owners)]
    rows, act, slope, tags, counts, own, *outgoing = pl.pallas_call(
        functools.partial(forward_body, owners, local, room, parts),
        out_shape=[
            jax.ShapeDtypeStruct((slots, width), bf16),
            jax.ShapeDtypeStruct((slots, units), bf16),
            jax.ShapeDtypeStruct((slots, units), f32),
            jax.ShapeDtypeStruct((slots, extra), f32),
            jax.ShapeDtypeStruct((1, extra), f32),
        ]
        + [jax.ShapeDtypeStruct((height, actions), f32)] * parts,
        in_specs=[VMEM] * (owners + 4),
        out_specs=[VMEM] * (5 + parts),
        scratch_shapes=[pltpu.VMEM((slots, actions), f32)],
        cost_estimate=pl.CostEstimate(
            flops=2 * slots * 2 * width * (hidden + units), bytes_accessed=2 << 20, transcendentals=0
        ),
        compiler_params=pltpu.CompilerParams(vmem_limit_bytes=24 * 1024 * 1024),
    )(*blocks, teach_in, teach_out, student_up, student_down)
    mine = lax.axis_index("mdl")
    total = own
    for k in range(1, parts):
        total = total + send(outgoing[k - 1], "mdl", k)
    for other in [send(counts, "stud", k) for k in range(1, studs)]:
        counts = counts + other
    weight = jnp.sum(tags * jnp.where(counts > 0, 2.0 / counts, 0.0), axis=1)
    weight = lax.dynamic_index_in_dim(weight.reshape(parts, height), mine, 0, False)
    scaled = (total * weight[:, None]).astype(bf16)
    chunks = [scaled] + [send(scaled, "mdl", k) for k in range(1, parts)]
    grad_up, grad_down = pl.pallas_call(
        functools.partial(backward_body, parts),
        out_shape=[
            jax.ShapeDtypeStruct((width, units), f32),
            jax.ShapeDtypeStruct((actions, units), f32),
        ],
        in_specs=[VMEM] * (parts + 4),
        out_specs=[VMEM] * 2,
        scratch_shapes=[pltpu.VMEM((slots, actions), f32)],
        cost_estimate=pl.CostEstimate(
            flops=6 * slots * width * units, bytes_accessed=2 << 20, transcendentals=0
        ),
        compiler_params=pltpu.CompilerParams(vmem_limit_bytes=24 * 1024 * 1024),
    )(*chunks, rows, act, slope, student_down)
    heights = (width // (owners * studs), actions // (owners * studs))

    def pieces(stud):
        return jnp.concatenate(
            [
                lax.dynamic_index_in_dim(g.reshape(owners, studs, h, units), stud, 1, False)
                for g, h in zip((grad_up, grad_down), heights)
            ],
            axis=1,
        )

    half = pieces(lax.axis_index("stud"))
    for k in range(1, studs):
        half = half + send(pieces(partner_to(studs, lax.axis_index("stud"), k)), "stud", k)
    me = lax.axis_index("teach")
    part = lax.dynamic_index_in_dim(half, me, 0, False)
    arrived = [
        send(lax.dynamic_index_in_dim(half, partner_to(owners, me, k), 0, False).astype(bf16), "teach", k)
        for k in range(1, owners)
    ]
    for piece in arrived:
        part = part + piece.astype(f32)
    return part[: heights[0]], part[heights[0] :]


def solution(mesh):
    in_specs = (
        P(("teach", "stud"), None),
        P(("teach", "stud"), None),
        P(("teach", "stud"), None),
        P("teach", None, "mdl"),
        P("teach", "mdl", None),
        P(None, "mdl"),
        P(None, "mdl"),
    )
    out_specs = (P(("teach", "stud"), "mdl"), P(("teach", "stud"), "mdl"))
    return jax.shard_map(
        on_device, mesh=mesh, in_specs=in_specs, out_specs=out_specs, check_vma=False
    )
```

time: 160 us -> 48.2 us (0.30)
  waiting for transfers between devices: 114 us -> 22 us
  blocking collectives: 13.6 us -> 0 us
  between operations: 13.8 us -> 0.77 us
  starting transfers between devices: 9.11 us -> 17.1 us
  matrix products: 5.19 us -> 0 us
  local copies, waits for them, and re-layouts: 2.82 us -> 6.24 us
    psum x1 -> x0, waiting for transfers between devices: 40.8 us -> none  [on_device(): error = lax.psum(partial_pred, 'mdl') - targets]
    reduce_scatter x1 -> x0, waiting for transfers between devices: 38.2 us -> none  [on_device(): lax.psum_scatter(grad_down, ('teach', 'stud'), scatter_dimension=0, tiled...]
    unnamed x4 -> x0, waiting for transfers between devices: 31.3 us -> none
    ppermute x0 -> x14, waiting for transfers between devices: none -> 22 us  [send(): lax.ppermute(block, axis, [(i, partner_to(size, i, step)) for i in range(...]
    ppermute x0 -> x14, starting transfers between devices: none -> 17.1 us  [send(): lax.ppermute(block, axis, [(i, partner_to(size, i, step)) for i in range(...]
    psum x1 -> x0, blocking collectives: 13.6 us -> none  [on_device(): counts = lax.psum(jnp.sum(member, axis=0), ('teach', 'stud'))]
    all_to_all x2 -> x0, starting transfers between devices: 9.06 us -> none  [the longest x1 5.29 us: on_device(): lax.all_to_all(outgoing, 'teach', split_axis=0, concat_axis=0, tiled=True)]
    dot_general x8 -> x0, matrix products: 5.19 us -> none  [the longest x1 1.19 us: on_device(): jnp.einsum('ntch,tha->ntca', hidden, teach_out, preferred_element_type=jn...]
  transfers between devices with their start and end apart: 5 -> 14, of which waited for: 4 -> 11; matrix products, arithmetic and copies ran while one was open for 2% -> 0% of each run, Pallas kernels for 0% -> 0%
where the time goes in v2:
time: 48.2 us; the launch traced here: 47.9 us
  waiting for transfers between devices  22 us (46%)
  starting transfers between devices  17.1 us (35%)
  local copies, waits for them, and re-layouts  6.24 us (13%)
  Pallas kernels  1.43 us (3%)
  between operations  0.77 us (2%)
    ppermute x14, waiting for transfers between devices, send(): lax.ppermute(block, axis, [(i, partner_to(size, i, step)) for i in range(...  22 us
    ppermute x14, starting transfers between devices, send(): lax.ppermute(block, axis, [(i, partner_to(size, i, step)) for i in range(...  17.1 us
    unnamed x16, local copies, waits for them, and re-layouts  5.36 us
  transfers between devices with their start and end apart: 14, of which 11 were waited for; matrix products, arithmetic and copies ran while one was open for 0% of the time, Pallas kernels for 0%

profile of v2, /device:TPU:0, one launch (start us, length us, event | category | flops | bytes accessed | tf_op | source)
XLA Modules:
  0.0 47.9 jit_solution(9620017947084658250)
XLA Ops:
  0.6 0.6 %copy-done.6 = s32[128,1]{0,1:T(1,128)S(1)} copy-done((s32[128,1]{0,1:T(1,128)S(1)}, s32[128,1]{0,1:T(1,128)}, u32[]{:S(2)}) %copy-start.6) | copy-done | bytes 536
  1.3 0.9 %copy-done.5 = bf16[128,512]{1,0:T(8,128)(2,1)S(1)} copy-done((bf16[128,512]{1,0:T(8,128)(2,1)S(1)}, bf16[128,512]{1,0:T(8,128)(2,1)}, u32[]{:S(2)}) %copy-start.5) | copy-done | bytes 131096
  2.2 0.4 shard_map.86
  2.6 3.0 %collective-permute-start = (bf16[48,640]{1,0:T(8,128)(2,1)S(1)}, bf16[48,640]{1,0:T(8,128)(2,1)S(1)}, u32[]{:S(2)}, u32[]{:S(2)}) collective-permute-start(bf16[48,640]{1,0:T(8,128)(2,1)S(1)} %get-tuple-element.18), channel_id=1, source_target_pairs={{0,8},{8,0},{16,24},{24,16},{1,9},{9,1},{17,25},{25,17},{2,10},{10... | collective-permute-start | bytes 184328 | tf_op jit(solution)/shard_map/ppermute | solution.py:33
  5.6 1.5 %collective-permute-start.1 = (bf16[48,640]{1,0:T(8,128)(2,1)S(1)}, bf16[48,640]{1,0:T(8,128)(2,1)S(1)}, u32[]{:S(2)}, u32[]{:S(2)}) collective-permute-start(bf16[48,640]{1,0:T(8,128)(2,1)S(1)} %get-tuple-element.19), channel_id=1, source_target_pairs={{0,16},{8,24},{16,0},{24,8},{1,17},{9,25},{17,1},{25,9},{2,18},{10... | collective-permute-start | bytes 184328 | tf_op jit(solution)/shard_map/ppermute | solution.py:33
  7.1 0.7 %collective-permute-done.refs_1_ = bf16[48,640]{1,0:T(8,128)(2,1)S(1)} collective-permute-done((bf16[48,640]{1,0:T(8,128)(2,1)S(1)}, bf16[48,640]{1,0:T(8,128)(2,1)S(1)}, u32[]{:S(2)}, u32[]{:S(2)}) %collective-permute-start) | collective-permute-done | bytes 61472 | tf_op jit(solution)/shard_map/ppermute | solution.py:33
  7.8 2.0 %collective-permute-done.1.refs_2_ = bf16[48,640]{1,0:T(8,128)(2,1)S(1)} collective-permute-done((bf16[48,640]{1,0:T(8,128)(2,1)S(1)}, bf16[48,640]{1,0:T(8,128)(2,1)S(1)}, u32[]{:S(2)}, u32[]{:S(2)}) %collective-permute-start.1) | collective-permute-done | bytes 61472 | tf_op jit(solution)/shard_map/ppermute | solution.py:33
  9.8 2.4 %collective-permute-done.2.refs_3_ = bf16[48,640]{1,0:T(8,128)(2,1)S(1)} collective-permute-done((bf16[48,640]{1,0:T(8,128)(2,1)S(1)}, bf16[48,640]{1,0:T(8,128)(2,1)S(1)}, u32[]{:S(2)}, u32[]{:S(2)}) %collective-permute-start.2) | collective-permute-done | bytes 61472 | tf_op jit(solution)/shard_map/ppermute | solution.py:33
  12.2 0.9 %copy-done = bf16[512,256]{1,0:T(8,128)(2,1)S(1)} copy-done((bf16[512,256]{1,0:T(8,128)(2,1)S(1)}, bf16[512,256]{1,0:T(8,128)(2,1)}, u32[]{:S(2)}) %copy-start) | copy-done | bytes 262168
  13.2 0.9 %copy-done.2 = bf16[1,512,256]{2,1,0:T(8,128)(2,1)S(1)} copy-done((bf16[1,512,256]{2,1,0:T(8,128)(2,1)S(1)}, bf16[1,512,256]{2,1,0:T(8,128)(2,1)}, u32[]{:S(2)}) %copy-start.2) | copy-done | bytes 262168
  14.1 0.9 %copy-done.3 = bf16[1,256,512]{2,1,0:T(8,128)(2,1)S(1)} copy-done((bf16[1,256,512]{2,1,0:T(8,128)(2,1)S(1)}, bf16[1,256,512]{2,1,0:T(8,128)(2,1)}, u32[]{:S(2)}) %copy-start.3) | copy-done | bytes 262168
  15.1 0.9 %copy-done.4 = bf16[512,256]{1,0:T(8,128)(2,1)S(1)} copy-done((bf16[512,256]{1,0:T(8,128)(2,1)S(1)}, bf16[512,256]{1,0:T(8,128)(2,1)}, u32[]{:S(2)}) %copy-start.4) | copy-done | bytes 262168
  16.0 0.6 %shard_map.87 = (bf16[192,512]{1,0:T(8,128)(2,1)S(1)}, bf16[192,256]{1,0:T(8,128)(2,1)S(1)}, f32[192,256]{1,0:T(8,128)S(1)}, f32[192,128]{1,0:T(8,128)S(1)}, f32...) custom-call(bf16[48,640]{1,0:T(8,128)(2,1)S(1)} %get-tuple-element.1, ...), custom_call_target="tpu_custom_call" | custom-call | flops 201326592 | bytes 2097152 | tf_op jit(solution)/shard_map/pallas_call | solution.py:158
  16.7 1.6 %collective-permute-start.3 = (f32[48,512]{1,0:T(8,128)S(1)}, f32[48,512]{1,0:T(8,128)S(1)}, u32[]{:S(2)}, u32[]{:S(2)}) collective-permute-start(f32[48,512]{1,0:T(8,128)S(1)} %get-tuple-element.22), channel_id=1, source_target_pairs={{0,1},{1,0},{2,3},{3,2},{4,5},{5,4},{6,7},{7,6},{8,9},{9,8},{10,11... | collective-permute-start | bytes 294920 | tf_op jit(solution)/shard_map/ppermute | solution.py:33
  18.3 2.6 %collective-permute-start.4 = (f32[48,512]{1,0:T(8,128)S(1)}, f32[48,512]{1,0:T(8,128)S(1)}, u32[]{:S(2)}, u32[]{:S(2)}) collective-permute-start(f32[48,512]{1,0:T(8,128)S(1)} %get-tuple-element.23), channel_id=1, source_target_pairs={{0,2},{1,3},{2,0},{3,1},{4,6},{5,7},{6,4},{7,5},{8,10},{9,11},{10,... | collective-permute-start | bytes 294920 | tf_op jit(solution)/shard_map/ppermute | solution.py:33
  20.9 0.2 collective-permute-start.5
  21.4 0.5 %collective-permute-done.3 = f32[48,512]{1,0:T(8,128)S(1)} collective-permute-done((f32[48,512]{1,0:T(8,128)S(1)}, f32[48,512]{1,0:T(8,128)S(1)}, u32[]{:S(2)}, u32[]{:S(2)}) %collective-permute-start.3) | collective-permute-done | bytes 98336 | tf_op jit(solution)/shard_map/ppermute | solution.py:33
  21.9 7.2 %collective-permute-done.4 = f32[48,512]{1,0:T(8,128)S(1)} collective-permute-done((f32[48,512]{1,0:T(8,128)S(1)}, f32[48,512]{1,0:T(8,128)S(1)}, u32[]{:S(2)}, u32[]{:S(2)}) %collective-permute-start.4) | collective-permute-done | bytes 98336 | tf_op jit(solution)/shard_map/ppermute | solution.py:33
  29.2 1.9 %collective-permute-start.7 = (bf16[48,512]{1,0:T(8,128)(2,1)S(1)}, bf16[48,512]{1,0:T(8,128)(2,1)S(1)}, u32[]{:S(2)}, u32[]{:S(2)}) collective-permute-start(bf16[48,512]{1,0:T(8,128)(2,1)S(1)} %multiply_convert_fusion.refs_0_), channel_id=1, source_target_pairs={{0,1},{1,0},{2,3},{3,2},{4,5},{5,4},{6,7},{7,6},{8,9},{9,8},{10,11... | collective-permute-start | bytes 147464 | tf_op jit(solution)/shard_map/ppermute | solution.py:33
  31.1 1.2 %collective-permute-start.8 = (bf16[48,512]{1,0:T(8,128)(2,1)S(1)}, bf16[48,512]{1,0:T(8,128)(2,1)S(1)}, u32[]{:S(2)}, u32[]{:S(2)}) collective-permute-start(bf16[48,512]{1,0:T(8,128)(2,1)S(1)} %multiply_convert_fusion.refs_0_), channel_id=1, source_target_pairs={{0,2},{1,3},{2,0},{3,1},{4,6},{5,7},{6,4},{7,5},{8,10},{9,11},{10,... | collective-permute-start | bytes 147464 | tf_op jit(solution)/shard_map/ppermute | solution.py:33
  32.3 1.3 %collective-permute-start.9 = (bf16[48,512]{1,0:T(8,128)(2,1)S(1)}, bf16[48,512]{1,0:T(8,128)(2,1)S(1)}, u32[]{:S(2)}, u32[]{:S(2)}) collective-permute-start(bf16[48,512]{1,0:T(8,128)(2,1)S(1)} %multiply_convert_fusion.refs_0_), channel_id=1, source_target_pairs={{0,3},{1,2},{2,1},{3,0},{4,7},{5,6},{6,5},{7,4},{8,11},{9,10},{10,... | collective-permute-start | bytes 147464 | tf_op jit(solution)/shard_map/ppermute | solution.py:33
  33.6 3.5 %collective-permute-done.8.refs_2_ = bf16[48,512]{1,0:T(8,128)(2,1)S(1)} collective-permute-done((bf16[48,512]{1,0:T(8,128)(2,1)S(1)}, bf16[48,512]{1,0:T(8,128)(2,1)S(1)}, u32[]{:S(2)}, u32[]{:S(2)}) %collective-permute-start.8) | collective-permute-done | bytes 49184 | tf_op jit(solution)/shard_map/ppermute | solution.py:33
  37.2 1.1 %collective-permute-done.9.refs_3_ = bf16[48,512]{1,0:T(8,128)(2,1)S(1)} collective-permute-done((bf16[48,512]{1,0:T(8,128)(2,1)S(1)}, bf16[48,512]{1,0:T(8,128)(2,1)S(1)}, u32[]{:S(2)}, u32[]{:S(2)}) %collective-permute-start.9) | collective-permute-done | bytes 49184 | tf_op jit(solution)/shard_map/ppermute | solution.py:33
  38.3 0.5 shard_map.88
  39.0 1.9 %collective-permute-done.10 = f32[4,128,256]{2,1,0:T(8,128)S(1)} collective-permute-done((f32[4,128,256]{2,1,0:T(8,128)S(1)}, f32[4,128,256]{2,1,0:T(8,128)S(1)}, u32[]{:S(2)}, u32[]{:S(2)}) %collective-permute-start.10) | collective-permute-done | bytes 524320 | tf_op jit(solution)/shard_map/ppermute | solution.py:33
  41.0 0.6 %collective-permute-start.11 = (bf16[128,256]{1,0:T(8,128)(2,1)S(1)}, bf16[128,256]{1,0:T(8,128)(2,1)S(1)}, u32[]{:S(2)}, u32[]{:S(2)}) collective-permute-start(bf16[128,256]{1,0:T(8,128)(2,1)S(1)} %get-tuple-element.32), channel_id=1, source_target_pairs={{0,8},{8,0},{16,24},{24,16},{1,9},{9,1},{17,25},{25,17},{2,10},{10... | collective-permute-start | bytes 196616 | tf_op jit(solution)/shard_map/ppermute | solution.py:33
  41.6 0.5 %collective-permute-start.12 = (bf16[128,256]{1,0:T(8,128)(2,1)S(1)}, bf16[128,256]{1,0:T(8,128)(2,1)S(1)}, u32[]{:S(2)}, u32[]{:S(2)}) collective-permute-start(bf16[128,256]{1,0:T(8,128)(2,1)S(1)} %get-tuple-element.34), channel_id=1, source_target_pairs={{0,16},{8,24},{16,0},{24,8},{1,17},{9,25},{17,1},{25,9},{2,18},{10... | collective-permute-start | bytes 196616 | tf_op jit(solution)/shard_map/ppermute | solution.py:33
  42.1 2.4 %collective-permute-start.13 = (bf16[128,256]{1,0:T(8,128)(2,1)S(1)}, bf16[128,256]{1,0:T(8,128)(2,1)S(1)}, u32[]{:S(2)}, u32[]{:S(2)}) collective-permute-start(bf16[128,256]{1,0:T(8,128)(2,1)S(1)} %get-tuple-element.33), channel_id=1, source_target_pairs={{0,24},{8,16},{16,8},{24,0},{1,25},{9,17},{17,9},{25,1},{2,26},{10... | collective-permute-start | bytes 196616 | tf_op jit(solution)/shard_map/ppermute | solution.py:33
  44.5 0.9 %collective-permute-done.11 = bf16[128,256]{1,0:T(8,128)(2,1)S(1)} collective-permute-done((bf16[128,256]{1,0:T(8,128)(2,1)S(1)}, bf16[128,256]{1,0:T(8,128)(2,1)S(1)}, u32[]{:S(2)}, u32[]{:S(2)}) %collective-permute-start.11) | collective-permute-done | bytes 65568 | tf_op jit(solution)/shard_map/ppermute | solution.py:33
  45.5 1.1 %collective-permute-done.12 = bf16[128,256]{1,0:T(8,128)(2,1)S(1)} collective-permute-done((bf16[128,256]{1,0:T(8,128)(2,1)S(1)}, bf16[128,256]{1,0:T(8,128)(2,1)S(1)}, u32[]{:S(2)}, u32[]{:S(2)}) %collective-permute-start.12) | collective-permute-done | bytes 65568 | tf_op jit(solution)/shard_map/ppermute | solution.py:33
  46.5 0.7 %collective-permute-done.13 = bf16[128,256]{1,0:T(8,128)(2,1)S(1)} collective-permute-done((bf16[128,256]{1,0:T(8,128)(2,1)S(1)}, bf16[128,256]{1,0:T(8,128)(2,1)S(1)}, u32[]{:S(2)}, u32[]{:S(2)}) %collective-permute-start.13) | collective-permute-done | bytes 65568 | tf_op jit(solution)/shard_map/ppermute | solution.py:33
  47.3 0.7 %fusion.7 = (f32[64,256]{1,0:T(8,128)}, f32[64,256]{1,0:T(8,128)}) fusion(f32[128,256]{1,0:T(8,128)S(1)} %fusion.1), kind=kLoop, calls=%fused_computation.21 | loop fusion | bytes 262144 | tf_op jit(solution)/shard_map/slice | solution.py:222
  (26 shorter events, 0.8 us)
Async XLA Ops:
  0.6 0.7 %copy-start.6 = (s32[128,1]{0,1:T(1,128)S(1)}, s32[128,1]{0,1:T(1,128)}, u32[]{:S(2)}) copy-start(s32[128,1]{0,1:T(1,128)} %param.8) | copy-start | bytes 1540
  0.6 0.7 %copy-start.7 = (s32[128,1]{0,1:T(1,128)S(1)}, s32[128,1]{0,1:T(1,128)}, u32[]{:S(2)}) copy-start(s32[128,1]{0,1:T(1,128)} %param.9) | copy-start | bytes 1540
  1.3 0.9 %copy-start.5 = (bf16[128,512]{1,0:T(8,128)(2,1)S(1)}, bf16[128,512]{1,0:T(8,128)(2,1)}, u32[]{:S(2)}) copy-start(bf16[128,512]{1,0:T(8,128)(2,1)} %states.1) | copy-start | bytes 393220
  2.6 5.3 %collective-permute-start = (bf16[48,640]{1,0:T(8,128)(2,1)S(1)}, bf16[48,640]{1,0:T(8,128)(2,1)S(1)}, u32[]{:S(2)}, u32[]{:S(2)}) collective-permute-start(bf16[48,640]{1,0:T(8,128)(2,1)S(1)} %get-tuple-element.18), channel_id=1, source_target_pairs={{0,8},{8,0},{16,24},{24,16},{1,9},{9,1},{17,25},{25,17},{2,10},{10... | collective-permute-start | bytes 184328 | tf_op jit(solution)/shard_map/ppermute | solution.py:33
  5.6 4.2 %collective-permute-start.1 = (bf16[48,640]{1,0:T(8,128)(2,1)S(1)}, bf16[48,640]{1,0:T(8,128)(2,1)S(1)}, u32[]{:S(2)}, u32[]{:S(2)}) collective-permute-start(bf16[48,640]{1,0:T(8,128)(2,1)S(1)} %get-tuple-element.19), channel_id=1, source_target_pairs={{0,16},{8,24},{16,0},{24,8},{1,17},{9,25},{17,1},{25,9},{2,18},{10... | collective-permute-start | bytes 184328 | tf_op jit(solution)/shard_map/ppermute | solution.py:33
  7.1 5.1 %collective-permute-start.2 = (bf16[48,640]{1,0:T(8,128)(2,1)S(1)}, bf16[48,640]{1,0:T(8,128)(2,1)S(1)}, u32[]{:S(2)}, u32[]{:S(2)}) collective-permute-start(bf16[48,640]{1,0:T(8,128)(2,1)S(1)} %get-tuple-element.20), channel_id=1, source_target_pairs={{0,24},{8,16},{16,8},{24,0},{1,25},{9,17},{17,9},{25,1},{2,26},{10... | collective-permute-start | bytes 184328 | tf_op jit(solution)/shard_map/ppermute | solution.py:33
  12.2 1.0 %copy-start = (bf16[512,256]{1,0:T(8,128)(2,1)S(1)}, bf16[512,256]{1,0:T(8,128)(2,1)}, u32[]{:S(2)}) copy-start(bf16[512,256]{1,0:T(8,128)(2,1)} %refs_7_.3) | copy-start | bytes 786436
  13.2 0.9 %copy-start.2 = (bf16[1,512,256]{2,1,0:T(8,128)(2,1)S(1)}, bf16[1,512,256]{2,1,0:T(8,128)(2,1)}, u32[]{:S(2)}) copy-start(bf16[1,512,256]{2,1,0:T(8,128)(2,1)} %refs_4_.1) | copy-start | bytes 786436
  14.1 0.9 %copy-start.3 = (bf16[1,256,512]{2,1,0:T(8,128)(2,1)S(1)}, bf16[1,256,512]{2,1,0:T(8,128)(2,1)}, u32[]{:S(2)}) copy-start(bf16[1,256,512]{2,1,0:T(8,128)(2,1)} %refs_5_.1) | copy-start | bytes 786436
  15.1 0.9 %copy-start.4 = (bf16[512,256]{1,0:T(8,128)(2,1)S(1)}, bf16[512,256]{1,0:T(8,128)(2,1)}, u32[]{:S(2)}) copy-start(bf16[512,256]{1,0:T(8,128)(2,1)} %refs_6_.1) | copy-start | bytes 786436
  16.6 4.5 %collective-permute-start.6 = (f32[1,128]{1,0:T(1,128)S(1)}, f32[1,128]{1,0:T(1,128)S(1)}, u32[]{:S(2)}, u32[]{:S(2)}) collective-permute-start(f32[1,128]{1,0:T(1,128)S(1)} %get-tuple-element.26), channel_id=1, source_target_pairs={{0,4},{4,0},{1,5},{5,1},{2,6},{6,2},{3,7},{7,3},{8,12},{12,8},{9,1... | collective-permute-start | bytes 1544 | tf_op jit(solution)/shard_map/ppermute | solution.py:33
  16.7 5.2 %collective-permute-start.3 = (f32[48,512]{1,0:T(8,128)S(1)}, f32[48,512]{1,0:T(8,128)S(1)}, u32[]{:S(2)}, u32[]{:S(2)}) collective-permute-start(f32[48,512]{1,0:T(8,128)S(1)} %get-tuple-element.22), channel_id=1, source_target_pairs={{0,1},{1,0},{2,3},{3,2},{4,5},{5,4},{6,7},{7,6},{8,9},{9,8},{10,11... | collective-permute-start | bytes 294920 | tf_op jit(solution)/shard_map/ppermute | solution.py:33
  18.3 10.8 %collective-permute-start.4 = (f32[48,512]{1,0:T(8,128)S(1)}, f32[48,512]{1,0:T(8,128)S(1)}, u32[]{:S(2)}, u32[]{:S(2)}) collective-permute-start(f32[48,512]{1,0:T(8,128)S(1)} %get-tuple-element.23), channel_id=1, source_target_pairs={{0,2},{1,3},{2,0},{3,1},{4,6},{5,7},{6,4},{7,5},{8,10},{9,11},{10,... | collective-permute-start | bytes 294920 | tf_op jit(solution)/shard_map/ppermute | solution.py:33
  20.9 8.2 %collective-permute-start.5 = (f32[48,512]{1,0:T(8,128)S(1)}, f32[48,512]{1,0:T(8,128)S(1)}, u32[]{:S(2)}, u32[]{:S(2)}) collective-permute-start(f32[48,512]{1,0:T(8,128)S(1)} %get-tuple-element.24), channel_id=1, source_target_pairs={{0,3},{1,2},{2,1},{3,0},{4,7},{5,6},{6,5},{7,4},{8,11},{9,10},{10,... | collective-permute-start | bytes 294920 | tf_op jit(solution)/shard_map/ppermute | solution.py:33
  21.3 17.0 %copy-start.1 = (bf16[512,256]{1,0:T(8,128)(2,1)S(1)}, bf16[512,256]{1,0:T(8,128)(2,1)}, u32[]{:S(2)}) copy-start(bf16[512,256]{1,0:T(8,128)(2,1)} %refs_7_.3) | copy-start | bytes 786436
  29.2 4.5 %collective-permute-start.7 = (bf16[48,512]{1,0:T(8,128)(2,1)S(1)}, bf16[48,512]{1,0:T(8,128)(2,1)S(1)}, u32[]{:S(2)}, u32[]{:S(2)}) collective-permute-start(bf16[48,512]{1,0:T(8,128)(2,1)S(1)} %multiply_convert_fusion.refs_0_), channel_id=1, source_target_pairs={{0,1},{1,0},{2,3},{3,2},{4,5},{5,4},{6,7},{7,6},{8,9},{9,8},{10,11... | collective-permute-start | bytes 147464 | tf_op jit(solution)/shard_map/ppermute | solution.py:33
  31.1 6.0 %collective-permute-start.8 = (bf16[48,512]{1,0:T(8,128)(2,1)S(1)}, bf16[48,512]{1,0:T(8,128)(2,1)S(1)}, u32[]{:S(2)}, u32[]{:S(2)}) collective-permute-start(bf16[48,512]{1,0:T(8,128)(2,1)S(1)} %multiply_convert_fusion.refs_0_), channel_id=1, source_target_pairs={{0,2},{1,3},{2,0},{3,1},{4,6},{5,7},{6,4},{7,5},{8,10},{9,11},{10,... | collective-permute-start | bytes 147464 | tf_op jit(solution)/shard_map/ppermute | solution.py:33
  32.3 5.9 %collective-permute-start.9 = (bf16[48,512]{1,0:T(8,128)(2,1)S(1)}, bf16[48,512]{1,0:T(8,128)(2,1)S(1)}, u32[]{:S(2)}, u32[]{:S(2)}) collective-permute-start(bf16[48,512]{1,0:T(8,128)(2,1)S(1)} %multiply_convert_fusion.refs_0_), channel_id=1, source_target_pairs={{0,3},{1,2},{2,1},{3,0},{4,7},{5,6},{6,5},{7,4},{8,11},{9,10},{10,... | collective-permute-start | bytes 147464 | tf_op jit(solution)/shard_map/ppermute | solution.py:33
  38.9 2.0 %collective-permute-start.10 = (f32[4,128,256]{2,1,0:T(8,128)S(1)}, f32[4,128,256]{2,1,0:T(8,128)S(1)}, u32[]{:S(2)}, u32[]{:S(2)}) collective-permute-start(f32[4,128,256]{2,1,0:T(8,128)S(1)} %pad_maximum_fusion), channel_id=1, source_target_pairs={{0,4},{4,0},{1,5},{5,1},{2,6},{6,2},{3,7},{7,3},{8,12},{12,8},{9,1... | collective-permute-start | bytes 1572872 | tf_op jit(solution)/shard_map/ppermute | solution.py:33
  41.0 4.5 %collective-permute-start.11 = (bf16[128,256]{1,0:T(8,128)(2,1)S(1)}, bf16[128,256]{1,0:T(8,128)(2,1)S(1)}, u32[]{:S(2)}, u32[]{:S(2)}) collective-permute-start(bf16[128,256]{1,0:T(8,128)(2,1)S(1)} %get-tuple-element.32), channel_id=1, source_target_pairs={{0,8},{8,0},{16,24},{24,16},{1,9},{9,1},{17,25},{25,17},{2,10},{10... | collective-permute-start | bytes 196616 | tf_op jit(solution)/shard_map/ppermute | solution.py:33
  41.6 5.0 %collective-permute-start.12 = (bf16[128,256]{1,0:T(8,128)(2,1)S(1)}, bf16[128,256]{1,0:T(8,128)(2,1)S(1)}, u32[]{:S(2)}, u32[]{:S(2)}) collective-permute-start(bf16[128,256]{1,0:T(8,128)(2,1)S(1)} %get-tuple-element.34), channel_id=1, source_target_pairs={{0,16},{8,24},{16,0},{24,8},{1,17},{9,25},{17,1},{25,9},{2,18},{10... | collective-permute-start | bytes 196616 | tf_op jit(solution)/shard_map/ppermute | solution.py:33
  42.1 5.2 %collective-permute-start.13 = (bf16[128,256]{1,0:T(8,128)(2,1)S(1)}, bf16[128,256]{1,0:T(8,128)(2,1)S(1)}, u32[]{:S(2)}, u32[]{:S(2)}) collective-permute-start(bf16[128,256]{1,0:T(8,128)(2,1)S(1)} %get-tuple-element.33), channel_id=1, source_target_pairs={{0,24},{8,16},{16,8},{24,0},{1,25},{9,17},{17,9},{25,1},{2,26},{10... | collective-permute-start | bytes 196616 | tf_op jit(solution)/shard_map/ppermute | solution.py:33

commit v3 on v2

--- a/solution.py
+++ b/solution.py
@@ -10,6 +10,7 @@
 LANES = 128
 ROW_TILE = 16
 VMEM = pl.BlockSpec(memory_space=pltpu.VMEM)
+HBM = pl.BlockSpec(memory_space=pltpu.HBM)
 
 
 def up_to(value, step):
@@ -33,26 +34,27 @@
     return lax.ppermute(block, axis, [(i, partner_to(size, i, step)) for i in range(size)])
 
 
-def call(body, outs, operands, flops):
-    moved = sum(a.size * a.dtype.itemsize for a in operands) + sum(
-        o.size * o.dtype.itemsize for o in outs
-    )
-    return pl.pallas_call(
-        body,
-        out_shape=outs,
-        in_specs=[VMEM] * len(operands),
-        out_specs=[VMEM] * len(outs),
-        cost_estimate=pl.CostEstimate(flops=flops, bytes_accessed=moved, transcendentals=0),
-        compiler_params=pltpu.CompilerParams(vmem_limit_bytes=24 * 1024 * 1024),
-    )(*operands)
-
-
 def dot(left, right, contract=((1,), (0,))):
     return lax.dot_general(left, right, (contract, ((), ())), preferred_element_type=jnp.float32)
 
 
-def dispatch_body(owners, local, room, extra, states, task, batch, *outs):
+def dispatch_body(owners, local, room, extra, *refs):
+    sources, refs = refs[:3], refs[3:]
+    weights, refs = refs[:4], refs[4:]
+    outs, refs = refs[:owners], refs[owners:]
+    weights_out, refs = refs[:4], refs[4:]
+    states, task, batch, sems = refs
     rows, width = states.shape
+    copies = [
+        pltpu.make_async_copy(source, target, sems.at[i])
+        for i, (source, target) in enumerate(
+            zip((*sources, *weights), (states, task, batch, *weights_out))
+        )
+    ]
+    for i in (1, 2, 0, 3, 4, 5, 6):
+        copies[i].start()
+    copies[1].wait()
+    copies[2].wait()
     me = lax.axis_index("teach")
     task_list, batch_list = task[...], batch[...]
     group = up_to(owners * local, ROW_TILE)
@@ -71,6 +73,7 @@
     chosen = (index == slot).astype(jnp.float32)
     head = (index % (local * room) == 0).astype(jnp.float32)
     member = (lax.broadcasted_iota(jnp.int32, (extra, rows), 0) == batch_list).astype(jnp.float32)
+    copies[0].wait()
     moved = dot(chosen.astype(jnp.bfloat16), states[...]).astype(jnp.bfloat16)
     tags = dot(
         (chosen + 2.0 * head).astype(jnp.bfloat16), member.astype(jnp.bfloat16), ((1,), (1,))
@@ -79,6 +82,8 @@
         span = slice(k * local * room, (k + 1) * local * room)
         out[:, :width] = moved[span]
         out[:, width:] = tags[span]
+    for copy in copies[3:]:
+        copy.wait()
 
 
 def forward_body(owners, local, room, parts, *refs):
@@ -148,12 +153,24 @@
     height = slots // parts
     f32, bf16 = jnp.float32, jnp.bfloat16
     block = jax.ShapeDtypeStruct((local * room, width + extra), bf16)
-    blocks = call(
+    weights = (teach_in, teach_out, student_up, student_down)
+    results = pl.pallas_call(
         functools.partial(dispatch_body, owners, local, room, extra),
-        [block] * owners,
-        (states, task_ids.reshape(1, row_count), student_batch.reshape(1, row_count)),
-        2 * slots * row_count * width,
-    )
+        out_shape=[pltpu.VMEM(block.shape, bf16)] * owners + [pltpu.VMEM(w.shape, w.dtype) for w in weights],
+        in_specs=[HBM] * 7,
+        out_specs=[VMEM] * (owners + 4),
+        scratch_shapes=[
+            pltpu.VMEM(states.shape, states.dtype),
+            pltpu.VMEM((1, row_count), jnp.int32),
+            pltpu.VMEM((1, row_count), jnp.int32),
+            pltpu.SemaphoreType.DMA((7,)),
+        ],
+        cost_estimate=pl.CostEstimate(
+            flops=2 * slots * row_count * width, bytes_accessed=2 << 20, transcendentals=0
+        ),
+        compiler_params=pltpu.CompilerParams(vmem_limit_bytes=56 * 1024 * 1024),
+    )(states, task_ids.reshape(1, row_count), student_batch.reshape(1, row_count), *weights)
+    blocks, weights = results[:owners], results[owners:]
     blocks = [blocks[0]] + [send(blocks[k], "teach", k) for k in range(1, owners)]
     rows, act, slope, tags, counts, own, *outgoing = pl.pallas_call(
         functools.partial(forward_body, owners, local, room, parts),
@@ -172,11 +189,11 @@
             flops=2 * slots * 2 * width * (hidden + units), bytes_accessed=2 << 20, transcendentals=0
         ),
         compiler_params=pltpu.CompilerParams(vmem_limit_bytes=24 * 1024 * 1024),
-    )(*blocks, teach_in, teach_out, student_up, student_down)
+    )(*blocks, *weights)
     mine = lax.axis_index("mdl")
     total = own
-    for k in range(1, parts):
-        total = total + send(outgoing[k - 1], "mdl", k)
+    for piece in [send(outgoing[k - 1], "mdl", k) for k in range(parts - 1, 0, -1)]:
+        total = total + piece
     for other in [send(counts, "stud", k) for k in range(1, studs)]:
         counts = counts + other
     weight = jnp.sum(tags * jnp.where(counts > 0, 2.0 / counts, 0.0), axis=1)
@@ -196,7 +213,7 @@
             flops=6 * slots * width * units, bytes_accessed=2 << 20, transcendentals=0
         ),
         compiler_params=pltpu.CompilerParams(vmem_limit_bytes=24 * 1024 * 1024),
-    )(*chunks, rows, act, slope, student_down)
+    )(*chunks, rows, act, slope, weights[3])
     heights = (width // (owners * studs), actions // (owners * studs))
 
     def pieces(stud):

time: 48.2 us -> 43.7 us (0.907)
  local copies, waits for them, and re-layouts: 6.24 us -> 0.88 us
  Pallas kernels: 1.43 us -> 2.42 us
    unnamed x16 -> x0, local copies, waits for them, and re-layouts: 5.36 us -> none
    pallas_call x1, Pallas kernels: 0.35 us -> 1.34 us  [on_device(): pl.pallas_call(functools.partial(dispatch_body, owners, local, room, extr...]
  transfers between devices with their start and end apart: 14 -> 14, of which waited for: 11 -> 12; matrix products, arithmetic and copies ran while one was open for 0% -> 0% of each run, Pallas kernels for 0% -> 0%
where the time goes in v3:
time: 43.7 us; the launch traced here: 43.6 us
  waiting for transfers between devices  22.1 us (51%)
  starting transfers between devices  17.1 us (39%)
  Pallas kernels  2.42 us (6%)
  local copies, waits for them, and re-layouts  0.88 us (2%)
  between operations  0.74 us (2%)
    ppermute x14, waiting for transfers between devices, send(): lax.ppermute(block, axis, [(i, partner_to(size, i, step)) for i in range(...  22.1 us
    ppermute x14, starting transfers between devices, send(): lax.ppermute(block, axis, [(i, partner_to(size, i, step)) for i in range(...  17.1 us
    pallas_call x1, Pallas kernels, on_device(): pl.pallas_call(functools.partial(dispatch_body, owners, local, room, extr...  1.34 us
  transfers between devices with their start and end apart: 14, of which 12 were waited for; matrix products, arithmetic and copies ran while one was open for 0% of the time, Pallas kernels for 0%

profile of v3, /device:TPU:0, one launch (start us, length us, event | category | flops | bytes accessed | tf_op | source)
XLA Modules:
  0.0 43.6 jit_solution(13860818676292584390)
XLA Ops:
  0.6 1.3 %shard_map.86 = (bf16[48,640]{1,0:T(8,128)(2,1)S(1)}, bf16[48,640]{1,0:T(8,128)(2,1)S(1)}, bf16[48,640]{1,0:T(8,128)(2,1)S(1)}, bf16[48,640]{1,0:T(8,128)(2,1)S(...) custom-call(bf16[128,512]{1,0:T(8,128)(2,1)} %refs_0_.1, ...), custom_call_target="tpu_custom_call" | custom-call | flops 25165824 | bytes 2097152 | tf_op jit(solution)/shard_map/pallas_call | solution.py:157
  2.0 3.0 %collective-permute-start = (bf16[48,640]{1,0:T(8,128)(2,1)S(1)}, bf16[48,640]{1,0:T(8,128)(2,1)S(1)}, u32[]{:S(2)}, u32[]{:S(2)}) collective-permute-start(bf16[48,640]{1,0:T(8,128)(2,1)S(1)} %get-tuple-element.22), channel_id=1, source_target_pairs={{0,8},{8,0},{16,24},{24,16},{1,9},{9,1},{17,25},{25,17},{2,10},{10... | collective-permute-start | bytes 184328 | tf_op jit(solution)/shard_map/ppermute | solution.py:34
  5.0 1.5 %collective-permute-start.1 = (bf16[48,640]{1,0:T(8,128)(2,1)S(1)}, bf16[48,640]{1,0:T(8,128)(2,1)S(1)}, u32[]{:S(2)}, u32[]{:S(2)}) collective-permute-start(bf16[48,640]{1,0:T(8,128)(2,1)S(1)} %get-tuple-element.23), channel_id=1, source_target_pairs={{0,16},{8,24},{16,0},{24,8},{1,17},{9,25},{17,1},{25,9},{2,18},{10... | collective-permute-start | bytes 184328 | tf_op jit(solution)/shard_map/ppermute | solution.py:34
  6.5 0.7 %collective-permute-done.refs_1_ = bf16[48,640]{1,0:T(8,128)(2,1)S(1)} collective-permute-done((bf16[48,640]{1,0:T(8,128)(2,1)S(1)}, bf16[48,640]{1,0:T(8,128)(2,1)S(1)}, u32[]{:S(2)}, u32[]{:S(2)}) %collective-permute-start) | collective-permute-done | bytes 61472 | tf_op jit(solution)/shard_map/ppermute | solution.py:34
  7.3 2.0 %collective-permute-done.1.refs_2_ = bf16[48,640]{1,0:T(8,128)(2,1)S(1)} collective-permute-done((bf16[48,640]{1,0:T(8,128)(2,1)S(1)}, bf16[48,640]{1,0:T(8,128)(2,1)S(1)}, u32[]{:S(2)}, u32[]{:S(2)}) %collective-permute-start.1) | collective-permute-done | bytes 61472 | tf_op jit(solution)/shard_map/ppermute | solution.py:34
  9.2 2.4 %collective-permute-done.2.refs_3_ = bf16[48,640]{1,0:T(8,128)(2,1)S(1)} collective-permute-done((bf16[48,640]{1,0:T(8,128)(2,1)S(1)}, bf16[48,640]{1,0:T(8,128)(2,1)S(1)}, u32[]{:S(2)}, u32[]{:S(2)}) %collective-permute-start.2) | collective-permute-done | bytes 61472 | tf_op jit(solution)/shard_map/ppermute | solution.py:34
  11.6 0.6 %shard_map.87 = (bf16[192,512]{1,0:T(8,128)(2,1)S(1)}, bf16[192,256]{1,0:T(8,128)(2,1)S(1)}, f32[192,256]{1,0:T(8,128)S(1)}, f32[192,128]{1,0:T(8,128)S(1)}, f32...) custom-call(bf16[48,640]{1,0:T(8,128)(2,1)S(1)} %get-tuple-element.2, ...), custom_call_target="tpu_custom_call" | custom-call | flops 201326592 | bytes 2097152 | tf_op jit(solution)/shard_map/pallas_call | solution.py:175
  12.2 0.1 collective-permute-start.6
  12.3 3.7 %collective-permute-start.3 = (f32[48,512]{1,0:T(8,128)S(1)}, f32[48,512]{1,0:T(8,128)S(1)}, u32[]{:S(2)}, u32[]{:S(2)}) collective-permute-start(f32[48,512]{1,0:T(8,128)S(1)} %get-tuple-element.30), channel_id=1, source_target_pairs={{0,3},{1,2},{2,1},{3,0},{4,7},{5,6},{6,5},{7,4},{8,11},{9,10},{10,... | collective-permute-start | bytes 294920 | tf_op jit(solution)/shard_map/ppermute | solution.py:34
  16.0 0.8 %collective-permute-start.5 = (f32[48,512]{1,0:T(8,128)S(1)}, f32[48,512]{1,0:T(8,128)S(1)}, u32[]{:S(2)}, u32[]{:S(2)}) collective-permute-start(f32[48,512]{1,0:T(8,128)S(1)} %get-tuple-element.32), channel_id=1, source_target_pairs={{0,1},{1,0},{2,3},{3,2},{4,5},{5,4},{6,7},{7,6},{8,9},{9,8},{10,11... | collective-permute-start | bytes 294920 | tf_op jit(solution)/shard_map/ppermute | solution.py:34
  16.8 0.1 multiply_reduce_fusion
  16.9 0.1 reshape.28
  17.0 2.9 %collective-permute-done.3 = f32[48,512]{1,0:T(8,128)S(1)} collective-permute-done((f32[48,512]{1,0:T(8,128)S(1)}, f32[48,512]{1,0:T(8,128)S(1)}, u32[]{:S(2)}, u32[]{:S(2)}) %collective-permute-start.3) | collective-permute-done | bytes 98336 | tf_op jit(solution)/shard_map/ppermute | solution.py:34
  19.9 5.0 %collective-permute-done.4 = f32[48,512]{1,0:T(8,128)S(1)} collective-permute-done((f32[48,512]{1,0:T(8,128)S(1)}, f32[48,512]{1,0:T(8,128)S(1)}, u32[]{:S(2)}, u32[]{:S(2)}) %collective-permute-start.4) | collective-permute-done | bytes 98336 | tf_op jit(solution)/shard_map/ppermute | solution.py:34
  24.9 0.1 multiply_convert_fusion.refs_0_
  24.9 0.6 %collective-permute-start.7 = (bf16[48,512]{1,0:T(8,128)(2,1)S(1)}, bf16[48,512]{1,0:T(8,128)(2,1)S(1)}, u32[]{:S(2)}, u32[]{:S(2)}) collective-permute-start(bf16[48,512]{1,0:T(8,128)(2,1)S(1)} %multiply_convert_fusion.refs_0_), channel_id=1, source_target_pairs={{0,1},{1,0},{2,3},{3,2},{4,5},{5,4},{6,7},{7,6},{8,9},{9,8},{10,11... | collective-permute-start | bytes 147464 | tf_op jit(solution)/shard_map/ppermute | solution.py:34
  25.5 2.5 %collective-permute-start.8 = (bf16[48,512]{1,0:T(8,128)(2,1)S(1)}, bf16[48,512]{1,0:T(8,128)(2,1)S(1)}, u32[]{:S(2)}, u32[]{:S(2)}) collective-permute-start(bf16[48,512]{1,0:T(8,128)(2,1)S(1)} %multiply_convert_fusion.refs_0_), channel_id=1, source_target_pairs={{0,2},{1,3},{2,0},{3,1},{4,6},{5,7},{6,4},{7,5},{8,10},{9,11},{10,... | collective-permute-start | bytes 147464 | tf_op jit(solution)/shard_map/ppermute | solution.py:34
  28.0 1.3 %collective-permute-start.9 = (bf16[48,512]{1,0:T(8,128)(2,1)S(1)}, bf16[48,512]{1,0:T(8,128)(2,1)S(1)}, u32[]{:S(2)}, u32[]{:S(2)}) collective-permute-start(bf16[48,512]{1,0:T(8,128)(2,1)S(1)} %multiply_convert_fusion.refs_0_), channel_id=1, source_target_pairs={{0,3},{1,2},{2,1},{3,0},{4,7},{5,6},{6,5},{7,4},{8,11},{9,10},{10,... | collective-permute-start | bytes 147464 | tf_op jit(solution)/shard_map/ppermute | solution.py:34
  29.4 1.6 %collective-permute-done.8.refs_2_ = bf16[48,512]{1,0:T(8,128)(2,1)S(1)} collective-permute-done((bf16[48,512]{1,0:T(8,128)(2,1)S(1)}, bf16[48,512]{1,0:T(8,128)(2,1)S(1)}, u32[]{:S(2)}, u32[]{:S(2)}) %collective-permute-start.8) | collective-permute-done | bytes 49184 | tf_op jit(solution)/shard_map/ppermute | solution.py:34
  31.0 2.9 %collective-permute-done.9.refs_3_ = bf16[48,512]{1,0:T(8,128)(2,1)S(1)} collective-permute-done((bf16[48,512]{1,0:T(8,128)(2,1)S(1)}, bf16[48,512]{1,0:T(8,128)(2,1)S(1)}, u32[]{:S(2)}, u32[]{:S(2)}) %collective-permute-start.9) | collective-permute-done | bytes 49184 | tf_op jit(solution)/shard_map/ppermute | solution.py:34
  33.9 0.5 %shard_map.88 = (f32[512,256]{1,0:T(8,128)S(1)}, f32[512,256]{1,0:T(8,128)S(1)}) custom-call(bf16[48,512]{1,0:T(8,128)(2,1)S(1)} %multiply_convert_fusion.refs_0_, bf16[48,512]{1,0:T(8,128)(2,1)S(1)} %collective-permute-done.7.refs_1_, bf16[48,512]{1,0:T(8,128)(2,1)S(1)} %collective-permute-done.8.refs_2_, ...), custom_call_target="tpu_custom_call" | custom-call | flops 150994944 | bytes 2097152 | tf_op jit(solution)/shard_map/pallas_call | solution.py:203
  34.4 0.1 dynamic-slice_bitcast_fusion.2
  34.5 0.1 collective-permute-start.10
  34.6 1.9 %collective-permute-done.10 = f32[4,128,256]{2,1,0:T(8,128)S(1)} collective-permute-done((f32[4,128,256]{2,1,0:T(8,128)S(1)}, f32[4,128,256]{2,1,0:T(8,128)S(1)}, u32[]{:S(2)}, u32[]{:S(2)}) %collective-permute-start.10) | collective-permute-done | bytes 524320 | tf_op jit(solution)/shard_map/ppermute | solution.py:34
  36.5 0.1 maximum_add_fusion
  36.6 0.6 %collective-permute-start.11 = (bf16[128,256]{1,0:T(8,128)(2,1)S(1)}, bf16[128,256]{1,0:T(8,128)(2,1)S(1)}, u32[]{:S(2)}, u32[]{:S(2)}) collective-permute-start(bf16[128,256]{1,0:T(8,128)(2,1)S(1)} %get-tuple-element.40), channel_id=1, source_target_pairs={{0,8},{8,0},{16,24},{24,16},{1,9},{9,1},{17,25},{25,17},{2,10},{10... | collective-permute-start | bytes 196616 | tf_op jit(solution)/shard_map/ppermute | solution.py:34
  37.2 0.5 %collective-permute-start.12 = (bf16[128,256]{1,0:T(8,128)(2,1)S(1)}, bf16[128,256]{1,0:T(8,128)(2,1)S(1)}, u32[]{:S(2)}, u32[]{:S(2)}) collective-permute-start(bf16[128,256]{1,0:T(8,128)(2,1)S(1)} %get-tuple-element.42), channel_id=1, source_target_pairs={{0,16},{8,24},{16,0},{24,8},{1,17},{9,25},{17,1},{25,9},{2,18},{10... | collective-permute-start | bytes 196616 | tf_op jit(solution)/shard_map/ppermute | solution.py:34
  37.7 2.4 %collective-permute-start.13 = (bf16[128,256]{1,0:T(8,128)(2,1)S(1)}, bf16[128,256]{1,0:T(8,128)(2,1)S(1)}, u32[]{:S(2)}, u32[]{:S(2)}) collective-permute-start(bf16[128,256]{1,0:T(8,128)(2,1)S(1)} %get-tuple-element.41), channel_id=1, source_target_pairs={{0,24},{8,16},{16,8},{24,0},{1,25},{9,17},{17,9},{25,1},{2,26},{10... | collective-permute-start | bytes 196616 | tf_op jit(solution)/shard_map/ppermute | solution.py:34
  40.2 0.9 %collective-permute-done.11 = bf16[128,256]{1,0:T(8,128)(2,1)S(1)} collective-permute-done((bf16[128,256]{1,0:T(8,128)(2,1)S(1)}, bf16[128,256]{1,0:T(8,128)(2,1)S(1)}, u32[]{:S(2)}, u32[]{:S(2)}) %collective-permute-start.11) | collective-permute-done | bytes 65568 | tf_op jit(solution)/shard_map/ppermute | solution.py:34
  41.1 1.1 %collective-permute-done.12 = bf16[128,256]{1,0:T(8,128)(2,1)S(1)} collective-permute-done((bf16[128,256]{1,0:T(8,128)(2,1)S(1)}, bf16[128,256]{1,0:T(8,128)(2,1)S(1)}, u32[]{:S(2)}, u32[]{:S(2)}) %collective-permute-start.12) | collective-permute-done | bytes 65568 | tf_op jit(solution)/shard_map/ppermute | solution.py:34
  42.2 0.7 %collective-permute-done.13 = bf16[128,256]{1,0:T(8,128)(2,1)S(1)} collective-permute-done((bf16[128,256]{1,0:T(8,128)(2,1)S(1)}, bf16[128,256]{1,0:T(8,128)(2,1)S(1)}, u32[]{:S(2)}, u32[]{:S(2)}) %collective-permute-start.13) | collective-permute-done | bytes 65568 | tf_op jit(solution)/shard_map/ppermute | solution.py:34
  42.9 0.7 %fusion.7 = (f32[64,256]{1,0:T(8,128)}, f32[64,256]{1,0:T(8,128)}) fusion(f32[128,256]{1,0:T(8,128)S(1)} %fusion.1), kind=kLoop, calls=%fused_computation.21 | loop fusion | bytes 262144 | tf_op jit(solution)/shard_map/slice | solution.py:239
  (10 shorter events, 0.2 us)
Async XLA Ops:
  2.0 5.3 %collective-permute-start = (bf16[48,640]{1,0:T(8,128)(2,1)S(1)}, bf16[48,640]{1,0:T(8,128)(2,1)S(1)}, u32[]{:S(2)}, u32[]{:S(2)}) collective-permute-start(bf16[48,640]{1,0:T(8,128)(2,1)S(1)} %get-tuple-element.22), channel_id=1, source_target_pairs={{0,8},{8,0},{16,24},{24,16},{1,9},{9,1},{17,25},{25,17},{2,10},{10... | collective-permute-start | bytes 184328 | tf_op jit(solution)/shard_map/ppermute | solution.py:34
  5.0 4.2 %collective-permute-start.1 = (bf16[48,640]{1,0:T(8,128)(2,1)S(1)}, bf16[48,640]{1,0:T(8,128)(2,1)S(1)}, u32[]{:S(2)}, u32[]{:S(2)}) collective-permute-start(bf16[48,640]{1,0:T(8,128)(2,1)S(1)} %get-tuple-element.23), channel_id=1, source_target_pairs={{0,16},{8,24},{16,0},{24,8},{1,17},{9,25},{17,1},{25,9},{2,18},{10... | collective-permute-start | bytes 184328 | tf_op jit(solution)/shard_map/ppermute | solution.py:34
  6.5 5.1 %collective-permute-start.2 = (bf16[48,640]{1,0:T(8,128)(2,1)S(1)}, bf16[48,640]{1,0:T(8,128)(2,1)S(1)}, u32[]{:S(2)}, u32[]{:S(2)}) collective-permute-start(bf16[48,640]{1,0:T(8,128)(2,1)S(1)} %get-tuple-element.24), channel_id=1, source_target_pairs={{0,24},{8,16},{16,8},{24,0},{1,25},{9,17},{17,9},{25,1},{2,26},{10... | collective-permute-start | bytes 184328 | tf_op jit(solution)/shard_map/ppermute | solution.py:34
  12.2 4.5 %collective-permute-start.6 = (f32[1,128]{1,0:T(1,128)S(1)}, f32[1,128]{1,0:T(1,128)S(1)}, u32[]{:S(2)}, u32[]{:S(2)}) collective-permute-start(f32[1,128]{1,0:T(1,128)S(1)} %get-tuple-element.34), channel_id=1, source_target_pairs={{0,4},{4,0},{1,5},{5,1},{2,6},{6,2},{3,7},{7,3},{8,12},{12,8},{9,1... | collective-permute-start | bytes 1544 | tf_op jit(solution)/shard_map/ppermute | solution.py:34
  12.3 7.6 %collective-permute-start.3 = (f32[48,512]{1,0:T(8,128)S(1)}, f32[48,512]{1,0:T(8,128)S(1)}, u32[]{:S(2)}, u32[]{:S(2)}) collective-permute-start(f32[48,512]{1,0:T(8,128)S(1)} %get-tuple-element.30), channel_id=1, source_target_pairs={{0,3},{1,2},{2,1},{3,0},{4,7},{5,6},{6,5},{7,4},{8,11},{9,10},{10,... | collective-permute-start | bytes 294920 | tf_op jit(solution)/shard_map/ppermute | solution.py:34
  16.0 8.9 %collective-permute-start.4 = (f32[48,512]{1,0:T(8,128)S(1)}, f32[48,512]{1,0:T(8,128)S(1)}, u32[]{:S(2)}, u32[]{:S(2)}) collective-permute-start(f32[48,512]{1,0:T(8,128)S(1)} %get-tuple-element.31), channel_id=1, source_target_pairs={{0,2},{1,3},{2,0},{3,1},{4,6},{5,7},{6,4},{7,5},{8,10},{9,11},{10,... | collective-permute-start | bytes 294920 | tf_op jit(solution)/shard_map/ppermute | solution.py:34
  16.0 8.9 %collective-permute-start.5 = (f32[48,512]{1,0:T(8,128)S(1)}, f32[48,512]{1,0:T(8,128)S(1)}, u32[]{:S(2)}, u32[]{:S(2)}) collective-permute-start(f32[48,512]{1,0:T(8,128)S(1)} %get-tuple-element.32), channel_id=1, source_target_pairs={{0,1},{1,0},{2,3},{3,2},{4,5},{5,4},{6,7},{7,6},{8,9},{9,8},{10,11... | collective-permute-start | bytes 294920 | tf_op jit(solution)/shard_map/ppermute | solution.py:34
  24.9 4.5 %collective-permute-start.7 = (bf16[48,512]{1,0:T(8,128)(2,1)S(1)}, bf16[48,512]{1,0:T(8,128)(2,1)S(1)}, u32[]{:S(2)}, u32[]{:S(2)}) collective-permute-start(bf16[48,512]{1,0:T(8,128)(2,1)S(1)} %multiply_convert_fusion.refs_0_), channel_id=1, source_target_pairs={{0,1},{1,0},{2,3},{3,2},{4,5},{5,4},{6,7},{7,6},{8,9},{9,8},{10,11... | collective-permute-start | bytes 147464 | tf_op jit(solution)/shard_map/ppermute | solution.py:34
  25.5 5.5 %collective-permute-start.8 = (bf16[48,512]{1,0:T(8,128)(2,1)S(1)}, bf16[48,512]{1,0:T(8,128)(2,1)S(1)}, u32[]{:S(2)}, u32[]{:S(2)}) collective-permute-start(bf16[48,512]{1,0:T(8,128)(2,1)S(1)} %multiply_convert_fusion.refs_0_), channel_id=1, source_target_pairs={{0,2},{1,3},{2,0},{3,1},{4,6},{5,7},{6,4},{7,5},{8,10},{9,11},{10,... | collective-permute-start | bytes 147464 | tf_op jit(solution)/shard_map/ppermute | solution.py:34
  28.0 5.9 %collective-permute-start.9 = (bf16[48,512]{1,0:T(8,128)(2,1)S(1)}, bf16[48,512]{1,0:T(8,128)(2,1)S(1)}, u32[]{:S(2)}, u32[]{:S(2)}) collective-permute-start(bf16[48,512]{1,0:T(8,128)(2,1)S(1)} %multiply_convert_fusion.refs_0_), channel_id=1, source_target_pairs={{0,3},{1,2},{2,1},{3,0},{4,7},{5,6},{6,5},{7,4},{8,11},{9,10},{10,... | collective-permute-start | bytes 147464 | tf_op jit(solution)/shard_map/ppermute | solution.py:34
  34.5 2.0 %collective-permute-start.10 = (f32[4,128,256]{2,1,0:T(8,128)S(1)}, f32[4,128,256]{2,1,0:T(8,128)S(1)}, u32[]{:S(2)}, u32[]{:S(2)}) collective-permute-start(f32[4,128,256]{2,1,0:T(8,128)S(1)} %pad_maximum_fusion), channel_id=1, source_target_pairs={{0,4},{4,0},{1,5},{5,1},{2,6},{6,2},{3,7},{7,3},{8,12},{12,8},{9,1... | collective-permute-start | bytes 1572872 | tf_op jit(solution)/shard_map/ppermute | solution.py:34
  36.6 4.5 %collective-permute-start.11 = (bf16[128,256]{1,0:T(8,128)(2,1)S(1)}, bf16[128,256]{1,0:T(8,128)(2,1)S(1)}, u32[]{:S(2)}, u32[]{:S(2)}) collective-permute-start(bf16[128,256]{1,0:T(8,128)(2,1)S(1)} %get-tuple-element.40), channel_id=1, source_target_pairs={{0,8},{8,0},{16,24},{24,16},{1,9},{9,1},{17,25},{25,17},{2,10},{10... | collective-permute-start | bytes 196616 | tf_op jit(solution)/shard_map/ppermute | solution.py:34
  37.2 5.0 %collective-permute-start.12 = (bf16[128,256]{1,0:T(8,128)(2,1)S(1)}, bf16[128,256]{1,0:T(8,128)(2,1)S(1)}, u32[]{:S(2)}, u32[]{:S(2)}) collective-permute-start(bf16[128,256]{1,0:T(8,128)(2,1)S(1)} %get-tuple-element.42), channel_id=1, source_target_pairs={{0,16},{8,24},{16,0},{24,8},{1,17},{9,25},{17,1},{25,9},{2,18},{10... | collective-permute-start | bytes 196616 | tf_op jit(solution)/shard_map/ppermute | solution.py:34
  37.7 5.2 %collective-permute-start.13 = (bf16[128,256]{1,0:T(8,128)(2,1)S(1)}, bf16[128,256]{1,0:T(8,128)(2,1)S(1)}, u32[]{:S(2)}, u32[]{:S(2)}) collective-permute-start(bf16[128,256]{1,0:T(8,128)(2,1)S(1)} %get-tuple-element.41), channel_id=1, source_target_pairs={{0,24},{8,16},{16,8},{24,0},{1,25},{9,17},{17,9},{25,1},{2,26},{10... | collective-permute-start | bytes 196616 | tf_op jit(solution)/shard_map/ppermute | solution.py:34

commit v4 on v3

--- a/solution.py
+++ b/solution.py
@@ -9,6 +9,8 @@
 
 LANES = 128
 ROW_TILE = 16
+PACK_ROWS = 16
+PACK_TOP = 14.0
 VMEM = pl.BlockSpec(memory_space=pltpu.VMEM)
 HBM = pl.BlockSpec(memory_space=pltpu.HBM)
 
@@ -32,6 +34,18 @@
 def send(block, axis, step):
     size = lax.axis_size(axis)
     return lax.ppermute(block, axis, [(i, partner_to(size, i, step)) for i in range(size)])
+
+
+def pack(value):
+    largest = jnp.max(jnp.abs(value))
+    power = jnp.clip(jnp.ceil(jnp.log2(largest)), -100.0, 100.0)
+    rows = jnp.broadcast_to(power, (PACK_ROWS, value.shape[1]))
+    return jnp.concatenate([value * jnp.exp2(PACK_TOP - power), rows]).astype(jnp.float16)
+
+
+def unpack(block):
+    block = block.astype(jnp.float32)
+    return block[:-PACK_ROWS] * jnp.exp2(block[-1:, :1] - PACK_TOP)
 
 
 def dot(left, right, contract=((1,), (0,))):
@@ -86,11 +100,11 @@
         copy.wait()
 
 
-def forward_body(owners, local, room, parts, *refs):
+def forward_body(owners, local, room, *refs):
     blocks, refs = refs[:owners], refs[owners:]
     teach_in, teach_out, student_up, student_down = refs[:4]
-    rows_out, act_out, slope_out, tags_out, counts_out, own = refs[4:10]
-    sends, error = refs[10:-1], refs[-1]
+    rows_out, act_out, slope_out, tags_out, counts_out, *halves = refs[4:-1]
+    error = refs[-1]
     width = student_up.shape[0]
     full = [block[...] for block in blocks]
     counts = None
@@ -119,20 +133,18 @@
         slope_out[span] = sig * (1.0 + pre * (1.0 - sig))
         error[span] = dot(act, student_down[...], ((1,), (1,))) - labels
     me = lax.axis_index("mdl")
-    height = own.shape[0]
-    own[...] = error[pl.ds(pl.multiple_of(me * height, 8), height)]
-    for k, out in enumerate(sends):
-        there = partner_to(parts, me, k + 1)
-        out[...] = error[pl.ds(pl.multiple_of(there * height, 8), height)]
-
-
-def backward_body(parts, *refs):
-    chunks, refs = refs[:parts], refs[parts:]
+    height = halves[0].shape[0]
+    for k, out in enumerate(halves):
+        out[...] = error[pl.ds(pl.multiple_of(((me & 1) ^ k) * height, 8), height)]
+
+
+def backward_body(*refs):
+    chunks, refs = refs[:2], refs[2:]
     rows, act, slope, student_down, grad_up, grad_down, scaled = refs
     me = lax.axis_index("mdl")
     height = chunks[0].shape[0]
     for k, chunk in enumerate(chunks):
-        there = partner_from(parts, me, k)
+        there = (me & 1) ^ k
         scaled[pl.ds(pl.multiple_of(there * height, 8), height)] = chunk[...].astype(jnp.float32)
     full = scaled[...].astype(jnp.bfloat16)
     grad_down[...] = dot(full, act[...], ((0,), (0,)))
@@ -150,7 +162,7 @@
     room = up_to(3 * row_count // (2 * teachers), ROW_TILE)
     extra = up_to(batches, LANES)
     slots = teachers * room
-    height = slots // parts
+    height = slots // 2
     f32, bf16 = jnp.float32, jnp.bfloat16
     block = jax.ShapeDtypeStruct((local * room, width + extra), bf16)
     weights = (teach_in, teach_out, student_up, student_down)
@@ -172,8 +184,8 @@
     )(states, task_ids.reshape(1, row_count), student_batch.reshape(1, row_count), *weights)
     blocks, weights = results[:owners], results[owners:]
     blocks = [blocks[0]] + [send(blocks[k], "teach", k) for k in range(1, owners)]
-    rows, act, slope, tags, counts, own, *outgoing = pl.pallas_call(
-        functools.partial(forward_body, owners, local, room, parts),
+    rows, act, slope, tags, counts, own, other = pl.pallas_call(
+        functools.partial(forward_body, owners, local, room),
         out_shape=[
             jax.ShapeDtypeStruct((slots, width), bf16),
             jax.ShapeDtypeStruct((slots, units), bf16),
@@ -181,32 +193,33 @@
             jax.ShapeDtypeStruct((slots, extra), f32),
             jax.ShapeDtypeStruct((1, extra), f32),
         ]
-        + [jax.ShapeDtypeStruct((height, actions), f32)] * parts,
+        + [jax.ShapeDtypeStruct((height, actions), f32)] * 2,
         in_specs=[VMEM] * (owners + 4),
-        out_specs=[VMEM] * (5 + parts),
+        out_specs=[VMEM] * 7,
         scratch_shapes=[pltpu.VMEM((slots, actions), f32)],
         cost_estimate=pl.CostEstimate(
             flops=2 * slots * 2 * width * (hidden + units), bytes_accessed=2 << 20, transcendentals=0
         ),
         compiler_params=pltpu.CompilerParams(vmem_limit_bytes=24 * 1024 * 1024),
     )(*blocks, *weights)
-    mine = lax.axis_index("mdl")
-    total = own
-    for piece in [send(outgoing[k - 1], "mdl", k) for k in range(parts - 1, 0, -1)]:
-        total = total + piece
-    for other in [send(counts, "stud", k) for k in range(1, studs)]:
-        counts = counts + other
+    total = own + unpack(send(pack(other), "mdl", 1))
+    step = 2
+    while step < parts:
+        total = total + unpack(send(pack(total), "mdl", step))
+        step *= 2
+    for piece in [send(counts, "stud", k) for k in range(1, studs)]:
+        counts = counts + piece
     weight = jnp.sum(tags * jnp.where(counts > 0, 2.0 / counts, 0.0), axis=1)
-    weight = lax.dynamic_index_in_dim(weight.reshape(parts, height), mine, 0, False)
+    weight = lax.dynamic_index_in_dim(weight.reshape(2, height), lax.axis_index("mdl") & 1, 0, False)
     scaled = (total * weight[:, None]).astype(bf16)
-    chunks = [scaled] + [send(scaled, "mdl", k) for k in range(1, parts)]
+    chunks = [scaled, send(scaled, "mdl", 1)]
     grad_up, grad_down = pl.pallas_call(
-        functools.partial(backward_body, parts),
+        backward_body,
         out_shape=[
             jax.ShapeDtypeStruct((width, units), f32),
             jax.ShapeDtypeStruct((actions, units), f32),
         ],
-        in_specs=[VMEM] * (parts + 4),
+        in_specs=[VMEM] * 6,
         out_specs=[VMEM] * 2,
         scratch_shapes=[pltpu.VMEM((slots, actions), f32)],
         cost_estimate=pl.CostEstimate(

time: 43.7 us -> 46.3 us (1.059)
  starting transfers between devices: 17.1 us -> 13.3 us
  between operations: 0.74 us -> 3.66 us
  other arithmetic: 0.33 us -> 1.65 us
  local copies, waits for them, and re-layouts: 0.88 us -> 1.95 us
  waiting for transfers between devices: 22.1 us -> 23.1 us
    ppermute x14 -> x11, starting transfers between devices: 17.1 us -> 13.3 us  [send(): lax.ppermute(block, axis, [(i, partner_to(size, i, step)) for i in range(...]
    reduce_max x0 -> x2, other arithmetic: none -> 1.24 us  [pack(): largest = jnp.max(jnp.abs(value))]
    ppermute x14 -> x11, waiting for transfers between devices: 22.1 us -> 23.1 us  [send(): lax.ppermute(block, axis, [(i, partner_to(size, i, step)) for i in range(...]
    slice x0 -> x2, local copies, waits for them, and re-layouts: none -> 1.03 us  [unpack(): return block[:-PACK_ROWS] * jnp.exp2(block[-1:, :1] - PACK_TOP)]
  transfers between devices with their start and end apart: 14 -> 11, of which waited for: 12 -> 9; matrix products, arithmetic and copies ran while one was open for 0% -> 2% of each run, Pallas kernels for 0% -> 0%
where the time goes in v4:
time: 46.3 us; the launch traced here: 46.1 us
  waiting for transfers between devices  23.1 us (50%)
  starting transfers between devices  13.3 us (29%)
  between operations  3.66 us (8%)
  Pallas kernels  2.42 us (5%)
  local copies, waits for them, and re-layouts  1.95 us (4%)
  other arithmetic  1.65 us (4%)
    ppermute x11, waiting for transfers between devices, send(): lax.ppermute(block, axis, [(i, partner_to(size, i, step)) for i in range(...  23.1 us
    ppermute x11, starting transfers between devices, send(): lax.ppermute(block, axis, [(i, partner_to(size, i, step)) for i in range(...  13.3 us
    pallas_call x1, Pallas kernels, on_device(): pl.pallas_call(functools.partial(dispatch_body, owners, local, room, extr...  1.34 us
    reduce_max x2, other arithmetic, pack(): largest = jnp.max(jnp.abs(value))  1.24 us
    slice x2, local copies, waits for them, and re-layouts, unpack(): return block[:-PACK_ROWS] * jnp.exp2(block[-1:, :1] - PACK_TOP)  1.03 us
  transfers between devices with their start and end apart: 11, of which 9 were waited for; matrix products, arithmetic and copies ran while one was open for 2% of the time, Pallas kernels for 0%

profile of v4, /device:TPU:0, one launch (start us, length us, event | category | flops | bytes accessed | tf_op | source)
XLA Modules:
  0.0 46.1 jit_solution(18241581085496326917)
XLA Ops:
  0.6 1.3 %shard_map.86 = (bf16[48,640]{1,0:T(8,128)(2,1)S(1)}, bf16[48,640]{1,0:T(8,128)(2,1)S(1)}, bf16[48,640]{1,0:T(8,128)(2,1)S(1)}, bf16[48,640]{1,0:T(8,128)(2,1)S(...) custom-call(bf16[128,512]{1,0:T(8,128)(2,1)} %refs_0_.1, ...), custom_call_target="tpu_custom_call" | custom-call | flops 25165824 | bytes 2097152 | tf_op jit(solution)/shard_map/pallas_call | solution.py:169
  2.0 3.0 %collective-permute-start = (bf16[48,640]{1,0:T(8,128)(2,1)S(1)}, bf16[48,640]{1,0:T(8,128)(2,1)S(1)}, u32[]{:S(2)}, u32[]{:S(2)}) collective-permute-start(bf16[48,640]{1,0:T(8,128)(2,1)S(1)} %get-tuple-element.20), channel_id=1, source_target_pairs={{0,8},{8,0},{16,24},{24,16},{1,9},{9,1},{17,25},{25,17},{2,10},{10... | collective-permute-start | bytes 184328 | tf_op jit(solution)/shard_map/ppermute | solution.py:36
  5.0 1.5 %collective-permute-start.1 = (bf16[48,640]{1,0:T(8,128)(2,1)S(1)}, bf16[48,640]{1,0:T(8,128)(2,1)S(1)}, u32[]{:S(2)}, u32[]{:S(2)}) collective-permute-start(bf16[48,640]{1,0:T(8,128)(2,1)S(1)} %get-tuple-element.21), channel_id=1, source_target_pairs={{0,16},{8,24},{16,0},{24,8},{1,17},{9,25},{17,1},{25,9},{2,18},{10... | collective-permute-start | bytes 184328 | tf_op jit(solution)/shard_map/ppermute | solution.py:36
  6.5 0.7 %collective-permute-done.refs_1_ = bf16[48,640]{1,0:T(8,128)(2,1)S(1)} collective-permute-done((bf16[48,640]{1,0:T(8,128)(2,1)S(1)}, bf16[48,640]{1,0:T(8,128)(2,1)S(1)}, u32[]{:S(2)}, u32[]{:S(2)}) %collective-permute-start) | collective-permute-done | bytes 61472 | tf_op jit(solution)/shard_map/ppermute | solution.py:36
  7.3 2.0 %collective-permute-done.1.refs_2_ = bf16[48,640]{1,0:T(8,128)(2,1)S(1)} collective-permute-done((bf16[48,640]{1,0:T(8,128)(2,1)S(1)}, bf16[48,640]{1,0:T(8,128)(2,1)S(1)}, u32[]{:S(2)}, u32[]{:S(2)}) %collective-permute-start.1) | collective-permute-done | bytes 61472 | tf_op jit(solution)/shard_map/ppermute | solution.py:36
  9.2 2.4 %collective-permute-done.2.refs_3_ = bf16[48,640]{1,0:T(8,128)(2,1)S(1)} collective-permute-done((bf16[48,640]{1,0:T(8,128)(2,1)S(1)}, bf16[48,640]{1,0:T(8,128)(2,1)S(1)}, u32[]{:S(2)}, u32[]{:S(2)}) %collective-permute-start.2) | collective-permute-done | bytes 61472 | tf_op jit(solution)/shard_map/ppermute | solution.py:36
  11.6 0.6 %shard_map.87 = (bf16[192,512]{1,0:T(8,128)(2,1)S(1)}, bf16[192,256]{1,0:T(8,128)(2,1)S(1)}, f32[192,256]{1,0:T(8,128)S(1)}, f32[192,128]{1,0:T(8,128)S(1)}, f32...) custom-call(bf16[48,640]{1,0:T(8,128)(2,1)S(1)} %get-tuple-element.19.refs_0_, ...), custom_call_target="tpu_custom_call" | custom-call | flops 201326592 | bytes 2097152 | tf_op jit(solution)/shard_map/pallas_call | solution.py:187
  12.2 0.1 collective-permute-start.5
  12.3 0.6 %abs_reduce_fusion.1 = f32[]{:T(128)} fusion(f32[96,512]{1,0:T(8,128)S(1)} %get-tuple-element.28), kind=kLoop, calls=%fused_computation.15 | loop fusion | flops 98303 | bytes 196612 | tf_op jit(solution)/shard_map/reduce_max | solution.py:40
  13.7 1.7 %collective-permute-start.3 = (f16[112,512]{1,0:T(8,128)(2,1)S(1)}, f16[112,512]{1,0:T(8,128)(2,1)S(1)}, u32[]{:S(2)}, u32[]{:S(2)}) collective-permute-start(f16[112,512]{1,0:T(8,128)(2,1)S(1)} %concatenate.12), channel_id=1, source_target_pairs={{0,1},{1,0},{2,3},{3,2},{4,5},{5,4},{6,7},{7,6},{8,9},{9,8},{10,11... | collective-permute-start | bytes 344072 | tf_op jit(solution)/shard_map/ppermute | solution.py:36
  15.4 3.9 %collective-permute-done.3 = f16[112,512]{1,0:T(8,128)(2,1)S(1)} collective-permute-done((f16[112,512]{1,0:T(8,128)(2,1)S(1)}, f16[112,512]{1,0:T(8,128)(2,1)S(1)}, u32[]{:S(2)}, u32[]{:S(2)}) %collective-permute-start.3) | collective-permute-done | bytes 114720 | tf_op jit(solution)/shard_map/ppermute | solution.py:36
  19.4 0.5 %slice.25 = f32[1,1]{1,0:T(1,128)} slice(f32[112,512]{1,0:T(8,128)S(1)} %convert_element_type.38), slice={[111:112], [0:1]} | slice | bytes 8 | tf_op jit(solution)/shard_map/slice | solution.py:48
  20.6 0.6 %abs_reduce_fusion = (f32[]{:T(128)}, f32[96,512]{1,0:T(8,128)S(1)}) fusion(f32[96,512]{1,0:T(8,128)S(1)} %get-tuple-element.27, f32[]{:T(128)} %bitcast.2, f32[112,512]{1,0:T(8,128)S(1)} %convert_element_type.38), kind=kLoop, calls=%fused_computation.13 | loop fusion | flops 196607 | bytes 589832 | tf_op jit(solution)/shard_map/reduce_max | solution.py:40
  22.0 2.7 %collective-permute-start.4 = (f16[112,512]{1,0:T(8,128)(2,1)S(1)}, f16[112,512]{1,0:T(8,128)(2,1)S(1)}, u32[]{:S(2)}, u32[]{:S(2)}) collective-permute-start(f16[112,512]{1,0:T(8,128)(2,1)S(1)} %concatenate.13), channel_id=1, source_target_pairs={{0,2},{1,3},{2,0},{3,1},{4,6},{5,7},{6,4},{7,5},{8,10},{9,11},{10,... | collective-permute-start | bytes 344072 | tf_op jit(solution)/shard_map/ppermute | solution.py:36
  24.7 0.1 multiply_reduce_fusion
  24.8 0.1 reshape.28
  24.9 5.3 %collective-permute-done.4 = f16[112,512]{1,0:T(8,128)(2,1)S(1)} collective-permute-done((f16[112,512]{1,0:T(8,128)(2,1)S(1)}, f16[112,512]{1,0:T(8,128)(2,1)S(1)}, u32[]{:S(2)}, u32[]{:S(2)}) %collective-permute-start.4) | collective-permute-done | bytes 114720 | tf_op jit(solution)/shard_map/ppermute | solution.py:36
  30.2 0.5 %slice.27 = f32[1,1]{1,0:T(1,128)} slice(f32[112,512]{1,0:T(8,128)S(1)} %convert_element_type.39), slice={[111:112], [0:1]} | slice | bytes 8 | tf_op jit(solution)/shard_map/slice | solution.py:48
  31.4 0.1 fusion.2.refs_0_
  31.5 0.7 %collective-permute-start.6 = (bf16[96,512]{1,0:T(8,128)(2,1)S(1)}, bf16[96,512]{1,0:T(8,128)(2,1)S(1)}, u32[]{:S(2)}, u32[]{:S(2)}) collective-permute-start(bf16[96,512]{1,0:T(8,128)(2,1)S(1)} %fusion.2.refs_0_), channel_id=1, source_target_pairs={{0,1},{1,0},{2,3},{3,2},{4,5},{5,4},{6,7},{7,6},{8,9},{9,8},{10,11... | collective-permute-start | bytes 294920 | tf_op jit(solution)/shard_map/ppermute | solution.py:36
  32.3 3.9 %collective-permute-done.6.refs_1_ = bf16[96,512]{1,0:T(8,128)(2,1)S(1)} collective-permute-done((bf16[96,512]{1,0:T(8,128)(2,1)S(1)}, bf16[96,512]{1,0:T(8,128)(2,1)S(1)}, u32[]{:S(2)}, u32[]{:S(2)}) %collective-permute-start.6) | collective-permute-done | bytes 98336 | tf_op jit(solution)/shard_map/ppermute | solution.py:36
  36.2 0.5 %shard_map.88 = (f32[512,256]{1,0:T(8,128)S(1)}, f32[512,256]{1,0:T(8,128)S(1)}) custom-call(bf16[96,512]{1,0:T(8,128)(2,1)S(1)} %fusion.2.refs_0_, bf16[96,512]{1,0:T(8,128)(2,1)S(1)} %collective-permute-done.6.refs_1_, bf16[192,512]{1,0:T(8,128)(2,1)S(1)} %get-tuple-element.31.refs_2_, bf16[192,256]{1,0:T(8,128)(2,1)S(1)} %get-tuple-element.32.refs_3_, ...), custom_call_target="tpu_custom_call" | custom-call | flops 150994944 | bytes 2097152 | tf_op jit(solution)/shard_map/pallas_call | solution.py:216
  36.7 0.1 dynamic-slice_bitcast_fusion.2
  36.8 0.1 collective-permute-start.7
  36.9 1.9 %collective-permute-done.7 = f32[4,128,256]{2,1,0:T(8,128)S(1)} collective-permute-done((f32[4,128,256]{2,1,0:T(8,128)S(1)}, f32[4,128,256]{2,1,0:T(8,128)S(1)}, u32[]{:S(2)}, u32[]{:S(2)}) %collective-permute-start.7) | collective-permute-done | bytes 524320 | tf_op jit(solution)/shard_map/ppermute | solution.py:36
  38.8 0.1 maximum_add_fusion
  38.9 0.5 %collective-permute-start.10 = (bf16[128,256]{1,0:T(8,128)(2,1)S(1)}, bf16[128,256]{1,0:T(8,128)(2,1)S(1)}, u32[]{:S(2)}, u32[]{:S(2)}) collective-permute-start(bf16[128,256]{1,0:T(8,128)(2,1)S(1)} %get-tuple-element.39), channel_id=1, source_target_pairs={{0,24},{8,16},{16,8},{24,0},{1,25},{9,17},{17,9},{25,1},{2,26},{10... | collective-permute-start | bytes 196616 | tf_op jit(solution)/shard_map/ppermute | solution.py:36
  39.4 1.5 %collective-permute-start.8 = (bf16[128,256]{1,0:T(8,128)(2,1)S(1)}, bf16[128,256]{1,0:T(8,128)(2,1)S(1)}, u32[]{:S(2)}, u32[]{:S(2)}) collective-permute-start(bf16[128,256]{1,0:T(8,128)(2,1)S(1)} %get-tuple-element.38), channel_id=1, source_target_pairs={{0,8},{8,0},{16,24},{24,16},{1,9},{9,1},{17,25},{25,17},{2,10},{10... | collective-permute-start | bytes 196616 | tf_op jit(solution)/shard_map/ppermute | solution.py:36
  41.0 1.5 %collective-permute-start.9 = (bf16[128,256]{1,0:T(8,128)(2,1)S(1)}, bf16[128,256]{1,0:T(8,128)(2,1)S(1)}, u32[]{:S(2)}, u32[]{:S(2)}) collective-permute-start(bf16[128,256]{1,0:T(8,128)(2,1)S(1)} %get-tuple-element.40), channel_id=1, source_target_pairs={{0,16},{8,24},{16,0},{24,8},{1,17},{9,25},{17,1},{25,9},{2,18},{10... | collective-permute-start | bytes 196616 | tf_op jit(solution)/shard_map/ppermute | solution.py:36
  42.5 2.3 %collective-permute-done.10 = bf16[128,256]{1,0:T(8,128)(2,1)S(1)} collective-permute-done((bf16[128,256]{1,0:T(8,128)(2,1)S(1)}, bf16[128,256]{1,0:T(8,128)(2,1)S(1)}, u32[]{:S(2)}, u32[]{:S(2)}) %collective-permute-start.10) | collective-permute-done | bytes 65568 | tf_op jit(solution)/shard_map/ppermute | solution.py:36
  44.7 0.7 %collective-permute-done.9 = bf16[128,256]{1,0:T(8,128)(2,1)S(1)} collective-permute-done((bf16[128,256]{1,0:T(8,128)(2,1)S(1)}, bf16[128,256]{1,0:T(8,128)(2,1)S(1)}, u32[]{:S(2)}, u32[]{:S(2)}) %collective-permute-start.9) | collective-permute-done | bytes 65568 | tf_op jit(solution)/shard_map/ppermute | solution.py:36
  45.5 0.7 %fusion.12 = (f32[64,256]{1,0:T(8,128)}, f32[64,256]{1,0:T(8,128)}) fusion(f32[128,256]{1,0:T(8,128)S(1)} %fusion.5), kind=kLoop, calls=%fused_computation.30 | loop fusion | bytes 262144 | tf_op jit(solution)/shard_map/slice | solution.py:252
  (14 shorter events, 0.3 us)
Async XLA Ops:
  2.0 5.3 %collective-permute-start = (bf16[48,640]{1,0:T(8,128)(2,1)S(1)}, bf16[48,640]{1,0:T(8,128)(2,1)S(1)}, u32[]{:S(2)}, u32[]{:S(2)}) collective-permute-start(bf16[48,640]{1,0:T(8,128)(2,1)S(1)} %get-tuple-element.20), channel_id=1, source_target_pairs={{0,8},{8,0},{16,24},{24,16},{1,9},{9,1},{17,25},{25,17},{2,10},{10... | collective-permute-start | bytes 184328 | tf_op jit(solution)/shard_map/ppermute | solution.py:36
  5.0 4.2 %collective-permute-start.1 = (bf16[48,640]{1,0:T(8,128)(2,1)S(1)}, bf16[48,640]{1,0:T(8,128)(2,1)S(1)}, u32[]{:S(2)}, u32[]{:S(2)}) collective-permute-start(bf16[48,640]{1,0:T(8,128)(2,1)S(1)} %get-tuple-element.21), channel_id=1, source_target_pairs={{0,16},{8,24},{16,0},{24,8},{1,17},{9,25},{17,1},{25,9},{2,18},{10... | collective-permute-start | bytes 184328 | tf_op jit(solution)/shard_map/ppermute | solution.py:36
  6.5 5.1 %collective-permute-start.2 = (bf16[48,640]{1,0:T(8,128)(2,1)S(1)}, bf16[48,640]{1,0:T(8,128)(2,1)S(1)}, u32[]{:S(2)}, u32[]{:S(2)}) collective-permute-start(bf16[48,640]{1,0:T(8,128)(2,1)S(1)} %get-tuple-element.22), channel_id=1, source_target_pairs={{0,24},{8,16},{16,8},{24,0},{1,25},{9,17},{17,9},{25,1},{2,26},{10... | collective-permute-start | bytes 184328 | tf_op jit(solution)/shard_map/ppermute | solution.py:36
  12.2 3.2 %collective-permute-start.5 = (f32[1,128]{1,0:T(1,128)S(1)}, f32[1,128]{1,0:T(1,128)S(1)}, u32[]{:S(2)}, u32[]{:S(2)}) collective-permute-start(f32[1,128]{1,0:T(1,128)S(1)} %get-tuple-element.30), channel_id=1, source_target_pairs={{0,4},{4,0},{1,5},{5,1},{2,6},{6,2},{3,7},{7,3},{8,12},{12,8},{9,1... | collective-permute-start | bytes 1544 | tf_op jit(solution)/shard_map/ppermute | solution.py:36
  13.7 5.6 %collective-permute-start.3 = (f16[112,512]{1,0:T(8,128)(2,1)S(1)}, f16[112,512]{1,0:T(8,128)(2,1)S(1)}, u32[]{:S(2)}, u32[]{:S(2)}) collective-permute-start(f16[112,512]{1,0:T(8,128)(2,1)S(1)} %concatenate.12), channel_id=1, source_target_pairs={{0,1},{1,0},{2,3},{3,2},{4,5},{5,4},{6,7},{7,6},{8,9},{9,8},{10,11... | collective-permute-start | bytes 344072 | tf_op jit(solution)/shard_map/ppermute | solution.py:36
  22.0 8.2 %collective-permute-start.4 = (f16[112,512]{1,0:T(8,128)(2,1)S(1)}, f16[112,512]{1,0:T(8,128)(2,1)S(1)}, u32[]{:S(2)}, u32[]{:S(2)}) collective-permute-start(f16[112,512]{1,0:T(8,128)(2,1)S(1)} %concatenate.13), channel_id=1, source_target_pairs={{0,2},{1,3},{2,0},{3,1},{4,6},{5,7},{6,4},{7,5},{8,10},{9,11},{10,... | collective-permute-start | bytes 344072 | tf_op jit(solution)/shard_map/ppermute | solution.py:36
  31.5 4.7 %collective-permute-start.6 = (bf16[96,512]{1,0:T(8,128)(2,1)S(1)}, bf16[96,512]{1,0:T(8,128)(2,1)S(1)}, u32[]{:S(2)}, u32[]{:S(2)}) collective-permute-start(bf16[96,512]{1,0:T(8,128)(2,1)S(1)} %fusion.2.refs_0_), channel_id=1, source_target_pairs={{0,1},{1,0},{2,3},{3,2},{4,5},{5,4},{6,7},{7,6},{8,9},{9,8},{10,11... | collective-permute-start | bytes 294920 | tf_op jit(solution)/shard_map/ppermute | solution.py:36
  36.8 2.0 %collective-permute-start.7 = (f32[4,128,256]{2,1,0:T(8,128)S(1)}, f32[4,128,256]{2,1,0:T(8,128)S(1)}, u32[]{:S(2)}, u32[]{:S(2)}) collective-permute-start(f32[4,128,256]{2,1,0:T(8,128)S(1)} %pad_maximum_fusion), channel_id=1, source_target_pairs={{0,4},{4,0},{1,5},{5,1},{2,6},{6,2},{3,7},{7,3},{8,12},{12,8},{9,1... | collective-permute-start | bytes 1572872 | tf_op jit(solution)/shard_map/ppermute | solution.py:36
  38.9 5.8 %collective-permute-start.10 = (bf16[128,256]{1,0:T(8,128)(2,1)S(1)}, bf16[128,256]{1,0:T(8,128)(2,1)S(1)}, u32[]{:S(2)}, u32[]{:S(2)}) collective-permute-start(bf16[128,256]{1,0:T(8,128)(2,1)S(1)} %get-tuple-element.39), channel_id=1, source_target_pairs={{0,24},{8,16},{16,8},{24,0},{1,25},{9,17},{17,9},{25,1},{2,26},{10... | collective-permute-start | bytes 196616 | tf_op jit(solution)/shard_map/ppermute | solution.py:36
  39.4 5.3 %collective-permute-start.8 = (bf16[128,256]{1,0:T(8,128)(2,1)S(1)}, bf16[128,256]{1,0:T(8,128)(2,1)S(1)}, u32[]{:S(2)}, u32[]{:S(2)}) collective-permute-start(bf16[128,256]{1,0:T(8,128)(2,1)S(1)} %get-tuple-element.38), channel_id=1, source_target_pairs={{0,8},{8,0},{16,24},{24,16},{1,9},{9,1},{17,25},{25,17},{2,10},{10... | collective-permute-start | bytes 196616 | tf_op jit(solution)/shard_map/ppermute | solution.py:36
  41.0 4.5 %collective-permute-start.9 = (bf16[128,256]{1,0:T(8,128)(2,1)S(1)}, bf16[128,256]{1,0:T(8,128)(2,1)S(1)}, u32[]{:S(2)}, u32[]{:S(2)}) collective-permute-start(bf16[128,256]{1,0:T(8,128)(2,1)S(1)} %get-tuple-element.40), channel_id=1, source_target_pairs={{0,16},{8,24},{16,0},{24,8},{1,17},{9,25},{17,1},{25,9},{2,18},{10... | collective-permute-start | bytes 196616 | tf_op jit(solution)/shard_map/ppermute | solution.py:36

commit v5 on v4

--- a/solution.py
+++ b/solution.py
@@ -9,8 +9,9 @@
 
 LANES = 128
 ROW_TILE = 16
-PACK_ROWS = 16
+PACK_ROWS = 8
 PACK_TOP = 14.0
+TINY = 1e-37
 VMEM = pl.BlockSpec(memory_space=pltpu.VMEM)
 HBM = pl.BlockSpec(memory_space=pltpu.HBM)
 
@@ -36,16 +37,21 @@
     return lax.ppermute(block, axis, [(i, partner_to(size, i, step)) for i in range(size)])
 
 
-def pack(value):
-    largest = jnp.max(jnp.abs(value))
-    power = jnp.clip(jnp.ceil(jnp.log2(largest)), -100.0, 100.0)
-    rows = jnp.broadcast_to(power, (PACK_ROWS, value.shape[1]))
-    return jnp.concatenate([value * jnp.exp2(PACK_TOP - power), rows]).astype(jnp.float16)
+def pack(value, out):
+    height = value.shape[0]
+    largest = jnp.max(jnp.max(jnp.abs(value), axis=0, keepdims=True), axis=1, keepdims=True)
+    power = jnp.clip(jnp.ceil(jnp.log2(jnp.maximum(largest, TINY))), -100.0, 100.0)
+    out[:height] = value * jnp.exp2(PACK_TOP - power)
+    out[height:] = jnp.broadcast_to(power, (PACK_ROWS, value.shape[1]))
 
 
 def unpack(block):
-    block = block.astype(jnp.float32)
-    return block[:-PACK_ROWS] * jnp.exp2(block[-1:, :1] - PACK_TOP)
+    height = block.shape[0] - PACK_ROWS
+    return block[:height] * jnp.exp2(block[height : height + 1, :1] - PACK_TOP)
+
+
+def cross(block, step):
+    return send(block.astype(jnp.float16), "mdl", step).astype(jnp.float32)
 
 
 def dot(left, right, contract=((1,), (0,))):
@@ -103,8 +109,7 @@
 def forward_body(owners, local, room, *refs):
     blocks, refs = refs[:owners], refs[owners:]
     teach_in, teach_out, student_up, student_down = refs[:4]
-    rows_out, act_out, slope_out, tags_out, counts_out, *halves = refs[4:-1]
-    error = refs[-1]
+    rows_out, act_out, slope_out, tags_out, counts_out, own, other, error = refs[4:]
     width = student_up.shape[0]
     full = [block[...] for block in blocks]
     counts = None
@@ -133,9 +138,29 @@
         slope_out[span] = sig * (1.0 + pre * (1.0 - sig))
         error[span] = dot(act, student_down[...], ((1,), (1,))) - labels
     me = lax.axis_index("mdl")
-    height = halves[0].shape[0]
-    for k, out in enumerate(halves):
-        out[...] = error[pl.ds(pl.multiple_of(((me & 1) ^ k) * height, 8), height)]
+    height = own.shape[0]
+    own[...] = error[pl.ds(pl.multiple_of((me & 1) * height, 8), height)]
+    pack(error[pl.ds(pl.multiple_of(((me & 1) ^ 1) * height, 8), height)], other)
+
+
+def pair_body(own, arrived, total, packed):
+    value = own[...] + unpack(arrived)
+    total[...] = value
+    pack(value, packed)
+
+
+def scale_body(studs, *refs):
+    own, arrived, tags = refs[:3]
+    counts, scaled = refs[3:-1], refs[-1]
+    all_counts = counts[0][...]
+    for piece in counts[1:]:
+        all_counts = all_counts + piece[...]
+    height = own.shape[0]
+    me = lax.axis_index("mdl")
+    tag = tags[pl.ds(pl.multiple_of((me & 1) * height, 8), height)]
+    inverse = jnp.where(all_counts > 0, 2.0 / all_counts, 0.0)
+    weight = jnp.sum(tag * inverse, axis=1, keepdims=True)
+    scaled[...] = ((own[...] + unpack(arrived)) * weight).astype(scaled.dtype)
 
 
 def backward_body(*refs):
@@ -164,6 +189,8 @@
     slots = teachers * room
     height = slots // 2
     f32, bf16 = jnp.float32, jnp.bfloat16
+    half = jax.ShapeDtypeStruct((height, actions), f32)
+    packed = jax.ShapeDtypeStruct((height + PACK_ROWS, actions), f32)
     block = jax.ShapeDtypeStruct((local * room, width + extra), bf16)
     weights = (teach_in, teach_out, student_up, student_down)
     results = pl.pallas_call(
@@ -193,7 +220,7 @@
             jax.ShapeDtypeStruct((slots, extra), f32),
             jax.ShapeDtypeStruct((1, extra), f32),
         ]
-        + [jax.ShapeDtypeStruct((height, actions), f32)] * 2,
+        + [half, packed],
         in_specs=[VMEM] * (owners + 4),
         out_specs=[VMEM] * 7,
         scratch_shapes=[pltpu.VMEM((slots, actions), f32)],
@@ -202,16 +229,21 @@
         ),
         compiler_params=pltpu.CompilerParams(vmem_limit_bytes=24 * 1024 * 1024),
     )(*blocks, *weights)
-    total = own + unpack(send(pack(other), "mdl", 1))
     step = 2
+    arrived = cross(other, 1)
     while step < parts:
-        total = total + unpack(send(pack(total), "mdl", step))
+        own, other = pl.pallas_call(
+            pair_body, out_shape=[half, packed], in_specs=[VMEM] * 2, out_specs=[VMEM] * 2
+        )(own, arrived)
+        arrived = cross(other, step)
         step *= 2
-    for piece in [send(counts, "stud", k) for k in range(1, studs)]:
-        counts = counts + piece
-    weight = jnp.sum(tags * jnp.where(counts > 0, 2.0 / counts, 0.0), axis=1)
-    weight = lax.dynamic_index_in_dim(weight.reshape(2, height), lax.axis_index("mdl") & 1, 0, False)
-    scaled = (total * weight[:, None]).astype(bf16)
+    counts = [counts] + [send(counts, "stud", k) for k in range(1, studs)]
+    scaled = pl.pallas_call(
+        functools.partial(scale_body, studs),
+        out_shape=jax.ShapeDtypeStruct((height, actions), bf16),
+        in_specs=[VMEM] * (3 + studs),
+        out_specs=VMEM,
+    )(own, arrived, tags, *counts)
     chunks = [scaled, send(scaled, "mdl", 1)]
     grad_up, grad_down = pl.pallas_call(
         backward_body,

time: 46.3 us -> 47 us (1.015)
  Pallas kernels: 2.42 us -> 6.33 us
  between operations: 3.66 us -> 0.77 us
  waiting for transfers between devices: 23.1 us -> 21.3 us
  other arithmetic: 1.65 us -> 2.49 us
  local copies, waits for them, and re-layouts: 1.95 us -> 2.79 us
    pallas_call x0 -> x2, Pallas kernels: none -> 3.79 us  [the longest x1 1.91 us: on_device(): pl.pallas_call(pair_body, out_shape=[half, packed], in_specs=[VMEM] * 2,...]
    convert_element_type x3 -> x4, other arithmetic: 0.12 us -> 2.35 us  [cross(): return send(block.astype(jnp.float16), 'mdl', step).astype(jnp.float32)]
    unnamed x0 -> x10, local copies, waits for them, and re-layouts: none -> 2 us
    ppermute x11, waiting for transfers between devices: 23.1 us -> 21.3 us  [send(): lax.ppermute(block, axis, [(i, partner_to(size, i, step)) for i in range(...]
    reduce_max x2 -> x0, other arithmetic: 1.24 us -> none  [pack(): largest = jnp.max(jnp.abs(value))]
    slice x2 -> x0, local copies, waits for them, and re-layouts: 1.03 us -> none  [unpack(): return block[:-PACK_ROWS] * jnp.exp2(block[-1:, :1] - PACK_TOP)]
  transfers between devices with their start and end apart: 11 -> 11, of which waited for: 9 -> 9; matrix products, arithmetic and copies ran while one was open for 2% -> 1% of each run, Pallas kernels for 0% -> 0%
where the time goes in v5:
time: 47 us; the launch traced here: 46.8 us
  waiting for transfers between devices  21.3 us (45%)
  starting transfers between devices  13.1 us (28%)
  Pallas kernels  6.33 us (13%)
  local copies, waits for them, and re-layouts  2.79 us (6%)
  other arithmetic  2.49 us (5%)
  between operations  0.77 us (2%)
    ppermute x11, waiting for transfers between devices, send(): lax.ppermute(block, axis, [(i, partner_to(size, i, step)) for i in range(...  21.3 us
    ppermute x11, starting transfers between devices, send(): lax.ppermute(block, axis, [(i, partner_to(size, i, step)) for i in range(...  13.1 us
    convert_element_type x4, other arithmetic, cross(): return send(block.astype(jnp.float16), 'mdl', step).astype(jnp.float32)  2.35 us
    unnamed x10, local copies, waits for them, and re-layouts  2 us
    pallas_call x1, Pallas kernels, on_device(): pl.pallas_call(pair_body, out_shape=[half, packed], in_specs=[VMEM] * 2,...  1.91 us
    pallas_call x1, Pallas kernels, on_device(): pl.pallas_call(functools.partial(scale_body, studs), out_shape=jax.ShapeD...  1.88 us
    pallas_call x1, Pallas kernels, on_device(): pl.pallas_call(functools.partial(dispatch_body, owners, local, room, extr...  1.34 us
  transfers between devices with their start and end apart: 11, of which 9 were waited for; matrix products, arithmetic and copies ran while one was open for 1% of the time, Pallas kernels for 0%

profile of v5, /device:TPU:0, one launch (start us, length us, event | category | flops | bytes accessed | tf_op | source)
XLA Modules:
  0.0 46.8 jit_solution(14802545781246162467)
XLA Ops:
  0.6 1.3 %shard_map.86 = (bf16[48,640]{1,0:T(8,128)(2,1)S(1)}, bf16[48,640]{1,0:T(8,128)(2,1)S(1)}, bf16[48,640]{1,0:T(8,128)(2,1)S(1)}, bf16[48,640]{1,0:T(8,128)(2,1)S(...) custom-call(bf16[128,512]{1,0:T(8,128)(2,1)} %refs_0_.1, ...), custom_call_target="tpu_custom_call" | custom-call | flops 25165824 | bytes 2097152 | tf_op jit(solution)/shard_map/pallas_call | solution.py:196
  2.0 3.0 %collective-permute-start = (bf16[48,640]{1,0:T(8,128)(2,1)S(1)}, bf16[48,640]{1,0:T(8,128)(2,1)S(1)}, u32[]{:S(2)}, u32[]{:S(2)}) collective-permute-start(bf16[48,640]{1,0:T(8,128)(2,1)S(1)} %get-tuple-element.22), channel_id=1, source_target_pairs={{0,8},{8,0},{16,24},{24,16},{1,9},{9,1},{17,25},{25,17},{2,10},{10... | collective-permute-start | bytes 184328 | tf_op jit(solution)/shard_map/ppermute | solution.py:37
  5.0 1.5 %collective-permute-start.1 = (bf16[48,640]{1,0:T(8,128)(2,1)S(1)}, bf16[48,640]{1,0:T(8,128)(2,1)S(1)}, u32[]{:S(2)}, u32[]{:S(2)}) collective-permute-start(bf16[48,640]{1,0:T(8,128)(2,1)S(1)} %get-tuple-element.23), channel_id=1, source_target_pairs={{0,16},{8,24},{16,0},{24,8},{1,17},{9,25},{17,1},{25,9},{2,18},{10... | collective-permute-start | bytes 184328 | tf_op jit(solution)/shard_map/ppermute | solution.py:37
  6.5 0.7 %collective-permute-done.refs_1_ = bf16[48,640]{1,0:T(8,128)(2,1)S(1)} collective-permute-done((bf16[48,640]{1,0:T(8,128)(2,1)S(1)}, bf16[48,640]{1,0:T(8,128)(2,1)S(1)}, u32[]{:S(2)}, u32[]{:S(2)}) %collective-permute-start) | collective-permute-done | bytes 61472 | tf_op jit(solution)/shard_map/ppermute | solution.py:37
  7.3 2.0 %collective-permute-done.1.refs_2_ = bf16[48,640]{1,0:T(8,128)(2,1)S(1)} collective-permute-done((bf16[48,640]{1,0:T(8,128)(2,1)S(1)}, bf16[48,640]{1,0:T(8,128)(2,1)S(1)}, u32[]{:S(2)}, u32[]{:S(2)}) %collective-permute-start.1) | collective-permute-done | bytes 61472 | tf_op jit(solution)/shard_map/ppermute | solution.py:37
  9.2 2.4 %collective-permute-done.2.refs_3_ = bf16[48,640]{1,0:T(8,128)(2,1)S(1)} collective-permute-done((bf16[48,640]{1,0:T(8,128)(2,1)S(1)}, bf16[48,640]{1,0:T(8,128)(2,1)S(1)}, u32[]{:S(2)}, u32[]{:S(2)}) %collective-permute-start.2) | collective-permute-done | bytes 61472 | tf_op jit(solution)/shard_map/ppermute | solution.py:37
  11.6 0.7 %shard_map.87 = (bf16[192,512]{1,0:T(8,128)(2,1)S(1)}, bf16[192,256]{1,0:T(8,128)(2,1)S(1)}, f32[192,256]{1,0:T(8,128)S(1)}, f32[192,128]{1,0:T(8,128)S(1)}, f32...) custom-call(bf16[48,640]{1,0:T(8,128)(2,1)S(1)} %get-tuple-element.21.refs_0_, ...), custom_call_target="tpu_custom_call" | custom-call | flops 201326592 | bytes 2097152 | tf_op jit(solution)/shard_map/pallas_call | solution.py:214
  12.4 0.6 %copy-done.2 = f32[192,128]{1,0:T(8,128)} copy-done((f32[192,128]{1,0:T(8,128)}, f32[192,128]{1,0:T(8,128)S(1)}, u32[]{:S(2)}) %copy-start.2) | copy-done | bytes 98328
  13.0 1.6 %collective-permute-start.3 = (f16[104,512]{1,0:T(8,128)(2,1)S(1)}, f16[104,512]{1,0:T(8,128)(2,1)S(1)}, u32[]{:S(2)}, u32[]{:S(2)}) collective-permute-start(f16[104,512]{1,0:T(8,128)(2,1)S(1)} %convert_element_type.39), channel_id=1, source_target_pairs={{0,1},{1,0},{2,3},{3,2},{4,5},{5,4},{6,7},{7,6},{8,9},{9,8},{10,11... | collective-permute-start | bytes 319496 | tf_op jit(solution)/shard_map/ppermute | solution.py:37
  14.6 3.1 %collective-permute-done.3 = f16[104,512]{1,0:T(8,128)(2,1)S(1)} collective-permute-done((f16[104,512]{1,0:T(8,128)(2,1)S(1)}, f16[104,512]{1,0:T(8,128)(2,1)S(1)}, u32[]{:S(2)}, u32[]{:S(2)}) %collective-permute-start.3) | collective-permute-done | bytes 106528 | tf_op jit(solution)/shard_map/ppermute | solution.py:37
  17.7 0.7 %convert_element_type.40.arrived = f32[104,512]{1,0:T(8,128)} convert(f16[104,512]{1,0:T(8,128)(2,1)S(1)} %collective-permute-done.3) | non-fusion elementwise | flops 53248 | bytes 319488 | tf_op jit(solution)/shard_map/convert_element_type | solution.py:54
  18.4 1.9 %shard_map.88 = (f32[96,512]{1,0:T(8,128)}, f32[104,512]{1,0:T(8,128)}) custom-call(f32[96,512]{1,0:T(8,128)} %copy-done.1, f32[104,512]{1,0:T(8,128)} %convert_element_type.40.arrived), custom_call_target="tpu_custom_call" | custom-call | tf_op jit(solution)/shard_map/pallas_call | solution.py:235
  20.3 0.9 %convert_element_type.41 = f16[104,512]{1,0:T(8,128)(2,1)S(1)} convert(f32[104,512]{1,0:T(8,128)} %get-tuple-element.32) | non-fusion elementwise | flops 53248 | bytes 319488 | tf_op jit(solution)/shard_map/convert_element_type | solution.py:54
  21.3 2.7 %collective-permute-start.4 = (f16[104,512]{1,0:T(8,128)(2,1)S(1)}, f16[104,512]{1,0:T(8,128)(2,1)S(1)}, u32[]{:S(2)}, u32[]{:S(2)}) collective-permute-start(f16[104,512]{1,0:T(8,128)(2,1)S(1)} %convert_element_type.41), channel_id=1, source_target_pairs={{0,2},{1,3},{2,0},{3,1},{4,6},{5,7},{6,4},{7,5},{8,10},{9,11},{10,... | collective-permute-start | bytes 319496 | tf_op jit(solution)/shard_map/ppermute | solution.py:37
  23.9 4.1 %collective-permute-done.4 = f16[104,512]{1,0:T(8,128)(2,1)S(1)} collective-permute-done((f16[104,512]{1,0:T(8,128)(2,1)S(1)}, f16[104,512]{1,0:T(8,128)(2,1)S(1)}, u32[]{:S(2)}, u32[]{:S(2)}) %collective-permute-start.4) | collective-permute-done | bytes 106528 | tf_op jit(solution)/shard_map/ppermute | solution.py:37
  28.1 0.7 %convert_element_type.42.refs_1_ = f32[104,512]{1,0:T(8,128)} convert(f16[104,512]{1,0:T(8,128)(2,1)S(1)} %collective-permute-done.4) | non-fusion elementwise | flops 53248 | bytes 319488 | tf_op jit(solution)/shard_map/convert_element_type | solution.py:54
  28.8 0.5 %copy-done.4 = f32[1,128]{1,0:T(1,128)} copy-done((f32[1,128]{1,0:T(1,128)}, f32[1,128]{1,0:T(1,128)S(1)}, u32[]{:S(2)}) %copy-start.4) | copy-done | bytes 536
  29.3 1.9 %shard_map.89.refs_0_ = bf16[96,512]{1,0:T(8,128)(2,1)} custom-call(f32[96,512]{1,0:T(8,128)} %get-tuple-element.31.refs_0_, f32[104,512]{1,0:T(8,128)} %convert_element_type.42.refs_1_, f32[192,128]{1,0:T(8,128)} %copy-done.2, f32[1,128]{1,0:T(1,128)} %copy-done.3, f32[1,128]{1,0:T(1,128)} %copy-done.4), custom_call_target="tpu_custom_call" | custom-call | tf_op jit(solution)/shard_map/pallas_call | solution.py:241
  31.2 0.7 %collective-permute-start.6 = (bf16[96,512]{1,0:T(8,128)(2,1)}, bf16[96,512]{1,0:T(8,128)(2,1)S(1)}, u32[]{:S(2)}, u32[]{:S(2)}) collective-permute-start(bf16[96,512]{1,0:T(8,128)(2,1)} %shard_map.89.refs_0_), channel_id=1, source_target_pairs={{0,1},{1,0},{2,3},{3,2},{4,5},{5,4},{6,7},{7,6},{8,9},{9,8},{10,11... | collective-permute-start | bytes 294920 | tf_op jit(solution)/shard_map/ppermute | solution.py:37
  31.8 4.2 %collective-permute-done.6.refs_1_ = bf16[96,512]{1,0:T(8,128)(2,1)S(1)} collective-permute-done((bf16[96,512]{1,0:T(8,128)(2,1)}, bf16[96,512]{1,0:T(8,128)(2,1)S(1)}, u32[]{:S(2)}, u32[]{:S(2)}) %collective-permute-start.6) | collective-permute-done | bytes 98336 | tf_op jit(solution)/shard_map/ppermute | solution.py:37
  36.0 0.9 %copy-done = bf16[96,512]{1,0:T(8,128)(2,1)S(1)} copy-done((bf16[96,512]{1,0:T(8,128)(2,1)S(1)}, bf16[96,512]{1,0:T(8,128)(2,1)}, u32[]{:S(2)}) %copy-start) | copy-done | bytes 98328
  36.9 0.5 %shard_map.90 = (f32[512,256]{1,0:T(8,128)S(1)}, f32[512,256]{1,0:T(8,128)S(1)}) custom-call(bf16[96,512]{1,0:T(8,128)(2,1)S(1)} %copy-done, bf16[96,512]{1,0:T(8,128)(2,1)S(1)} %collective-permute-done.6.refs_1_, bf16[192,512]{1,0:T(8,128)(2,1)S(1)} %get-tuple-element.35.refs_2_, bf16[192,256]{1,0:T(8,128)(2,1)S(1)} %get-tuple-element.36.refs_3_, ...), custom_call_target="tpu_custom_call" | custom-call | flops 150994944 | bytes 2097152 | tf_op jit(solution)/shard_map/pallas_call | solution.py:248
  37.4 0.1 dynamic-slice_bitcast_fusion.2
  37.5 0.1 collective-permute-start.7
  37.6 1.9 %collective-permute-done.7 = f32[4,128,256]{2,1,0:T(8,128)S(1)} collective-permute-done((f32[4,128,256]{2,1,0:T(8,128)S(1)}, f32[4,128,256]{2,1,0:T(8,128)S(1)}, u32[]{:S(2)}, u32[]{:S(2)}) %collective-permute-start.7) | collective-permute-done | bytes 524320 | tf_op jit(solution)/shard_map/ppermute | solution.py:37
  39.5 0.1 maximum_add_fusion
  39.6 0.1 collective-permute-start.10
  39.7 2.0 %collective-permute-start.8 = (bf16[128,256]{1,0:T(8,128)(2,1)S(1)}, bf16[128,256]{1,0:T(8,128)(2,1)S(1)}, u32[]{:S(2)}, u32[]{:S(2)}) collective-permute-start(bf16[128,256]{1,0:T(8,128)(2,1)S(1)} %get-tuple-element.40), channel_id=1, source_target_pairs={{0,8},{8,0},{16,24},{24,16},{1,9},{9,1},{17,25},{25,17},{2,10},{10... | collective-permute-start | bytes 196616 | tf_op jit(solution)/shard_map/ppermute | solution.py:37
  41.6 1.5 %collective-permute-start.9 = (bf16[128,256]{1,0:T(8,128)(2,1)S(1)}, bf16[128,256]{1,0:T(8,128)(2,1)S(1)}, u32[]{:S(2)}, u32[]{:S(2)}) collective-permute-start(bf16[128,256]{1,0:T(8,128)(2,1)S(1)} %get-tuple-element.42), channel_id=1, source_target_pairs={{0,16},{8,24},{16,0},{24,8},{1,17},{9,25},{17,1},{25,9},{2,18},{10... | collective-permute-start | bytes 196616 | tf_op jit(solution)/shard_map/ppermute | solution.py:37
  43.2 2.3 %collective-permute-done.10 = bf16[128,256]{1,0:T(8,128)(2,1)S(1)} collective-permute-done((bf16[128,256]{1,0:T(8,128)(2,1)S(1)}, bf16[128,256]{1,0:T(8,128)(2,1)S(1)}, u32[]{:S(2)}, u32[]{:S(2)}) %collective-permute-start.10) | collective-permute-done | bytes 65568 | tf_op jit(solution)/shard_map/ppermute | solution.py:37
  45.4 0.7 %collective-permute-done.9 = bf16[128,256]{1,0:T(8,128)(2,1)S(1)} collective-permute-done((bf16[128,256]{1,0:T(8,128)(2,1)S(1)}, bf16[128,256]{1,0:T(8,128)(2,1)S(1)}, u32[]{:S(2)}, u32[]{:S(2)}) %collective-permute-start.9) | collective-permute-done | bytes 65568 | tf_op jit(solution)/shard_map/ppermute | solution.py:37
  46.1 0.7 %fusion.5 = (f32[64,256]{1,0:T(8,128)}, f32[64,256]{1,0:T(8,128)}) fusion(f32[128,256]{1,0:T(8,128)S(1)} %fusion.1), kind=kLoop, calls=%fused_computation.15 | loop fusion | bytes 262144 | tf_op jit(solution)/shard_map/slice | solution.py:284
  (15 shorter events, 0.2 us)
Async XLA Ops:
  2.0 5.3 %collective-permute-start = (bf16[48,640]{1,0:T(8,128)(2,1)S(1)}, bf16[48,640]{1,0:T(8,128)(2,1)S(1)}, u32[]{:S(2)}, u32[]{:S(2)}) collective-permute-start(bf16[48,640]{1,0:T(8,128)(2,1)S(1)} %get-tuple-element.22), channel_id=1, source_target_pairs={{0,8},{8,0},{16,24},{24,16},{1,9},{9,1},{17,25},{25,17},{2,10},{10... | collective-permute-start | bytes 184328 | tf_op jit(solution)/shard_map/ppermute | solution.py:37
  5.0 4.2 %collective-permute-start.1 = (bf16[48,640]{1,0:T(8,128)(2,1)S(1)}, bf16[48,640]{1,0:T(8,128)(2,1)S(1)}, u32[]{:S(2)}, u32[]{:S(2)}) collective-permute-start(bf16[48,640]{1,0:T(8,128)(2,1)S(1)} %get-tuple-element.23), channel_id=1, source_target_pairs={{0,16},{8,24},{16,0},{24,8},{1,17},{9,25},{17,1},{25,9},{2,18},{10... | collective-permute-start | bytes 184328 | tf_op jit(solution)/shard_map/ppermute | solution.py:37
  6.5 5.1 %collective-permute-start.2 = (bf16[48,640]{1,0:T(8,128)(2,1)S(1)}, bf16[48,640]{1,0:T(8,128)(2,1)S(1)}, u32[]{:S(2)}, u32[]{:S(2)}) collective-permute-start(bf16[48,640]{1,0:T(8,128)(2,1)S(1)} %get-tuple-element.24), channel_id=1, source_target_pairs={{0,24},{8,16},{16,8},{24,0},{1,25},{9,17},{17,9},{25,1},{2,26},{10... | collective-permute-start | bytes 184328 | tf_op jit(solution)/shard_map/ppermute | solution.py:37
  12.4 0.6 %copy-start.2 = (f32[192,128]{1,0:T(8,128)}, f32[192,128]{1,0:T(8,128)S(1)}, u32[]{:S(2)}) copy-start(f32[192,128]{1,0:T(8,128)S(1)} %get-tuple-element.33.refs_2_) | copy-start | bytes 294916
  12.4 6.0 %copy-start.1 = (f32[96,512]{1,0:T(8,128)}, f32[96,512]{1,0:T(8,128)S(1)}, u32[]{:S(2)}) copy-start(f32[96,512]{1,0:T(8,128)S(1)} %get-tuple-element.29.own) | copy-start | bytes 589828
  12.4 11.5 %copy-start.3 = (f32[1,128]{1,0:T(1,128)}, f32[1,128]{1,0:T(1,128)S(1)}, u32[]{:S(2)}) copy-start(f32[1,128]{1,0:T(1,128)S(1)} %get-tuple-element.34.refs_3_) | copy-start | bytes 1540
  13.0 4.7 %collective-permute-start.3 = (f16[104,512]{1,0:T(8,128)(2,1)S(1)}, f16[104,512]{1,0:T(8,128)(2,1)S(1)}, u32[]{:S(2)}, u32[]{:S(2)}) collective-permute-start(f16[104,512]{1,0:T(8,128)(2,1)S(1)} %convert_element_type.39), channel_id=1, source_target_pairs={{0,1},{1,0},{2,3},{3,2},{4,5},{5,4},{6,7},{7,6},{8,9},{9,8},{10,11... | collective-permute-start | bytes 319496 | tf_op jit(solution)/shard_map/ppermute | solution.py:37
  21.3 6.8 %collective-permute-start.4 = (f16[104,512]{1,0:T(8,128)(2,1)S(1)}, f16[104,512]{1,0:T(8,128)(2,1)S(1)}, u32[]{:S(2)}, u32[]{:S(2)}) collective-permute-start(f16[104,512]{1,0:T(8,128)(2,1)S(1)} %convert_element_type.41), channel_id=1, source_target_pairs={{0,2},{1,3},{2,0},{3,1},{4,6},{5,7},{6,4},{7,5},{8,10},{9,11},{10,... | collective-permute-start | bytes 319496 | tf_op jit(solution)/shard_map/ppermute | solution.py:37
  23.9 4.8 %collective-permute-start.5 = (f32[1,128]{1,0:T(1,128)S(1)}, f32[1,128]{1,0:T(1,128)S(1)}, u32[]{:S(2)}, u32[]{:S(2)}) collective-permute-start(f32[1,128]{1,0:T(1,128)S(1)} %get-tuple-element.34.refs_3_), channel_id=1, source_target_pairs={{0,4},{4,0},{1,5},{5,1},{2,6},{6,2},{3,7},{7,3},{8,12},{12,8},{9,1... | collective-permute-start | bytes 1544 | tf_op jit(solution)/shard_map/ppermute | solution.py:37
  28.8 0.5 %copy-start.4 = (f32[1,128]{1,0:T(1,128)}, f32[1,128]{1,0:T(1,128)S(1)}, u32[]{:S(2)}) copy-start(f32[1,128]{1,0:T(1,128)S(1)} %collective-permute-done.5.refs_4_) | copy-start | bytes 1540
  31.2 4.8 %collective-permute-start.6 = (bf16[96,512]{1,0:T(8,128)(2,1)}, bf16[96,512]{1,0:T(8,128)(2,1)S(1)}, u32[]{:S(2)}, u32[]{:S(2)}) collective-permute-start(bf16[96,512]{1,0:T(8,128)(2,1)} %shard_map.89.refs_0_), channel_id=1, source_target_pairs={{0,1},{1,0},{2,3},{3,2},{4,5},{5,4},{6,7},{7,6},{8,9},{9,8},{10,11... | collective-permute-start | bytes 294920 | tf_op jit(solution)/shard_map/ppermute | solution.py:37
  36.0 0.9 %copy-start = (bf16[96,512]{1,0:T(8,128)(2,1)S(1)}, bf16[96,512]{1,0:T(8,128)(2,1)}, u32[]{:S(2)}) copy-start(bf16[96,512]{1,0:T(8,128)(2,1)} %shard_map.89.refs_0_) | copy-start | bytes 294916
  37.5 2.0 %collective-permute-start.7 = (f32[4,128,256]{2,1,0:T(8,128)S(1)}, f32[4,128,256]{2,1,0:T(8,128)S(1)}, u32[]{:S(2)}, u32[]{:S(2)}) collective-permute-start(f32[4,128,256]{2,1,0:T(8,128)S(1)} %pad_maximum_fusion), channel_id=1, source_target_pairs={{0,4},{4,0},{1,5},{5,1},{2,6},{6,2},{3,7},{7,3},{8,12},{12,8},{9,1... | collective-permute-start | bytes 1572872 | tf_op jit(solution)/shard_map/ppermute | solution.py:37
  39.6 5.8 %collective-permute-start.10 = (bf16[128,256]{1,0:T(8,128)(2,1)S(1)}, bf16[128,256]{1,0:T(8,128)(2,1)S(1)}, u32[]{:S(2)}, u32[]{:S(2)}) collective-permute-start(bf16[128,256]{1,0:T(8,128)(2,1)S(1)} %get-tuple-element.41), channel_id=1, source_target_pairs={{0,24},{8,16},{16,8},{24,0},{1,25},{9,17},{17,9},{25,1},{2,26},{10... | collective-permute-start | bytes 196616 | tf_op jit(solution)/shard_map/ppermute | solution.py:37
  39.7 5.7 %collective-permute-start.8 = (bf16[128,256]{1,0:T(8,128)(2,1)S(1)}, bf16[128,256]{1,0:T(8,128)(2,1)S(1)}, u32[]{:S(2)}, u32[]{:S(2)}) collective-permute-start(bf16[128,256]{1,0:T(8,128)(2,1)S(1)} %get-tuple-element.40), channel_id=1, source_target_pairs={{0,8},{8,0},{16,24},{24,16},{1,9},{9,1},{17,25},{25,17},{2,10},{10... | collective-permute-start | bytes 196616 | tf_op jit(solution)/shard_map/ppermute | solution.py:37
  41.6 4.5 %collective-permute-start.9 = (bf16[128,256]{1,0:T(8,128)(2,1)S(1)}, bf16[128,256]{1,0:T(8,128)(2,1)S(1)}, u32[]{:S(2)}, u32[]{:S(2)}) collective-permute-start(bf16[128,256]{1,0:T(8,128)(2,1)S(1)} %get-tuple-element.42), channel_id=1, source_target_pairs={{0,16},{8,24},{16,0},{24,8},{1,17},{9,25},{17,1},{25,9},{2,18},{10... | collective-permute-start | bytes 196616 | tf_op jit(solution)/shard_map/ppermute | solution.py:37

commit v6 on v5

--- a/solution.py
+++ b/solution.py
@@ -14,6 +14,7 @@
 TINY = 1e-37
 VMEM = pl.BlockSpec(memory_space=pltpu.VMEM)
 HBM = pl.BlockSpec(memory_space=pltpu.HBM)
+SMALL = pltpu.CompilerParams(vmem_limit_bytes=16 * 1024 * 1024)
 
 
 def up_to(value, step):
@@ -227,13 +228,17 @@
         cost_estimate=pl.CostEstimate(
             flops=2 * slots * 2 * width * (hidden + units), bytes_accessed=2 << 20, transcendentals=0
         ),
-        compiler_params=pltpu.CompilerParams(vmem_limit_bytes=24 * 1024 * 1024),
+        compiler_params=SMALL,
     )(*blocks, *weights)
     step = 2
     arrived = cross(other, 1)
     while step < parts:
         own, other = pl.pallas_call(
-            pair_body, out_shape=[half, packed], in_specs=[VMEM] * 2, out_specs=[VMEM] * 2
+            pair_body,
+            out_shape=[half, packed],
+            in_specs=[VMEM] * 2,
+            out_specs=[VMEM] * 2,
+            compiler_params=SMALL,
         )(own, arrived)
         arrived = cross(other, step)
         step *= 2
@@ -243,6 +248,7 @@
         out_shape=jax.ShapeDtypeStruct((height, actions), bf16),
         in_specs=[VMEM] * (3 + studs),
         out_specs=VMEM,
+        compiler_params=SMALL,
     )(own, arrived, tags, *counts)
     chunks = [scaled, send(scaled, "mdl", 1)]
     grad_up, grad_down = pl.pallas_call(
@@ -257,7 +263,7 @@
         cost_estimate=pl.CostEstimate(
             flops=6 * slots * width * units, bytes_accessed=2 << 20, transcendentals=0
         ),
-        compiler_params=pltpu.CompilerParams(vmem_limit_bytes=24 * 1024 * 1024),
+        compiler_params=SMALL,
     )(*chunks, rows, act, slope, weights[3])
     heights = (width // (owners * studs), actions // (owners * studs))
 

time: 47 us -> 39.1 us (0.83)
  Pallas kernels: 6.33 us -> 2.88 us
  other arithmetic: 2.49 us -> 0.2 us
  local copies, waits for them, and re-layouts: 2.79 us -> 0.79 us
  waiting for transfers between devices: 21.3 us -> 20.8 us
    convert_element_type x4, other arithmetic: 2.35 us -> 0.06 us  [cross(): return send(block.astype(jnp.float16), 'mdl', step).astype(jnp.float32)]
    unnamed x10 -> x0, local copies, waits for them, and re-layouts: 2 us -> none
    pallas_call x1, Pallas kernels: 1.88 us -> 0.14 us  [on_device(): pl.pallas_call(functools.partial(scale_body, studs), out_shape=jax.ShapeD...]
    pallas_call x1, Pallas kernels: 1.91 us -> 0.21 us  [on_device(): pl.pallas_call(pair_body, out_shape=[half, packed], in_specs=[VMEM] * 2,...]
    ppermute x11, waiting for transfers between devices: 21.3 us -> 20.8 us  [send(): lax.ppermute(block, axis, [(i, partner_to(size, i, step)) for i in range(...]
  transfers between devices with their start and end apart: 11 -> 11, of which waited for: 9 -> 9; matrix products, arithmetic and copies ran while one was open for 1% -> 0% of each run, Pallas kernels for 0% -> 0%
where the time goes in v6:
time: 39.1 us; the launch traced here: 39 us
  waiting for transfers between devices  20.8 us (53%)
  starting transfers between devices  13.5 us (35%)
  Pallas kernels  2.88 us (7%)
  local copies, waits for them, and re-layouts  0.79 us (2%)
  between operations  0.78 us (2%)
    ppermute x11, waiting for transfers between devices, send(): lax.ppermute(block, axis, [(i, partner_to(size, i, step)) for i in range(...  20.8 us
    ppermute x11, starting transfers between devices, send(): lax.ppermute(block, axis, [(i, partner_to(size, i, step)) for i in range(...  13.5 us
    pallas_call x1, Pallas kernels, on_device(): pl.pallas_call(functools.partial(dispatch_body, owners, local, room, extr...  1.34 us
  transfers between devices with their start and end apart: 11, of which 9 were waited for; matrix products, arithmetic and copies ran while one was open for 0% of the time, Pallas kernels for 0%

profile of v6, /device:TPU:0, one launch (start us, length us, event | category | flops | bytes accessed | tf_op | source)
XLA Modules:
  0.0 39.0 jit_solution(14963931679290012959)
XLA Ops:
  0.6 1.3 %shard_map.86 = (bf16[48,640]{1,0:T(8,128)(2,1)S(1)}, bf16[48,640]{1,0:T(8,128)(2,1)S(1)}, bf16[48,640]{1,0:T(8,128)(2,1)S(1)}, bf16[48,640]{1,0:T(8,128)(2,1)S(...) custom-call(bf16[128,512]{1,0:T(8,128)(2,1)} %refs_0_.1, ...), custom_call_target="tpu_custom_call" | custom-call | flops 25165824 | bytes 2097152 | tf_op jit(solution)/shard_map/pallas_call | solution.py:197
  2.0 3.0 %collective-permute-start = (bf16[48,640]{1,0:T(8,128)(2,1)S(1)}, bf16[48,640]{1,0:T(8,128)(2,1)S(1)}, u32[]{:S(2)}, u32[]{:S(2)}) collective-permute-start(bf16[48,640]{1,0:T(8,128)(2,1)S(1)} %get-tuple-element.22), channel_id=1, source_target_pairs={{0,8},{8,0},{16,24},{24,16},{1,9},{9,1},{17,25},{25,17},{2,10},{10... | collective-permute-start | bytes 184328 | tf_op jit(solution)/shard_map/ppermute | solution.py:38
  5.0 1.5 %collective-permute-start.1 = (bf16[48,640]{1,0:T(8,128)(2,1)S(1)}, bf16[48,640]{1,0:T(8,128)(2,1)S(1)}, u32[]{:S(2)}, u32[]{:S(2)}) collective-permute-start(bf16[48,640]{1,0:T(8,128)(2,1)S(1)} %get-tuple-element.23), channel_id=1, source_target_pairs={{0,16},{8,24},{16,0},{24,8},{1,17},{9,25},{17,1},{25,9},{2,18},{10... | collective-permute-start | bytes 184328 | tf_op jit(solution)/shard_map/ppermute | solution.py:38
  6.5 0.0 collective-permute-start.2
  6.5 0.7 %collective-permute-done.refs_1_ = bf16[48,640]{1,0:T(8,128)(2,1)S(1)} collective-permute-done((bf16[48,640]{1,0:T(8,128)(2,1)S(1)}, bf16[48,640]{1,0:T(8,128)(2,1)S(1)}, u32[]{:S(2)}, u32[]{:S(2)}) %collective-permute-start) | collective-permute-done | bytes 61472 | tf_op jit(solution)/shard_map/ppermute | solution.py:38
  7.3 2.0 %collective-permute-done.1.refs_2_ = bf16[48,640]{1,0:T(8,128)(2,1)S(1)} collective-permute-done((bf16[48,640]{1,0:T(8,128)(2,1)S(1)}, bf16[48,640]{1,0:T(8,128)(2,1)S(1)}, u32[]{:S(2)}, u32[]{:S(2)}) %collective-permute-start.1) | collective-permute-done | bytes 61472 | tf_op jit(solution)/shard_map/ppermute | solution.py:38
  9.2 2.4 %collective-permute-done.2.refs_3_ = bf16[48,640]{1,0:T(8,128)(2,1)S(1)} collective-permute-done((bf16[48,640]{1,0:T(8,128)(2,1)S(1)}, bf16[48,640]{1,0:T(8,128)(2,1)S(1)}, u32[]{:S(2)}, u32[]{:S(2)}) %collective-permute-start.2) | collective-permute-done | bytes 61472 | tf_op jit(solution)/shard_map/ppermute | solution.py:38
  11.6 0.7 %shard_map.87 = (bf16[192,512]{1,0:T(8,128)(2,1)S(1)}, bf16[192,256]{1,0:T(8,128)(2,1)S(1)}, f32[192,256]{1,0:T(8,128)S(1)}, f32[192,128]{1,0:T(8,128)S(1)}, f32...) custom-call(bf16[48,640]{1,0:T(8,128)(2,1)S(1)} %get-tuple-element.21.refs_0_, ...), custom_call_target="tpu_custom_call" | custom-call | flops 201326592 | bytes 2097152 | tf_op jit(solution)/shard_map/pallas_call | solution.py:215
  12.4 1.7 %collective-permute-start.3 = (f16[104,512]{1,0:T(8,128)(2,1)S(1)}, f16[104,512]{1,0:T(8,128)(2,1)S(1)}, u32[]{:S(2)}, u32[]{:S(2)}) collective-permute-start(f16[104,512]{1,0:T(8,128)(2,1)S(1)} %convert_element_type.39), channel_id=1, source_target_pairs={{0,1},{1,0},{2,3},{3,2},{4,5},{5,4},{6,7},{7,6},{8,9},{9,8},{10,11... | collective-permute-start | bytes 319496 | tf_op jit(solution)/shard_map/ppermute | solution.py:38
  14.0 3.1 %collective-permute-done.3 = f16[104,512]{1,0:T(8,128)(2,1)S(1)} collective-permute-done((f16[104,512]{1,0:T(8,128)(2,1)S(1)}, f16[104,512]{1,0:T(8,128)(2,1)S(1)}, u32[]{:S(2)}, u32[]{:S(2)}) %collective-permute-start.3) | collective-permute-done | bytes 106528 | tf_op jit(solution)/shard_map/ppermute | solution.py:38
  17.2 0.2 shard_map.88
  17.4 2.9 %collective-permute-start.4 = (f16[104,512]{1,0:T(8,128)(2,1)S(1)}, f16[104,512]{1,0:T(8,128)(2,1)S(1)}, u32[]{:S(2)}, u32[]{:S(2)}) collective-permute-start(f16[104,512]{1,0:T(8,128)(2,1)S(1)} %convert_element_type.41), channel_id=1, source_target_pairs={{0,2},{1,3},{2,0},{3,1},{4,6},{5,7},{6,4},{7,5},{8,10},{9,11},{10,... | collective-permute-start | bytes 319496 | tf_op jit(solution)/shard_map/ppermute | solution.py:38
  20.3 0.0 collective-permute-start.5
  20.3 3.9 %collective-permute-done.4 = f16[104,512]{1,0:T(8,128)(2,1)S(1)} collective-permute-done((f16[104,512]{1,0:T(8,128)(2,1)S(1)}, f16[104,512]{1,0:T(8,128)(2,1)S(1)}, u32[]{:S(2)}, u32[]{:S(2)}) %collective-permute-start.4) | collective-permute-done | bytes 106528 | tf_op jit(solution)/shard_map/ppermute | solution.py:38
  24.2 0.0 collective-permute-done.5.refs_4_
  24.3 0.1 shard_map.89.refs_0_
  24.4 0.9 %collective-permute-start.6 = (bf16[96,512]{1,0:T(8,128)(2,1)S(1)}, bf16[96,512]{1,0:T(8,128)(2,1)S(1)}, u32[]{:S(2)}, u32[]{:S(2)}) collective-permute-start(bf16[96,512]{1,0:T(8,128)(2,1)S(1)} %shard_map.89.refs_0_), channel_id=1, source_target_pairs={{0,1},{1,0},{2,3},{3,2},{4,5},{5,4},{6,7},{7,6},{8,9},{9,8},{10,11... | collective-permute-start | bytes 294920 | tf_op jit(solution)/shard_map/ppermute | solution.py:38
  25.3 3.8 %collective-permute-done.6.refs_1_ = bf16[96,512]{1,0:T(8,128)(2,1)S(1)} collective-permute-done((bf16[96,512]{1,0:T(8,128)(2,1)S(1)}, bf16[96,512]{1,0:T(8,128)(2,1)S(1)}, u32[]{:S(2)}, u32[]{:S(2)}) %collective-permute-start.6) | collective-permute-done | bytes 98336 | tf_op jit(solution)/shard_map/ppermute | solution.py:38
  29.1 0.5 %shard_map.90 = (f32[512,256]{1,0:T(8,128)S(1)}, f32[512,256]{1,0:T(8,128)S(1)}) custom-call(bf16[96,512]{1,0:T(8,128)(2,1)S(1)} %shard_map.89.refs_0_, bf16[96,512]{1,0:T(8,128)(2,1)S(1)} %collective-permute-done.6.refs_1_, bf16[192,512]{1,0:T(8,128)(2,1)S(1)} %get-tuple-element.35.refs_2_, bf16[192,256]{1,0:T(8,128)(2,1)S(1)} %get-tuple-element.36.refs_3_, ...), custom_call_target="tpu_custom_call" | custom-call | flops 150994944 | bytes 2097152 | tf_op jit(solution)/shard_map/pallas_call | solution.py:254
  29.6 0.1 dynamic-slice_bitcast_fusion.2
  29.7 0.1 collective-permute-start.7
  29.8 1.9 %collective-permute-done.7 = f32[4,128,256]{2,1,0:T(8,128)S(1)} collective-permute-done((f32[4,128,256]{2,1,0:T(8,128)S(1)}, f32[4,128,256]{2,1,0:T(8,128)S(1)}, u32[]{:S(2)}, u32[]{:S(2)}) %collective-permute-start.7) | collective-permute-done | bytes 524320 | tf_op jit(solution)/shard_map/ppermute | solution.py:38
  31.7 0.1 maximum_add_fusion
  31.8 0.1 collective-permute-start.10
  31.9 2.0 %collective-permute-start.8 = (bf16[128,256]{1,0:T(8,128)(2,1)S(1)}, bf16[128,256]{1,0:T(8,128)(2,1)S(1)}, u32[]{:S(2)}, u32[]{:S(2)}) collective-permute-start(bf16[128,256]{1,0:T(8,128)(2,1)S(1)} %get-tuple-element.40), channel_id=1, source_target_pairs={{0,8},{8,0},{16,24},{24,16},{1,9},{9,1},{17,25},{25,17},{2,10},{10... | collective-permute-start | bytes 196616 | tf_op jit(solution)/shard_map/ppermute | solution.py:38
  33.8 1.5 %collective-permute-start.9 = (bf16[128,256]{1,0:T(8,128)(2,1)S(1)}, bf16[128,256]{1,0:T(8,128)(2,1)S(1)}, u32[]{:S(2)}, u32[]{:S(2)}) collective-permute-start(bf16[128,256]{1,0:T(8,128)(2,1)S(1)} %get-tuple-element.42), channel_id=1, source_target_pairs={{0,16},{8,24},{16,0},{24,8},{1,17},{9,25},{17,1},{25,9},{2,18},{10... | collective-permute-start | bytes 196616 | tf_op jit(solution)/shard_map/ppermute | solution.py:38
  35.3 2.3 %collective-permute-done.10 = bf16[128,256]{1,0:T(8,128)(2,1)S(1)} collective-permute-done((bf16[128,256]{1,0:T(8,128)(2,1)S(1)}, bf16[128,256]{1,0:T(8,128)(2,1)S(1)}, u32[]{:S(2)}, u32[]{:S(2)}) %collective-permute-start.10) | collective-permute-done | bytes 65568 | tf_op jit(solution)/shard_map/ppermute | solution.py:38
  37.6 0.0 collective-permute-done.8
  37.6 0.7 %collective-permute-done.9 = bf16[128,256]{1,0:T(8,128)(2,1)S(1)} collective-permute-done((bf16[128,256]{1,0:T(8,128)(2,1)S(1)}, bf16[128,256]{1,0:T(8,128)(2,1)S(1)}, u32[]{:S(2)}, u32[]{:S(2)}) %collective-permute-start.9) | collective-permute-done | bytes 65568 | tf_op jit(solution)/shard_map/ppermute | solution.py:38
  38.3 0.7 %fusion.5 = (f32[64,256]{1,0:T(8,128)}, f32[64,256]{1,0:T(8,128)}) fusion(f32[128,256]{1,0:T(8,128)S(1)} %fusion.1), kind=kLoop, calls=%fused_computation.15 | loop fusion | bytes 262144 | tf_op jit(solution)/shard_map/slice | solution.py:290
  (7 shorter events, 0.2 us)
Async XLA Ops:
  2.0 5.3 %collective-permute-start = (bf16[48,640]{1,0:T(8,128)(2,1)S(1)}, bf16[48,640]{1,0:T(8,128)(2,1)S(1)}, u32[]{:S(2)}, u32[]{:S(2)}) collective-permute-start(bf16[48,640]{1,0:T(8,128)(2,1)S(1)} %get-tuple-element.22), channel_id=1, source_target_pairs={{0,8},{8,0},{16,24},{24,16},{1,9},{9,1},{17,25},{25,17},{2,10},{10... | collective-permute-start | bytes 184328 | tf_op jit(solution)/shard_map/ppermute | solution.py:38
  5.0 4.2 %collective-permute-start.1 = (bf16[48,640]{1,0:T(8,128)(2,1)S(1)}, bf16[48,640]{1,0:T(8,128)(2,1)S(1)}, u32[]{:S(2)}, u32[]{:S(2)}) collective-permute-start(bf16[48,640]{1,0:T(8,128)(2,1)S(1)} %get-tuple-element.23), channel_id=1, source_target_pairs={{0,16},{8,24},{16,0},{24,8},{1,17},{9,25},{17,1},{25,9},{2,18},{10... | collective-permute-start | bytes 184328 | tf_op jit(solution)/shard_map/ppermute | solution.py:38
  6.5 5.1 %collective-permute-start.2 = (bf16[48,640]{1,0:T(8,128)(2,1)S(1)}, bf16[48,640]{1,0:T(8,128)(2,1)S(1)}, u32[]{:S(2)}, u32[]{:S(2)}) collective-permute-start(bf16[48,640]{1,0:T(8,128)(2,1)S(1)} %get-tuple-element.24), channel_id=1, source_target_pairs={{0,24},{8,16},{16,8},{24,0},{1,25},{9,17},{17,9},{25,1},{2,26},{10... | collective-permute-start | bytes 184328 | tf_op jit(solution)/shard_map/ppermute | solution.py:38
  12.4 4.8 %collective-permute-start.3 = (f16[104,512]{1,0:T(8,128)(2,1)S(1)}, f16[104,512]{1,0:T(8,128)(2,1)S(1)}, u32[]{:S(2)}, u32[]{:S(2)}) collective-permute-start(f16[104,512]{1,0:T(8,128)(2,1)S(1)} %convert_element_type.39), channel_id=1, source_target_pairs={{0,1},{1,0},{2,3},{3,2},{4,5},{5,4},{6,7},{7,6},{8,9},{9,8},{10,11... | collective-permute-start | bytes 319496 | tf_op jit(solution)/shard_map/ppermute | solution.py:38
  17.4 6.8 %collective-permute-start.4 = (f16[104,512]{1,0:T(8,128)(2,1)S(1)}, f16[104,512]{1,0:T(8,128)(2,1)S(1)}, u32[]{:S(2)}, u32[]{:S(2)}) collective-permute-start(f16[104,512]{1,0:T(8,128)(2,1)S(1)} %convert_element_type.41), channel_id=1, source_target_pairs={{0,2},{1,3},{2,0},{3,1},{4,6},{5,7},{6,4},{7,5},{8,10},{9,11},{10,... | collective-permute-start | bytes 319496 | tf_op jit(solution)/shard_map/ppermute | solution.py:38
  20.3 4.0 %collective-permute-start.5 = (f32[1,128]{1,0:T(1,128)S(1)}, f32[1,128]{1,0:T(1,128)S(1)}, u32[]{:S(2)}, u32[]{:S(2)}) collective-permute-start(f32[1,128]{1,0:T(1,128)S(1)} %get-tuple-element.34.refs_3_), channel_id=1, source_target_pairs={{0,4},{4,0},{1,5},{5,1},{2,6},{6,2},{3,7},{7,3},{8,12},{12,8},{9,1... | collective-permute-start | bytes 1544 | tf_op jit(solution)/shard_map/ppermute | solution.py:38
  24.4 4.7 %collective-permute-start.6 = (bf16[96,512]{1,0:T(8,128)(2,1)S(1)}, bf16[96,512]{1,0:T(8,128)(2,1)S(1)}, u32[]{:S(2)}, u32[]{:S(2)}) collective-permute-start(bf16[96,512]{1,0:T(8,128)(2,1)S(1)} %shard_map.89.refs_0_), channel_id=1, source_target_pairs={{0,1},{1,0},{2,3},{3,2},{4,5},{5,4},{6,7},{7,6},{8,9},{9,8},{10,11... | collective-permute-start | bytes 294920 | tf_op jit(solution)/shard_map/ppermute | solution.py:38
  29.7 2.0 %collective-permute-start.7 = (f32[4,128,256]{2,1,0:T(8,128)S(1)}, f32[4,128,256]{2,1,0:T(8,128)S(1)}, u32[]{:S(2)}, u32[]{:S(2)}) collective-permute-start(f32[4,128,256]{2,1,0:T(8,128)S(1)} %pad_maximum_fusion), channel_id=1, source_target_pairs={{0,4},{4,0},{1,5},{5,1},{2,6},{6,2},{3,7},{7,3},{8,12},{12,8},{9,1... | collective-permute-start | bytes 1572872 | tf_op jit(solution)/shard_map/ppermute | solution.py:38
  31.8 5.8 %collective-permute-start.10 = (bf16[128,256]{1,0:T(8,128)(2,1)S(1)}, bf16[128,256]{1,0:T(8,128)(2,1)S(1)}, u32[]{:S(2)}, u32[]{:S(2)}) collective-permute-start(bf16[128,256]{1,0:T(8,128)(2,1)S(1)} %get-tuple-element.41), channel_id=1, source_target_pairs={{0,24},{8,16},{16,8},{24,0},{1,25},{9,17},{17,9},{25,1},{2,26},{10... | collective-permute-start | bytes 196616 | tf_op jit(solution)/shard_map/ppermute | solution.py:38
  31.9 5.7 %collective-permute-start.8 = (bf16[128,256]{1,0:T(8,128)(2,1)S(1)}, bf16[128,256]{1,0:T(8,128)(2,1)S(1)}, u32[]{:S(2)}, u32[]{:S(2)}) collective-permute-start(bf16[128,256]{1,0:T(8,128)(2,1)S(1)} %get-tuple-element.40), channel_id=1, source_target_pairs={{0,8},{8,0},{16,24},{24,16},{1,9},{9,1},{17,25},{25,17},{2,10},{10... | collective-permute-start | bytes 196616 | tf_op jit(solution)/shard_map/ppermute | solution.py:38
  33.8 4.5 %collective-permute-start.9 = (bf16[128,256]{1,0:T(8,128)(2,1)S(1)}, bf16[128,256]{1,0:T(8,128)(2,1)S(1)}, u32[]{:S(2)}, u32[]{:S(2)}) collective-permute-start(bf16[128,256]{1,0:T(8,128)(2,1)S(1)} %get-tuple-element.42), channel_id=1, source_target_pairs={{0,16},{8,24},{16,0},{24,8},{1,17},{9,25},{17,1},{25,9},{2,18},{10... | collective-permute-start | bytes 196616 | tf_op jit(solution)/shard_map/ppermute | solution.py:38

commit v7 on v5

v7 whole, which is shorter than its diff:
```python
import functools

import jax
import jax.numpy as jnp
from jax import lax
from jax.experimental import pallas as pl
from jax.experimental.pallas import tpu as pltpu
from jax.sharding import PartitionSpec as P

LANES = 128
ROW_TILE = 16
PACK_ROWS = 8
PACK_TOP = 14.0
TINY = 1e-37
VMEM = pl.BlockSpec(memory_space=pltpu.VMEM)
HBM = pl.BlockSpec(memory_space=pltpu.HBM)
SMALL = pltpu.CompilerParams(vmem_limit_bytes=16 * 1024 * 1024)
LARGE = pltpu.CompilerParams(vmem_limit_bytes=56 * 1024 * 1024)


def up_to(value, step):
    return -(-value // step) * step


def is_power(size):
    return size & (size - 1) == 0


def partner_to(size, me, step):
    return me ^ step if is_power(size) else (me + step) % size


def partner_from(size, me, step):
    return me ^ step if is_power(size) else (me + size - step) % size


def send(block, axis, step):
    size = lax.axis_size(axis)
    return lax.ppermute(block, axis, [(i, partner_to(size, i, step)) for i in range(size)])


def pack(value, out):
    height = value.shape[0]
    largest = jnp.max(jnp.max(jnp.abs(value), axis=0, keepdims=True), axis=1, keepdims=True)
    power = jnp.clip(jnp.ceil(jnp.log2(jnp.maximum(largest, TINY))), -100.0, 100.0)
    out[:height] = value * jnp.exp2(PACK_TOP - power)
    out[height:] = jnp.broadcast_to(power, (PACK_ROWS, value.shape[1]))


def unpack(block):
    height = block.shape[0] - PACK_ROWS
    return block[:height] * jnp.exp2(block[height : height + 1, :1] - PACK_TOP)


def cross(block, step):
    return send(block.astype(jnp.float16), "mdl", step).astype(jnp.float32)


def dot(left, right, contract=((1,), (0,))):
    return lax.dot_general(left, right, (contract, ((), ())), preferred_element_type=jnp.float32)


def dispatch_body(owners, local, room, extra, *refs):
    sources, refs = refs[:3], refs[3:]
    outs, refs = refs[:owners], refs[owners:]
    states, task, batch, sems = refs
    rows, width = states.shape
    copies = [
        pltpu.make_async_copy(source, target, sems.at[i])
        for i, (source, target) in enumerate(zip(sources, (states, task, batch)))
    ]
    for i in (1, 2, 0):
        copies[i].start()
    copies[1].wait()
    copies[2].wait()
    me = lax.axis_index("teach")
    task_list, batch_list = task[...], batch[...]
    group = up_to(owners * local, ROW_TILE)
    named = lax.broadcasted_iota(jnp.int32, (group, rows), 0) == task_list
    earlier = lax.broadcasted_iota(jnp.int32, (rows, rows), 0) < lax.broadcasted_iota(
        jnp.int32, (rows, rows), 1
    )
    named = named.astype(jnp.float32)
    before = dot(named.astype(jnp.bfloat16), earlier.astype(jnp.float32).astype(jnp.bfloat16))
    before = jnp.sum(before * named, axis=0, keepdims=True).astype(jnp.int32)
    owner = task_list // local if local > 1 else task_list
    step = owner ^ me if is_power(owners) else (owner - me + owners) % owners
    place = step * local + task_list % local if local > 1 else step
    slot = place * room + before
    index = lax.broadcasted_iota(jnp.int32, (owners * local * room, rows), 0)
    chosen = (index == slot).astype(jnp.float32)
    head = (index % (local * room) == 0).astype(jnp.float32)
    member = (lax.broadcasted_iota(jnp.int32, (extra, rows), 0) == batch_list).astype(jnp.float32)
    tags = dot(
        (chosen + 2.0 * head).astype(jnp.bfloat16), member.astype(jnp.bfloat16), ((1,), (1,))
    ).astype(jnp.bfloat16)
    copies[0].wait()
    moved = dot(chosen.astype(jnp.bfloat16), states[...]).astype(jnp.bfloat16)
    for k, out in enumerate(outs):
        span = slice(k * local * room, (k + 1) * local * room)
        out[:, :width] = moved[span]
        out[:, width:] = tags[span]


def weights_body(*refs):
    sources, outs, sems = refs[1:5], refs[5:9], refs[9]
    copies = [
        pltpu.make_async_copy(source, target, sems.at[i])
        for i, (source, target) in enumerate(zip(sources, outs))
    ]
    for copy in copies:
        copy.start()
    for copy in copies:
        copy.wait()


def student(rows, student_up):
    pre = dot(rows, student_up[...])
    sig = 1.0 / (1.0 + jnp.exp(-pre))
    return (pre * sig).astype(jnp.bfloat16), sig * (1.0 + pre * (1.0 - sig))


def half_error(local, first, rows, weights, act_out, slope_out):
    teach_in, teach_out, student_up, student_down = weights
    per_teacher = 2 * rows.shape[0] // local
    labels = None
    for l in range(local):
        hidden = dot(rows, teach_in[l])
        hidden = hidden / (1.0 + jnp.exp(-hidden))
        if local > 1:
            index = first + lax.broadcasted_iota(jnp.int32, hidden.shape, 0)
            hidden = jnp.where(index // per_teacher == l, hidden, 0.0)
        part = dot(hidden.astype(jnp.bfloat16), teach_out[l])
        labels = part if labels is None else labels + part
    act, slope = student(rows, student_up)
    act_out[...] = act
    slope_out[...] = slope
    return dot(act, student_down[...], ((1,), (1,))) - labels


def half_start(height, other):
    me = lax.axis_index("mdl")
    return pl.multiple_of(((me & 1) ^ other) * height, ROW_TILE)


def forward_other_body(owners, local, room, *refs):
    blocks, refs = refs[:owners], refs[owners:]
    weights, refs = refs[:4], refs[4:]
    rows_own, rows_other, tags_out, counts_out, packed, act, slope, rows_all, tags_all = refs
    width = rows_own.shape[1]
    full = [block[...] for block in blocks]
    counts = None
    for block in full:
        mine = jnp.floor(block[:1, width:].astype(jnp.float32) * 0.5)
        counts = mine if counts is None else counts + mine
    counts_out[...] = counts
    for l in range(local):
        for k, block in enumerate(full):
            start = (l * owners + k) * room
            rows_all[start : start + room] = block[l * room : (l + 1) * room, :width]
            tag = block[l * room : (l + 1) * room, width:].astype(jnp.float32)
            if l == 0:
                head = lax.broadcasted_iota(jnp.int32, tag.shape, 0) == 0
                tag = jnp.where(head, tag - 2.0 * jnp.floor(tag * 0.5), tag)
            tags_all[start : start + room] = tag
    height = rows_own.shape[0]
    mine, there = half_start(height, 0), half_start(height, 1)
    rows_own[...] = rows_all[pl.ds(mine, height)]
    tags_out[...] = tags_all[pl.ds(mine, height)]
    rows = rows_all[pl.ds(there, height)]
    rows_other[...] = rows
    pack(half_error(local, there, rows, weights, act, slope), packed)


def forward_own_body(local, rows, *refs):
    weights, (error, act, slope) = refs[:4], refs[4:]
    first = half_start(rows.shape[0], 0)
    error[...] = half_error(local, first, rows[...], weights, act, slope)


def neighbour_body(rows_own, rows_other, student_up, act_own, slope_own, act_other, slope_other):
    act_own[...], slope_own[...] = student(rows_own[...], student_up)
    act_other[...], slope_other[...] = student(rows_other[...], student_up)


def pair_body(own, arrived, total, packed):
    value = own[...] + unpack(arrived)
    total[...] = value
    pack(value, packed)


def scale_body(*refs):
    own, arrived, tags = refs[:3]
    counts, scaled = refs[3:-1], refs[-1]
    all_counts = counts[0][...]
    for piece in counts[1:]:
        all_counts = all_counts + piece[...]
    inverse = jnp.where(all_counts > 0, 2.0 / all_counts, 0.0)
    weight = jnp.sum(tags[...] * inverse, axis=1, keepdims=True)
    scaled[...] = ((own[...] + unpack(arrived)) * weight).astype(scaled.dtype)


def backward_body(first, groups, *refs):
    student_down, refs = refs[0], refs[1:]
    grad_up, grad_down = refs[-2:]
    if first:
        up, down = None, None
    else:
        up, down = refs[4 * groups][...], refs[4 * groups + 1][...]
    for i in range(groups):
        scaled, rows, act, slope = refs[4 * i : 4 * i + 4]
        error = scaled[...]
        part = dot(error, act[...], ((0,), (0,)))
        down = part if down is None else down + part
        pre_grad = (dot(error, student_down[...]) * slope[...]).astype(jnp.bfloat16)
        part = dot(rows[...], pre_grad, ((0,), (0,)))
        up = part if up is None else up + part
    grad_up[...] = up
    grad_down[...] = down


def kernel(body, outs, operands, flops, scratch=(), params=SMALL, places=None):
    return pl.pallas_call(
        body,
        out_shape=outs,
        in_specs=places or [VMEM] * len(operands),
        out_specs=[VMEM] * len(outs),
        scratch_shapes=list(scratch),
        cost_estimate=pl.CostEstimate(flops=flops, bytes_accessed=1 << 18, transcendentals=0),
        compiler_params=params,
    )(*operands)


def on_device(states, task_ids, student_batch, teach_in, teach_out, student_up, student_down):
    row_count, width = states.shape
    owners, studs, parts = lax.axis_size("teach"), lax.axis_size("stud"), lax.axis_size("mdl")
    local, _, hidden = teach_in.shape
    actions = teach_out.shape[2]
    units = student_up.shape[1]
    teachers, batches = owners * local, owners * studs
    room = up_to(3 * row_count // (2 * teachers), ROW_TILE)
    extra = up_to(batches, LANES)
    slots = teachers * room
    height = slots // 2
    f32, bf16 = jnp.float32, jnp.bfloat16

    def shape(rows, columns, dtype):
        return jax.ShapeDtypeStruct((rows, columns), dtype)

    half, packed = shape(height, actions, f32), shape(height + PACK_ROWS, actions, f32)
    half_rows = shape(height, width, bf16)
    half_act, half_slope = shape(height, units, bf16), shape(height, units, f32)
    tokens = [ids.reshape(1, row_count) for ids in (task_ids, student_batch)]
    blocks = kernel(
        functools.partial(dispatch_body, owners, local, room, extra),
        [pltpu.VMEM((local * room, width + extra), bf16)] * owners,
        (states, *tokens),
        2 * slots * row_count * width,
        [pltpu.VMEM(a.shape, a.dtype) for a in (states, *tokens)] + [pltpu.SemaphoreType.DMA((3,))],
        LARGE,
        [HBM] * 3,
    )
    arrived = {k: send(blocks[k], "teach", k) for k in range(owners - 1, 0, -1)}
    weights = (teach_in, teach_out, student_up, student_down)
    weights = kernel(
        weights_body,
        [pltpu.VMEM(w.shape, w.dtype) for w in weights],
        (blocks[0], *[pltpu.with_memory_space_constraint(w, pltpu.HBM) for w in weights]),
        0,
        [pltpu.SemaphoreType.DMA((4,))],
        SMALL,
        [VMEM] + [HBM] * 4,
    )
    blocks = [blocks[0]] + [arrived[k] for k in range(1, owners)]
    work = 2 * height * 2 * width * (hidden + units)
    rows_own, rows_other, tags, counts, other, act_other, slope_other = kernel(
        functools.partial(forward_other_body, owners, local, room),
        [half_rows, half_rows, shape(height, extra, f32), shape(1, extra, f32), packed]
        + [half_act, half_slope],
        (*blocks, *weights),
        work,
        [pltpu.VMEM((slots, width), bf16), pltpu.VMEM((slots, extra), f32)],
    )
    arrived = cross(other, 1)
    own, act_own, slope_own = kernel(
        functools.partial(forward_own_body, local),
        [half, half_act, half_slope],
        (rows_own, *weights),
        work,
    )
    all_counts, mates = [counts], []
    for k in range(1, studs):
        all_counts.append(send(counts, "stud", k))
        mates.append((send(rows_own, "stud", k), send(rows_other, "stud", k)))
    own, arrived, all_counts, mates = lax.optimization_barrier((own, arrived, all_counts, mates))
    step = 2
    while step < parts:
        own, other = kernel(pair_body, [half, packed], (own, arrived), 0)
        arrived = cross(other, step)
        step *= 2
    groups = [(rows_own, act_own, slope_own, rows_other, act_other, slope_other)]
    for first, second in mates:
        known = kernel(
            neighbour_body,
            [half_act, half_slope] * 2,
            (first, second, weights[2]),
            4 * height * width * units,
        )
        groups.append((first, *known[:2], second, *known[2:]))
    own, arrived, groups = lax.optimization_barrier((own, arrived, groups))
    (scaled,) = kernel(scale_body, [shape(height, actions, bf16)], (own, arrived, tags, *all_counts), 0)
    from_pair = send(scaled, "mdl", 1)
    ours = [scaled] + [send(scaled, "stud", k) for k in range(1, studs)]
    work = 6 * height * width * units
    grads = [shape(width, units, f32), shape(actions, units, f32)]
    sums = kernel(
        functools.partial(backward_body, True, studs),
        grads,
        [weights[3]] + [a for s, g in zip(ours, groups) for a in (s, *g[:3])],
        studs * work,
    )
    from_pair, sums = lax.optimization_barrier((from_pair, sums))
    for k in range(studs):
        theirs = send(from_pair, "stud", k) if k else from_pair
        sums = kernel(
            functools.partial(backward_body, False, 1),
            grads,
            (weights[3], theirs, *groups[k][3:], *sums),
            work,
        )
    grad_up, grad_down = sums
    heights = (width // (owners * studs), actions // (owners * studs))

    def pieces(stud):
        return jnp.concatenate(
            [
                lax.dynamic_index_in_dim(g.reshape(owners, studs, h, units), stud, 1, False)
                for g, h in zip((grad_up, grad_down), heights)
            ],
            axis=1,
        )

    half = pieces(lax.axis_index("stud"))
    me = lax.axis_index("teach")
    part = lax.dynamic_index_in_dim(half, me, 0, False)
    arrived = [
        send(lax.dynamic_index_in_dim(half, partner_to(owners, me, k), 0, False).astype(bf16), "teach", k)
        for k in range(owners - 1, 0, -1)
    ]
    for piece in arrived:
        part = part + piece.astype(f32)
    return part[: heights[0]], part[heights[0] :]


def solution(mesh):
    in_specs = (
        P(("teach", "stud"), None),
        P(("teach", "stud"), None),
        P(("teach", "stud"), None),
        P("teach", None, "mdl"),
        P("teach", "mdl", None),
        P(None, "mdl"),
        P(None, "mdl"),
    )
    out_specs = (P(("teach", "stud"), "mdl"), P(("teach", "stud"), "mdl"))
    return jax.shard_map(
        on_device, mesh=mesh, in_specs=in_specs, out_specs=out_specs, check_vma=False
    )
```

time: 47 us -> 38.4 us (0.82)
  waiting for transfers between devices: 21.3 us -> 17.4 us
  other arithmetic: 2.49 us -> 0.13 us
  local copies, waits for them, and re-layouts: 2.79 us -> 0.7 us
  Pallas kernels: 6.33 us -> 5.51 us
  starting transfers between devices: 13.1 us -> 13.7 us
    ppermute x11 -> x14, waiting for transfers between devices: 21.3 us -> 17.4 us  [send(): lax.ppermute(block, axis, [(i, partner_to(size, i, step)) for i in range(...]
    convert_element_type x4, other arithmetic: 2.35 us -> 0.06 us  [cross(): return send(block.astype(jnp.float16), 'mdl', step).astype(jnp.float32)]
    unnamed x10 -> x0, local copies, waits for them, and re-layouts: 2 us -> none
    pallas_call x5 -> x10, Pallas kernels: 6.33 us -> 5.51 us  [kernel(): pl.pallas_call(body, out_shape=outs, in_specs=places or [VMEM] * len(oper...]
    ppermute x11 -> x14, starting transfers between devices: 13.1 us -> 13.7 us  [send(): lax.ppermute(block, axis, [(i, partner_to(size, i, step)) for i in range(...]
  transfers between devices with their start and end apart: 11 -> 14, of which waited for: 9 -> 9; matrix products, arithmetic and copies ran while one was open for 1% -> 0% of each run, Pallas kernels for 0% -> 8%
where the time goes in v7:
time: 38.4 us; the launch traced here: 38.3 us
  waiting for transfers between devices  17.4 us (45%)
  starting transfers between devices  13.7 us (36%)
  Pallas kernels  5.51 us (14%)
  between operations  0.81 us (2%)
  local copies, waits for them, and re-layouts  0.7 us (2%)
    ppermute x14, waiting for transfers between devices, send(): lax.ppermute(block, axis, [(i, partner_to(size, i, step)) for i in range(...  17.4 us
    ppermute x14, starting transfers between devices, send(): lax.ppermute(block, axis, [(i, partner_to(size, i, step)) for i in range(...  13.7 us
    pallas_call x10, Pallas kernels, kernel(): pl.pallas_call(body, out_shape=outs, in_specs=places or [VMEM] * len(oper...  5.51 us
  transfers between devices with their start and end apart: 14, of which 9 were waited for; matrix products, arithmetic and copies ran while one was open for 0% of the time, Pallas kernels for 8%

profile of v7, /device:TPU:0, one launch (start us, length us, event | category | flops | bytes accessed | tf_op | source)
XLA Modules:
  0.0 38.3 jit_solution(3572821500108705031)
XLA Ops:
  0.6 1.2 %shard_map.86 = (bf16[48,640]{1,0:T(8,128)(2,1)S(1)}, bf16[48,640]{1,0:T(8,128)(2,1)S(1)}, bf16[48,640]{1,0:T(8,128)(2,1)S(1)}, bf16[48,640]{1,0:T(8,128)(2,1)S(1)}) custom-call(bf16[128,512]{1,0:T(8,128)(2,1)} %refs_0_.1, s32[1,128]{1,0:T(1,128)} %bitcast.24, s32[1,128]{1,0:T(1,128)} %bitcast.25), custom_call_target="tpu_custom_call" | custom-call | flops 25165824 | bytes 262144 | tf_op jit(solution)/shard_map/pallas_call | solution.py:223
  1.8 3.0 %collective-permute-start = (bf16[48,640]{1,0:T(8,128)(2,1)S(1)}, bf16[48,640]{1,0:T(8,128)(2,1)S(1)}, u32[]{:S(2)}, u32[]{:S(2)}) collective-permute-start(bf16[48,640]{1,0:T(8,128)(2,1)S(1)} %get-tuple-element.57), channel_id=1, source_target_pairs={{0,8},{8,0},{16,24},{24,16},{1,9},{9,1},{17,25},{25,17},{2,10},{10... | collective-permute-start | bytes 184328 | tf_op jit(solution)/shard_map/ppermute | solution.py:39
  4.8 1.5 %collective-permute-start.1 = (bf16[48,640]{1,0:T(8,128)(2,1)S(1)}, bf16[48,640]{1,0:T(8,128)(2,1)S(1)}, u32[]{:S(2)}, u32[]{:S(2)}) collective-permute-start(bf16[48,640]{1,0:T(8,128)(2,1)S(1)} %get-tuple-element.58), channel_id=1, source_target_pairs={{0,16},{8,24},{16,0},{24,8},{1,17},{9,25},{17,1},{25,9},{2,18},{10... | collective-permute-start | bytes 184328 | tf_op jit(solution)/shard_map/ppermute | solution.py:39
  6.4 0.0 collective-permute-start.2
  6.4 1.2 %shard_map.87 = (bf16[1,512,256]{2,1,0:T(8,128)(2,1)S(1)}, bf16[1,256,512]{2,1,0:T(8,128)(2,1)S(1)}, bf16[512,256]{1,0:T(8,128)(2,1)S(1)}, bf16[512,256]{1,0:T(8,128)(2,1)S(1)}) custom-call(bf16[48,640]{1,0:T(8,128)(2,1)S(1)} %get-tuple-element.55.refs_0_, bf16[1,512,256]{2,1,0:T(8,128)(2,1)} %refs_1_.1, bf16[1,256,512]{2,1,0:T(8,128)(2,1)} %refs_2_.1, ...), custom_call_target="tpu_custom_call" | custom-call | bytes 262144 | tf_op jit(solution)/shard_map/pallas_call | solution.py:223
  7.6 0.0 collective-permute-done.refs_1_
  7.6 1.4 %collective-permute-done.1.refs_2_ = bf16[48,640]{1,0:T(8,128)(2,1)S(1)} collective-permute-done((bf16[48,640]{1,0:T(8,128)(2,1)S(1)}, bf16[48,640]{1,0:T(8,128)(2,1)S(1)}, u32[]{:S(2)}, u32[]{:S(2)}) %collective-permute-start.1) | collective-permute-done | bytes 61472 | tf_op jit(solution)/shard_map/ppermute | solution.py:39
  9.1 2.4 %collective-permute-done.2.refs_3_ = bf16[48,640]{1,0:T(8,128)(2,1)S(1)} collective-permute-done((bf16[48,640]{1,0:T(8,128)(2,1)S(1)}, bf16[48,640]{1,0:T(8,128)(2,1)S(1)}, u32[]{:S(2)}, u32[]{:S(2)}) %collective-permute-start.2) | collective-permute-done | bytes 61472 | tf_op jit(solution)/shard_map/ppermute | solution.py:39
  11.5 0.6 %shard_map.88 = (bf16[96,512]{1,0:T(8,128)(2,1)S(1)}, bf16[96,512]{1,0:T(8,128)(2,1)S(1)}, f32[96,128]{1,0:T(8,128)S(1)}, f32[1,128]{1,0:T(1,128)S(1)}, f32[104,...) custom-call(bf16[48,640]{1,0:T(8,128)(2,1)S(1)} %get-tuple-element.55.refs_0_, ...), custom_call_target="tpu_custom_call" | custom-call | flops 100663296 | bytes 262144 | tf_op jit(solution)/shard_map/pallas_call | solution.py:223
  12.1 1.6 %collective-permute-start.3 = (f16[104,512]{1,0:T(8,128)(2,1)S(1)}, f16[104,512]{1,0:T(8,128)(2,1)S(1)}, u32[]{:S(2)}, u32[]{:S(2)}) collective-permute-start(f16[104,512]{1,0:T(8,128)(2,1)S(1)} %convert_element_type.39), channel_id=1, source_target_pairs={{0,1},{1,0},{2,3},{3,2},{4,5},{5,4},{6,7},{7,6},{8,9},{9,8},{10,11... | collective-permute-start | bytes 319496 | tf_op jit(solution)/shard_map/ppermute | solution.py:39
  13.7 0.5 %collective-permute-start.6 = (bf16[96,512]{1,0:T(8,128)(2,1)S(1)}, bf16[96,512]{1,0:T(8,128)(2,1)S(1)}, u32[]{:S(2)}, u32[]{:S(2)}) collective-permute-start(bf16[96,512]{1,0:T(8,128)(2,1)S(1)} %get-tuple-element.99.refs_2_), channel_id=1, source_target_pairs={{0,4},{4,0},{1,5},{5,1},{2,6},{6,2},{3,7},{7,3},{8,12},{12,8},{9,1... | collective-permute-start | bytes 294920 | tf_op jit(solution)/shard_map/ppermute | solution.py:39
  14.2 0.4 %shard_map.89 = (f32[96,512]{1,0:T(8,128)S(1)}, bf16[96,256]{1,0:T(8,128)(2,1)S(1)}, f32[96,256]{1,0:T(8,128)S(1)}) custom-call(bf16[96,512]{1,0:T(8,128)(2,1)S(1)} %get-tuple-element.87.rows.refs_2_, bf16[1,512,256]{2,1,0:T(8,128)(2,1)S(1)} %get-tuple-element.60.refs_4_.refs_0_, bf16[1,256,512]{2,1,0:T(8,128)(2,1)S(1)} %get-tuple-element.61.refs_5_.refs_1_, ...), custom_call_target="tpu_custom_call" | custom-call | flops 100663296 | bytes 262144 | tf_op jit(solution)/shard_map/pallas_call | solution.py:223
  14.7 2.2 %collective-permute-done.3 = f16[104,512]{1,0:T(8,128)(2,1)S(1)} collective-permute-done((f16[104,512]{1,0:T(8,128)(2,1)S(1)}, f16[104,512]{1,0:T(8,128)(2,1)S(1)}, u32[]{:S(2)}, u32[]{:S(2)}) %collective-permute-start.3) | collective-permute-done | bytes 106528 | tf_op jit(solution)/shard_map/ppermute | solution.py:39
  16.9 0.2 shard_map.90
  17.1 2.6 %collective-permute-start.7 = (f16[104,512]{1,0:T(8,128)(2,1)S(1)}, f16[104,512]{1,0:T(8,128)(2,1)S(1)}, u32[]{:S(2)}, u32[]{:S(2)}) collective-permute-start(f16[104,512]{1,0:T(8,128)(2,1)S(1)} %convert_element_type.41), channel_id=1, source_target_pairs={{0,2},{1,3},{2,0},{3,1},{4,6},{5,7},{6,4},{7,5},{8,10},{9,11},{10,... | collective-permute-start | bytes 319496 | tf_op jit(solution)/shard_map/ppermute | solution.py:39
  19.8 0.3 shard_map.91
  20.1 3.9 %collective-permute-done.7 = f16[104,512]{1,0:T(8,128)(2,1)S(1)} collective-permute-done((f16[104,512]{1,0:T(8,128)(2,1)S(1)}, f16[104,512]{1,0:T(8,128)(2,1)S(1)}, u32[]{:S(2)}, u32[]{:S(2)}) %collective-permute-start.7) | collective-permute-done | bytes 106528 | tf_op jit(solution)/shard_map/ppermute | solution.py:39
  24.0 0.1 shard_map.92.refs_1_
  24.1 0.1 collective-permute-start.9
  24.2 0.7 %collective-permute-start.8 = (bf16[96,512]{1,0:T(8,128)(2,1)S(1)}, bf16[96,512]{1,0:T(8,128)(2,1)S(1)}, u32[]{:S(2)}, u32[]{:S(2)}) collective-permute-start(bf16[96,512]{1,0:T(8,128)(2,1)S(1)} %shard_map.92.refs_1_), channel_id=1, source_target_pairs={{0,1},{1,0},{2,3},{3,2},{4,5},{5,4},{6,7},{7,6},{8,9},{9,8},{10,11... | collective-permute-start | bytes 294920 | tf_op jit(solution)/shard_map/ppermute | solution.py:39
  24.9 0.6 %collective-permute-done.9.refs_5_ = bf16[96,512]{1,0:T(8,128)(2,1)S(1)} collective-permute-done((bf16[96,512]{1,0:T(8,128)(2,1)S(1)}, bf16[96,512]{1,0:T(8,128)(2,1)S(1)}, u32[]{:S(2)}, u32[]{:S(2)}) %collective-permute-start.9) | collective-permute-done | bytes 98336 | tf_op jit(solution)/shard_map/ppermute | solution.py:39
  25.5 0.6 %shard_map.93 = (f32[512,256]{1,0:T(8,128)S(1)}, f32[512,256]{1,0:T(8,128)S(1)}) custom-call(bf16[512,256]{1,0:T(8,128)(2,1)S(1)} %get-tuple-element.56.refs_7_.refs_3_.refs_0_, bf16[96,512]{1,0:T(8,128)(2,1)S(1)} %shard_map.92.refs_1_, bf16[96,512]{1,0:T(8,128)(2,1)S(1)} %get-tuple-element.87.rows.refs_2_, bf16[96,256]{1,0:T(8,128)(2,1)S(1)} %get-tuple-element.88.refs_3_, ...), custom_call_target="tpu_custom_call" | custom-call | flops 150994944 | bytes 262144 | tf_op jit(solution)/shard_map/pallas_call | solution.py:223
  26.1 3.3 %collective-permute-done.8.refs_1_ = bf16[96,512]{1,0:T(8,128)(2,1)S(1)} collective-permute-done((bf16[96,512]{1,0:T(8,128)(2,1)S(1)}, bf16[96,512]{1,0:T(8,128)(2,1)S(1)}, u32[]{:S(2)}, u32[]{:S(2)}) %collective-permute-start.8) | collective-permute-done | bytes 98336 | tf_op jit(solution)/shard_map/ppermute | solution.py:39
  29.4 0.4 %shard_map.94 = (f32[512,256]{1,0:T(8,128)S(1)}, f32[512,256]{1,0:T(8,128)S(1)}) custom-call(bf16[512,256]{1,0:T(8,128)(2,1)S(1)} %get-tuple-element.56.refs_7_.refs_3_.refs_0_, bf16[96,512]{1,0:T(8,128)(2,1)S(1)} %collective-permute-done.8.refs_1_, bf16[96,512]{1,0:T(8,128)(2,1)S(1)} %get-tuple-element.99.refs_2_, ...), custom_call_target="tpu_custom_call" | custom-call | flops 75497472 | bytes 262144 | tf_op jit(solution)/shard_map/pallas_call | solution.py:223
  29.9 0.8 %collective-permute-done.10.refs_1_ = bf16[96,512]{1,0:T(8,128)(2,1)S(1)} collective-permute-done((bf16[96,512]{1,0:T(8,128)(2,1)S(1)}, bf16[96,512]{1,0:T(8,128)(2,1)S(1)}, u32[]{:S(2)}, u32[]{:S(2)}) %collective-permute-start.10) | collective-permute-done | bytes 98336 | tf_op jit(solution)/shard_map/ppermute | solution.py:39
  30.7 0.4 %shard_map.95 = (f32[512,256]{1,0:T(8,128)S(1)}, f32[512,256]{1,0:T(8,128)S(1)}) custom-call(bf16[512,256]{1,0:T(8,128)(2,1)S(1)} %get-tuple-element.56.refs_7_.refs_3_.refs_0_, bf16[96,512]{1,0:T(8,128)(2,1)S(1)} %collective-permute-done.10.refs_1_, bf16[96,512]{1,0:T(8,128)(2,1)S(1)} %collective-permute-done.6.rows_other.refs_2_, ...), custom_call_target="tpu_custom_call" | custom-call | flops 75497472 | bytes 262144 | tf_op jit(solution)/shard_map/pallas_call | solution.py:223
  31.2 0.1 collective-permute-start.11
  31.3 2.0 %collective-permute-start.12 = (bf16[128,256]{1,0:T(8,128)(2,1)S(1)}, bf16[128,256]{1,0:T(8,128)(2,1)S(1)}, u32[]{:S(2)}, u32[]{:S(2)}) collective-permute-start(bf16[128,256]{1,0:T(8,128)(2,1)S(1)} %get-tuple-element.109), channel_id=1, source_target_pairs={{0,16},{8,24},{16,0},{24,8},{1,17},{9,25},{17,1},{25,9},{2,18},{10... | collective-permute-start | bytes 196616 | tf_op jit(solution)/shard_map/ppermute | solution.py:39
  33.3 1.5 %collective-permute-start.13 = (bf16[128,256]{1,0:T(8,128)(2,1)S(1)}, bf16[128,256]{1,0:T(8,128)(2,1)S(1)}, u32[]{:S(2)}, u32[]{:S(2)}) collective-permute-start(bf16[128,256]{1,0:T(8,128)(2,1)S(1)} %get-tuple-element.110), channel_id=1, source_target_pairs={{0,8},{8,0},{16,24},{24,16},{1,9},{9,1},{17,25},{25,17},{2,10},{10... | collective-permute-start | bytes 196616 | tf_op jit(solution)/shard_map/ppermute | solution.py:39
  34.8 2.3 %collective-permute-done.11 = bf16[128,256]{1,0:T(8,128)(2,1)S(1)} collective-permute-done((bf16[128,256]{1,0:T(8,128)(2,1)S(1)}, bf16[128,256]{1,0:T(8,128)(2,1)S(1)}, u32[]{:S(2)}, u32[]{:S(2)}) %collective-permute-start.11) | collective-permute-done | bytes 65568 | tf_op jit(solution)/shard_map/ppermute | solution.py:39
  37.1 0.5 %collective-permute-done.13 = bf16[128,256]{1,0:T(8,128)(2,1)S(1)} collective-permute-done((bf16[128,256]{1,0:T(8,128)(2,1)S(1)}, bf16[128,256]{1,0:T(8,128)(2,1)S(1)}, u32[]{:S(2)}, u32[]{:S(2)}) %collective-permute-start.13) | collective-permute-done | bytes 65568 | tf_op jit(solution)/shard_map/ppermute | solution.py:39
  37.6 0.7 %fusion.14 = (f32[64,256]{1,0:T(8,128)}, f32[64,256]{1,0:T(8,128)}) fusion(f32[128,256]{1,0:T(8,128)S(1)} %fusion.6), kind=kLoop, calls=%fused_computation.24 | loop fusion | bytes 262144 | tf_op jit(solution)/shard_map/slice | solution.py:352
  (14 shorter events, 0.2 us)
Async XLA Ops:
  1.8 5.8 %collective-permute-start = (bf16[48,640]{1,0:T(8,128)(2,1)S(1)}, bf16[48,640]{1,0:T(8,128)(2,1)S(1)}, u32[]{:S(2)}, u32[]{:S(2)}) collective-permute-start(bf16[48,640]{1,0:T(8,128)(2,1)S(1)} %get-tuple-element.57), channel_id=1, source_target_pairs={{0,8},{8,0},{16,24},{24,16},{1,9},{9,1},{17,25},{25,17},{2,10},{10... | collective-permute-start | bytes 184328 | tf_op jit(solution)/shard_map/ppermute | solution.py:39
  4.8 4.2 %collective-permute-start.1 = (bf16[48,640]{1,0:T(8,128)(2,1)S(1)}, bf16[48,640]{1,0:T(8,128)(2,1)S(1)}, u32[]{:S(2)}, u32[]{:S(2)}) collective-permute-start(bf16[48,640]{1,0:T(8,128)(2,1)S(1)} %get-tuple-element.58), channel_id=1, source_target_pairs={{0,16},{8,24},{16,0},{24,8},{1,17},{9,25},{17,1},{25,9},{2,18},{10... | collective-permute-start | bytes 184328 | tf_op jit(solution)/shard_map/ppermute | solution.py:39
  6.4 5.1 %collective-permute-start.2 = (bf16[48,640]{1,0:T(8,128)(2,1)S(1)}, bf16[48,640]{1,0:T(8,128)(2,1)S(1)}, u32[]{:S(2)}, u32[]{:S(2)}) collective-permute-start(bf16[48,640]{1,0:T(8,128)(2,1)S(1)} %get-tuple-element.59), channel_id=1, source_target_pairs={{0,24},{8,16},{16,8},{24,0},{1,25},{9,17},{17,9},{25,1},{2,26},{10... | collective-permute-start | bytes 184328 | tf_op jit(solution)/shard_map/ppermute | solution.py:39
  12.1 4.8 %collective-permute-start.3 = (f16[104,512]{1,0:T(8,128)(2,1)S(1)}, f16[104,512]{1,0:T(8,128)(2,1)S(1)}, u32[]{:S(2)}, u32[]{:S(2)}) collective-permute-start(f16[104,512]{1,0:T(8,128)(2,1)S(1)} %convert_element_type.39), channel_id=1, source_target_pairs={{0,1},{1,0},{2,3},{3,2},{4,5},{5,4},{6,7},{7,6},{8,9},{9,8},{10,11... | collective-permute-start | bytes 319496 | tf_op jit(solution)/shard_map/ppermute | solution.py:39
  13.7 3.2 %collective-permute-start.5 = (bf16[96,512]{1,0:T(8,128)(2,1)S(1)}, bf16[96,512]{1,0:T(8,128)(2,1)S(1)}, u32[]{:S(2)}, u32[]{:S(2)}) collective-permute-start(bf16[96,512]{1,0:T(8,128)(2,1)S(1)} %get-tuple-element.87.rows.refs_2_), channel_id=1, source_target_pairs={{0,4},{4,0},{1,5},{5,1},{2,6},{6,2},{3,7},{7,3},{8,12},{12,8},{9,1... | collective-permute-start | bytes 294920 | tf_op jit(solution)/shard_map/ppermute | solution.py:39
  13.7 3.2 %collective-permute-start.6 = (bf16[96,512]{1,0:T(8,128)(2,1)S(1)}, bf16[96,512]{1,0:T(8,128)(2,1)S(1)}, u32[]{:S(2)}, u32[]{:S(2)}) collective-permute-start(bf16[96,512]{1,0:T(8,128)(2,1)S(1)} %get-tuple-element.99.refs_2_), channel_id=1, source_target_pairs={{0,4},{4,0},{1,5},{5,1},{2,6},{6,2},{3,7},{7,3},{8,12},{12,8},{9,1... | collective-permute-start | bytes 294920 | tf_op jit(solution)/shard_map/ppermute | solution.py:39
  14.2 2.6 %collective-permute-start.4 = (f32[1,128]{1,0:T(1,128)S(1)}, f32[1,128]{1,0:T(1,128)S(1)}, u32[]{:S(2)}, u32[]{:S(2)}) collective-permute-start(f32[1,128]{1,0:T(1,128)S(1)} %get-tuple-element.85.refs_3_), channel_id=1, source_target_pairs={{0,4},{4,0},{1,5},{5,1},{2,6},{6,2},{3,7},{7,3},{8,12},{12,8},{9,1... | collective-permute-start | bytes 1544 | tf_op jit(solution)/shard_map/ppermute | solution.py:39
  17.1 6.8 %collective-permute-start.7 = (f16[104,512]{1,0:T(8,128)(2,1)S(1)}, f16[104,512]{1,0:T(8,128)(2,1)S(1)}, u32[]{:S(2)}, u32[]{:S(2)}) collective-permute-start(f16[104,512]{1,0:T(8,128)(2,1)S(1)} %convert_element_type.41), channel_id=1, source_target_pairs={{0,2},{1,3},{2,0},{3,1},{4,6},{5,7},{6,4},{7,5},{8,10},{9,11},{10,... | collective-permute-start | bytes 319496 | tf_op jit(solution)/shard_map/ppermute | solution.py:39
  24.1 1.4 %collective-permute-start.9 = (bf16[96,512]{1,0:T(8,128)(2,1)S(1)}, bf16[96,512]{1,0:T(8,128)(2,1)S(1)}, u32[]{:S(2)}, u32[]{:S(2)}) collective-permute-start(bf16[96,512]{1,0:T(8,128)(2,1)S(1)} %shard_map.92.refs_1_), channel_id=1, source_target_pairs={{0,4},{4,0},{1,5},{5,1},{2,6},{6,2},{3,7},{7,3},{8,12},{12,8},{9,1... | collective-permute-start | bytes 294920 | tf_op jit(solution)/shard_map/ppermute | solution.py:39
  24.2 5.2 %collective-permute-start.8 = (bf16[96,512]{1,0:T(8,128)(2,1)S(1)}, bf16[96,512]{1,0:T(8,128)(2,1)S(1)}, u32[]{:S(2)}, u32[]{:S(2)}) collective-permute-start(bf16[96,512]{1,0:T(8,128)(2,1)S(1)} %shard_map.92.refs_1_), channel_id=1, source_target_pairs={{0,1},{1,0},{2,3},{3,2},{4,5},{5,4},{6,7},{7,6},{8,9},{9,8},{10,11... | collective-permute-start | bytes 294920 | tf_op jit(solution)/shard_map/ppermute | solution.py:39
  29.4 1.3 %collective-permute-start.10 = (bf16[96,512]{1,0:T(8,128)(2,1)S(1)}, bf16[96,512]{1,0:T(8,128)(2,1)S(1)}, u32[]{:S(2)}, u32[]{:S(2)}) collective-permute-start(bf16[96,512]{1,0:T(8,128)(2,1)S(1)} %collective-permute-done.8.refs_1_), channel_id=1, source_target_pairs={{0,4},{4,0},{1,5},{5,1},{2,6},{6,2},{3,7},{7,3},{8,12},{12,8},{9,1... | collective-permute-start | bytes 294920 | tf_op jit(solution)/shard_map/ppermute | solution.py:39
  31.2 5.8 %collective-permute-start.11 = (bf16[128,256]{1,0:T(8,128)(2,1)S(1)}, bf16[128,256]{1,0:T(8,128)(2,1)S(1)}, u32[]{:S(2)}, u32[]{:S(2)}) collective-permute-start(bf16[128,256]{1,0:T(8,128)(2,1)S(1)} %get-tuple-element.108), channel_id=1, source_target_pairs={{0,24},{8,16},{16,8},{24,0},{1,25},{9,17},{17,9},{25,1},{2,26},{10... | collective-permute-start | bytes 196616 | tf_op jit(solution)/shard_map/ppermute | solution.py:39
  31.3 5.7 %collective-permute-start.12 = (bf16[128,256]{1,0:T(8,128)(2,1)S(1)}, bf16[128,256]{1,0:T(8,128)(2,1)S(1)}, u32[]{:S(2)}, u32[]{:S(2)}) collective-permute-start(bf16[128,256]{1,0:T(8,128)(2,1)S(1)} %get-tuple-element.109), channel_id=1, source_target_pairs={{0,16},{8,24},{16,0},{24,8},{1,17},{9,25},{17,1},{25,9},{2,18},{10... | collective-permute-start | bytes 196616 | tf_op jit(solution)/shard_map/ppermute | solution.py:39
  33.3 4.3 %collective-permute-start.13 = (bf16[128,256]{1,0:T(8,128)(2,1)S(1)}, bf16[128,256]{1,0:T(8,128)(2,1)S(1)}, u32[]{:S(2)}, u32[]{:S(2)}) collective-permute-start(bf16[128,256]{1,0:T(8,128)(2,1)S(1)} %get-tuple-element.110), channel_id=1, source_target_pairs={{0,8},{8,0},{16,24},{24,16},{1,9},{9,1},{17,25},{25,17},{2,10},{10... | collective-permute-start | bytes 196616 | tf_op jit(solution)/shard_map/ppermute | solution.py:39

commit v8 on v7

--- a/solution.py
+++ b/solution.py
@@ -271,7 +271,7 @@
         SMALL,
         [VMEM] + [HBM] * 4,
     )
-    blocks = [blocks[0]] + [arrived[k] for k in range(1, owners)]
+    blocks = [blocks[0]] + list(arrived.values())
     work = 2 * height * 2 * width * (hidden + units)
     rows_own, rows_other, tags, counts, other, act_other, slope_other = kernel(
         functools.partial(forward_other_body, owners, local, room),

time: 38.4 us -> 37.7 us (0.982)
  waiting for transfers between devices: 17.4 us -> 16.6 us
    ppermute x14, waiting for transfers between devices: 17.4 us -> 16.6 us  [send(): lax.ppermute(block, axis, [(i, partner_to(size, i, step)) for i in range(...]
  transfers between devices with their start and end apart: 14 -> 14, of which waited for: 9 -> 11; matrix products, arithmetic and copies ran while one was open for 0% -> 0% of each run, Pallas kernels for 8% -> 8%
where the time goes in v8:
time: 37.7 us; the launch traced here: 37.6 us
  waiting for transfers between devices  16.6 us (44%)
  starting transfers between devices  13.8 us (37%)
  Pallas kernels  5.52 us (15%)
  between operations  0.79 us (2%)
  local copies, waits for them, and re-layouts  0.7 us (2%)
    ppermute x14, waiting for transfers between devices, send(): lax.ppermute(block, axis, [(i, partner_to(size, i, step)) for i in range(...  16.6 us
    ppermute x14, starting transfers between devices, send(): lax.ppermute(block, axis, [(i, partner_to(size, i, step)) for i in range(...  13.8 us
    pallas_call x10, Pallas kernels, kernel(): pl.pallas_call(body, out_shape=outs, in_specs=places or [VMEM] * len(oper...  5.52 us
  transfers between devices with their start and end apart: 14, of which 11 were waited for; matrix products, arithmetic and copies ran while one was open for 0% of the time, Pallas kernels for 8%

profile of v8, /device:TPU:0, one launch (start us, length us, event | category | flops | bytes accessed | tf_op | source)
XLA Modules:
  0.0 37.6 jit_solution(13478956758565406784)
XLA Ops:
  0.6 1.2 %shard_map.86 = (bf16[48,640]{1,0:T(8,128)(2,1)S(1)}, bf16[48,640]{1,0:T(8,128)(2,1)S(1)}, bf16[48,640]{1,0:T(8,128)(2,1)S(1)}, bf16[48,640]{1,0:T(8,128)(2,1)S(1)}) custom-call(bf16[128,512]{1,0:T(8,128)(2,1)} %refs_0_.1, s32[1,128]{1,0:T(1,128)} %bitcast.24, s32[1,128]{1,0:T(1,128)} %bitcast.25), custom_call_target="tpu_custom_call" | custom-call | flops 25165824 | bytes 262144 | tf_op jit(solution)/shard_map/pallas_call | solution.py:223
  1.8 4.0 %collective-permute-start = (bf16[48,640]{1,0:T(8,128)(2,1)S(1)}, bf16[48,640]{1,0:T(8,128)(2,1)S(1)}, u32[]{:S(2)}, u32[]{:S(2)}) collective-permute-start(bf16[48,640]{1,0:T(8,128)(2,1)S(1)} %get-tuple-element.57), channel_id=1, source_target_pairs={{0,24},{8,16},{16,8},{24,0},{1,25},{9,17},{17,9},{25,1},{2,26},{10... | collective-permute-start | bytes 184328 | tf_op jit(solution)/shard_map/ppermute | solution.py:39
  5.8 0.5 %collective-permute-start.1 = (bf16[48,640]{1,0:T(8,128)(2,1)S(1)}, bf16[48,640]{1,0:T(8,128)(2,1)S(1)}, u32[]{:S(2)}, u32[]{:S(2)}) collective-permute-start(bf16[48,640]{1,0:T(8,128)(2,1)S(1)} %get-tuple-element.58), channel_id=1, source_target_pairs={{0,16},{8,24},{16,0},{24,8},{1,17},{9,25},{17,1},{25,9},{2,18},{10... | collective-permute-start | bytes 184328 | tf_op jit(solution)/shard_map/ppermute | solution.py:39
  6.3 0.1 collective-permute-start.2
  6.4 1.2 %shard_map.87 = (bf16[1,512,256]{2,1,0:T(8,128)(2,1)S(1)}, bf16[1,256,512]{2,1,0:T(8,128)(2,1)S(1)}, bf16[512,256]{1,0:T(8,128)(2,1)S(1)}, bf16[512,256]{1,0:T(8,128)(2,1)S(1)}) custom-call(bf16[48,640]{1,0:T(8,128)(2,1)S(1)} %get-tuple-element.55.refs_0_, bf16[1,512,256]{2,1,0:T(8,128)(2,1)} %refs_1_.1, bf16[1,256,512]{2,1,0:T(8,128)(2,1)} %refs_2_.1, ...), custom_call_target="tpu_custom_call" | custom-call | bytes 262144 | tf_op jit(solution)/shard_map/pallas_call | solution.py:223
  7.7 0.3 collective-permute-done.refs_1_
  8.0 2.0 %collective-permute-done.1.refs_2_ = bf16[48,640]{1,0:T(8,128)(2,1)S(1)} collective-permute-done((bf16[48,640]{1,0:T(8,128)(2,1)S(1)}, bf16[48,640]{1,0:T(8,128)(2,1)S(1)}, u32[]{:S(2)}, u32[]{:S(2)}) %collective-permute-start.1) | collective-permute-done | bytes 61472 | tf_op jit(solution)/shard_map/ppermute | solution.py:39
  10.0 0.5 %collective-permute-done.2.refs_3_ = bf16[48,640]{1,0:T(8,128)(2,1)S(1)} collective-permute-done((bf16[48,640]{1,0:T(8,128)(2,1)S(1)}, bf16[48,640]{1,0:T(8,128)(2,1)S(1)}, u32[]{:S(2)}, u32[]{:S(2)}) %collective-permute-start.2) | collective-permute-done | bytes 61472 | tf_op jit(solution)/shard_map/ppermute | solution.py:39
  10.5 0.6 %shard_map.88 = (bf16[96,512]{1,0:T(8,128)(2,1)S(1)}, bf16[96,512]{1,0:T(8,128)(2,1)S(1)}, f32[96,128]{1,0:T(8,128)S(1)}, f32[1,128]{1,0:T(1,128)S(1)}, f32[104,...) custom-call(bf16[48,640]{1,0:T(8,128)(2,1)S(1)} %get-tuple-element.55.refs_0_, ...), custom_call_target="tpu_custom_call" | custom-call | flops 100663296 | bytes 262144 | tf_op jit(solution)/shard_map/pallas_call | solution.py:223
  11.1 1.6 %collective-permute-start.3 = (f16[104,512]{1,0:T(8,128)(2,1)S(1)}, f16[104,512]{1,0:T(8,128)(2,1)S(1)}, u32[]{:S(2)}, u32[]{:S(2)}) collective-permute-start(f16[104,512]{1,0:T(8,128)(2,1)S(1)} %convert_element_type.39), channel_id=1, source_target_pairs={{0,1},{1,0},{2,3},{3,2},{4,5},{5,4},{6,7},{7,6},{8,9},{9,8},{10,11... | collective-permute-start | bytes 319496 | tf_op jit(solution)/shard_map/ppermute | solution.py:39
  12.8 0.5 %collective-permute-start.6 = (bf16[96,512]{1,0:T(8,128)(2,1)S(1)}, bf16[96,512]{1,0:T(8,128)(2,1)S(1)}, u32[]{:S(2)}, u32[]{:S(2)}) collective-permute-start(bf16[96,512]{1,0:T(8,128)(2,1)S(1)} %get-tuple-element.99.refs_2_), channel_id=1, source_target_pairs={{0,4},{4,0},{1,5},{5,1},{2,6},{6,2},{3,7},{7,3},{8,12},{12,8},{9,1... | collective-permute-start | bytes 294920 | tf_op jit(solution)/shard_map/ppermute | solution.py:39
  13.3 0.4 %shard_map.89 = (f32[96,512]{1,0:T(8,128)S(1)}, bf16[96,256]{1,0:T(8,128)(2,1)S(1)}, f32[96,256]{1,0:T(8,128)S(1)}) custom-call(bf16[96,512]{1,0:T(8,128)(2,1)S(1)} %get-tuple-element.87.rows.refs_2_, bf16[1,512,256]{2,1,0:T(8,128)(2,1)S(1)} %get-tuple-element.60.refs_4_.refs_0_, bf16[1,256,512]{2,1,0:T(8,128)(2,1)S(1)} %get-tuple-element.61.refs_5_.refs_1_, ...), custom_call_target="tpu_custom_call" | custom-call | flops 100663296 | bytes 262144 | tf_op jit(solution)/shard_map/pallas_call | solution.py:223
  13.7 2.2 %collective-permute-done.3 = f16[104,512]{1,0:T(8,128)(2,1)S(1)} collective-permute-done((f16[104,512]{1,0:T(8,128)(2,1)S(1)}, f16[104,512]{1,0:T(8,128)(2,1)S(1)}, u32[]{:S(2)}, u32[]{:S(2)}) %collective-permute-start.3) | collective-permute-done | bytes 106528 | tf_op jit(solution)/shard_map/ppermute | solution.py:39
  15.9 0.2 shard_map.90
  16.2 2.7 %collective-permute-start.7 = (f16[104,512]{1,0:T(8,128)(2,1)S(1)}, f16[104,512]{1,0:T(8,128)(2,1)S(1)}, u32[]{:S(2)}, u32[]{:S(2)}) collective-permute-start(f16[104,512]{1,0:T(8,128)(2,1)S(1)} %convert_element_type.41), channel_id=1, source_target_pairs={{0,2},{1,3},{2,0},{3,1},{4,6},{5,7},{6,4},{7,5},{8,10},{9,11},{10,... | collective-permute-start | bytes 319496 | tf_op jit(solution)/shard_map/ppermute | solution.py:39
  18.8 0.3 shard_map.91
  19.1 3.9 %collective-permute-done.7 = f16[104,512]{1,0:T(8,128)(2,1)S(1)} collective-permute-done((f16[104,512]{1,0:T(8,128)(2,1)S(1)}, f16[104,512]{1,0:T(8,128)(2,1)S(1)}, u32[]{:S(2)}, u32[]{:S(2)}) %collective-permute-start.7) | collective-permute-done | bytes 106528 | tf_op jit(solution)/shard_map/ppermute | solution.py:39
  23.0 0.1 shard_map.92.refs_1_
  23.2 0.1 collective-permute-start.9
  23.2 0.7 %collective-permute-start.8 = (bf16[96,512]{1,0:T(8,128)(2,1)S(1)}, bf16[96,512]{1,0:T(8,128)(2,1)S(1)}, u32[]{:S(2)}, u32[]{:S(2)}) collective-permute-start(bf16[96,512]{1,0:T(8,128)(2,1)S(1)} %shard_map.92.refs_1_), channel_id=1, source_target_pairs={{0,1},{1,0},{2,3},{3,2},{4,5},{5,4},{6,7},{7,6},{8,9},{9,8},{10,11... | collective-permute-start | bytes 294920 | tf_op jit(solution)/shard_map/ppermute | solution.py:39
  24.0 0.5 %collective-permute-done.9.refs_5_ = bf16[96,512]{1,0:T(8,128)(2,1)S(1)} collective-permute-done((bf16[96,512]{1,0:T(8,128)(2,1)S(1)}, bf16[96,512]{1,0:T(8,128)(2,1)S(1)}, u32[]{:S(2)}, u32[]{:S(2)}) %collective-permute-start.9) | collective-permute-done | bytes 98336 | tf_op jit(solution)/shard_map/ppermute | solution.py:39
  24.5 0.6 %shard_map.93 = (f32[512,256]{1,0:T(8,128)S(1)}, f32[512,256]{1,0:T(8,128)S(1)}) custom-call(bf16[512,256]{1,0:T(8,128)(2,1)S(1)} %get-tuple-element.56.refs_7_.refs_3_.refs_0_, bf16[96,512]{1,0:T(8,128)(2,1)S(1)} %shard_map.92.refs_1_, bf16[96,512]{1,0:T(8,128)(2,1)S(1)} %get-tuple-element.87.rows.refs_2_, bf16[96,256]{1,0:T(8,128)(2,1)S(1)} %get-tuple-element.88.refs_3_, ...), custom_call_target="tpu_custom_call" | custom-call | flops 150994944 | bytes 262144 | tf_op jit(solution)/shard_map/pallas_call | solution.py:223
  25.1 3.3 %collective-permute-done.8.refs_1_ = bf16[96,512]{1,0:T(8,128)(2,1)S(1)} collective-permute-done((bf16[96,512]{1,0:T(8,128)(2,1)S(1)}, bf16[96,512]{1,0:T(8,128)(2,1)S(1)}, u32[]{:S(2)}, u32[]{:S(2)}) %collective-permute-start.8) | collective-permute-done | bytes 98336 | tf_op jit(solution)/shard_map/ppermute | solution.py:39
  28.4 0.4 %shard_map.94 = (f32[512,256]{1,0:T(8,128)S(1)}, f32[512,256]{1,0:T(8,128)S(1)}) custom-call(bf16[512,256]{1,0:T(8,128)(2,1)S(1)} %get-tuple-element.56.refs_7_.refs_3_.refs_0_, bf16[96,512]{1,0:T(8,128)(2,1)S(1)} %collective-permute-done.8.refs_1_, bf16[96,512]{1,0:T(8,128)(2,1)S(1)} %get-tuple-element.99.refs_2_, ...), custom_call_target="tpu_custom_call" | custom-call | flops 75497472 | bytes 262144 | tf_op jit(solution)/shard_map/pallas_call | solution.py:223
  28.9 0.8 %collective-permute-done.10.refs_1_ = bf16[96,512]{1,0:T(8,128)(2,1)S(1)} collective-permute-done((bf16[96,512]{1,0:T(8,128)(2,1)S(1)}, bf16[96,512]{1,0:T(8,128)(2,1)S(1)}, u32[]{:S(2)}, u32[]{:S(2)}) %collective-permute-start.10) | collective-permute-done | bytes 98336 | tf_op jit(solution)/shard_map/ppermute | solution.py:39
  29.7 0.4 %shard_map.95 = (f32[512,256]{1,0:T(8,128)S(1)}, f32[512,256]{1,0:T(8,128)S(1)}) custom-call(bf16[512,256]{1,0:T(8,128)(2,1)S(1)} %get-tuple-element.56.refs_7_.refs_3_.refs_0_, bf16[96,512]{1,0:T(8,128)(2,1)S(1)} %collective-permute-done.10.refs_1_, bf16[96,512]{1,0:T(8,128)(2,1)S(1)} %collective-permute-done.6.rows_other.refs_2_, ...), custom_call_target="tpu_custom_call" | custom-call | flops 75497472 | bytes 262144 | tf_op jit(solution)/shard_map/pallas_call | solution.py:223
  30.3 1.6 %collective-permute-start.11 = (bf16[128,256]{1,0:T(8,128)(2,1)S(1)}, bf16[128,256]{1,0:T(8,128)(2,1)S(1)}, u32[]{:S(2)}, u32[]{:S(2)}) collective-permute-start(bf16[128,256]{1,0:T(8,128)(2,1)S(1)} %get-tuple-element.108), channel_id=1, source_target_pairs={{0,24},{8,16},{16,8},{24,0},{1,25},{9,17},{17,9},{25,1},{2,26},{10... | collective-permute-start | bytes 196616 | tf_op jit(solution)/shard_map/ppermute | solution.py:39
  31.8 0.5 %collective-permute-start.12 = (bf16[128,256]{1,0:T(8,128)(2,1)S(1)}, bf16[128,256]{1,0:T(8,128)(2,1)S(1)}, u32[]{:S(2)}, u32[]{:S(2)}) collective-permute-start(bf16[128,256]{1,0:T(8,128)(2,1)S(1)} %get-tuple-element.109), channel_id=1, source_target_pairs={{0,16},{8,24},{16,0},{24,8},{1,17},{9,25},{17,1},{25,9},{2,18},{10... | collective-permute-start | bytes 196616 | tf_op jit(solution)/shard_map/ppermute | solution.py:39
  32.3 1.5 %collective-permute-start.13 = (bf16[128,256]{1,0:T(8,128)(2,1)S(1)}, bf16[128,256]{1,0:T(8,128)(2,1)S(1)}, u32[]{:S(2)}, u32[]{:S(2)}) collective-permute-start(bf16[128,256]{1,0:T(8,128)(2,1)S(1)} %get-tuple-element.110), channel_id=1, source_target_pairs={{0,8},{8,0},{16,24},{24,16},{1,9},{9,1},{17,25},{25,17},{2,10},{10... | collective-permute-start | bytes 196616 | tf_op jit(solution)/shard_map/ppermute | solution.py:39
  33.8 1.7 %collective-permute-done.11 = bf16[128,256]{1,0:T(8,128)(2,1)S(1)} collective-permute-done((bf16[128,256]{1,0:T(8,128)(2,1)S(1)}, bf16[128,256]{1,0:T(8,128)(2,1)S(1)}, u32[]{:S(2)}, u32[]{:S(2)}) %collective-permute-start.11) | collective-permute-done | bytes 65568 | tf_op jit(solution)/shard_map/ppermute | solution.py:39
  35.6 1.2 %collective-permute-done.12 = bf16[128,256]{1,0:T(8,128)(2,1)S(1)} collective-permute-done((bf16[128,256]{1,0:T(8,128)(2,1)S(1)}, bf16[128,256]{1,0:T(8,128)(2,1)S(1)}, u32[]{:S(2)}, u32[]{:S(2)}) %collective-permute-start.12) | collective-permute-done | bytes 65568 | tf_op jit(solution)/shard_map/ppermute | solution.py:39
  36.9 0.7 %fusion.14 = (f32[64,256]{1,0:T(8,128)}, f32[64,256]{1,0:T(8,128)}) fusion(f32[128,256]{1,0:T(8,128)S(1)} %fusion.6), kind=kLoop, calls=%fused_computation.24 | loop fusion | bytes 262144 | tf_op jit(solution)/shard_map/slice | solution.py:352
  (14 shorter events, 0.2 us)
Async XLA Ops:
  1.8 6.2 %collective-permute-start = (bf16[48,640]{1,0:T(8,128)(2,1)S(1)}, bf16[48,640]{1,0:T(8,128)(2,1)S(1)}, u32[]{:S(2)}, u32[]{:S(2)}) collective-permute-start(bf16[48,640]{1,0:T(8,128)(2,1)S(1)} %get-tuple-element.57), channel_id=1, source_target_pairs={{0,24},{8,16},{16,8},{24,0},{1,25},{9,17},{17,9},{25,1},{2,26},{10... | collective-permute-start | bytes 184328 | tf_op jit(solution)/shard_map/ppermute | solution.py:39
  5.8 4.2 %collective-permute-start.1 = (bf16[48,640]{1,0:T(8,128)(2,1)S(1)}, bf16[48,640]{1,0:T(8,128)(2,1)S(1)}, u32[]{:S(2)}, u32[]{:S(2)}) collective-permute-start(bf16[48,640]{1,0:T(8,128)(2,1)S(1)} %get-tuple-element.58), channel_id=1, source_target_pairs={{0,16},{8,24},{16,0},{24,8},{1,17},{9,25},{17,1},{25,9},{2,18},{10... | collective-permute-start | bytes 184328 | tf_op jit(solution)/shard_map/ppermute | solution.py:39
  6.3 4.2 %collective-permute-start.2 = (bf16[48,640]{1,0:T(8,128)(2,1)S(1)}, bf16[48,640]{1,0:T(8,128)(2,1)S(1)}, u32[]{:S(2)}, u32[]{:S(2)}) collective-permute-start(bf16[48,640]{1,0:T(8,128)(2,1)S(1)} %get-tuple-element.59), channel_id=1, source_target_pairs={{0,8},{8,0},{16,24},{24,16},{1,9},{9,1},{17,25},{25,17},{2,10},{10... | collective-permute-start | bytes 184328 | tf_op jit(solution)/shard_map/ppermute | solution.py:39
  11.1 4.8 %collective-permute-start.3 = (f16[104,512]{1,0:T(8,128)(2,1)S(1)}, f16[104,512]{1,0:T(8,128)(2,1)S(1)}, u32[]{:S(2)}, u32[]{:S(2)}) collective-permute-start(f16[104,512]{1,0:T(8,128)(2,1)S(1)} %convert_element_type.39), channel_id=1, source_target_pairs={{0,1},{1,0},{2,3},{3,2},{4,5},{5,4},{6,7},{7,6},{8,9},{9,8},{10,11... | collective-permute-start | bytes 319496 | tf_op jit(solution)/shard_map/ppermute | solution.py:39
  12.8 3.2 %collective-permute-start.5 = (bf16[96,512]{1,0:T(8,128)(2,1)S(1)}, bf16[96,512]{1,0:T(8,128)(2,1)S(1)}, u32[]{:S(2)}, u32[]{:S(2)}) collective-permute-start(bf16[96,512]{1,0:T(8,128)(2,1)S(1)} %get-tuple-element.87.rows.refs_2_), channel_id=1, source_target_pairs={{0,4},{4,0},{1,5},{5,1},{2,6},{6,2},{3,7},{7,3},{8,12},{12,8},{9,1... | collective-permute-start | bytes 294920 | tf_op jit(solution)/shard_map/ppermute | solution.py:39
  12.8 3.2 %collective-permute-start.6 = (bf16[96,512]{1,0:T(8,128)(2,1)S(1)}, bf16[96,512]{1,0:T(8,128)(2,1)S(1)}, u32[]{:S(2)}, u32[]{:S(2)}) collective-permute-start(bf16[96,512]{1,0:T(8,128)(2,1)S(1)} %get-tuple-element.99.refs_2_), channel_id=1, source_target_pairs={{0,4},{4,0},{1,5},{5,1},{2,6},{6,2},{3,7},{7,3},{8,12},{12,8},{9,1... | collective-permute-start | bytes 294920 | tf_op jit(solution)/shard_map/ppermute | solution.py:39
  13.3 2.6 %collective-permute-start.4 = (f32[1,128]{1,0:T(1,128)S(1)}, f32[1,128]{1,0:T(1,128)S(1)}, u32[]{:S(2)}, u32[]{:S(2)}) collective-permute-start(f32[1,128]{1,0:T(1,128)S(1)} %get-tuple-element.85.refs_3_), channel_id=1, source_target_pairs={{0,4},{4,0},{1,5},{5,1},{2,6},{6,2},{3,7},{7,3},{8,12},{12,8},{9,1... | collective-permute-start | bytes 1544 | tf_op jit(solution)/shard_map/ppermute | solution.py:39
  16.2 6.8 %collective-permute-start.7 = (f16[104,512]{1,0:T(8,128)(2,1)S(1)}, f16[104,512]{1,0:T(8,128)(2,1)S(1)}, u32[]{:S(2)}, u32[]{:S(2)}) collective-permute-start(f16[104,512]{1,0:T(8,128)(2,1)S(1)} %convert_element_type.41), channel_id=1, source_target_pairs={{0,2},{1,3},{2,0},{3,1},{4,6},{5,7},{6,4},{7,5},{8,10},{9,11},{10,... | collective-permute-start | bytes 319496 | tf_op jit(solution)/shard_map/ppermute | solution.py:39
  23.2 1.4 %collective-permute-start.9 = (bf16[96,512]{1,0:T(8,128)(2,1)S(1)}, bf16[96,512]{1,0:T(8,128)(2,1)S(1)}, u32[]{:S(2)}, u32[]{:S(2)}) collective-permute-start(bf16[96,512]{1,0:T(8,128)(2,1)S(1)} %shard_map.92.refs_1_), channel_id=1, source_target_pairs={{0,4},{4,0},{1,5},{5,1},{2,6},{6,2},{3,7},{7,3},{8,12},{12,8},{9,1... | collective-permute-start | bytes 294920 | tf_op jit(solution)/shard_map/ppermute | solution.py:39
  23.2 5.2 %collective-permute-start.8 = (bf16[96,512]{1,0:T(8,128)(2,1)S(1)}, bf16[96,512]{1,0:T(8,128)(2,1)S(1)}, u32[]{:S(2)}, u32[]{:S(2)}) collective-permute-start(bf16[96,512]{1,0:T(8,128)(2,1)S(1)} %shard_map.92.refs_1_), channel_id=1, source_target_pairs={{0,1},{1,0},{2,3},{3,2},{4,5},{5,4},{6,7},{7,6},{8,9},{9,8},{10,11... | collective-permute-start | bytes 294920 | tf_op jit(solution)/shard_map/ppermute | solution.py:39
  28.4 1.3 %collective-permute-start.10 = (bf16[96,512]{1,0:T(8,128)(2,1)S(1)}, bf16[96,512]{1,0:T(8,128)(2,1)S(1)}, u32[]{:S(2)}, u32[]{:S(2)}) collective-permute-start(bf16[96,512]{1,0:T(8,128)(2,1)S(1)} %collective-permute-done.8.refs_1_), channel_id=1, source_target_pairs={{0,4},{4,0},{1,5},{5,1},{2,6},{6,2},{3,7},{7,3},{8,12},{12,8},{9,1... | collective-permute-start | bytes 294920 | tf_op jit(solution)/shard_map/ppermute | solution.py:39
  30.3 5.3 %collective-permute-start.11 = (bf16[128,256]{1,0:T(8,128)(2,1)S(1)}, bf16[128,256]{1,0:T(8,128)(2,1)S(1)}, u32[]{:S(2)}, u32[]{:S(2)}) collective-permute-start(bf16[128,256]{1,0:T(8,128)(2,1)S(1)} %get-tuple-element.108), channel_id=1, source_target_pairs={{0,24},{8,16},{16,8},{24,0},{1,25},{9,17},{17,9},{25,1},{2,26},{10... | collective-permute-start | bytes 196616 | tf_op jit(solution)/shard_map/ppermute | solution.py:39
  31.8 5.0 %collective-permute-start.12 = (bf16[128,256]{1,0:T(8,128)(2,1)S(1)}, bf16[128,256]{1,0:T(8,128)(2,1)S(1)}, u32[]{:S(2)}, u32[]{:S(2)}) collective-permute-start(bf16[128,256]{1,0:T(8,128)(2,1)S(1)} %get-tuple-element.109), channel_id=1, source_target_pairs={{0,16},{8,24},{16,0},{24,8},{1,17},{9,25},{17,1},{25,9},{2,18},{10... | collective-permute-start | bytes 196616 | tf_op jit(solution)/shard_map/ppermute | solution.py:39
  32.3 4.5 %collective-permute-start.13 = (bf16[128,256]{1,0:T(8,128)(2,1)S(1)}, bf16[128,256]{1,0:T(8,128)(2,1)S(1)}, u32[]{:S(2)}, u32[]{:S(2)}) collective-permute-start(bf16[128,256]{1,0:T(8,128)(2,1)S(1)} %get-tuple-element.110), channel_id=1, source_target_pairs={{0,8},{8,0},{16,24},{24,16},{1,9},{9,1},{17,25},{25,17},{2,10},{10... | collective-permute-start | bytes 196616 | tf_op jit(solution)/shard_map/ppermute | solution.py:39

commit v9 on v8

--- a/solution.py
+++ b/solution.py
@@ -288,45 +288,49 @@
         (rows_own, *weights),
         work,
     )
+    step = 2
+    while step < parts:
+        own, other = kernel(pair_body, [half, packed], (own, arrived), 0)
+        arrived = cross(other, step)
+        step *= 2
     all_counts, mates = [counts], []
     for k in range(1, studs):
         all_counts.append(send(counts, "stud", k))
         mates.append((send(rows_own, "stud", k), send(rows_other, "stud", k)))
     own, arrived, all_counts, mates = lax.optimization_barrier((own, arrived, all_counts, mates))
-    step = 2
-    while step < parts:
-        own, other = kernel(pair_body, [half, packed], (own, arrived), 0)
-        arrived = cross(other, step)
-        step *= 2
-    groups = [(rows_own, act_own, slope_own, rows_other, act_other, slope_other)]
-    for first, second in mates:
-        known = kernel(
+    (scaled,) = kernel(scale_body, [shape(height, actions, bf16)], (own, arrived, tags, *all_counts), 0)
+    from_pair = send(scaled, "mdl", 1)
+    known = [
+        kernel(
             neighbour_body,
             [half_act, half_slope] * 2,
             (first, second, weights[2]),
             4 * height * width * units,
         )
-        groups.append((first, *known[:2], second, *known[2:]))
-    own, arrived, groups = lax.optimization_barrier((own, arrived, groups))
-    (scaled,) = kernel(scale_body, [shape(height, actions, bf16)], (own, arrived, tags, *all_counts), 0)
-    from_pair = send(scaled, "mdl", 1)
-    ours = [scaled] + [send(scaled, "stud", k) for k in range(1, studs)]
+        for first, second in mates
+    ]
     work = 6 * height * width * units
     grads = [shape(width, units, f32), shape(actions, units, f32)]
     sums = kernel(
-        functools.partial(backward_body, True, studs),
+        functools.partial(backward_body, True, 1),
         grads,
-        [weights[3]] + [a for s, g in zip(ours, groups) for a in (s, *g[:3])],
-        studs * work,
-    )
-    from_pair, sums = lax.optimization_barrier((from_pair, sums))
-    for k in range(studs):
-        theirs = send(from_pair, "stud", k) if k else from_pair
+        (weights[3], scaled, rows_own, act_own, slope_own),
+        work,
+    )
+    scaled, from_pair, sums, known = lax.optimization_barrier((scaled, from_pair, sums, known))
+    theirs = [(send(scaled, "stud", k), send(from_pair, "stud", k)) for k in range(1, studs)]
+    sums = kernel(
+        functools.partial(backward_body, False, 1),
+        grads,
+        (weights[3], from_pair, rows_other, act_other, slope_other, *sums),
+        work,
+    )
+    for error, rows, state in zip(theirs, mates, known):
         sums = kernel(
-            functools.partial(backward_body, False, 1),
+            functools.partial(backward_body, False, 2),
             grads,
-            (weights[3], theirs, *groups[k][3:], *sums),
-            work,
+            (weights[3], error[0], rows[0], *state[:2], error[1], rows[1], *state[2:], *sums),
+            2 * work,
         )
     grad_up, grad_down = sums
     heights = (width // (owners * studs), actions // (owners * studs))

time: 37.7 us -> 37.8 us (level)
  waiting for transfers between devices: 16.6 us -> 16.1 us
  starting transfers between devices: 13.8 us -> 14.2 us
    ppermute x14, waiting for transfers between devices: 16.6 us -> 16.1 us  [send(): lax.ppermute(block, axis, [(i, partner_to(size, i, step)) for i in range(...]
    ppermute x14, starting transfers between devices: 13.8 us -> 14.2 us  [send(): lax.ppermute(block, axis, [(i, partner_to(size, i, step)) for i in range(...]
  transfers between devices with their start and end apart: 14 -> 14, of which waited for: 11 -> 11; matrix products, arithmetic and copies ran while one was open for 0% -> 0% of each run, Pallas kernels for 8% -> 7%
where the time goes in v9:
time: 37.8 us; the launch traced here: 37.6 us
  waiting for transfers between devices  16.1 us (43%)
  starting transfers between devices  14.2 us (38%)
  Pallas kernels  5.64 us (15%)
  between operations  0.78 us (2%)
  local copies, waits for them, and re-layouts  0.71 us (2%)
    ppermute x14, waiting for transfers between devices, send(): lax.ppermute(block, axis, [(i, partner_to(size, i, step)) for i in range(...  16.1 us
    ppermute x14, starting transfers between devices, send(): lax.ppermute(block, axis, [(i, partner_to(size, i, step)) for i in range(...  14.2 us
    pallas_call x10, Pallas kernels, kernel(): pl.pallas_call(body, out_shape=outs, in_specs=places or [VMEM] * len(oper...  5.64 us
  transfers between devices with their start and end apart: 14, of which 11 were waited for; matrix products, arithmetic and copies ran while one was open for 0% of the time, Pallas kernels for 7%

profile of v9, /device:TPU:0, one launch (start us, length us, event | category | flops | bytes accessed | tf_op | source)
XLA Modules:
  0.0 37.6 jit_solution(9671066769243416492)
XLA Ops:
  0.6 1.2 %shard_map.86 = (bf16[48,640]{1,0:T(8,128)(2,1)S(1)}, bf16[48,640]{1,0:T(8,128)(2,1)S(1)}, bf16[48,640]{1,0:T(8,128)(2,1)S(1)}, bf16[48,640]{1,0:T(8,128)(2,1)S(1)}) custom-call(bf16[128,512]{1,0:T(8,128)(2,1)} %refs_0_.1, s32[1,128]{1,0:T(1,128)} %bitcast.24, s32[1,128]{1,0:T(1,128)} %bitcast.25), custom_call_target="tpu_custom_call" | custom-call | flops 25165824 | bytes 262144 | tf_op jit(solution)/shard_map/pallas_call | solution.py:223
  1.8 4.0 %collective-permute-start = (bf16[48,640]{1,0:T(8,128)(2,1)S(1)}, bf16[48,640]{1,0:T(8,128)(2,1)S(1)}, u32[]{:S(2)}, u32[]{:S(2)}) collective-permute-start(bf16[48,640]{1,0:T(8,128)(2,1)S(1)} %get-tuple-element.48), channel_id=1, source_target_pairs={{0,24},{8,16},{16,8},{24,0},{1,25},{9,17},{17,9},{25,1},{2,26},{10... | collective-permute-start | bytes 184328 | tf_op jit(solution)/shard_map/ppermute | solution.py:39
  5.8 0.5 %collective-permute-start.1 = (bf16[48,640]{1,0:T(8,128)(2,1)S(1)}, bf16[48,640]{1,0:T(8,128)(2,1)S(1)}, u32[]{:S(2)}, u32[]{:S(2)}) collective-permute-start(bf16[48,640]{1,0:T(8,128)(2,1)S(1)} %get-tuple-element.49), channel_id=1, source_target_pairs={{0,16},{8,24},{16,0},{24,8},{1,17},{9,25},{17,1},{25,9},{2,18},{10... | collective-permute-start | bytes 184328 | tf_op jit(solution)/shard_map/ppermute | solution.py:39
  6.3 0.1 collective-permute-start.2
  6.4 1.2 %shard_map.87 = (bf16[1,512,256]{2,1,0:T(8,128)(2,1)S(1)}, bf16[1,256,512]{2,1,0:T(8,128)(2,1)S(1)}, bf16[512,256]{1,0:T(8,128)(2,1)S(1)}, bf16[512,256]{1,0:T(8,128)(2,1)S(1)}) custom-call(bf16[48,640]{1,0:T(8,128)(2,1)S(1)} %get-tuple-element.46.refs_0_, bf16[1,512,256]{2,1,0:T(8,128)(2,1)} %refs_1_.1, bf16[1,256,512]{2,1,0:T(8,128)(2,1)} %refs_2_.1, ...), custom_call_target="tpu_custom_call" | custom-call | bytes 262144 | tf_op jit(solution)/shard_map/pallas_call | solution.py:223
  7.7 0.3 collective-permute-done.refs_1_
  8.0 2.0 %collective-permute-done.1.refs_2_ = bf16[48,640]{1,0:T(8,128)(2,1)S(1)} collective-permute-done((bf16[48,640]{1,0:T(8,128)(2,1)S(1)}, bf16[48,640]{1,0:T(8,128)(2,1)S(1)}, u32[]{:S(2)}, u32[]{:S(2)}) %collective-permute-start.1) | collective-permute-done | bytes 61472 | tf_op jit(solution)/shard_map/ppermute | solution.py:39
  10.0 0.5 %collective-permute-done.2.refs_3_ = bf16[48,640]{1,0:T(8,128)(2,1)S(1)} collective-permute-done((bf16[48,640]{1,0:T(8,128)(2,1)S(1)}, bf16[48,640]{1,0:T(8,128)(2,1)S(1)}, u32[]{:S(2)}, u32[]{:S(2)}) %collective-permute-start.2) | collective-permute-done | bytes 61472 | tf_op jit(solution)/shard_map/ppermute | solution.py:39
  10.5 0.6 %shard_map.88 = (bf16[96,512]{1,0:T(8,128)(2,1)S(1)}, bf16[96,512]{1,0:T(8,128)(2,1)S(1)}, f32[96,128]{1,0:T(8,128)S(1)}, f32[1,128]{1,0:T(1,128)S(1)}, f32[104,...) custom-call(bf16[48,640]{1,0:T(8,128)(2,1)S(1)} %get-tuple-element.46.refs_0_, ...), custom_call_target="tpu_custom_call" | custom-call | flops 100663296 | bytes 262144 | tf_op jit(solution)/shard_map/pallas_call | solution.py:223
  11.1 1.6 %collective-permute-start.3 = (f16[104,512]{1,0:T(8,128)(2,1)S(1)}, f16[104,512]{1,0:T(8,128)(2,1)S(1)}, u32[]{:S(2)}, u32[]{:S(2)}) collective-permute-start(f16[104,512]{1,0:T(8,128)(2,1)S(1)} %convert_element_type.39), channel_id=1, source_target_pairs={{0,1},{1,0},{2,3},{3,2},{4,5},{5,4},{6,7},{7,6},{8,9},{9,8},{10,11... | collective-permute-start | bytes 319496 | tf_op jit(solution)/shard_map/ppermute | solution.py:39
  12.8 0.4 %shard_map.89 = (f32[96,512]{1,0:T(8,128)S(1)}, bf16[96,256]{1,0:T(8,128)(2,1)S(1)}, f32[96,256]{1,0:T(8,128)S(1)}) custom-call(bf16[96,512]{1,0:T(8,128)(2,1)S(1)} %get-tuple-element.54.rows.refs_2_, bf16[1,512,256]{2,1,0:T(8,128)(2,1)S(1)} %get-tuple-element.51.refs_4_.refs_0_, bf16[1,256,512]{2,1,0:T(8,128)(2,1)S(1)} %get-tuple-element.52.refs_5_.refs_1_, ...), custom_call_target="tpu_custom_call" | custom-call | flops 100663296 | bytes 262144 | tf_op jit(solution)/shard_map/pallas_call | solution.py:223
  13.2 2.7 %collective-permute-done.3 = f16[104,512]{1,0:T(8,128)(2,1)S(1)} collective-permute-done((f16[104,512]{1,0:T(8,128)(2,1)S(1)}, f16[104,512]{1,0:T(8,128)(2,1)S(1)}, u32[]{:S(2)}, u32[]{:S(2)}) %collective-permute-start.3) | collective-permute-done | bytes 106528 | tf_op jit(solution)/shard_map/ppermute | solution.py:39
  15.9 0.2 shard_map.90
  16.1 2.7 %collective-permute-start.4 = (f16[104,512]{1,0:T(8,128)(2,1)S(1)}, f16[104,512]{1,0:T(8,128)(2,1)S(1)}, u32[]{:S(2)}, u32[]{:S(2)}) collective-permute-start(f16[104,512]{1,0:T(8,128)(2,1)S(1)} %convert_element_type.41), channel_id=1, source_target_pairs={{0,2},{1,3},{2,0},{3,1},{4,6},{5,7},{6,4},{7,5},{8,10},{9,11},{10,... | collective-permute-start | bytes 319496 | tf_op jit(solution)/shard_map/ppermute | solution.py:39
  18.8 0.5 %collective-permute-start.7 = (bf16[96,512]{1,0:T(8,128)(2,1)S(1)}, bf16[96,512]{1,0:T(8,128)(2,1)S(1)}, u32[]{:S(2)}, u32[]{:S(2)}) collective-permute-start(bf16[96,512]{1,0:T(8,128)(2,1)S(1)} %get-tuple-element.60.refs_2_), channel_id=1, source_target_pairs={{0,4},{4,0},{1,5},{5,1},{2,6},{6,2},{3,7},{7,3},{8,12},{12,8},{9,1... | collective-permute-start | bytes 294920 | tf_op jit(solution)/shard_map/ppermute | solution.py:39
  19.3 3.6 %collective-permute-done.4 = f16[104,512]{1,0:T(8,128)(2,1)S(1)} collective-permute-done((f16[104,512]{1,0:T(8,128)(2,1)S(1)}, f16[104,512]{1,0:T(8,128)(2,1)S(1)}, u32[]{:S(2)}, u32[]{:S(2)}) %collective-permute-start.4) | collective-permute-done | bytes 106528 | tf_op jit(solution)/shard_map/ppermute | solution.py:39
  23.0 0.1 shard_map.91.refs_1_
  23.2 0.7 %collective-permute-start.8 = (bf16[96,512]{1,0:T(8,128)(2,1)S(1)}, bf16[96,512]{1,0:T(8,128)(2,1)S(1)}, u32[]{:S(2)}, u32[]{:S(2)}) collective-permute-start(bf16[96,512]{1,0:T(8,128)(2,1)S(1)} %shard_map.91.refs_1_), channel_id=1, source_target_pairs={{0,1},{1,0},{2,3},{3,2},{4,5},{5,4},{6,7},{7,6},{8,9},{9,8},{10,11... | collective-permute-start | bytes 294920 | tf_op jit(solution)/shard_map/ppermute | solution.py:39
  23.9 0.3 shard_map.93
  24.2 0.4 %shard_map.92 = (f32[512,256]{1,0:T(8,128)S(1)}, f32[512,256]{1,0:T(8,128)S(1)}) custom-call(bf16[512,256]{1,0:T(8,128)(2,1)S(1)} %get-tuple-element.47.refs_7_.refs_3_.refs_0_, bf16[96,512]{1,0:T(8,128)(2,1)S(1)} %shard_map.91.refs_1_, bf16[96,512]{1,0:T(8,128)(2,1)S(1)} %get-tuple-element.54.rows.refs_2_, bf16[96,256]{1,0:T(8,128)(2,1)S(1)} %get-tuple-element.66.refs_3_, ...), custom_call_target="tpu_custom_call" | custom-call | flops 75497472 | bytes 262144 | tf_op jit(solution)/shard_map/pallas_call | solution.py:223
  24.6 3.2 %collective-permute-done.8.refs_1_ = bf16[96,512]{1,0:T(8,128)(2,1)S(1)} collective-permute-done((bf16[96,512]{1,0:T(8,128)(2,1)S(1)}, bf16[96,512]{1,0:T(8,128)(2,1)S(1)}, u32[]{:S(2)}, u32[]{:S(2)}) %collective-permute-start.8) | collective-permute-done | bytes 98336 | tf_op jit(solution)/shard_map/ppermute | solution.py:39
  27.8 0.5 %collective-permute-start.9 = (bf16[96,512]{1,0:T(8,128)(2,1)S(1)}, bf16[96,512]{1,0:T(8,128)(2,1)S(1)}, u32[]{:S(2)}, u32[]{:S(2)}) collective-permute-start(bf16[96,512]{1,0:T(8,128)(2,1)S(1)} %shard_map.91.refs_1_), channel_id=1, source_target_pairs={{0,4},{4,0},{1,5},{5,1},{2,6},{6,2},{3,7},{7,3},{8,12},{12,8},{9,1... | collective-permute-start | bytes 294920 | tf_op jit(solution)/shard_map/ppermute | solution.py:39
  28.3 0.4 %shard_map.94 = (f32[512,256]{1,0:T(8,128)S(1)}, f32[512,256]{1,0:T(8,128)S(1)}) custom-call(bf16[512,256]{1,0:T(8,128)(2,1)S(1)} %get-tuple-element.47.refs_7_.refs_3_.refs_0_, bf16[96,512]{1,0:T(8,128)(2,1)S(1)} %collective-permute-done.8.refs_1_, bf16[96,512]{1,0:T(8,128)(2,1)S(1)} %get-tuple-element.60.refs_2_, ...), custom_call_target="tpu_custom_call" | custom-call | flops 75497472 | bytes 262144 | tf_op jit(solution)/shard_map/pallas_call | solution.py:223
  28.8 0.3 collective-permute-done.10.refs_5_
  29.1 0.2 collective-permute-done.9.refs_1_
  29.3 0.7 %shard_map.95 = (f32[512,256]{1,0:T(8,128)S(1)}, f32[512,256]{1,0:T(8,128)S(1)}) custom-call(bf16[512,256]{1,0:T(8,128)(2,1)S(1)} %get-tuple-element.47.refs_7_.refs_3_.refs_0_, bf16[96,512]{1,0:T(8,128)(2,1)S(1)} %collective-permute-done.9.refs_1_, bf16[96,512]{1,0:T(8,128)(2,1)S(1)} %collective-permute-done.6.rows_own.refs_2_, ...), custom_call_target="tpu_custom_call" | custom-call | flops 150994944 | bytes 262144 | tf_op jit(solution)/shard_map/pallas_call | solution.py:223
  30.1 1.6 %collective-permute-start.11 = (bf16[128,256]{1,0:T(8,128)(2,1)S(1)}, bf16[128,256]{1,0:T(8,128)(2,1)S(1)}, u32[]{:S(2)}, u32[]{:S(2)}) collective-permute-start(bf16[128,256]{1,0:T(8,128)(2,1)S(1)} %get-tuple-element.90), channel_id=1, source_target_pairs={{0,24},{8,16},{16,8},{24,0},{1,25},{9,17},{17,9},{25,1},{2,26},{10... | collective-permute-start | bytes 196616 | tf_op jit(solution)/shard_map/ppermute | solution.py:39
  31.7 0.1 collective-permute-start.12
  31.8 1.9 %collective-permute-start.13 = (bf16[128,256]{1,0:T(8,128)(2,1)S(1)}, bf16[128,256]{1,0:T(8,128)(2,1)S(1)}, u32[]{:S(2)}, u32[]{:S(2)}) collective-permute-start(bf16[128,256]{1,0:T(8,128)(2,1)S(1)} %get-tuple-element.92), channel_id=1, source_target_pairs={{0,8},{8,0},{16,24},{24,16},{1,9},{9,1},{17,25},{25,17},{2,10},{10... | collective-permute-start | bytes 196616 | tf_op jit(solution)/shard_map/ppermute | solution.py:39
  33.7 1.9 %collective-permute-done.11 = bf16[128,256]{1,0:T(8,128)(2,1)S(1)} collective-permute-done((bf16[128,256]{1,0:T(8,128)(2,1)S(1)}, bf16[128,256]{1,0:T(8,128)(2,1)S(1)}, u32[]{:S(2)}, u32[]{:S(2)}) %collective-permute-start.11) | collective-permute-done | bytes 65568 | tf_op jit(solution)/shard_map/ppermute | solution.py:39
  35.5 1.3 %collective-permute-done.12 = bf16[128,256]{1,0:T(8,128)(2,1)S(1)} collective-permute-done((bf16[128,256]{1,0:T(8,128)(2,1)S(1)}, bf16[128,256]{1,0:T(8,128)(2,1)S(1)}, u32[]{:S(2)}, u32[]{:S(2)}) %collective-permute-start.12) | collective-permute-done | bytes 65568 | tf_op jit(solution)/shard_map/ppermute | solution.py:39
  36.9 0.7 %fusion.14 = (f32[64,256]{1,0:T(8,128)}, f32[64,256]{1,0:T(8,128)}) fusion(f32[128,256]{1,0:T(8,128)S(1)} %fusion.6), kind=kLoop, calls=%fused_computation.24 | loop fusion | bytes 262144 | tf_op jit(solution)/shard_map/slice | solution.py:356
  (14 shorter events, 0.3 us)
Async XLA Ops:
  1.8 6.2 %collective-permute-start = (bf16[48,640]{1,0:T(8,128)(2,1)S(1)}, bf16[48,640]{1,0:T(8,128)(2,1)S(1)}, u32[]{:S(2)}, u32[]{:S(2)}) collective-permute-start(bf16[48,640]{1,0:T(8,128)(2,1)S(1)} %get-tuple-element.48), channel_id=1, source_target_pairs={{0,24},{8,16},{16,8},{24,0},{1,25},{9,17},{17,9},{25,1},{2,26},{10... | collective-permute-start | bytes 184328 | tf_op jit(solution)/shard_map/ppermute | solution.py:39
  5.8 4.2 %collective-permute-start.1 = (bf16[48,640]{1,0:T(8,128)(2,1)S(1)}, bf16[48,640]{1,0:T(8,128)(2,1)S(1)}, u32[]{:S(2)}, u32[]{:S(2)}) collective-permute-start(bf16[48,640]{1,0:T(8,128)(2,1)S(1)} %get-tuple-element.49), channel_id=1, source_target_pairs={{0,16},{8,24},{16,0},{24,8},{1,17},{9,25},{17,1},{25,9},{2,18},{10... | collective-permute-start | bytes 184328 | tf_op jit(solution)/shard_map/ppermute | solution.py:39
  6.3 4.2 %collective-permute-start.2 = (bf16[48,640]{1,0:T(8,128)(2,1)S(1)}, bf16[48,640]{1,0:T(8,128)(2,1)S(1)}, u32[]{:S(2)}, u32[]{:S(2)}) collective-permute-start(bf16[48,640]{1,0:T(8,128)(2,1)S(1)} %get-tuple-element.50), channel_id=1, source_target_pairs={{0,8},{8,0},{16,24},{24,16},{1,9},{9,1},{17,25},{25,17},{2,10},{10... | collective-permute-start | bytes 184328 | tf_op jit(solution)/shard_map/ppermute | solution.py:39
  11.1 4.8 %collective-permute-start.3 = (f16[104,512]{1,0:T(8,128)(2,1)S(1)}, f16[104,512]{1,0:T(8,128)(2,1)S(1)}, u32[]{:S(2)}, u32[]{:S(2)}) collective-permute-start(f16[104,512]{1,0:T(8,128)(2,1)S(1)} %convert_element_type.39), channel_id=1, source_target_pairs={{0,1},{1,0},{2,3},{3,2},{4,5},{5,4},{6,7},{7,6},{8,9},{9,8},{10,11... | collective-permute-start | bytes 319496 | tf_op jit(solution)/shard_map/ppermute | solution.py:39
  16.1 6.8 %collective-permute-start.4 = (f16[104,512]{1,0:T(8,128)(2,1)S(1)}, f16[104,512]{1,0:T(8,128)(2,1)S(1)}, u32[]{:S(2)}, u32[]{:S(2)}) collective-permute-start(f16[104,512]{1,0:T(8,128)(2,1)S(1)} %convert_element_type.41), channel_id=1, source_target_pairs={{0,2},{1,3},{2,0},{3,1},{4,6},{5,7},{6,4},{7,5},{8,10},{9,11},{10,... | collective-permute-start | bytes 319496 | tf_op jit(solution)/shard_map/ppermute | solution.py:39
  18.8 4.2 %collective-permute-start.6 = (bf16[96,512]{1,0:T(8,128)(2,1)S(1)}, bf16[96,512]{1,0:T(8,128)(2,1)S(1)}, u32[]{:S(2)}, u32[]{:S(2)}) collective-permute-start(bf16[96,512]{1,0:T(8,128)(2,1)S(1)} %get-tuple-element.54.rows.refs_2_), channel_id=1, source_target_pairs={{0,4},{4,0},{1,5},{5,1},{2,6},{6,2},{3,7},{7,3},{8,12},{12,8},{9,1... | collective-permute-start | bytes 294920 | tf_op jit(solution)/shard_map/ppermute | solution.py:39
  18.8 4.2 %collective-permute-start.7 = (bf16[96,512]{1,0:T(8,128)(2,1)S(1)}, bf16[96,512]{1,0:T(8,128)(2,1)S(1)}, u32[]{:S(2)}, u32[]{:S(2)}) collective-permute-start(bf16[96,512]{1,0:T(8,128)(2,1)S(1)} %get-tuple-element.60.refs_2_), channel_id=1, source_target_pairs={{0,4},{4,0},{1,5},{5,1},{2,6},{6,2},{3,7},{7,3},{8,12},{12,8},{9,1... | collective-permute-start | bytes 294920 | tf_op jit(solution)/shard_map/ppermute | solution.py:39
  19.3 3.7 %collective-permute-start.5 = (f32[1,128]{1,0:T(1,128)S(1)}, f32[1,128]{1,0:T(1,128)S(1)}, u32[]{:S(2)}, u32[]{:S(2)}) collective-permute-start(f32[1,128]{1,0:T(1,128)S(1)} %get-tuple-element.64.refs_3_), channel_id=1, source_target_pairs={{0,4},{4,0},{1,5},{5,1},{2,6},{6,2},{3,7},{7,3},{8,12},{12,8},{9,1... | collective-permute-start | bytes 1544 | tf_op jit(solution)/shard_map/ppermute | solution.py:39
  23.2 4.7 %collective-permute-start.8 = (bf16[96,512]{1,0:T(8,128)(2,1)S(1)}, bf16[96,512]{1,0:T(8,128)(2,1)S(1)}, u32[]{:S(2)}, u32[]{:S(2)}) collective-permute-start(bf16[96,512]{1,0:T(8,128)(2,1)S(1)} %shard_map.91.refs_1_), channel_id=1, source_target_pairs={{0,1},{1,0},{2,3},{3,2},{4,5},{5,4},{6,7},{7,6},{8,9},{9,8},{10,11... | collective-permute-start | bytes 294920 | tf_op jit(solution)/shard_map/ppermute | solution.py:39
  27.8 1.3 %collective-permute-start.10 = (bf16[96,512]{1,0:T(8,128)(2,1)S(1)}, bf16[96,512]{1,0:T(8,128)(2,1)S(1)}, u32[]{:S(2)}, u32[]{:S(2)}) collective-permute-start(bf16[96,512]{1,0:T(8,128)(2,1)S(1)} %collective-permute-done.8.refs_1_), channel_id=1, source_target_pairs={{0,4},{4,0},{1,5},{5,1},{2,6},{6,2},{3,7},{7,3},{8,12},{12,8},{9,1... | collective-permute-start | bytes 294920 | tf_op jit(solution)/shard_map/ppermute | solution.py:39
  27.8 1.5 %collective-permute-start.9 = (bf16[96,512]{1,0:T(8,128)(2,1)S(1)}, bf16[96,512]{1,0:T(8,128)(2,1)S(1)}, u32[]{:S(2)}, u32[]{:S(2)}) collective-permute-start(bf16[96,512]{1,0:T(8,128)(2,1)S(1)} %shard_map.91.refs_1_), channel_id=1, source_target_pairs={{0,4},{4,0},{1,5},{5,1},{2,6},{6,2},{3,7},{7,3},{8,12},{12,8},{9,1... | collective-permute-start | bytes 294920 | tf_op jit(solution)/shard_map/ppermute | solution.py:39
  30.1 5.4 %collective-permute-start.11 = (bf16[128,256]{1,0:T(8,128)(2,1)S(1)}, bf16[128,256]{1,0:T(8,128)(2,1)S(1)}, u32[]{:S(2)}, u32[]{:S(2)}) collective-permute-start(bf16[128,256]{1,0:T(8,128)(2,1)S(1)} %get-tuple-element.90), channel_id=1, source_target_pairs={{0,24},{8,16},{16,8},{24,0},{1,25},{9,17},{17,9},{25,1},{2,26},{10... | collective-permute-start | bytes 196616 | tf_op jit(solution)/shard_map/ppermute | solution.py:39
  31.7 5.2 %collective-permute-start.12 = (bf16[128,256]{1,0:T(8,128)(2,1)S(1)}, bf16[128,256]{1,0:T(8,128)(2,1)S(1)}, u32[]{:S(2)}, u32[]{:S(2)}) collective-permute-start(bf16[128,256]{1,0:T(8,128)(2,1)S(1)} %get-tuple-element.91), channel_id=1, source_target_pairs={{0,16},{8,24},{16,0},{24,8},{1,17},{9,25},{17,1},{25,9},{2,18},{10... | collective-permute-start | bytes 196616 | tf_op jit(solution)/shard_map/ppermute | solution.py:39
  31.8 5.1 %collective-permute-start.13 = (bf16[128,256]{1,0:T(8,128)(2,1)S(1)}, bf16[128,256]{1,0:T(8,128)(2,1)S(1)}, u32[]{:S(2)}, u32[]{:S(2)}) collective-permute-start(bf16[128,256]{1,0:T(8,128)(2,1)S(1)} %get-tuple-element.92), channel_id=1, source_target_pairs={{0,8},{8,0},{16,24},{24,16},{1,9},{9,1},{17,25},{25,17},{2,10},{10... | collective-permute-start | bytes 196616 | tf_op jit(solution)/shard_map/ppermute | solution.py:39

commit v10 on v9

--- a/solution.py
+++ b/solution.py
@@ -120,34 +120,11 @@
     return (pre * sig).astype(jnp.bfloat16), sig * (1.0 + pre * (1.0 - sig))
 
 
-def half_error(local, first, rows, weights, act_out, slope_out):
-    teach_in, teach_out, student_up, student_down = weights
-    per_teacher = 2 * rows.shape[0] // local
-    labels = None
-    for l in range(local):
-        hidden = dot(rows, teach_in[l])
-        hidden = hidden / (1.0 + jnp.exp(-hidden))
-        if local > 1:
-            index = first + lax.broadcasted_iota(jnp.int32, hidden.shape, 0)
-            hidden = jnp.where(index // per_teacher == l, hidden, 0.0)
-        part = dot(hidden.astype(jnp.bfloat16), teach_out[l])
-        labels = part if labels is None else labels + part
-    act, slope = student(rows, student_up)
-    act_out[...] = act
-    slope_out[...] = slope
-    return dot(act, student_down[...], ((1,), (1,))) - labels
-
-
-def half_start(height, other):
-    me = lax.axis_index("mdl")
-    return pl.multiple_of(((me & 1) ^ other) * height, ROW_TILE)
-
-
-def forward_other_body(owners, local, room, *refs):
+def forward_body(owners, local, room, *refs):
     blocks, refs = refs[:owners], refs[owners:]
-    weights, refs = refs[:4], refs[4:]
-    rows_own, rows_other, tags_out, counts_out, packed, act, slope, rows_all, tags_all = refs
-    width = rows_own.shape[1]
+    teach_in, teach_out, student_up, student_down = refs[:4]
+    rows_out, tags_out, counts_out, error_out, packed, act_out, slope_out = refs[4:]
+    width = rows_out.shape[1]
     full = [block[...] for block in blocks]
     counts = None
     for block in full:
@@ -155,32 +132,27 @@
         counts = mine if counts is None else counts + mine
     counts_out[...] = counts
     for l in range(local):
+        span = slice(l * owners * room, (l + 1) * owners * room)
         for k, block in enumerate(full):
             start = (l * owners + k) * room
-            rows_all[start : start + room] = block[l * room : (l + 1) * room, :width]
+            rows_out[start : start + room] = block[l * room : (l + 1) * room, :width]
             tag = block[l * room : (l + 1) * room, width:].astype(jnp.float32)
             if l == 0:
                 head = lax.broadcasted_iota(jnp.int32, tag.shape, 0) == 0
                 tag = jnp.where(head, tag - 2.0 * jnp.floor(tag * 0.5), tag)
-            tags_all[start : start + room] = tag
-    height = rows_own.shape[0]
-    mine, there = half_start(height, 0), half_start(height, 1)
-    rows_own[...] = rows_all[pl.ds(mine, height)]
-    tags_out[...] = tags_all[pl.ds(mine, height)]
-    rows = rows_all[pl.ds(there, height)]
-    rows_other[...] = rows
-    pack(half_error(local, there, rows, weights, act, slope), packed)
-
-
-def forward_own_body(local, rows, *refs):
-    weights, (error, act, slope) = refs[:4], refs[4:]
-    first = half_start(rows.shape[0], 0)
-    error[...] = half_error(local, first, rows[...], weights, act, slope)
-
-
-def neighbour_body(rows_own, rows_other, student_up, act_own, slope_own, act_other, slope_other):
-    act_own[...], slope_own[...] = student(rows_own[...], student_up)
-    act_other[...], slope_other[...] = student(rows_other[...], student_up)
+            tags_out[start : start + room] = tag
+        rows = rows_out[span]
+        hidden = dot(rows, teach_in[l])
+        hidden = (hidden / (1.0 + jnp.exp(-hidden))).astype(jnp.bfloat16)
+        act, slope = student(rows, student_up)
+        act_out[span] = act
+        slope_out[span] = slope
+        error_out[span] = dot(act, student_down[...], ((1,), (1,))) - dot(hidden, teach_out[l])
+    pack(error_out[...], packed)
+
+
+def neighbour_body(rows, student_up, act, slope):
+    act[...], slope[...] = student(rows[...], student_up)
 
 
 def pair_body(own, arrived, total, packed):
@@ -241,15 +213,13 @@
     room = up_to(3 * row_count // (2 * teachers), ROW_TILE)
     extra = up_to(batches, LANES)
     slots = teachers * room
-    height = slots // 2
     f32, bf16 = jnp.float32, jnp.bfloat16
 
     def shape(rows, columns, dtype):
         return jax.ShapeDtypeStruct((rows, columns), dtype)
 
-    half, packed = shape(height, actions, f32), shape(height + PACK_ROWS, actions, f32)
-    half_rows = shape(height, width, bf16)
-    half_act, half_slope = shape(height, units, bf16), shape(height, units, f32)
+    whole, packed = shape(slots, actions, f32), shape(slots + PACK_ROWS, actions, f32)
+    state = [shape(slots, units, bf16), shape(slots, units, f32)]
     tokens = [ids.reshape(1, row_count) for ids in (task_ids, student_batch)]
     blocks = kernel(
         functools.partial(dispatch_body, owners, local, room, extra),
@@ -272,65 +242,43 @@
         [VMEM] + [HBM] * 4,
     )
     blocks = [blocks[0]] + list(arrived.values())
-    work = 2 * height * 2 * width * (hidden + units)
-    rows_own, rows_other, tags, counts, other, act_other, slope_other = kernel(
-        functools.partial(forward_other_body, owners, local, room),
-        [half_rows, half_rows, shape(height, extra, f32), shape(1, extra, f32), packed]
-        + [half_act, half_slope],
+    rows, tags, counts, error, other, act, slope = kernel(
+        functools.partial(forward_body, owners, local, room),
+        [shape(slots, width, bf16), shape(slots, extra, f32), shape(1, extra, f32), whole, packed]
+        + state,
         (*blocks, *weights),
-        work,
-        [pltpu.VMEM((slots, width), bf16), pltpu.VMEM((slots, extra), f32)],
+        4 * slots * width * (hidden + units),
     )
     arrived = cross(other, 1)
-    own, act_own, slope_own = kernel(
-        functools.partial(forward_own_body, local),
-        [half, half_act, half_slope],
-        (rows_own, *weights),
-        work,
-    )
     step = 2
     while step < parts:
-        own, other = kernel(pair_body, [half, packed], (own, arrived), 0)
+        error, other = kernel(pair_body, [whole, packed], (error, arrived), 0)
         arrived = cross(other, step)
         step *= 2
     all_counts, mates = [counts], []
     for k in range(1, studs):
         all_counts.append(send(counts, "stud", k))
-        mates.append((send(rows_own, "stud", k), send(rows_other, "stud", k)))
-    own, arrived, all_counts, mates = lax.optimization_barrier((own, arrived, all_counts, mates))
-    (scaled,) = kernel(scale_body, [shape(height, actions, bf16)], (own, arrived, tags, *all_counts), 0)
-    from_pair = send(scaled, "mdl", 1)
+        mates.append(send(rows, "stud", k))
     known = [
-        kernel(
-            neighbour_body,
-            [half_act, half_slope] * 2,
-            (first, second, weights[2]),
-            4 * height * width * units,
-        )
-        for first, second in mates
+        kernel(neighbour_body, state, (theirs, weights[2]), 2 * slots * width * units)
+        for theirs in mates
     ]
-    work = 6 * height * width * units
+    error, arrived, all_counts, mates, known = lax.optimization_barrier(
+        (error, arrived, all_counts, mates, known)
+    )
+    (scaled,) = kernel(scale_body, [shape(slots, actions, bf16)], (error, arrived, tags, *all_counts), 0)
+    work = 6 * slots * width * units
     grads = [shape(width, units, f32), shape(actions, units, f32)]
+    theirs = [send(scaled, "stud", k) for k in range(1, studs)]
     sums = kernel(
-        functools.partial(backward_body, True, 1),
-        grads,
-        (weights[3], scaled, rows_own, act_own, slope_own),
-        work,
-    )
-    scaled, from_pair, sums, known = lax.optimization_barrier((scaled, from_pair, sums, known))
-    theirs = [(send(scaled, "stud", k), send(from_pair, "stud", k)) for k in range(1, studs)]
-    sums = kernel(
-        functools.partial(backward_body, False, 1),
-        grads,
-        (weights[3], from_pair, rows_other, act_other, slope_other, *sums),
-        work,
-    )
-    for error, rows, state in zip(theirs, mates, known):
+        functools.partial(backward_body, True, 1), grads, (weights[3], scaled, rows, act, slope), work
+    )
+    for scaled, rows, state in zip(theirs, mates, known):
         sums = kernel(
-            functools.partial(backward_body, False, 2),
+            functools.partial(backward_body, False, 1),
             grads,
-            (weights[3], error[0], rows[0], *state[:2], error[1], rows[1], *state[2:], *sums),
-            2 * work,
+            (weights[3], scaled, rows, *state, *sums),
+            work,
         )
     grad_up, grad_down = sums
     heights = (width // (owners * studs), actions // (owners * studs))

time: 37.8 us -> 38.2 us (1.011)
  waiting for transfers between devices: 16.1 us -> 18.6 us
  starting transfers between devices: 14.2 us -> 13 us
  Pallas kernels: 5.64 us -> 4.73 us
    ppermute x14 -> x11, waiting for transfers between devices: 16.1 us -> 18.6 us  [send(): lax.ppermute(block, axis, [(i, partner_to(size, i, step)) for i in range(...]
    ppermute x14 -> x11, starting transfers between devices: 14.2 us -> 13 us  [send(): lax.ppermute(block, axis, [(i, partner_to(size, i, step)) for i in range(...]
    pallas_call x10 -> x8, Pallas kernels: 5.64 us -> 4.73 us  [kernel(): pl.pallas_call(body, out_shape=outs, in_specs=places or [VMEM] * len(oper...]
  transfers between devices with their start and end apart: 14 -> 11, of which waited for: 11 -> 10; matrix products, arithmetic and copies ran while one was open for 0% -> 0% of each run, Pallas kernels for 7% -> 5%
where the time goes in v10:
time: 38.2 us; the launch traced here: 38.1 us
  waiting for transfers between devices  18.6 us (49%)
  starting transfers between devices  13 us (34%)
  Pallas kernels  4.73 us (12%)
  between operations  0.79 us (2%)
  local copies, waits for them, and re-layouts  0.71 us (2%)
    ppermute x11, waiting for transfers between devices, send(): lax.ppermute(block, axis, [(i, partner_to(size, i, step)) for i in range(...  18.6 us
    ppermute x11, starting transfers between devices, send(): lax.ppermute(block, axis, [(i, partner_to(size, i, step)) for i in range(...  13 us
    pallas_call x8, Pallas kernels, kernel(): pl.pallas_call(body, out_shape=outs, in_specs=places or [VMEM] * len(oper...  4.73 us
  transfers between devices with their start and end apart: 11, of which 10 were waited for; matrix products, arithmetic and copies ran while one was open for 0% of the time, Pallas kernels for 5%

profile of v10, /device:TPU:0, one launch (start us, length us, event | category | flops | bytes accessed | tf_op | source)
XLA Modules:
  0.0 38.1 jit_solution(15632085070461807234)
XLA Ops:
  0.6 1.2 %shard_map.86 = (bf16[48,640]{1,0:T(8,128)(2,1)S(1)}, bf16[48,640]{1,0:T(8,128)(2,1)S(1)}, bf16[48,640]{1,0:T(8,128)(2,1)S(1)}, bf16[48,640]{1,0:T(8,128)(2,1)S(1)}) custom-call(bf16[128,512]{1,0:T(8,128)(2,1)} %refs_0_.1, s32[1,128]{1,0:T(1,128)} %bitcast.24, s32[1,128]{1,0:T(1,128)} %bitcast.25), custom_call_target="tpu_custom_call" | custom-call | flops 25165824 | bytes 262144 | tf_op jit(solution)/shard_map/pallas_call | solution.py:195
  1.8 4.0 %collective-permute-start = (bf16[48,640]{1,0:T(8,128)(2,1)S(1)}, bf16[48,640]{1,0:T(8,128)(2,1)S(1)}, u32[]{:S(2)}, u32[]{:S(2)}) collective-permute-start(bf16[48,640]{1,0:T(8,128)(2,1)S(1)} %get-tuple-element.34), channel_id=1, source_target_pairs={{0,24},{8,16},{16,8},{24,0},{1,25},{9,17},{17,9},{25,1},{2,26},{10... | collective-permute-start | bytes 184328 | tf_op jit(solution)/shard_map/ppermute | solution.py:39
  5.8 0.5 %collective-permute-start.1 = (bf16[48,640]{1,0:T(8,128)(2,1)S(1)}, bf16[48,640]{1,0:T(8,128)(2,1)S(1)}, u32[]{:S(2)}, u32[]{:S(2)}) collective-permute-start(bf16[48,640]{1,0:T(8,128)(2,1)S(1)} %get-tuple-element.35), channel_id=1, source_target_pairs={{0,16},{8,24},{16,0},{24,8},{1,17},{9,25},{17,1},{25,9},{2,18},{10... | collective-permute-start | bytes 184328 | tf_op jit(solution)/shard_map/ppermute | solution.py:39
  6.3 0.1 collective-permute-start.2
  6.4 1.2 %shard_map.87 = (bf16[1,512,256]{2,1,0:T(8,128)(2,1)S(1)}, bf16[1,256,512]{2,1,0:T(8,128)(2,1)S(1)}, bf16[512,256]{1,0:T(8,128)(2,1)S(1)}, bf16[512,256]{1,0:T(8,128)(2,1)S(1)}) custom-call(bf16[48,640]{1,0:T(8,128)(2,1)S(1)} %get-tuple-element.32.refs_0_, bf16[1,512,256]{2,1,0:T(8,128)(2,1)} %refs_1_.1, bf16[1,256,512]{2,1,0:T(8,128)(2,1)} %refs_2_.1, ...), custom_call_target="tpu_custom_call" | custom-call | bytes 262144 | tf_op jit(solution)/shard_map/pallas_call | solution.py:195
  7.7 0.3 collective-permute-done.refs_1_
  8.0 2.0 %collective-permute-done.1.refs_2_ = bf16[48,640]{1,0:T(8,128)(2,1)S(1)} collective-permute-done((bf16[48,640]{1,0:T(8,128)(2,1)S(1)}, bf16[48,640]{1,0:T(8,128)(2,1)S(1)}, u32[]{:S(2)}, u32[]{:S(2)}) %collective-permute-start.1) | collective-permute-done | bytes 61472 | tf_op jit(solution)/shard_map/ppermute | solution.py:39
  10.0 0.5 %collective-permute-done.2.refs_3_ = bf16[48,640]{1,0:T(8,128)(2,1)S(1)} collective-permute-done((bf16[48,640]{1,0:T(8,128)(2,1)S(1)}, bf16[48,640]{1,0:T(8,128)(2,1)S(1)}, u32[]{:S(2)}, u32[]{:S(2)}) %collective-permute-start.2) | collective-permute-done | bytes 61472 | tf_op jit(solution)/shard_map/ppermute | solution.py:39
  10.5 0.7 %shard_map.88 = (bf16[192,512]{1,0:T(8,128)(2,1)S(1)}, f32[192,128]{1,0:T(8,128)S(1)}, f32[1,128]{1,0:T(1,128)S(1)}, f32[192,512]{1,0:T(8,128)S(1)}, f32[200,512...) custom-call(bf16[48,640]{1,0:T(8,128)(2,1)S(1)} %get-tuple-element.32.refs_0_, ...), custom_call_target="tpu_custom_call" | custom-call | flops 201326592 | bytes 262144 | tf_op jit(solution)/shard_map/pallas_call | solution.py:195
  11.2 1.6 %collective-permute-start.3 = (f16[200,512]{1,0:T(8,128)(2,1)S(1)}, f16[200,512]{1,0:T(8,128)(2,1)S(1)}, u32[]{:S(2)}, u32[]{:S(2)}) collective-permute-start(f16[200,512]{1,0:T(8,128)(2,1)S(1)} %convert_element_type.39), channel_id=1, source_target_pairs={{0,1},{1,0},{2,3},{3,2},{4,5},{5,4},{6,7},{7,6},{8,9},{9,8},{10,11... | collective-permute-start | bytes 614408 | tf_op jit(solution)/shard_map/ppermute | solution.py:39
  12.9 4.2 %collective-permute-done.3 = f16[200,512]{1,0:T(8,128)(2,1)S(1)} collective-permute-done((f16[200,512]{1,0:T(8,128)(2,1)S(1)}, f16[200,512]{1,0:T(8,128)(2,1)S(1)}, u32[]{:S(2)}, u32[]{:S(2)}) %collective-permute-start.3) | collective-permute-done | bytes 204832 | tf_op jit(solution)/shard_map/ppermute | solution.py:39
  17.1 0.3 shard_map.89
  17.4 2.7 %collective-permute-start.4 = (f16[200,512]{1,0:T(8,128)(2,1)S(1)}, f16[200,512]{1,0:T(8,128)(2,1)S(1)}, u32[]{:S(2)}, u32[]{:S(2)}) collective-permute-start(f16[200,512]{1,0:T(8,128)(2,1)S(1)} %convert_element_type.41), channel_id=1, source_target_pairs={{0,2},{1,3},{2,0},{3,1},{4,6},{5,7},{6,4},{7,5},{8,10},{9,11},{10,... | collective-permute-start | bytes 614408 | tf_op jit(solution)/shard_map/ppermute | solution.py:39
  20.1 0.0 collective-permute-start.6
  20.1 0.5 %collective-permute-start.5 = (f32[1,128]{1,0:T(1,128)S(1)}, f32[1,128]{1,0:T(1,128)S(1)}, u32[]{:S(2)}, u32[]{:S(2)}) collective-permute-start(f32[1,128]{1,0:T(1,128)S(1)} %get-tuple-element.51.refs_3_), channel_id=1, source_target_pairs={{0,4},{4,0},{1,5},{5,1},{2,6},{6,2},{3,7},{7,3},{8,12},{12,8},{9,1... | collective-permute-start | bytes 1544 | tf_op jit(solution)/shard_map/ppermute | solution.py:39
  20.6 0.9 %collective-permute-done.6.rows.refs_2_ = bf16[192,512]{1,0:T(8,128)(2,1)S(1)} collective-permute-done((bf16[192,512]{1,0:T(8,128)(2,1)S(1)}, bf16[192,512]{1,0:T(8,128)(2,1)S(1)}, u32[]{:S(2)}, u32[]{:S(2)}) %collective-permute-start.6) | collective-permute-done | bytes 196640 | tf_op jit(solution)/shard_map/ppermute | solution.py:39
  21.5 0.2 shard_map.90
  21.8 5.3 %collective-permute-done.4 = f16[200,512]{1,0:T(8,128)(2,1)S(1)} collective-permute-done((f16[200,512]{1,0:T(8,128)(2,1)S(1)}, f16[200,512]{1,0:T(8,128)(2,1)S(1)}, u32[]{:S(2)}, u32[]{:S(2)}) %collective-permute-start.4) | collective-permute-done | bytes 204832 | tf_op jit(solution)/shard_map/ppermute | solution.py:39
  27.1 0.0 collective-permute-done.5.refs_4_
  27.1 0.2 shard_map.91.refs_1_
  27.3 0.1 collective-permute-start.7
  27.4 0.5 %shard_map.92 = (f32[512,256]{1,0:T(8,128)S(1)}, f32[512,256]{1,0:T(8,128)S(1)}) custom-call(bf16[512,256]{1,0:T(8,128)(2,1)S(1)} %get-tuple-element.33.refs_7_.refs_0_, bf16[192,512]{1,0:T(8,128)(2,1)S(1)} %shard_map.91.refs_1_, bf16[192,512]{1,0:T(8,128)(2,1)S(1)} %get-tuple-element.45.refs_2_, bf16[192,256]{1,0:T(8,128)(2,1)S(1)} %get-tuple-element.56.refs_3_, ...), custom_call_target="tpu_custom_call" | custom-call | flops 150994944 | bytes 262144 | tf_op jit(solution)/shard_map/pallas_call | solution.py:195
  27.9 0.9 %collective-permute-done.7.refs_1_ = bf16[192,512]{1,0:T(8,128)(2,1)S(1)} collective-permute-done((bf16[192,512]{1,0:T(8,128)(2,1)S(1)}, bf16[192,512]{1,0:T(8,128)(2,1)S(1)}, u32[]{:S(2)}, u32[]{:S(2)}) %collective-permute-start.7) | collective-permute-done | bytes 196640 | tf_op jit(solution)/shard_map/ppermute | solution.py:39
  28.9 0.5 %shard_map.93 = (f32[512,256]{1,0:T(8,128)S(1)}, f32[512,256]{1,0:T(8,128)S(1)}) custom-call(bf16[512,256]{1,0:T(8,128)(2,1)S(1)} %get-tuple-element.33.refs_7_.refs_0_, bf16[192,512]{1,0:T(8,128)(2,1)S(1)} %collective-permute-done.7.refs_1_, bf16[192,512]{1,0:T(8,128)(2,1)S(1)} %collective-permute-done.6.rows.refs_2_, ...), custom_call_target="tpu_custom_call" | custom-call | flops 150994944 | bytes 262144 | tf_op jit(solution)/shard_map/pallas_call | solution.py:195
  29.3 0.1 dynamic-slice_bitcast_fusion
  29.4 1.8 %collective-permute-start.10 = (bf16[128,256]{1,0:T(8,128)(2,1)S(1)}, bf16[128,256]{1,0:T(8,128)(2,1)S(1)}, u32[]{:S(2)}, u32[]{:S(2)}) collective-permute-start(bf16[128,256]{1,0:T(8,128)(2,1)S(1)} %get-tuple-element.64), channel_id=1, source_target_pairs={{0,8},{8,0},{16,24},{24,16},{1,9},{9,1},{17,25},{25,17},{2,10},{10... | collective-permute-start | bytes 196616 | tf_op jit(solution)/shard_map/ppermute | solution.py:39
  31.2 1.2 %collective-permute-start.8 = (bf16[128,256]{1,0:T(8,128)(2,1)S(1)}, bf16[128,256]{1,0:T(8,128)(2,1)S(1)}, u32[]{:S(2)}, u32[]{:S(2)}) collective-permute-start(bf16[128,256]{1,0:T(8,128)(2,1)S(1)} %get-tuple-element.62), channel_id=1, source_target_pairs={{0,24},{8,16},{16,8},{24,0},{1,25},{9,17},{17,9},{25,1},{2,26},{10... | collective-permute-start | bytes 196616 | tf_op jit(solution)/shard_map/ppermute | solution.py:39
  32.4 0.6 %collective-permute-start.9 = (bf16[128,256]{1,0:T(8,128)(2,1)S(1)}, bf16[128,256]{1,0:T(8,128)(2,1)S(1)}, u32[]{:S(2)}, u32[]{:S(2)}) collective-permute-start(bf16[128,256]{1,0:T(8,128)(2,1)S(1)} %get-tuple-element.63), channel_id=1, source_target_pairs={{0,16},{8,24},{16,0},{24,8},{1,17},{9,25},{17,1},{25,9},{2,18},{10... | collective-permute-start | bytes 196616 | tf_op jit(solution)/shard_map/ppermute | solution.py:39
  33.0 0.9 %collective-permute-done.10 = bf16[128,256]{1,0:T(8,128)(2,1)S(1)} collective-permute-done((bf16[128,256]{1,0:T(8,128)(2,1)S(1)}, bf16[128,256]{1,0:T(8,128)(2,1)S(1)}, u32[]{:S(2)}, u32[]{:S(2)}) %collective-permute-start.10) | collective-permute-done | bytes 65568 | tf_op jit(solution)/shard_map/ppermute | solution.py:39
  33.9 2.5 %collective-permute-done.8 = bf16[128,256]{1,0:T(8,128)(2,1)S(1)} collective-permute-done((bf16[128,256]{1,0:T(8,128)(2,1)S(1)}, bf16[128,256]{1,0:T(8,128)(2,1)S(1)}, u32[]{:S(2)}, u32[]{:S(2)}) %collective-permute-start.8) | collective-permute-done | bytes 65568 | tf_op jit(solution)/shard_map/ppermute | solution.py:39
  36.4 0.9 %collective-permute-done.9 = bf16[128,256]{1,0:T(8,128)(2,1)S(1)} collective-permute-done((bf16[128,256]{1,0:T(8,128)(2,1)S(1)}, bf16[128,256]{1,0:T(8,128)(2,1)S(1)}, u32[]{:S(2)}, u32[]{:S(2)}) %collective-permute-start.9) | collective-permute-done | bytes 65568 | tf_op jit(solution)/shard_map/ppermute | solution.py:39
  37.4 0.7 %fusion.14 = (f32[64,256]{1,0:T(8,128)}, f32[64,256]{1,0:T(8,128)}) fusion(f32[128,256]{1,0:T(8,128)S(1)} %fusion.6), kind=kLoop, calls=%fused_computation.24 | loop fusion | bytes 262144 | tf_op jit(solution)/shard_map/slice | solution.py:304
  (6 shorter events, 0.2 us)
Async XLA Ops:
  1.8 6.2 %collective-permute-start = (bf16[48,640]{1,0:T(8,128)(2,1)S(1)}, bf16[48,640]{1,0:T(8,128)(2,1)S(1)}, u32[]{:S(2)}, u32[]{:S(2)}) collective-permute-start(bf16[48,640]{1,0:T(8,128)(2,1)S(1)} %get-tuple-element.34), channel_id=1, source_target_pairs={{0,24},{8,16},{16,8},{24,0},{1,25},{9,17},{17,9},{25,1},{2,26},{10... | collective-permute-start | bytes 184328 | tf_op jit(solution)/shard_map/ppermute | solution.py:39
  5.8 4.2 %collective-permute-start.1 = (bf16[48,640]{1,0:T(8,128)(2,1)S(1)}, bf16[48,640]{1,0:T(8,128)(2,1)S(1)}, u32[]{:S(2)}, u32[]{:S(2)}) collective-permute-start(bf16[48,640]{1,0:T(8,128)(2,1)S(1)} %get-tuple-element.35), channel_id=1, source_target_pairs={{0,16},{8,24},{16,0},{24,8},{1,17},{9,25},{17,1},{25,9},{2,18},{10... | collective-permute-start | bytes 184328 | tf_op jit(solution)/shard_map/ppermute | solution.py:39
  6.3 4.2 %collective-permute-start.2 = (bf16[48,640]{1,0:T(8,128)(2,1)S(1)}, bf16[48,640]{1,0:T(8,128)(2,1)S(1)}, u32[]{:S(2)}, u32[]{:S(2)}) collective-permute-start(bf16[48,640]{1,0:T(8,128)(2,1)S(1)} %get-tuple-element.36), channel_id=1, source_target_pairs={{0,8},{8,0},{16,24},{24,16},{1,9},{9,1},{17,25},{25,17},{2,10},{10... | collective-permute-start | bytes 184328 | tf_op jit(solution)/shard_map/ppermute | solution.py:39
  11.2 5.8 %collective-permute-start.3 = (f16[200,512]{1,0:T(8,128)(2,1)S(1)}, f16[200,512]{1,0:T(8,128)(2,1)S(1)}, u32[]{:S(2)}, u32[]{:S(2)}) collective-permute-start(f16[200,512]{1,0:T(8,128)(2,1)S(1)} %convert_element_type.39), channel_id=1, source_target_pairs={{0,1},{1,0},{2,3},{3,2},{4,5},{5,4},{6,7},{7,6},{8,9},{9,8},{10,11... | collective-permute-start | bytes 614408 | tf_op jit(solution)/shard_map/ppermute | solution.py:39
  17.4 9.7 %collective-permute-start.4 = (f16[200,512]{1,0:T(8,128)(2,1)S(1)}, f16[200,512]{1,0:T(8,128)(2,1)S(1)}, u32[]{:S(2)}, u32[]{:S(2)}) collective-permute-start(f16[200,512]{1,0:T(8,128)(2,1)S(1)} %convert_element_type.41), channel_id=1, source_target_pairs={{0,2},{1,3},{2,0},{3,1},{4,6},{5,7},{6,4},{7,5},{8,10},{9,11},{10,... | collective-permute-start | bytes 614408 | tf_op jit(solution)/shard_map/ppermute | solution.py:39
  20.1 1.4 %collective-permute-start.6 = (bf16[192,512]{1,0:T(8,128)(2,1)S(1)}, bf16[192,512]{1,0:T(8,128)(2,1)S(1)}, u32[]{:S(2)}, u32[]{:S(2)}) collective-permute-start(bf16[192,512]{1,0:T(8,128)(2,1)S(1)} %get-tuple-element.45.refs_2_), channel_id=1, source_target_pairs={{0,4},{4,0},{1,5},{5,1},{2,6},{6,2},{3,7},{7,3},{8,12},{12,8},{9,1... | collective-permute-start | bytes 589832 | tf_op jit(solution)/shard_map/ppermute | solution.py:39
  20.1 7.1 %collective-permute-start.5 = (f32[1,128]{1,0:T(1,128)S(1)}, f32[1,128]{1,0:T(1,128)S(1)}, u32[]{:S(2)}, u32[]{:S(2)}) collective-permute-start(f32[1,128]{1,0:T(1,128)S(1)} %get-tuple-element.51.refs_3_), channel_id=1, source_target_pairs={{0,4},{4,0},{1,5},{5,1},{2,6},{6,2},{3,7},{7,3},{8,12},{12,8},{9,1... | collective-permute-start | bytes 1544 | tf_op jit(solution)/shard_map/ppermute | solution.py:39
  27.3 1.5 %collective-permute-start.7 = (bf16[192,512]{1,0:T(8,128)(2,1)S(1)}, bf16[192,512]{1,0:T(8,128)(2,1)S(1)}, u32[]{:S(2)}, u32[]{:S(2)}) collective-permute-start(bf16[192,512]{1,0:T(8,128)(2,1)S(1)} %shard_map.91.refs_1_), channel_id=1, source_target_pairs={{0,4},{4,0},{1,5},{5,1},{2,6},{6,2},{3,7},{7,3},{8,12},{12,8},{9,1... | collective-permute-start | bytes 589832 | tf_op jit(solution)/shard_map/ppermute | solution.py:39
  29.4 4.5 %collective-permute-start.10 = (bf16[128,256]{1,0:T(8,128)(2,1)S(1)}, bf16[128,256]{1,0:T(8,128)(2,1)S(1)}, u32[]{:S(2)}, u32[]{:S(2)}) collective-permute-start(bf16[128,256]{1,0:T(8,128)(2,1)S(1)} %get-tuple-element.64), channel_id=1, source_target_pairs={{0,8},{8,0},{16,24},{24,16},{1,9},{9,1},{17,25},{25,17},{2,10},{10... | collective-permute-start | bytes 196616 | tf_op jit(solution)/shard_map/ppermute | solution.py:39
  31.2 5.2 %collective-permute-start.8 = (bf16[128,256]{1,0:T(8,128)(2,1)S(1)}, bf16[128,256]{1,0:T(8,128)(2,1)S(1)}, u32[]{:S(2)}, u32[]{:S(2)}) collective-permute-start(bf16[128,256]{1,0:T(8,128)(2,1)S(1)} %get-tuple-element.62), channel_id=1, source_target_pairs={{0,24},{8,16},{16,8},{24,0},{1,25},{9,17},{17,9},{25,1},{2,26},{10... | collective-permute-start | bytes 196616 | tf_op jit(solution)/shard_map/ppermute | solution.py:39
  32.4 4.9 %collective-permute-start.9 = (bf16[128,256]{1,0:T(8,128)(2,1)S(1)}, bf16[128,256]{1,0:T(8,128)(2,1)S(1)}, u32[]{:S(2)}, u32[]{:S(2)}) collective-permute-start(bf16[128,256]{1,0:T(8,128)(2,1)S(1)} %get-tuple-element.63), channel_id=1, source_target_pairs={{0,16},{8,24},{16,0},{24,8},{1,17},{9,25},{17,1},{25,9},{2,18},{10... | collective-permute-start | bytes 196616 | tf_op jit(solution)/shard_map/ppermute | solution.py:39

commit v11 on v10

--- a/solution.py
+++ b/solution.py
@@ -151,8 +151,29 @@
     pack(error_out[...], packed)
 
 
-def neighbour_body(rows, student_up, act, slope):
-    act[...], slope[...] = student(rows[...], student_up)
+def chosen_columns(columns, owners, studs):
+    height = columns // (owners * studs)
+    shape = (owners * height, columns)
+    row = lax.broadcasted_iota(jnp.int32, shape, 0)
+    column = lax.broadcasted_iota(jnp.int32, shape, 1)
+    owner = partner_to(owners, lax.axis_index("teach"), row // height)
+    wanted = (owner * studs + lax.axis_index("stud")) * height + row % height
+    return (column == wanted).astype(jnp.float32).astype(jnp.bfloat16)
+
+
+def turn(value, owners, studs):
+    chosen = chosen_columns(value.shape[1], owners, studs)
+    return dot(chosen, value, ((1,), (1,))).astype(jnp.bfloat16)
+
+
+def ahead_body(owners, studs, own, rows, student_up, *refs):
+    if own:
+        _, turned, handed = refs
+        handed[...] = rows[...]
+    else:
+        turned, act, slope = refs
+        act[...], slope[...] = student(rows[...], student_up)
+    turned[...] = turn(rows[...], owners, studs)
 
 
 def pair_body(own, arrived, total, packed):
@@ -172,33 +193,47 @@
     scaled[...] = ((own[...] + unpack(arrived)) * weight).astype(scaled.dtype)
 
 
-def backward_body(first, groups, *refs):
-    student_down, refs = refs[0], refs[1:]
-    grad_up, grad_down = refs[-2:]
-    if first:
-        up, down = None, None
-    else:
-        up, down = refs[4 * groups][...], refs[4 * groups + 1][...]
-    for i in range(groups):
-        scaled, rows, act, slope = refs[4 * i : 4 * i + 4]
-        error = scaled[...]
-        part = dot(error, act[...], ((0,), (0,)))
-        down = part if down is None else down + part
-        pre_grad = (dot(error, student_down[...]) * slope[...]).astype(jnp.bfloat16)
-        part = dot(rows[...], pre_grad, ((0,), (0,)))
-        up = part if up is None else up + part
-    grad_up[...] = up
-    grad_down[...] = down
-
-
-def kernel(body, outs, operands, flops, scratch=(), params=SMALL, places=None):
+def backward_body(owners, studs, earlier, scaled, turned, act, slope, student_down, *refs):
+    error = scaled[...]
+    down = dot(turn(error, owners, studs), act[...])
+    pre_grad = (dot(error, student_down[...]) * slope[...]).astype(jnp.bfloat16)
+    up = dot(turned[...], pre_grad)
+    if earlier:
+        up, down = up + refs[0][...], down + refs[1][...]
+    outs = refs[2 * earlier :]
+    if len(outs) == 2:
+        outs[0][...], outs[1][...] = up, down
+        return
+    high, low = up.shape[0] // owners, down.shape[0] // owners
+    for k, out in enumerate(outs):
+        block = [up[k * high : (k + 1) * high], down[k * low : (k + 1) * low]]
+        out[...] = jnp.concatenate(block).astype(out.dtype)
+
+
+def closing_body(*refs):
+    pieces, (grad_up, grad_down, up, down, sems) = refs[:-5], refs[-5:]
+    total = pieces[0][...]
+    for piece in pieces[1:]:
+        total = total + piece[...].astype(jnp.float32)
+    cut = up.shape[0]
+    up[...] = total[:cut]
+    first = pltpu.make_async_copy(up, grad_up, sems.at[0])
+    first.start()
+    down[...] = total[cut:]
+    second = pltpu.make_async_copy(down, grad_down, sems.at[1])
+    second.start()
+    first.wait()
+    second.wait()
+
+
+def kernel(body, outs, operands, flops, scratch=(), params=SMALL, places=None, to=VMEM):
     return pl.pallas_call(
         body,
         out_shape=outs,
         in_specs=places or [VMEM] * len(operands),
-        out_specs=[VMEM] * len(outs),
+        out_specs=[to] * len(outs),
         scratch_shapes=list(scratch),
-        cost_estimate=pl.CostEstimate(flops=flops, bytes_accessed=1 << 18, transcendentals=0),
+        cost_estimate=pl.CostEstimate(flops=flops, bytes_accessed=0, transcendentals=0),
         compiler_params=params,
     )(*operands)
 
@@ -255,53 +290,49 @@
         error, other = kernel(pair_body, [whole, packed], (error, arrived), 0)
         arrived = cross(other, step)
         step *= 2
-    all_counts, mates = [counts], []
+    ahead = functools.partial(ahead_body, owners, studs, False)
+    turned = shape(width // studs, slots, bf16)
+    ours, handed = kernel(
+        functools.partial(ahead_body, owners, studs, True),
+        [turned, shape(slots, width, bf16)],
+        (rows, weights[2], error),
+        0,
+    )
+    all_counts, known = [counts], []
     for k in range(1, studs):
         all_counts.append(send(counts, "stud", k))
-        mates.append(send(rows, "stud", k))
-    known = [
-        kernel(neighbour_body, state, (theirs, weights[2]), 2 * slots * width * units)
-        for theirs in mates
-    ]
-    error, arrived, all_counts, mates, known = lax.optimization_barrier(
-        (error, arrived, all_counts, mates, known)
+        theirs = send(handed, "stud", k)
+        known.append(
+            kernel(ahead, [turned] + state, (theirs, weights[2]), 0)
+        )
+    error, arrived, all_counts, known, ours = lax.optimization_barrier(
+        (error, arrived, all_counts, known, ours)
     )
     (scaled,) = kernel(scale_body, [shape(slots, actions, bf16)], (error, arrived, tags, *all_counts), 0)
     work = 6 * slots * width * units
-    grads = [shape(width, units, f32), shape(actions, units, f32)]
-    theirs = [send(scaled, "stud", k) for k in range(1, studs)]
-    sums = kernel(
-        functools.partial(backward_body, True, 1), grads, (weights[3], scaled, rows, act, slope), work
-    )
-    for scaled, rows, state in zip(theirs, mates, known):
+    grads = [shape(width // studs, units, f32), shape(actions // studs, units, f32)]
+    heights = [g.shape[0] // owners for g in grads]
+    blocks = [shape(sum(heights), units, f32)] + [shape(sum(heights), units, bf16)] * (owners - 1)
+    errors = [scaled] + [send(scaled, "stud", k) for k in range(1, studs)]
+    states = [[ours, act, slope]] + known
+    sums = []
+    for k, (error, state) in enumerate(zip(errors, states)):
         sums = kernel(
-            functools.partial(backward_body, False, 1),
-            grads,
-            (weights[3], scaled, rows, *state, *sums),
+            functools.partial(backward_body, owners, studs, k > 0),
+            blocks if k == studs - 1 else grads,
+            (error, *state, weights[3], *sums),
             work,
         )
-    grad_up, grad_down = sums
-    heights = (width // (owners * studs), actions // (owners * studs))
-
-    def pieces(stud):
-        return jnp.concatenate(
-            [
-                lax.dynamic_index_in_dim(g.reshape(owners, studs, h, units), stud, 1, False)
-                for g, h in zip((grad_up, grad_down), heights)
-            ],
-            axis=1,
-        )
-
-    half = pieces(lax.axis_index("stud"))
-    me = lax.axis_index("teach")
-    part = lax.dynamic_index_in_dim(half, me, 0, False)
-    arrived = [
-        send(lax.dynamic_index_in_dim(half, partner_to(owners, me, k), 0, False).astype(bf16), "teach", k)
-        for k in range(owners - 1, 0, -1)
-    ]
-    for piece in arrived:
-        part = part + piece.astype(f32)
-    return part[: heights[0]], part[heights[0] :]
+    pieces = [sums[0]] + [send(sums[k], "teach", k) for k in (*range(owners - 2, 0, -1), owners - 1)]
+    outs = [shape(h, units, f32) for h in heights]
+    return kernel(
+        closing_body,
+        outs,
+        pieces,
+        0,
+        [pltpu.VMEM(o.shape, f32) for o in outs] + [pltpu.SemaphoreType.DMA((2,))],
+        to=HBM,
+    )
 
 
 def solution(mesh):

time: 38.2 us -> 37.7 us (0.987)
  Pallas kernels: 4.73 us -> 5.94 us
  waiting for transfers between devices: 18.6 us -> 17.6 us
  local copies, waits for them, and re-layouts: 0.71 us -> 0 us
    pallas_call x8 -> x10, Pallas kernels: 4.73 us -> 5.94 us  [kernel(): pl.pallas_call(body, out_shape=outs, in_specs=places or [VMEM] * len(oper...]
    ppermute x11, waiting for transfers between devices: 18.6 us -> 17.6 us  [send(): lax.ppermute(block, axis, [(i, partner_to(size, i, step)) for i in range(...]
    slice x1 -> x0, local copies, waits for them, and re-layouts: 0.66 us -> none  [on_device(): return (part[:heights[0]], part[heights[0]:])]
  transfers between devices with their start and end apart: 11 -> 11, of which waited for: 10 -> 10; matrix products, arithmetic and copies ran while one was open for 0% -> 0% of each run, Pallas kernels for 5% -> 7%
where the time goes in v11:
time: 37.7 us; the launch traced here: 37.5 us
  waiting for transfers between devices  17.6 us (47%)
  starting transfers between devices  13.1 us (35%)
  Pallas kernels  5.94 us (16%)
  between operations  0.76 us (2%)
    ppermute x11, waiting for transfers between devices, send(): lax.ppermute(block, axis, [(i, partner_to(size, i, step)) for i in range(...  17.6 us
    ppermute x11, starting transfers between devices, send(): lax.ppermute(block, axis, [(i, partner_to(size, i, step)) for i in range(...  13.1 us
    pallas_call x10, Pallas kernels, kernel(): pl.pallas_call(body, out_shape=outs, in_specs=places or [VMEM] * len(oper...  5.94 us
  transfers between devices with their start and end apart: 11, of which 10 were waited for; matrix products, arithmetic and copies ran while one was open for 0% of the time, Pallas kernels for 7%

profile of v11, /device:TPU:0, one launch (start us, length us, event | category | flops | bytes accessed | tf_op | source)
XLA Modules:
  0.0 37.5 jit_solution(5917145785311293408)
XLA Ops:
  0.6 1.2 %shard_map.86 = (bf16[48,640]{1,0:T(8,128)(2,1)S(1)}, bf16[48,640]{1,0:T(8,128)(2,1)S(1)}, bf16[48,640]{1,0:T(8,128)(2,1)S(1)}, bf16[48,640]{1,0:T(8,128)(2,1)S(1)}) custom-call(bf16[128,512]{1,0:T(8,128)(2,1)} %refs_0_.1, s32[1,128]{1,0:T(1,128)} %bitcast.2, s32[1,128]{1,0:T(1,128)} %bitcast.3), custom_call_target="tpu_custom_call" | custom-call | flops 25165824 | tf_op jit(solution)/shard_map/pallas_call | solution.py:230
  1.8 4.0 %collective-permute-start = (bf16[48,640]{1,0:T(8,128)(2,1)S(1)}, bf16[48,640]{1,0:T(8,128)(2,1)S(1)}, u32[]{:S(2)}, u32[]{:S(2)}) collective-permute-start(bf16[48,640]{1,0:T(8,128)(2,1)S(1)} %get-tuple-element.39), channel_id=1, source_target_pairs={{0,24},{8,16},{16,8},{24,0},{1,25},{9,17},{17,9},{25,1},{2,26},{10... | collective-permute-start | bytes 184328 | tf_op jit(solution)/shard_map/ppermute | solution.py:39
  5.8 0.5 %collective-permute-start.1 = (bf16[48,640]{1,0:T(8,128)(2,1)S(1)}, bf16[48,640]{1,0:T(8,128)(2,1)S(1)}, u32[]{:S(2)}, u32[]{:S(2)}) collective-permute-start(bf16[48,640]{1,0:T(8,128)(2,1)S(1)} %get-tuple-element.40), channel_id=1, source_target_pairs={{0,16},{8,24},{16,0},{24,8},{1,17},{9,25},{17,1},{25,9},{2,18},{10... | collective-permute-start | bytes 184328 | tf_op jit(solution)/shard_map/ppermute | solution.py:39
  6.3 0.1 collective-permute-start.2
  6.4 1.2 %shard_map.87 = (bf16[1,512,256]{2,1,0:T(8,128)(2,1)S(1)}, bf16[1,256,512]{2,1,0:T(8,128)(2,1)S(1)}, bf16[512,256]{1,0:T(8,128)(2,1)S(1)}, bf16[512,256]{1,0:T(8,128)(2,1)S(1)}) custom-call(bf16[48,640]{1,0:T(8,128)(2,1)S(1)} %get-tuple-element.38.refs_0_, bf16[1,512,256]{2,1,0:T(8,128)(2,1)} %refs_1_.1, bf16[1,256,512]{2,1,0:T(8,128)(2,1)} %refs_2_.1, ...), custom_call_target="tpu_custom_call" | custom-call | tf_op jit(solution)/shard_map/pallas_call | solution.py:230
  7.7 0.3 collective-permute-done.refs_1_
  8.0 2.0 %collective-permute-done.1.refs_2_ = bf16[48,640]{1,0:T(8,128)(2,1)S(1)} collective-permute-done((bf16[48,640]{1,0:T(8,128)(2,1)S(1)}, bf16[48,640]{1,0:T(8,128)(2,1)S(1)}, u32[]{:S(2)}, u32[]{:S(2)}) %collective-permute-start.1) | collective-permute-done | bytes 61472 | tf_op jit(solution)/shard_map/ppermute | solution.py:39
  10.0 0.5 %collective-permute-done.2.refs_3_ = bf16[48,640]{1,0:T(8,128)(2,1)S(1)} collective-permute-done((bf16[48,640]{1,0:T(8,128)(2,1)S(1)}, bf16[48,640]{1,0:T(8,128)(2,1)S(1)}, u32[]{:S(2)}, u32[]{:S(2)}) %collective-permute-start.2) | collective-permute-done | bytes 61472 | tf_op jit(solution)/shard_map/ppermute | solution.py:39
  10.5 0.7 %shard_map.88 = (bf16[192,512]{1,0:T(8,128)(2,1)S(1)}, f32[192,128]{1,0:T(8,128)S(1)}, f32[1,128]{1,0:T(1,128)S(1)}, f32[192,512]{1,0:T(8,128)S(1)}, f32[200,512...) custom-call(bf16[48,640]{1,0:T(8,128)(2,1)S(1)} %get-tuple-element.38.refs_0_, ...), custom_call_target="tpu_custom_call" | custom-call | flops 201326592 | tf_op jit(solution)/shard_map/pallas_call | solution.py:230
  11.2 1.6 %collective-permute-start.3 = (f16[200,512]{1,0:T(8,128)(2,1)S(1)}, f16[200,512]{1,0:T(8,128)(2,1)S(1)}, u32[]{:S(2)}, u32[]{:S(2)}) collective-permute-start(f16[200,512]{1,0:T(8,128)(2,1)S(1)} %convert_element_type.12), channel_id=1, source_target_pairs={{0,1},{1,0},{2,3},{3,2},{4,5},{5,4},{6,7},{7,6},{8,9},{9,8},{10,11... | collective-permute-start | bytes 614408 | tf_op jit(solution)/shard_map/ppermute | solution.py:39
  12.9 4.2 %collective-permute-done.3 = f16[200,512]{1,0:T(8,128)(2,1)S(1)} collective-permute-done((f16[200,512]{1,0:T(8,128)(2,1)S(1)}, f16[200,512]{1,0:T(8,128)(2,1)S(1)}, u32[]{:S(2)}, u32[]{:S(2)}) %collective-permute-start.3) | collective-permute-done | bytes 204832 | tf_op jit(solution)/shard_map/ppermute | solution.py:39
  17.1 0.3 shard_map.89
  17.4 2.7 %collective-permute-start.4 = (f16[200,512]{1,0:T(8,128)(2,1)S(1)}, f16[200,512]{1,0:T(8,128)(2,1)S(1)}, u32[]{:S(2)}, u32[]{:S(2)}) collective-permute-start(f16[200,512]{1,0:T(8,128)(2,1)S(1)} %convert_element_type.14), channel_id=1, source_target_pairs={{0,2},{1,3},{2,0},{3,1},{4,6},{5,7},{6,4},{7,5},{8,10},{9,11},{10,... | collective-permute-start | bytes 614408 | tf_op jit(solution)/shard_map/ppermute | solution.py:39
  20.1 0.2 shard_map.90
  20.3 0.1 collective-permute-start.6
  20.4 0.5 %collective-permute-start.5 = (f32[1,128]{1,0:T(1,128)S(1)}, f32[1,128]{1,0:T(1,128)S(1)}, u32[]{:S(2)}, u32[]{:S(2)}) collective-permute-start(f32[1,128]{1,0:T(1,128)S(1)} %get-tuple-element.60.refs_3_), channel_id=1, source_target_pairs={{0,4},{4,0},{1,5},{5,1},{2,6},{6,2},{3,7},{7,3},{8,12},{12,8},{9,1... | collective-permute-start | bytes 1544 | tf_op jit(solution)/shard_map/ppermute | solution.py:39
  20.9 0.9 %collective-permute-done.6.rows = bf16[192,512]{1,0:T(8,128)(2,1)S(1)} collective-permute-done((bf16[192,512]{1,0:T(8,128)(2,1)S(1)}, bf16[192,512]{1,0:T(8,128)(2,1)S(1)}, u32[]{:S(2)}, u32[]{:S(2)}) %collective-permute-start.6) | collective-permute-done | bytes 196640 | tf_op jit(solution)/shard_map/ppermute | solution.py:39
  21.8 0.3 shard_map.91
  22.1 4.9 %collective-permute-done.4 = f16[200,512]{1,0:T(8,128)(2,1)S(1)} collective-permute-done((f16[200,512]{1,0:T(8,128)(2,1)S(1)}, f16[200,512]{1,0:T(8,128)(2,1)S(1)}, u32[]{:S(2)}, u32[]{:S(2)}) %collective-permute-start.4) | collective-permute-done | bytes 204832 | tf_op jit(solution)/shard_map/ppermute | solution.py:39
  27.1 0.0 collective-permute-done.5.refs_4_
  27.1 0.2 shard_map.92.scaled
  27.3 0.1 collective-permute-start.7
  27.4 0.7 %shard_map.93 = (f32[256,256]{1,0:T(8,128)S(1)}, f32[256,256]{1,0:T(8,128)S(1)}) custom-call(bf16[192,512]{1,0:T(8,128)(2,1)S(1)} %shard_map.92.scaled, bf16[256,192]{1,0:T(8,128)(2,1)S(1)} %get-tuple-element.65.turned, bf16[192,256]{1,0:T(8,128)(2,1)S(1)} %get-tuple-element.66.act, f32[192,256]{1,0:T(8,128)S(1)} %get-tuple-element.67.slope, ...), custom_call_target="tpu_custom_call" | custom-call | flops 150994944 | tf_op jit(solution)/shard_map/pallas_call | solution.py:230
  28.1 0.7 %collective-permute-done.7.scaled = bf16[192,512]{1,0:T(8,128)(2,1)S(1)} collective-permute-done((bf16[192,512]{1,0:T(8,128)(2,1)S(1)}, bf16[192,512]{1,0:T(8,128)(2,1)S(1)}, u32[]{:S(2)}, u32[]{:S(2)}) %collective-permute-start.7) | collective-permute-done | bytes 196640 | tf_op jit(solution)/shard_map/ppermute | solution.py:39
  28.9 0.5 %shard_map.94 = (f32[128,256]{1,0:T(8,128)S(1)}, bf16[128,256]{1,0:T(8,128)(2,1)S(1)}, bf16[128,256]{1,0:T(8,128)(2,1)S(1)}, bf16[128,256]{1,0:T(8,128)(2,1)S(1)}) custom-call(bf16[192,512]{1,0:T(8,128)(2,1)S(1)} %collective-permute-done.7.scaled, bf16[256,192]{1,0:T(8,128)(2,1)S(1)} %get-tuple-element.62.turned, ...), custom_call_target="tpu_custom_call" | custom-call | flops 150994944 | tf_op jit(solution)/shard_map/pallas_call | solution.py:230
  29.3 1.8 %collective-permute-start.10 = (bf16[128,256]{1,0:T(8,128)(2,1)S(1)}, bf16[128,256]{1,0:T(8,128)(2,1)S(1)}, u32[]{:S(2)}, u32[]{:S(2)}) collective-permute-start(bf16[128,256]{1,0:T(8,128)(2,1)S(1)} %get-tuple-element.73), channel_id=1, source_target_pairs={{0,24},{8,16},{16,8},{24,0},{1,25},{9,17},{17,9},{25,1},{2,26},{10... | collective-permute-start | bytes 196616 | tf_op jit(solution)/shard_map/ppermute | solution.py:39
  31.1 1.4 %collective-permute-start.8 = (bf16[128,256]{1,0:T(8,128)(2,1)S(1)}, bf16[128,256]{1,0:T(8,128)(2,1)S(1)}, u32[]{:S(2)}, u32[]{:S(2)}) collective-permute-start(bf16[128,256]{1,0:T(8,128)(2,1)S(1)} %get-tuple-element.71), channel_id=1, source_target_pairs={{0,16},{8,24},{16,0},{24,8},{1,17},{9,25},{17,1},{25,9},{2,18},{10... | collective-permute-start | bytes 196616 | tf_op jit(solution)/shard_map/ppermute | solution.py:39
  32.6 0.3 collective-permute-start.9
  32.9 1.7 %collective-permute-done.10.refs_3_ = bf16[128,256]{1,0:T(8,128)(2,1)S(1)} collective-permute-done((bf16[128,256]{1,0:T(8,128)(2,1)S(1)}, bf16[128,256]{1,0:T(8,128)(2,1)S(1)}, u32[]{:S(2)}, u32[]{:S(2)}) %collective-permute-start.10) | collective-permute-done | bytes 65568 | tf_op jit(solution)/shard_map/ppermute | solution.py:39
  34.6 1.2 %collective-permute-done.8.refs_1_ = bf16[128,256]{1,0:T(8,128)(2,1)S(1)} collective-permute-done((bf16[128,256]{1,0:T(8,128)(2,1)S(1)}, bf16[128,256]{1,0:T(8,128)(2,1)S(1)}, u32[]{:S(2)}, u32[]{:S(2)}) %collective-permute-start.8) | collective-permute-done | bytes 65568 | tf_op jit(solution)/shard_map/ppermute | solution.py:39
  35.8 1.0 %collective-permute-done.9.refs_2_ = bf16[128,256]{1,0:T(8,128)(2,1)S(1)} collective-permute-done((bf16[128,256]{1,0:T(8,128)(2,1)S(1)}, bf16[128,256]{1,0:T(8,128)(2,1)S(1)}, u32[]{:S(2)}, u32[]{:S(2)}) %collective-permute-start.9) | collective-permute-done | bytes 65568 | tf_op jit(solution)/shard_map/ppermute | solution.py:39
  36.8 0.7 %shard_map.95 = (f32[64,256]{1,0:T(8,128)}, f32[64,256]{1,0:T(8,128)}) custom-call(f32[128,256]{1,0:T(8,128)S(1)} %get-tuple-element.70.refs_0_, bf16[128,256]{1,0:T(8,128)(2,1)S(1)} %collective-permute-done.8.refs_1_, bf16[128,256]{1,0:T(8,128)(2,1)S(1)} %collective-permute-done.9.refs_2_, bf16[128,256]{1,0:T(8,128)(2,1)S(1)} %collective-permute-done.10.refs_3_), custom_call_target="tpu_custom_call" | custom-call | tf_op jit(solution)/shard_map/pallas_call | solution.py:230
  (4 shorter events, 0.1 us)
Async XLA Ops:
  1.8 6.2 %collective-permute-start = (bf16[48,640]{1,0:T(8,128)(2,1)S(1)}, bf16[48,640]{1,0:T(8,128)(2,1)S(1)}, u32[]{:S(2)}, u32[]{:S(2)}) collective-permute-start(bf16[48,640]{1,0:T(8,128)(2,1)S(1)} %get-tuple-element.39), channel_id=1, source_target_pairs={{0,24},{8,16},{16,8},{24,0},{1,25},{9,17},{17,9},{25,1},{2,26},{10... | collective-permute-start | bytes 184328 | tf_op jit(solution)/shard_map/ppermute | solution.py:39
  5.8 4.2 %collective-permute-start.1 = (bf16[48,640]{1,0:T(8,128)(2,1)S(1)}, bf16[48,640]{1,0:T(8,128)(2,1)S(1)}, u32[]{:S(2)}, u32[]{:S(2)}) collective-permute-start(bf16[48,640]{1,0:T(8,128)(2,1)S(1)} %get-tuple-element.40), channel_id=1, source_target_pairs={{0,16},{8,24},{16,0},{24,8},{1,17},{9,25},{17,1},{25,9},{2,18},{10... | collective-permute-start | bytes 184328 | tf_op jit(solution)/shard_map/ppermute | solution.py:39
  6.3 4.2 %collective-permute-start.2 = (bf16[48,640]{1,0:T(8,128)(2,1)S(1)}, bf16[48,640]{1,0:T(8,128)(2,1)S(1)}, u32[]{:S(2)}, u32[]{:S(2)}) collective-permute-start(bf16[48,640]{1,0:T(8,128)(2,1)S(1)} %get-tuple-element.41), channel_id=1, source_target_pairs={{0,8},{8,0},{16,24},{24,16},{1,9},{9,1},{17,25},{25,17},{2,10},{10... | collective-permute-start | bytes 184328 | tf_op jit(solution)/shard_map/ppermute | solution.py:39
  11.2 5.8 %collective-permute-start.3 = (f16[200,512]{1,0:T(8,128)(2,1)S(1)}, f16[200,512]{1,0:T(8,128)(2,1)S(1)}, u32[]{:S(2)}, u32[]{:S(2)}) collective-permute-start(f16[200,512]{1,0:T(8,128)(2,1)S(1)} %convert_element_type.12), channel_id=1, source_target_pairs={{0,1},{1,0},{2,3},{3,2},{4,5},{5,4},{6,7},{7,6},{8,9},{9,8},{10,11... | collective-permute-start | bytes 614408 | tf_op jit(solution)/shard_map/ppermute | solution.py:39
  17.4 9.7 %collective-permute-start.4 = (f16[200,512]{1,0:T(8,128)(2,1)S(1)}, f16[200,512]{1,0:T(8,128)(2,1)S(1)}, u32[]{:S(2)}, u32[]{:S(2)}) collective-permute-start(f16[200,512]{1,0:T(8,128)(2,1)S(1)} %convert_element_type.14), channel_id=1, source_target_pairs={{0,2},{1,3},{2,0},{3,1},{4,6},{5,7},{6,4},{7,5},{8,10},{9,11},{10,... | collective-permute-start | bytes 614408 | tf_op jit(solution)/shard_map/ppermute | solution.py:39
  20.3 1.5 %collective-permute-start.6 = (bf16[192,512]{1,0:T(8,128)(2,1)S(1)}, bf16[192,512]{1,0:T(8,128)(2,1)S(1)}, u32[]{:S(2)}, u32[]{:S(2)}) collective-permute-start(bf16[192,512]{1,0:T(8,128)(2,1)S(1)} %get-tuple-element.52), channel_id=1, source_target_pairs={{0,4},{4,0},{1,5},{5,1},{2,6},{6,2},{3,7},{7,3},{8,12},{12,8},{9,1... | collective-permute-start | bytes 589832 | tf_op jit(solution)/shard_map/ppermute | solution.py:39
  20.4 6.7 %collective-permute-start.5 = (f32[1,128]{1,0:T(1,128)S(1)}, f32[1,128]{1,0:T(1,128)S(1)}, u32[]{:S(2)}, u32[]{:S(2)}) collective-permute-start(f32[1,128]{1,0:T(1,128)S(1)} %get-tuple-element.60.refs_3_), channel_id=1, source_target_pairs={{0,4},{4,0},{1,5},{5,1},{2,6},{6,2},{3,7},{7,3},{8,12},{12,8},{9,1... | collective-permute-start | bytes 1544 | tf_op jit(solution)/shard_map/ppermute | solution.py:39
  27.3 1.5 %collective-permute-start.7 = (bf16[192,512]{1,0:T(8,128)(2,1)S(1)}, bf16[192,512]{1,0:T(8,128)(2,1)S(1)}, u32[]{:S(2)}, u32[]{:S(2)}) collective-permute-start(bf16[192,512]{1,0:T(8,128)(2,1)S(1)} %shard_map.92.scaled), channel_id=1, source_target_pairs={{0,4},{4,0},{1,5},{5,1},{2,6},{6,2},{3,7},{7,3},{8,12},{12,8},{9,1... | collective-permute-start | bytes 589832 | tf_op jit(solution)/shard_map/ppermute | solution.py:39
  29.3 5.3 %collective-permute-start.10 = (bf16[128,256]{1,0:T(8,128)(2,1)S(1)}, bf16[128,256]{1,0:T(8,128)(2,1)S(1)}, u32[]{:S(2)}, u32[]{:S(2)}) collective-permute-start(bf16[128,256]{1,0:T(8,128)(2,1)S(1)} %get-tuple-element.73), channel_id=1, source_target_pairs={{0,24},{8,16},{16,8},{24,0},{1,25},{9,17},{17,9},{25,1},{2,26},{10... | collective-permute-start | bytes 196616 | tf_op jit(solution)/shard_map/ppermute | solution.py:39
  31.1 4.7 %collective-permute-start.8 = (bf16[128,256]{1,0:T(8,128)(2,1)S(1)}, bf16[128,256]{1,0:T(8,128)(2,1)S(1)}, u32[]{:S(2)}, u32[]{:S(2)}) collective-permute-start(bf16[128,256]{1,0:T(8,128)(2,1)S(1)} %get-tuple-element.71), channel_id=1, source_target_pairs={{0,16},{8,24},{16,0},{24,8},{1,17},{9,25},{17,1},{25,9},{2,18},{10... | collective-permute-start | bytes 196616 | tf_op jit(solution)/shard_map/ppermute | solution.py:39
  32.6 4.3 %collective-permute-start.9 = (bf16[128,256]{1,0:T(8,128)(2,1)S(1)}, bf16[128,256]{1,0:T(8,128)(2,1)S(1)}, u32[]{:S(2)}, u32[]{:S(2)}) collective-permute-start(bf16[128,256]{1,0:T(8,128)(2,1)S(1)} %get-tuple-element.72), channel_id=1, source_target_pairs={{0,8},{8,0},{16,24},{24,16},{1,9},{9,1},{17,25},{25,17},{2,10},{10... | collective-permute-start | bytes 196616 | tf_op jit(solution)/shard_map/ppermute | solution.py:39

commit v12 on v11

--- a/solution.py
+++ b/solution.py
@@ -123,7 +123,8 @@
 def forward_body(owners, local, room, *refs):
     blocks, refs = refs[:owners], refs[owners:]
     teach_in, teach_out, student_up, student_down = refs[:4]
-    rows_out, tags_out, counts_out, error_out, packed, act_out, slope_out = refs[4:]
+    tags_out, counts_out, act_out, slope_out = refs[4:8]
+    halves, rows_halves, (rows_out, error_out) = refs[8:12], refs[12:14], refs[14:]
     width = rows_out.shape[1]
     full = [block[...] for block in blocks]
     counts = None
@@ -148,7 +149,12 @@
         act_out[span] = act
         slope_out[span] = slope
         error_out[span] = dot(act, student_down[...], ((1,), (1,))) - dot(hidden, teach_out[l])
-    pack(error_out[...], packed)
+    height = halves[0].shape[0]
+    for i in range(2):
+        rows_halves[i][...] = rows_out[i * height : (i + 1) * height]
+        value = error_out[i * height : (i + 1) * height]
+        halves[2 * i][...] = value
+        pack(value, halves[2 * i + 1])
 
 
 def chosen_columns(columns, owners, studs):
@@ -166,31 +172,35 @@
     return dot(chosen, value, ((1,), (1,))).astype(jnp.bfloat16)
 
 
-def ahead_body(owners, studs, own, rows, student_up, *refs):
-    if own:
-        _, turned, handed = refs
-        handed[...] = rows[...]
-    else:
-        turned, act, slope = refs
-        act[...], slope[...] = student(rows[...], student_up)
-    turned[...] = turn(rows[...], owners, studs)
-
-
-def pair_body(own, arrived, total, packed):
-    value = own[...] + unpack(arrived)
-    total[...] = value
-    pack(value, packed)
+def ahead_body(owners, studs, first, second, student_up, _, turned, *state):
+    rows = jnp.concatenate([first[...], second[...]])
+    turned[...] = turn(rows, owners, studs)
+    if state:
+        state[0][...], state[1][...] = student(rows, student_up)
+
+
+def pair_body(*refs):
+    for i in range(2):
+        own, arrived = refs[2 * i : 2 * i + 2]
+        total, packed = refs[2 * i + 4 : 2 * i + 6]
+        value = own[...] + unpack(arrived)
+        total[...] = value
+        pack(value, packed)
 
 
 def scale_body(*refs):
-    own, arrived, tags = refs[:3]
-    counts, scaled = refs[3:-1], refs[-1]
+    own, tags = (*refs[2:4], *refs[:2]), refs[4]
+    counts, scaled = refs[5:-1], refs[-1]
     all_counts = counts[0][...]
     for piece in counts[1:]:
         all_counts = all_counts + piece[...]
     inverse = jnp.where(all_counts > 0, 2.0 / all_counts, 0.0)
     weight = jnp.sum(tags[...] * inverse, axis=1, keepdims=True)
-    scaled[...] = ((own[...] + unpack(arrived)) * weight).astype(scaled.dtype)
+    height = own[0].shape[0]
+    for i in range(2):
+        span = slice(i * height, (i + 1) * height)
+        total = own[2 * i][...] + unpack(own[2 * i + 1])
+        scaled[span] = (total * weight[span]).astype(scaled.dtype)
 
 
 def backward_body(owners, studs, earlier, scaled, turned, act, slope, student_down, *refs):
@@ -253,7 +263,8 @@
     def shape(rows, columns, dtype):
         return jax.ShapeDtypeStruct((rows, columns), dtype)
 
-    whole, packed = shape(slots, actions, f32), shape(slots + PACK_ROWS, actions, f32)
+    height = slots // 2
+    half, packed = shape(height, actions, f32), shape(height + PACK_ROWS, actions, f32)
     state = [shape(slots, units, bf16), shape(slots, units, f32)]
     tokens = [ids.reshape(1, row_count) for ids in (task_ids, student_batch)]
     blocks = kernel(
@@ -277,38 +288,36 @@
         [VMEM] + [HBM] * 4,
     )
     blocks = [blocks[0]] + list(arrived.values())
-    rows, tags, counts, error, other, act, slope = kernel(
+    tags, counts, act, slope, first, first_out, second, second_out, *rows = kernel(
         functools.partial(forward_body, owners, local, room),
-        [shape(slots, width, bf16), shape(slots, extra, f32), shape(1, extra, f32), whole, packed]
-        + state,
+        [shape(slots, extra, f32), shape(1, extra, f32), *state]
+        + [half, packed] * 2
+        + [shape(height, width, bf16)] * 2,
         (*blocks, *weights),
         4 * slots * width * (hidden + units),
-    )
-    arrived = cross(other, 1)
-    step = 2
-    while step < parts:
-        error, other = kernel(pair_body, [whole, packed], (error, arrived), 0)
-        arrived = cross(other, step)
-        step *= 2
-    ahead = functools.partial(ahead_body, owners, studs, False)
-    turned = shape(width // studs, slots, bf16)
-    ours, handed = kernel(
-        functools.partial(ahead_body, owners, studs, True),
-        [turned, shape(slots, width, bf16)],
-        (rows, weights[2], error),
-        0,
-    )
-    all_counts, known = [counts], []
+        [pltpu.VMEM((slots, width), bf16), pltpu.VMEM((slots, actions), f32)],
+    )
+    steps = [1 << i for i in range(parts.bit_length() - 1)]
+    first_in, second_in = cross(first_out, steps[0]), cross(second_out, steps[-1])
+    all_counts, mates = [counts], []
     for k in range(1, studs):
         all_counts.append(send(counts, "stud", k))
-        theirs = send(handed, "stud", k)
-        known.append(
-            kernel(ahead, [turned] + state, (theirs, weights[2]), 0)
+        mates.append([send(part, "stud", k) for part in rows])
+    first_in, second_in, all_counts, mates = lax.optimization_barrier(
+        (first_in, second_in, all_counts, mates)
+    )
+    for there, back in zip(steps[1:], steps[-2::-1]):
+        first, first_out, second, second_out = kernel(
+            pair_body, [half, packed] * 2, (first, first_in, second, second_in), 0
         )
-    error, arrived, all_counts, known, ours = lax.optimization_barrier(
-        (error, arrived, all_counts, known, ours)
-    )
-    (scaled,) = kernel(scale_body, [shape(slots, actions, bf16)], (error, arrived, tags, *all_counts), 0)
+        first_in, second_in = cross(first_out, there), cross(second_out, back)
+    ahead = functools.partial(ahead_body, owners, studs)
+    turned = shape(width // studs, slots, bf16)
+    (ours,) = kernel(ahead, [turned], (*rows, weights[2], second), 0)
+    known = [kernel(ahead, [turned] + state, (*theirs, weights[2], second), 0) for theirs in mates]
+    sums = (second, second_in, first, first_in)
+    sums, all_counts, known, ours = lax.optimization_barrier((sums, all_counts, known, ours))
+    (scaled,) = kernel(scale_body, [shape(slots, actions, bf16)], (*sums, tags, *all_counts), 0)
     work = 6 * slots * width * units
     grads = [shape(width // studs, units, f32), shape(actions // studs, units, f32)]
     heights = [g.shape[0] // owners for g in grads]
@@ -323,7 +332,7 @@
             (error, *state, weights[3], *sums),
             work,
         )
-    pieces = [sums[0]] + [send(sums[k], "teach", k) for k in (*range(owners - 2, 0, -1), owners - 1)]
+    pieces = [sums[0]] + [send(sums[k], "teach", k) for k in range(owners - 1, 0, -1)]
     outs = [shape(h, units, f32) for h in heights]
     return kernel(
         closing_body,

time: 37.7 us -> 35.5 us (0.942)
  waiting for transfers between devices: 17.6 us -> 11.9 us
  starting transfers between devices: 13.1 us -> 16.6 us
    ppermute x11 -> x14, waiting for transfers between devices: 17.6 us -> 11.9 us  [send(): lax.ppermute(block, axis, [(i, partner_to(size, i, step)) for i in range(...]
    ppermute x11 -> x14, starting transfers between devices: 13.1 us -> 16.6 us  [send(): lax.ppermute(block, axis, [(i, partner_to(size, i, step)) for i in range(...]
  transfers between devices with their start and end apart: 11 -> 14, of which waited for: 10 -> 10; matrix products, arithmetic and copies ran while one was open for 0% -> 0% of each run, Pallas kernels for 7% -> 7%
where the time goes in v12:
time: 35.5 us; the launch traced here: 35.3 us
  starting transfers between devices  16.6 us (47%)
  waiting for transfers between devices  11.9 us (34%)
  Pallas kernels  5.91 us (17%)
  between operations  0.79 us (2%)
    ppermute x14, starting transfers between devices, send(): lax.ppermute(block, axis, [(i, partner_to(size, i, step)) for i in range(...  16.6 us
    ppermute x14, waiting for transfers between devices, send(): lax.ppermute(block, axis, [(i, partner_to(size, i, step)) for i in range(...  11.9 us
    pallas_call x10, Pallas kernels, kernel(): pl.pallas_call(body, out_shape=outs, in_specs=places or [VMEM] * len(oper...  5.91 us
  transfers between devices with their start and end apart: 14, of which 10 were waited for; matrix products, arithmetic and copies ran while one was open for 0% of the time, Pallas kernels for 7%

profile of v12, /device:TPU:0, one launch (start us, length us, event | category | flops | bytes accessed | tf_op | source)
XLA Modules:
  0.0 35.3 jit_solution(5314457378990933748)
XLA Ops:
  0.6 1.2 %shard_map.86 = (bf16[48,640]{1,0:T(8,128)(2,1)S(1)}, bf16[48,640]{1,0:T(8,128)(2,1)S(1)}, bf16[48,640]{1,0:T(8,128)(2,1)S(1)}, bf16[48,640]{1,0:T(8,128)(2,1)S(1)}) custom-call(bf16[128,512]{1,0:T(8,128)(2,1)} %refs_0_.1, s32[1,128]{1,0:T(1,128)} %bitcast.2, s32[1,128]{1,0:T(1,128)} %bitcast.3), custom_call_target="tpu_custom_call" | custom-call | flops 25165824 | tf_op jit(solution)/shard_map/pallas_call | solution.py:240
  1.8 4.0 %collective-permute-start = (bf16[48,640]{1,0:T(8,128)(2,1)S(1)}, bf16[48,640]{1,0:T(8,128)(2,1)S(1)}, u32[]{:S(2)}, u32[]{:S(2)}) collective-permute-start(bf16[48,640]{1,0:T(8,128)(2,1)S(1)} %get-tuple-element.50), channel_id=1, source_target_pairs={{0,24},{8,16},{16,8},{24,0},{1,25},{9,17},{17,9},{25,1},{2,26},{10... | collective-permute-start | bytes 184328 | tf_op jit(solution)/shard_map/ppermute | solution.py:39
  5.8 0.5 %collective-permute-start.1 = (bf16[48,640]{1,0:T(8,128)(2,1)S(1)}, bf16[48,640]{1,0:T(8,128)(2,1)S(1)}, u32[]{:S(2)}, u32[]{:S(2)}) collective-permute-start(bf16[48,640]{1,0:T(8,128)(2,1)S(1)} %get-tuple-element.51), channel_id=1, source_target_pairs={{0,16},{8,24},{16,0},{24,8},{1,17},{9,25},{17,1},{25,9},{2,18},{10... | collective-permute-start | bytes 184328 | tf_op jit(solution)/shard_map/ppermute | solution.py:39
  6.3 0.1 collective-permute-start.2
  6.4 1.2 %shard_map.87 = (bf16[1,512,256]{2,1,0:T(8,128)(2,1)S(1)}, bf16[1,256,512]{2,1,0:T(8,128)(2,1)S(1)}, bf16[512,256]{1,0:T(8,128)(2,1)S(1)}, bf16[512,256]{1,0:T(8,128)(2,1)S(1)}) custom-call(bf16[48,640]{1,0:T(8,128)(2,1)S(1)} %get-tuple-element.49.refs_0_, bf16[1,512,256]{2,1,0:T(8,128)(2,1)} %refs_1_.1, bf16[1,256,512]{2,1,0:T(8,128)(2,1)} %refs_2_.1, ...), custom_call_target="tpu_custom_call" | custom-call | tf_op jit(solution)/shard_map/pallas_call | solution.py:240
  7.7 0.3 collective-permute-done.refs_1_
  8.0 2.0 %collective-permute-done.1.refs_2_ = bf16[48,640]{1,0:T(8,128)(2,1)S(1)} collective-permute-done((bf16[48,640]{1,0:T(8,128)(2,1)S(1)}, bf16[48,640]{1,0:T(8,128)(2,1)S(1)}, u32[]{:S(2)}, u32[]{:S(2)}) %collective-permute-start.1) | collective-permute-done | bytes 61472 | tf_op jit(solution)/shard_map/ppermute | solution.py:39
  10.0 0.5 %collective-permute-done.2.refs_3_ = bf16[48,640]{1,0:T(8,128)(2,1)S(1)} collective-permute-done((bf16[48,640]{1,0:T(8,128)(2,1)S(1)}, bf16[48,640]{1,0:T(8,128)(2,1)S(1)}, u32[]{:S(2)}, u32[]{:S(2)}) %collective-permute-start.2) | collective-permute-done | bytes 61472 | tf_op jit(solution)/shard_map/ppermute | solution.py:39
  10.5 0.7 %shard_map.88 = (f32[192,128]{1,0:T(8,128)S(1)}, f32[1,128]{1,0:T(1,128)S(1)}, bf16[192,256]{1,0:T(8,128)(2,1)S(1)}, f32[192,256]{1,0:T(8,128)S(1)}, f32[96,512]...) custom-call(bf16[48,640]{1,0:T(8,128)(2,1)S(1)} %get-tuple-element.4, ...), custom_call_target="tpu_custom_call" | custom-call | flops 201326592 | tf_op jit(solution)/shard_map/pallas_call | solution.py:240
  11.2 2.7 %collective-permute-start.4 = (f16[104,512]{1,0:T(8,128)(2,1)S(1)}, f16[104,512]{1,0:T(8,128)(2,1)S(1)}, u32[]{:S(2)}, u32[]{:S(2)}) collective-permute-start(f16[104,512]{1,0:T(8,128)(2,1)S(1)} %convert_element_type.26), channel_id=1, source_target_pairs={{0,2},{1,3},{2,0},{3,1},{4,6},{5,7},{6,4},{7,5},{8,10},{9,11},{10,... | collective-permute-start | bytes 319496 | tf_op jit(solution)/shard_map/ppermute | solution.py:39
  13.9 1.6 %collective-permute-start.3 = (f16[104,512]{1,0:T(8,128)(2,1)S(1)}, f16[104,512]{1,0:T(8,128)(2,1)S(1)}, u32[]{:S(2)}, u32[]{:S(2)}) collective-permute-start(f16[104,512]{1,0:T(8,128)(2,1)S(1)} %convert_element_type.24), channel_id=1, source_target_pairs={{0,1},{1,0},{2,3},{3,2},{4,5},{5,4},{6,7},{7,6},{8,9},{9,8},{10,11... | collective-permute-start | bytes 319496 | tf_op jit(solution)/shard_map/ppermute | solution.py:39
  15.5 0.5 %collective-permute-start.7 = (bf16[96,512]{1,0:T(8,128)(2,1)S(1)}, bf16[96,512]{1,0:T(8,128)(2,1)S(1)}, u32[]{:S(2)}, u32[]{:S(2)}) collective-permute-start(bf16[96,512]{1,0:T(8,128)(2,1)S(1)} %get-tuple-element.62.second), channel_id=1, source_target_pairs={{0,4},{4,0},{1,5},{5,1},{2,6},{6,2},{3,7},{7,3},{8,12},{12,8},{9,1... | collective-permute-start | bytes 294920 | tf_op jit(solution)/shard_map/ppermute | solution.py:39
  16.0 2.1 %collective-permute-done.4 = f16[104,512]{1,0:T(8,128)(2,1)S(1)} collective-permute-done((f16[104,512]{1,0:T(8,128)(2,1)S(1)}, f16[104,512]{1,0:T(8,128)(2,1)S(1)}, u32[]{:S(2)}, u32[]{:S(2)}) %collective-permute-start.4) | collective-permute-done | bytes 106528 | tf_op jit(solution)/shard_map/ppermute | solution.py:39
  18.1 0.5 %collective-permute-done.3 = f16[104,512]{1,0:T(8,128)(2,1)S(1)} collective-permute-done((f16[104,512]{1,0:T(8,128)(2,1)S(1)}, f16[104,512]{1,0:T(8,128)(2,1)S(1)}, u32[]{:S(2)}, u32[]{:S(2)}) %collective-permute-start.3) | collective-permute-done | bytes 106528 | tf_op jit(solution)/shard_map/ppermute | solution.py:39
  18.7 0.2 shard_map.89
  19.0 1.0 %collective-permute-start.9 = (f16[104,512]{1,0:T(8,128)(2,1)S(1)}, f16[104,512]{1,0:T(8,128)(2,1)S(1)}, u32[]{:S(2)}, u32[]{:S(2)}) collective-permute-start(f16[104,512]{1,0:T(8,128)(2,1)S(1)} %convert_element_type.30), channel_id=1, source_target_pairs={{0,2},{1,3},{2,0},{3,1},{4,6},{5,7},{6,4},{7,5},{8,10},{9,11},{10,... | collective-permute-start | bytes 319496 | tf_op jit(solution)/shard_map/ppermute | solution.py:39
  20.1 2.6 %collective-permute-start.8 = (f16[104,512]{1,0:T(8,128)(2,1)S(1)}, f16[104,512]{1,0:T(8,128)(2,1)S(1)}, u32[]{:S(2)}, u32[]{:S(2)}) collective-permute-start(f16[104,512]{1,0:T(8,128)(2,1)S(1)} %convert_element_type.28), channel_id=1, source_target_pairs={{0,1},{1,0},{2,3},{3,2},{4,5},{5,4},{6,7},{7,6},{8,9},{9,8},{10,11... | collective-permute-start | bytes 319496 | tf_op jit(solution)/shard_map/ppermute | solution.py:39
  22.6 0.2 shard_map.91.turned
  22.9 0.3 shard_map.90
  23.2 2.6 %collective-permute-done.9 = f16[104,512]{1,0:T(8,128)(2,1)S(1)} collective-permute-done((f16[104,512]{1,0:T(8,128)(2,1)S(1)}, f16[104,512]{1,0:T(8,128)(2,1)S(1)}, u32[]{:S(2)}, u32[]{:S(2)}) %collective-permute-start.9) | collective-permute-done | bytes 106528 | tf_op jit(solution)/shard_map/ppermute | solution.py:39
  25.9 0.2 shard_map.92.scaled
  26.1 0.1 collective-permute-start.10
  26.2 0.7 %shard_map.93 = (f32[256,256]{1,0:T(8,128)S(1)}, f32[256,256]{1,0:T(8,128)S(1)}) custom-call(bf16[192,512]{1,0:T(8,128)(2,1)S(1)} %shard_map.92.scaled, bf16[256,192]{1,0:T(8,128)(2,1)S(1)} %shard_map.91.turned, bf16[192,256]{1,0:T(8,128)(2,1)S(1)} %get-tuple-element.88.act, f32[192,256]{1,0:T(8,128)S(1)} %get-tuple-element.89.slope, ...), custom_call_target="tpu_custom_call" | custom-call | flops 150994944 | tf_op jit(solution)/shard_map/pallas_call | solution.py:240
  26.8 0.7 %collective-permute-done.10.scaled = bf16[192,512]{1,0:T(8,128)(2,1)S(1)} collective-permute-done((bf16[192,512]{1,0:T(8,128)(2,1)S(1)}, bf16[192,512]{1,0:T(8,128)(2,1)S(1)}, u32[]{:S(2)}, u32[]{:S(2)}) %collective-permute-start.10) | collective-permute-done | bytes 196640 | tf_op jit(solution)/shard_map/ppermute | solution.py:39
  27.6 0.5 %shard_map.94 = (f32[128,256]{1,0:T(8,128)S(1)}, bf16[128,256]{1,0:T(8,128)(2,1)S(1)}, bf16[128,256]{1,0:T(8,128)(2,1)S(1)}, bf16[128,256]{1,0:T(8,128)(2,1)S(1)}) custom-call(bf16[192,512]{1,0:T(8,128)(2,1)S(1)} %collective-permute-done.10.scaled, bf16[256,192]{1,0:T(8,128)(2,1)S(1)} %get-tuple-element.84.turned, ...), custom_call_target="tpu_custom_call" | custom-call | flops 150994944 | tf_op jit(solution)/shard_map/pallas_call | solution.py:240
  28.1 1.6 %collective-permute-start.11 = (bf16[128,256]{1,0:T(8,128)(2,1)S(1)}, bf16[128,256]{1,0:T(8,128)(2,1)S(1)}, u32[]{:S(2)}, u32[]{:S(2)}) collective-permute-start(bf16[128,256]{1,0:T(8,128)(2,1)S(1)} %get-tuple-element.93), channel_id=1, source_target_pairs={{0,24},{8,16},{16,8},{24,0},{1,25},{9,17},{17,9},{25,1},{2,26},{10... | collective-permute-start | bytes 196616 | tf_op jit(solution)/shard_map/ppermute | solution.py:39
  29.6 0.7 %collective-permute-start.12 = (bf16[128,256]{1,0:T(8,128)(2,1)S(1)}, bf16[128,256]{1,0:T(8,128)(2,1)S(1)}, u32[]{:S(2)}, u32[]{:S(2)}) collective-permute-start(bf16[128,256]{1,0:T(8,128)(2,1)S(1)} %get-tuple-element.94), channel_id=1, source_target_pairs={{0,16},{8,24},{16,0},{24,8},{1,17},{9,25},{17,1},{25,9},{2,18},{10... | collective-permute-start | bytes 196616 | tf_op jit(solution)/shard_map/ppermute | solution.py:39
  30.4 1.3 %collective-permute-start.13 = (bf16[128,256]{1,0:T(8,128)(2,1)S(1)}, bf16[128,256]{1,0:T(8,128)(2,1)S(1)}, u32[]{:S(2)}, u32[]{:S(2)}) collective-permute-start(bf16[128,256]{1,0:T(8,128)(2,1)S(1)} %get-tuple-element.95), channel_id=1, source_target_pairs={{0,8},{8,0},{16,24},{24,16},{1,9},{9,1},{17,25},{25,17},{2,10},{10... | collective-permute-start | bytes 196616 | tf_op jit(solution)/shard_map/ppermute | solution.py:39
  31.6 1.8 %collective-permute-done.11.refs_1_ = bf16[128,256]{1,0:T(8,128)(2,1)S(1)} collective-permute-done((bf16[128,256]{1,0:T(8,128)(2,1)S(1)}, bf16[128,256]{1,0:T(8,128)(2,1)S(1)}, u32[]{:S(2)}, u32[]{:S(2)}) %collective-permute-start.11) | collective-permute-done | bytes 65568 | tf_op jit(solution)/shard_map/ppermute | solution.py:39
  33.4 1.2 %collective-permute-done.12.refs_2_ = bf16[128,256]{1,0:T(8,128)(2,1)S(1)} collective-permute-done((bf16[128,256]{1,0:T(8,128)(2,1)S(1)}, bf16[128,256]{1,0:T(8,128)(2,1)S(1)}, u32[]{:S(2)}, u32[]{:S(2)}) %collective-permute-start.12) | collective-permute-done | bytes 65568 | tf_op jit(solution)/shard_map/ppermute | solution.py:39
  34.6 0.1 collective-permute-done.13.refs_3_
  34.6 0.7 %shard_map.95 = (f32[64,256]{1,0:T(8,128)}, f32[64,256]{1,0:T(8,128)}) custom-call(f32[128,256]{1,0:T(8,128)S(1)} %get-tuple-element.92.refs_0_, bf16[128,256]{1,0:T(8,128)(2,1)S(1)} %collective-permute-done.11.refs_1_, bf16[128,256]{1,0:T(8,128)(2,1)S(1)} %collective-permute-done.12.refs_2_, bf16[128,256]{1,0:T(8,128)(2,1)S(1)} %collective-permute-done.13.refs_3_), custom_call_target="tpu_custom_call" | custom-call | tf_op jit(solution)/shard_map/pallas_call | solution.py:240
  (14 shorter events, 0.1 us)
Async XLA Ops:
  1.8 6.2 %collective-permute-start = (bf16[48,640]{1,0:T(8,128)(2,1)S(1)}, bf16[48,640]{1,0:T(8,128)(2,1)S(1)}, u32[]{:S(2)}, u32[]{:S(2)}) collective-permute-start(bf16[48,640]{1,0:T(8,128)(2,1)S(1)} %get-tuple-element.50), channel_id=1, source_target_pairs={{0,24},{8,16},{16,8},{24,0},{1,25},{9,17},{17,9},{25,1},{2,26},{10... | collective-permute-start | bytes 184328 | tf_op jit(solution)/shard_map/ppermute | solution.py:39
  5.8 4.2 %collective-permute-start.1 = (bf16[48,640]{1,0:T(8,128)(2,1)S(1)}, bf16[48,640]{1,0:T(8,128)(2,1)S(1)}, u32[]{:S(2)}, u32[]{:S(2)}) collective-permute-start(bf16[48,640]{1,0:T(8,128)(2,1)S(1)} %get-tuple-element.51), channel_id=1, source_target_pairs={{0,16},{8,24},{16,0},{24,8},{1,17},{9,25},{17,1},{25,9},{2,18},{10... | collective-permute-start | bytes 184328 | tf_op jit(solution)/shard_map/ppermute | solution.py:39
  6.3 4.2 %collective-permute-start.2 = (bf16[48,640]{1,0:T(8,128)(2,1)S(1)}, bf16[48,640]{1,0:T(8,128)(2,1)S(1)}, u32[]{:S(2)}, u32[]{:S(2)}) collective-permute-start(bf16[48,640]{1,0:T(8,128)(2,1)S(1)} %get-tuple-element.52), channel_id=1, source_target_pairs={{0,8},{8,0},{16,24},{24,16},{1,9},{9,1},{17,25},{25,17},{2,10},{10... | collective-permute-start | bytes 184328 | tf_op jit(solution)/shard_map/ppermute | solution.py:39
  11.2 6.9 %collective-permute-start.4 = (f16[104,512]{1,0:T(8,128)(2,1)S(1)}, f16[104,512]{1,0:T(8,128)(2,1)S(1)}, u32[]{:S(2)}, u32[]{:S(2)}) collective-permute-start(f16[104,512]{1,0:T(8,128)(2,1)S(1)} %convert_element_type.26), channel_id=1, source_target_pairs={{0,2},{1,3},{2,0},{3,1},{4,6},{5,7},{6,4},{7,5},{8,10},{9,11},{10,... | collective-permute-start | bytes 319496 | tf_op jit(solution)/shard_map/ppermute | solution.py:39
  13.9 4.8 %collective-permute-start.3 = (f16[104,512]{1,0:T(8,128)(2,1)S(1)}, f16[104,512]{1,0:T(8,128)(2,1)S(1)}, u32[]{:S(2)}, u32[]{:S(2)}) collective-permute-start(f16[104,512]{1,0:T(8,128)(2,1)S(1)} %convert_element_type.24), channel_id=1, source_target_pairs={{0,1},{1,0},{2,3},{3,2},{4,5},{5,4},{6,7},{7,6},{8,9},{9,8},{10,11... | collective-permute-start | bytes 319496 | tf_op jit(solution)/shard_map/ppermute | solution.py:39
  15.5 3.2 %collective-permute-start.6 = (bf16[96,512]{1,0:T(8,128)(2,1)S(1)}, bf16[96,512]{1,0:T(8,128)(2,1)S(1)}, u32[]{:S(2)}, u32[]{:S(2)}) collective-permute-start(bf16[96,512]{1,0:T(8,128)(2,1)S(1)} %get-tuple-element.61.first), channel_id=1, source_target_pairs={{0,4},{4,0},{1,5},{5,1},{2,6},{6,2},{3,7},{7,3},{8,12},{12,8},{9,1... | collective-permute-start | bytes 294920 | tf_op jit(solution)/shard_map/ppermute | solution.py:39
  15.5 3.2 %collective-permute-start.7 = (bf16[96,512]{1,0:T(8,128)(2,1)S(1)}, bf16[96,512]{1,0:T(8,128)(2,1)S(1)}, u32[]{:S(2)}, u32[]{:S(2)}) collective-permute-start(bf16[96,512]{1,0:T(8,128)(2,1)S(1)} %get-tuple-element.62.second), channel_id=1, source_target_pairs={{0,4},{4,0},{1,5},{5,1},{2,6},{6,2},{3,7},{7,3},{8,12},{12,8},{9,1... | collective-permute-start | bytes 294920 | tf_op jit(solution)/shard_map/ppermute | solution.py:39
  16.0 2.7 %collective-permute-start.5 = (f32[1,128]{1,0:T(1,128)S(1)}, f32[1,128]{1,0:T(1,128)S(1)}, u32[]{:S(2)}, u32[]{:S(2)}) collective-permute-start(f32[1,128]{1,0:T(1,128)S(1)} %get-tuple-element.82.refs_5_), channel_id=1, source_target_pairs={{0,4},{4,0},{1,5},{5,1},{2,6},{6,2},{3,7},{7,3},{8,12},{12,8},{9,1... | collective-permute-start | bytes 1544 | tf_op jit(solution)/shard_map/ppermute | solution.py:39
  19.0 6.8 %collective-permute-start.9 = (f16[104,512]{1,0:T(8,128)(2,1)S(1)}, f16[104,512]{1,0:T(8,128)(2,1)S(1)}, u32[]{:S(2)}, u32[]{:S(2)}) collective-permute-start(f16[104,512]{1,0:T(8,128)(2,1)S(1)} %convert_element_type.30), channel_id=1, source_target_pairs={{0,2},{1,3},{2,0},{3,1},{4,6},{5,7},{6,4},{7,5},{8,10},{9,11},{10,... | collective-permute-start | bytes 319496 | tf_op jit(solution)/shard_map/ppermute | solution.py:39
  20.1 5.8 %collective-permute-start.8 = (f16[104,512]{1,0:T(8,128)(2,1)S(1)}, f16[104,512]{1,0:T(8,128)(2,1)S(1)}, u32[]{:S(2)}, u32[]{:S(2)}) collective-permute-start(f16[104,512]{1,0:T(8,128)(2,1)S(1)} %convert_element_type.28), channel_id=1, source_target_pairs={{0,1},{1,0},{2,3},{3,2},{4,5},{5,4},{6,7},{7,6},{8,9},{9,8},{10,11... | collective-permute-start | bytes 319496 | tf_op jit(solution)/shard_map/ppermute | solution.py:39
  26.1 1.5 %collective-permute-start.10 = (bf16[192,512]{1,0:T(8,128)(2,1)S(1)}, bf16[192,512]{1,0:T(8,128)(2,1)S(1)}, u32[]{:S(2)}, u32[]{:S(2)}) collective-permute-start(bf16[192,512]{1,0:T(8,128)(2,1)S(1)} %shard_map.92.scaled), channel_id=1, source_target_pairs={{0,4},{4,0},{1,5},{5,1},{2,6},{6,2},{3,7},{7,3},{8,12},{12,8},{9,1... | collective-permute-start | bytes 589832 | tf_op jit(solution)/shard_map/ppermute | solution.py:39
  28.1 5.3 %collective-permute-start.11 = (bf16[128,256]{1,0:T(8,128)(2,1)S(1)}, bf16[128,256]{1,0:T(8,128)(2,1)S(1)}, u32[]{:S(2)}, u32[]{:S(2)}) collective-permute-start(bf16[128,256]{1,0:T(8,128)(2,1)S(1)} %get-tuple-element.93), channel_id=1, source_target_pairs={{0,24},{8,16},{16,8},{24,0},{1,25},{9,17},{17,9},{25,1},{2,26},{10... | collective-permute-start | bytes 196616 | tf_op jit(solution)/shard_map/ppermute | solution.py:39
  29.6 4.9 %collective-permute-start.12 = (bf16[128,256]{1,0:T(8,128)(2,1)S(1)}, bf16[128,256]{1,0:T(8,128)(2,1)S(1)}, u32[]{:S(2)}, u32[]{:S(2)}) collective-permute-start(bf16[128,256]{1,0:T(8,128)(2,1)S(1)} %get-tuple-element.94), channel_id=1, source_target_pairs={{0,16},{8,24},{16,0},{24,8},{1,17},{9,25},{17,1},{25,9},{2,18},{10... | collective-permute-start | bytes 196616 | tf_op jit(solution)/shard_map/ppermute | solution.py:39
  30.4 4.3 %collective-permute-start.13 = (bf16[128,256]{1,0:T(8,128)(2,1)S(1)}, bf16[128,256]{1,0:T(8,128)(2,1)S(1)}, u32[]{:S(2)}, u32[]{:S(2)}) collective-permute-start(bf16[128,256]{1,0:T(8,128)(2,1)S(1)} %get-tuple-element.95), channel_id=1, source_target_pairs={{0,8},{8,0},{16,24},{24,16},{1,9},{9,1},{17,25},{25,17},{2,10},{10... | collective-permute-start | bytes 196616 | tf_op jit(solution)/shard_map/ppermute | solution.py:39

commit v13 on v12

--- a/solution.py
+++ b/solution.py
@@ -149,10 +149,10 @@
         act_out[span] = act
         slope_out[span] = slope
         error_out[span] = dot(act, student_down[...], ((1,), (1,))) - dot(hidden, teach_out[l])
-    height = halves[0].shape[0]
-    for i in range(2):
-        rows_halves[i][...] = rows_out[i * height : (i + 1) * height]
-        value = error_out[i * height : (i + 1) * height]
+    cut = halves[0].shape[0]
+    for i, span in enumerate((slice(0, cut), slice(cut, None))):
+        rows_halves[i][...] = rows_out[span]
+        value = error_out[span]
         halves[2 * i][...] = value
         pack(value, halves[2 * i + 1])
 
@@ -179,13 +179,11 @@
         state[0][...], state[1][...] = student(rows, student_up)
 
 
-def pair_body(*refs):
-    for i in range(2):
-        own, arrived = refs[2 * i : 2 * i + 2]
-        total, packed = refs[2 * i + 4 : 2 * i + 6]
-        value = own[...] + unpack(arrived)
-        total[...] = value
-        pack(value, packed)
+def pair_body(own, arrived, *refs):
+    total, packed = refs[-2:]
+    value = own[...] + unpack(arrived)
+    total[...] = value
+    pack(value, packed)
 
 
 def scale_body(*refs):
@@ -196,9 +194,8 @@
         all_counts = all_counts + piece[...]
     inverse = jnp.where(all_counts > 0, 2.0 / all_counts, 0.0)
     weight = jnp.sum(tags[...] * inverse, axis=1, keepdims=True)
-    height = own[0].shape[0]
-    for i in range(2):
-        span = slice(i * height, (i + 1) * height)
+    cut = own[0].shape[0]
+    for i, span in enumerate((slice(0, cut), slice(cut, None))):
         total = own[2 * i][...] + unpack(own[2 * i + 1])
         scaled[span] = (total * weight[span]).astype(scaled.dtype)
 
@@ -263,8 +260,8 @@
     def shape(rows, columns, dtype):
         return jax.ShapeDtypeStruct((rows, columns), dtype)
 
-    height = slots // 2
-    half, packed = shape(height, actions, f32), shape(height + PACK_ROWS, actions, f32)
+    heights = (slots // 2 + ROW_TILE, slots // 2 - ROW_TILE)
+    part = [[shape(h, actions, f32), shape(h + PACK_ROWS, actions, f32)] for h in heights]
     state = [shape(slots, units, bf16), shape(slots, units, f32)]
     tokens = [ids.reshape(1, row_count) for ids in (task_ids, student_batch)]
     blocks = kernel(
@@ -291,8 +288,9 @@
     tags, counts, act, slope, first, first_out, second, second_out, *rows = kernel(
         functools.partial(forward_body, owners, local, room),
         [shape(slots, extra, f32), shape(1, extra, f32), *state]
-        + [half, packed] * 2
-        + [shape(height, width, bf16)] * 2,
+        + part[0]
+        + part[1]
+        + [shape(h, width, bf16) for h in heights],
         (*blocks, *weights),
         4 * slots * width * (hidden + units),
         [pltpu.VMEM((slots, width), bf16), pltpu.VMEM((slots, actions), f32)],
@@ -303,14 +301,11 @@
     for k in range(1, studs):
         all_counts.append(send(counts, "stud", k))
         mates.append([send(part, "stud", k) for part in rows])
-    first_in, second_in, all_counts, mates = lax.optimization_barrier(
-        (first_in, second_in, all_counts, mates)
-    )
     for there, back in zip(steps[1:], steps[-2::-1]):
-        first, first_out, second, second_out = kernel(
-            pair_body, [half, packed] * 2, (first, first_in, second, second_in), 0
-        )
-        first_in, second_in = cross(first_out, there), cross(second_out, back)
+        first, first_out = kernel(pair_body, part[0], (first, first_in), 0)
+        first_in = cross(first_out, there)
+        second, second_out = kernel(pair_body, part[1], (second, second_in, first), 0)
+        second_in = cross(second_out, back)
     ahead = functools.partial(ahead_body, owners, studs)
     turned = shape(width // studs, slots, bf16)
     (ours,) = kernel(ahead, [turned], (*rows, weights[2], second), 0)

time: 35.5 us -> 36.1 us (1.017)
  waiting for transfers between devices: 11.9 us -> 13.9 us
  starting transfers between devices: 16.6 us -> 15.1 us
    ppermute x14, waiting for transfers between devices: 11.9 us -> 13.9 us  [send(): lax.ppermute(block, axis, [(i, partner_to(size, i, step)) for i in range(...]
    ppermute x14, starting transfers between devices: 16.6 us -> 15.1 us  [send(): lax.ppermute(block, axis, [(i, partner_to(size, i, step)) for i in range(...]
    pallas_call x10 -> x11, Pallas kernels: 5.91 us -> 6.1 us  [kernel(): pl.pallas_call(body, out_shape=outs, in_specs=places or [VMEM] * len(oper...]
  transfers between devices with their start and end apart: 14 -> 14, of which waited for: 10 -> 11; matrix products, arithmetic and copies ran while one was open for 0% -> 0% of each run, Pallas kernels for 7% -> 8%
where the time goes in v13:
time: 36.1 us; the launch traced here: 36 us
  starting transfers between devices  15.1 us (42%)
  waiting for transfers between devices  13.9 us (39%)
  Pallas kernels  6.1 us (17%)
  between operations  0.8 us (2%)
    ppermute x14, starting transfers between devices, send(): lax.ppermute(block, axis, [(i, partner_to(size, i, step)) for i in range(...  15.1 us
    ppermute x14, waiting for transfers between devices, send(): lax.ppermute(block, axis, [(i, partner_to(size, i, step)) for i in range(...  13.9 us
    pallas_call x11, Pallas kernels, kernel(): pl.pallas_call(body, out_shape=outs, in_specs=places or [VMEM] * len(oper...  6.1 us
  transfers between devices with their start and end apart: 14, of which 11 were waited for; matrix products, arithmetic and copies ran while one was open for 0% of the time, Pallas kernels for 8%

profile of v13, /device:TPU:0, one launch (start us, length us, event | category | flops | bytes accessed | tf_op | source)
XLA Modules:
  0.0 36.0 jit_solution(14220308429709438842)
XLA Ops:
  0.6 1.2 %shard_map.86 = (bf16[48,640]{1,0:T(8,128)(2,1)S(1)}, bf16[48,640]{1,0:T(8,128)(2,1)S(1)}, bf16[48,640]{1,0:T(8,128)(2,1)S(1)}, bf16[48,640]{1,0:T(8,128)(2,1)S(1)}) custom-call(bf16[128,512]{1,0:T(8,128)(2,1)} %refs_0_.1, s32[1,128]{1,0:T(1,128)} %bitcast.2, s32[1,128]{1,0:T(1,128)} %bitcast.3), custom_call_target="tpu_custom_call" | custom-call | flops 25165824 | tf_op jit(solution)/shard_map/pallas_call | solution.py:237
  1.8 4.0 %collective-permute-start = (bf16[48,640]{1,0:T(8,128)(2,1)S(1)}, bf16[48,640]{1,0:T(8,128)(2,1)S(1)}, u32[]{:S(2)}, u32[]{:S(2)}) collective-permute-start(bf16[48,640]{1,0:T(8,128)(2,1)S(1)} %get-tuple-element.44), channel_id=1, source_target_pairs={{0,24},{8,16},{16,8},{24,0},{1,25},{9,17},{17,9},{25,1},{2,26},{10... | collective-permute-start | bytes 184328 | tf_op jit(solution)/shard_map/ppermute | solution.py:39
  5.8 0.5 %collective-permute-start.1 = (bf16[48,640]{1,0:T(8,128)(2,1)S(1)}, bf16[48,640]{1,0:T(8,128)(2,1)S(1)}, u32[]{:S(2)}, u32[]{:S(2)}) collective-permute-start(bf16[48,640]{1,0:T(8,128)(2,1)S(1)} %get-tuple-element.45), channel_id=1, source_target_pairs={{0,16},{8,24},{16,0},{24,8},{1,17},{9,25},{17,1},{25,9},{2,18},{10... | collective-permute-start | bytes 184328 | tf_op jit(solution)/shard_map/ppermute | solution.py:39
  6.3 0.1 collective-permute-start.2
  6.4 1.2 %shard_map.87 = (bf16[1,512,256]{2,1,0:T(8,128)(2,1)S(1)}, bf16[1,256,512]{2,1,0:T(8,128)(2,1)S(1)}, bf16[512,256]{1,0:T(8,128)(2,1)S(1)}, bf16[512,256]{1,0:T(8,128)(2,1)S(1)}) custom-call(bf16[48,640]{1,0:T(8,128)(2,1)S(1)} %get-tuple-element.43.refs_0_, bf16[1,512,256]{2,1,0:T(8,128)(2,1)} %refs_1_.1, bf16[1,256,512]{2,1,0:T(8,128)(2,1)} %refs_2_.1, ...), custom_call_target="tpu_custom_call" | custom-call | tf_op jit(solution)/shard_map/pallas_call | solution.py:237
  7.7 0.3 collective-permute-done.refs_1_
  8.0 2.0 %collective-permute-done.1.refs_2_ = bf16[48,640]{1,0:T(8,128)(2,1)S(1)} collective-permute-done((bf16[48,640]{1,0:T(8,128)(2,1)S(1)}, bf16[48,640]{1,0:T(8,128)(2,1)S(1)}, u32[]{:S(2)}, u32[]{:S(2)}) %collective-permute-start.1) | collective-permute-done | bytes 61472 | tf_op jit(solution)/shard_map/ppermute | solution.py:39
  10.0 0.5 %collective-permute-done.2.refs_3_ = bf16[48,640]{1,0:T(8,128)(2,1)S(1)} collective-permute-done((bf16[48,640]{1,0:T(8,128)(2,1)S(1)}, bf16[48,640]{1,0:T(8,128)(2,1)S(1)}, u32[]{:S(2)}, u32[]{:S(2)}) %collective-permute-start.2) | collective-permute-done | bytes 61472 | tf_op jit(solution)/shard_map/ppermute | solution.py:39
  10.5 0.7 %shard_map.88 = (f32[192,128]{1,0:T(8,128)S(1)}, f32[1,128]{1,0:T(1,128)S(1)}, bf16[192,256]{1,0:T(8,128)(2,1)S(1)}, f32[192,256]{1,0:T(8,128)S(1)}, f32[112,512...) custom-call(bf16[48,640]{1,0:T(8,128)(2,1)S(1)} %get-tuple-element.4, ...), custom_call_target="tpu_custom_call" | custom-call | flops 201326592 | tf_op jit(solution)/shard_map/pallas_call | solution.py:237
  11.2 1.6 %collective-permute-start.4 = (f16[120,512]{1,0:T(8,128)(2,1)S(1)}, f16[120,512]{1,0:T(8,128)(2,1)S(1)}, u32[]{:S(2)}, u32[]{:S(2)}) collective-permute-start(f16[120,512]{1,0:T(8,128)(2,1)S(1)} %convert_element_type.26), channel_id=1, source_target_pairs={{0,1},{1,0},{2,3},{3,2},{4,5},{5,4},{6,7},{7,6},{8,9},{9,8},{10,11... | collective-permute-start | bytes 368648 | tf_op jit(solution)/shard_map/ppermute | solution.py:39
  12.9 2.7 %collective-permute-start.3 = (f16[88,512]{1,0:T(8,128)(2,1)S(1)}, f16[88,512]{1,0:T(8,128)(2,1)S(1)}, u32[]{:S(2)}, u32[]{:S(2)}) collective-permute-start(f16[88,512]{1,0:T(8,128)(2,1)S(1)} %convert_element_type.24), channel_id=1, source_target_pairs={{0,2},{1,3},{2,0},{3,1},{4,6},{5,7},{6,4},{7,5},{8,10},{9,11},{10,... | collective-permute-start | bytes 270344 | tf_op jit(solution)/shard_map/ppermute | solution.py:39
  15.5 1.4 %collective-permute-done.4 = f16[120,512]{1,0:T(8,128)(2,1)S(1)} collective-permute-done((f16[120,512]{1,0:T(8,128)(2,1)S(1)}, f16[120,512]{1,0:T(8,128)(2,1)S(1)}, u32[]{:S(2)}, u32[]{:S(2)}) %collective-permute-start.4) | collective-permute-done | bytes 122912 | tf_op jit(solution)/shard_map/ppermute | solution.py:39
  16.9 0.2 shard_map.89
  17.2 1.9 %collective-permute-start.6 = (f16[120,512]{1,0:T(8,128)(2,1)S(1)}, f16[120,512]{1,0:T(8,128)(2,1)S(1)}, u32[]{:S(2)}, u32[]{:S(2)}) collective-permute-start(f16[120,512]{1,0:T(8,128)(2,1)S(1)} %convert_element_type.30), channel_id=1, source_target_pairs={{0,2},{1,3},{2,0},{3,1},{4,6},{5,7},{6,4},{7,5},{8,10},{9,11},{10,... | collective-permute-start | bytes 368648 | tf_op jit(solution)/shard_map/ppermute | solution.py:39
  19.1 2.5 %collective-permute-done.3 = f16[88,512]{1,0:T(8,128)(2,1)S(1)} collective-permute-done((f16[88,512]{1,0:T(8,128)(2,1)S(1)}, f16[88,512]{1,0:T(8,128)(2,1)S(1)}, u32[]{:S(2)}, u32[]{:S(2)}) %collective-permute-start.3) | collective-permute-done | bytes 90144 | tf_op jit(solution)/shard_map/ppermute | solution.py:39
  21.6 0.2 shard_map.90
  21.9 0.1 collective-permute-start.5
  22.0 0.5 %collective-permute-start.7 = (f32[1,128]{1,0:T(1,128)S(1)}, f32[1,128]{1,0:T(1,128)S(1)}, u32[]{:S(2)}, u32[]{:S(2)}) collective-permute-start(f32[1,128]{1,0:T(1,128)S(1)} %get-tuple-element.70.refs_5_), channel_id=1, source_target_pairs={{0,4},{4,0},{1,5},{5,1},{2,6},{6,2},{3,7},{7,3},{8,12},{12,8},{9,1... | collective-permute-start | bytes 1544 | tf_op jit(solution)/shard_map/ppermute | solution.py:39
  22.5 0.2 shard_map.92.turned
  22.8 0.5 %collective-permute-done.9.second = bf16[80,512]{1,0:T(8,128)(2,1)S(1)} collective-permute-done((bf16[80,512]{1,0:T(8,128)(2,1)S(1)}, bf16[80,512]{1,0:T(8,128)(2,1)S(1)}, u32[]{:S(2)}, u32[]{:S(2)}) %collective-permute-start.9) | collective-permute-done | bytes 81952 | tf_op jit(solution)/shard_map/ppermute | solution.py:39
  23.3 0.3 shard_map.91
  23.6 2.8 %collective-permute-done.5 = f16[88,512]{1,0:T(8,128)(2,1)S(1)} collective-permute-done((f16[88,512]{1,0:T(8,128)(2,1)S(1)}, f16[88,512]{1,0:T(8,128)(2,1)S(1)}, u32[]{:S(2)}, u32[]{:S(2)}) %collective-permute-start.5) | collective-permute-done | bytes 90144 | tf_op jit(solution)/shard_map/ppermute | solution.py:39
  26.5 0.2 shard_map.93.scaled
  26.8 0.7 %shard_map.94 = (f32[256,256]{1,0:T(8,128)S(1)}, f32[256,256]{1,0:T(8,128)S(1)}) custom-call(bf16[192,512]{1,0:T(8,128)(2,1)S(1)} %shard_map.93.scaled, bf16[256,192]{1,0:T(8,128)(2,1)S(1)} %shard_map.92.turned, bf16[192,256]{1,0:T(8,128)(2,1)S(1)} %get-tuple-element.76.act, f32[192,256]{1,0:T(8,128)S(1)} %get-tuple-element.77.slope, ...), custom_call_target="tpu_custom_call" | custom-call | flops 150994944 | tf_op jit(solution)/shard_map/pallas_call | solution.py:237
  27.5 0.7 %collective-permute-done.10.scaled = bf16[192,512]{1,0:T(8,128)(2,1)S(1)} collective-permute-done((bf16[192,512]{1,0:T(8,128)(2,1)S(1)}, bf16[192,512]{1,0:T(8,128)(2,1)S(1)}, u32[]{:S(2)}, u32[]{:S(2)}) %collective-permute-start.10) | collective-permute-done | bytes 196640 | tf_op jit(solution)/shard_map/ppermute | solution.py:39
  28.2 0.5 %shard_map.95 = (f32[128,256]{1,0:T(8,128)S(1)}, bf16[128,256]{1,0:T(8,128)(2,1)S(1)}, bf16[128,256]{1,0:T(8,128)(2,1)S(1)}, bf16[128,256]{1,0:T(8,128)(2,1)S(1)}) custom-call(bf16[192,512]{1,0:T(8,128)(2,1)S(1)} %collective-permute-done.10.scaled, bf16[256,192]{1,0:T(8,128)(2,1)S(1)} %get-tuple-element.72.turned, ...), custom_call_target="tpu_custom_call" | custom-call | flops 150994944 | tf_op jit(solution)/shard_map/pallas_call | solution.py:237
  28.7 1.4 %collective-permute-start.11 = (bf16[128,256]{1,0:T(8,128)(2,1)S(1)}, bf16[128,256]{1,0:T(8,128)(2,1)S(1)}, u32[]{:S(2)}, u32[]{:S(2)}) collective-permute-start(bf16[128,256]{1,0:T(8,128)(2,1)S(1)} %get-tuple-element.81), channel_id=1, source_target_pairs={{0,24},{8,16},{16,8},{24,0},{1,25},{9,17},{17,9},{25,1},{2,26},{10... | collective-permute-start | bytes 196616 | tf_op jit(solution)/shard_map/ppermute | solution.py:39
  30.1 0.3 collective-permute-start.12
  30.4 1.9 %collective-permute-start.13 = (bf16[128,256]{1,0:T(8,128)(2,1)S(1)}, bf16[128,256]{1,0:T(8,128)(2,1)S(1)}, u32[]{:S(2)}, u32[]{:S(2)}) collective-permute-start(bf16[128,256]{1,0:T(8,128)(2,1)S(1)} %get-tuple-element.83), channel_id=1, source_target_pairs={{0,8},{8,0},{16,24},{24,16},{1,9},{9,1},{17,25},{25,17},{2,10},{10... | collective-permute-start | bytes 196616 | tf_op jit(solution)/shard_map/ppermute | solution.py:39
  32.3 1.9 %collective-permute-done.11.refs_1_ = bf16[128,256]{1,0:T(8,128)(2,1)S(1)} collective-permute-done((bf16[128,256]{1,0:T(8,128)(2,1)S(1)}, bf16[128,256]{1,0:T(8,128)(2,1)S(1)}, u32[]{:S(2)}, u32[]{:S(2)}) %collective-permute-start.11) | collective-permute-done | bytes 65568 | tf_op jit(solution)/shard_map/ppermute | solution.py:39
  34.2 1.0 %collective-permute-done.12.refs_2_ = bf16[128,256]{1,0:T(8,128)(2,1)S(1)} collective-permute-done((bf16[128,256]{1,0:T(8,128)(2,1)S(1)}, bf16[128,256]{1,0:T(8,128)(2,1)S(1)}, u32[]{:S(2)}, u32[]{:S(2)}) %collective-permute-start.12) | collective-permute-done | bytes 65568 | tf_op jit(solution)/shard_map/ppermute | solution.py:39
  35.3 0.7 %shard_map.96 = (f32[64,256]{1,0:T(8,128)}, f32[64,256]{1,0:T(8,128)}) custom-call(f32[128,256]{1,0:T(8,128)S(1)} %get-tuple-element.80.refs_0_, bf16[128,256]{1,0:T(8,128)(2,1)S(1)} %collective-permute-done.11.refs_1_, bf16[128,256]{1,0:T(8,128)(2,1)S(1)} %collective-permute-done.12.refs_2_, bf16[128,256]{1,0:T(8,128)(2,1)S(1)} %collective-permute-done.13.refs_3_), custom_call_target="tpu_custom_call" | custom-call | tf_op jit(solution)/shard_map/pallas_call | solution.py:237
  (15 shorter events, 0.3 us)
Async XLA Ops:
  1.8 6.2 %collective-permute-start = (bf16[48,640]{1,0:T(8,128)(2,1)S(1)}, bf16[48,640]{1,0:T(8,128)(2,1)S(1)}, u32[]{:S(2)}, u32[]{:S(2)}) collective-permute-start(bf16[48,640]{1,0:T(8,128)(2,1)S(1)} %get-tuple-element.44), channel_id=1, source_target_pairs={{0,24},{8,16},{16,8},{24,0},{1,25},{9,17},{17,9},{25,1},{2,26},{10... | collective-permute-start | bytes 184328 | tf_op jit(solution)/shard_map/ppermute | solution.py:39
  5.8 4.2 %collective-permute-start.1 = (bf16[48,640]{1,0:T(8,128)(2,1)S(1)}, bf16[48,640]{1,0:T(8,128)(2,1)S(1)}, u32[]{:S(2)}, u32[]{:S(2)}) collective-permute-start(bf16[48,640]{1,0:T(8,128)(2,1)S(1)} %get-tuple-element.45), channel_id=1, source_target_pairs={{0,16},{8,24},{16,0},{24,8},{1,17},{9,25},{17,1},{25,9},{2,18},{10... | collective-permute-start | bytes 184328 | tf_op jit(solution)/shard_map/ppermute | solution.py:39
  6.3 4.2 %collective-permute-start.2 = (bf16[48,640]{1,0:T(8,128)(2,1)S(1)}, bf16[48,640]{1,0:T(8,128)(2,1)S(1)}, u32[]{:S(2)}, u32[]{:S(2)}) collective-permute-start(bf16[48,640]{1,0:T(8,128)(2,1)S(1)} %get-tuple-element.46), channel_id=1, source_target_pairs={{0,8},{8,0},{16,24},{24,16},{1,9},{9,1},{17,25},{25,17},{2,10},{10... | collective-permute-start | bytes 184328 | tf_op jit(solution)/shard_map/ppermute | solution.py:39
  11.2 5.7 %collective-permute-start.4 = (f16[120,512]{1,0:T(8,128)(2,1)S(1)}, f16[120,512]{1,0:T(8,128)(2,1)S(1)}, u32[]{:S(2)}, u32[]{:S(2)}) collective-permute-start(f16[120,512]{1,0:T(8,128)(2,1)S(1)} %convert_element_type.26), channel_id=1, source_target_pairs={{0,1},{1,0},{2,3},{3,2},{4,5},{5,4},{6,7},{7,6},{8,9},{9,8},{10,11... | collective-permute-start | bytes 368648 | tf_op jit(solution)/shard_map/ppermute | solution.py:39
  12.9 8.7 %collective-permute-start.3 = (f16[88,512]{1,0:T(8,128)(2,1)S(1)}, f16[88,512]{1,0:T(8,128)(2,1)S(1)}, u32[]{:S(2)}, u32[]{:S(2)}) collective-permute-start(f16[88,512]{1,0:T(8,128)(2,1)S(1)} %convert_element_type.24), channel_id=1, source_target_pairs={{0,2},{1,3},{2,0},{3,1},{4,6},{5,7},{6,4},{7,5},{8,10},{9,11},{10,... | collective-permute-start | bytes 270344 | tf_op jit(solution)/shard_map/ppermute | solution.py:39
  17.2 9.3 %collective-permute-start.6 = (f16[120,512]{1,0:T(8,128)(2,1)S(1)}, f16[120,512]{1,0:T(8,128)(2,1)S(1)}, u32[]{:S(2)}, u32[]{:S(2)}) collective-permute-start(f16[120,512]{1,0:T(8,128)(2,1)S(1)} %convert_element_type.30), channel_id=1, source_target_pairs={{0,2},{1,3},{2,0},{3,1},{4,6},{5,7},{6,4},{7,5},{8,10},{9,11},{10,... | collective-permute-start | bytes 368648 | tf_op jit(solution)/shard_map/ppermute | solution.py:39
  19.1 4.2 %collective-permute-start.8 = (bf16[112,512]{1,0:T(8,128)(2,1)S(1)}, bf16[112,512]{1,0:T(8,128)(2,1)S(1)}, u32[]{:S(2)}, u32[]{:S(2)}) collective-permute-start(bf16[112,512]{1,0:T(8,128)(2,1)S(1)} %get-tuple-element.60.first), channel_id=1, source_target_pairs={{0,4},{4,0},{1,5},{5,1},{2,6},{6,2},{3,7},{7,3},{8,12},{12,8},{9,1... | collective-permute-start | bytes 344072 | tf_op jit(solution)/shard_map/ppermute | solution.py:39
  21.9 4.6 %collective-permute-start.5 = (f16[88,512]{1,0:T(8,128)(2,1)S(1)}, f16[88,512]{1,0:T(8,128)(2,1)S(1)}, u32[]{:S(2)}, u32[]{:S(2)}) collective-permute-start(f16[88,512]{1,0:T(8,128)(2,1)S(1)} %convert_element_type.28), channel_id=1, source_target_pairs={{0,1},{1,0},{2,3},{3,2},{4,5},{5,4},{6,7},{7,6},{8,9},{9,8},{10,11... | collective-permute-start | bytes 270344 | tf_op jit(solution)/shard_map/ppermute | solution.py:39
  21.9 1.3 %collective-permute-start.9 = (bf16[80,512]{1,0:T(8,128)(2,1)S(1)}, bf16[80,512]{1,0:T(8,128)(2,1)S(1)}, u32[]{:S(2)}, u32[]{:S(2)}) collective-permute-start(bf16[80,512]{1,0:T(8,128)(2,1)S(1)} %get-tuple-element.61.second), channel_id=1, source_target_pairs={{0,4},{4,0},{1,5},{5,1},{2,6},{6,2},{3,7},{7,3},{8,12},{12,8},{9,1... | collective-permute-start | bytes 245768 | tf_op jit(solution)/shard_map/ppermute | solution.py:39
  22.0 4.5 %collective-permute-start.7 = (f32[1,128]{1,0:T(1,128)S(1)}, f32[1,128]{1,0:T(1,128)S(1)}, u32[]{:S(2)}, u32[]{:S(2)}) collective-permute-start(f32[1,128]{1,0:T(1,128)S(1)} %get-tuple-element.70.refs_5_), channel_id=1, source_target_pairs={{0,4},{4,0},{1,5},{5,1},{2,6},{6,2},{3,7},{7,3},{8,12},{12,8},{9,1... | collective-permute-start | bytes 1544 | tf_op jit(solution)/shard_map/ppermute | solution.py:39
  26.7 1.5 %collective-permute-start.10 = (bf16[192,512]{1,0:T(8,128)(2,1)S(1)}, bf16[192,512]{1,0:T(8,128)(2,1)S(1)}, u32[]{:S(2)}, u32[]{:S(2)}) collective-permute-start(bf16[192,512]{1,0:T(8,128)(2,1)S(1)} %shard_map.93.scaled), channel_id=1, source_target_pairs={{0,4},{4,0},{1,5},{5,1},{2,6},{6,2},{3,7},{7,3},{8,12},{12,8},{9,1... | collective-permute-start | bytes 589832 | tf_op jit(solution)/shard_map/ppermute | solution.py:39
  28.7 5.5 %collective-permute-start.11 = (bf16[128,256]{1,0:T(8,128)(2,1)S(1)}, bf16[128,256]{1,0:T(8,128)(2,1)S(1)}, u32[]{:S(2)}, u32[]{:S(2)}) collective-permute-start(bf16[128,256]{1,0:T(8,128)(2,1)S(1)} %get-tuple-element.81), channel_id=1, source_target_pairs={{0,24},{8,16},{16,8},{24,0},{1,25},{9,17},{17,9},{25,1},{2,26},{10... | collective-permute-start | bytes 196616 | tf_op jit(solution)/shard_map/ppermute | solution.py:39
  30.1 5.1 %collective-permute-start.12 = (bf16[128,256]{1,0:T(8,128)(2,1)S(1)}, bf16[128,256]{1,0:T(8,128)(2,1)S(1)}, u32[]{:S(2)}, u32[]{:S(2)}) collective-permute-start(bf16[128,256]{1,0:T(8,128)(2,1)S(1)} %get-tuple-element.82), channel_id=1, source_target_pairs={{0,16},{8,24},{16,0},{24,8},{1,17},{9,25},{17,1},{25,9},{2,18},{10... | collective-permute-start | bytes 196616 | tf_op jit(solution)/shard_map/ppermute | solution.py:39
  30.4 4.9 %collective-permute-start.13 = (bf16[128,256]{1,0:T(8,128)(2,1)S(1)}, bf16[128,256]{1,0:T(8,128)(2,1)S(1)}, u32[]{:S(2)}, u32[]{:S(2)}) collective-permute-start(bf16[128,256]{1,0:T(8,128)(2,1)S(1)} %get-tuple-element.83), channel_id=1, source_target_pairs={{0,8},{8,0},{16,24},{24,16},{1,9},{9,1},{17,25},{25,17},{2,10},{10... | collective-permute-start | bytes 196616 | tf_op jit(solution)/shard_map/ppermute | solution.py:39

commit v14 on v13

--- a/solution.py
+++ b/solution.py
@@ -301,6 +301,7 @@
     for k in range(1, studs):
         all_counts.append(send(counts, "stud", k))
         mates.append([send(part, "stud", k) for part in rows])
+    first_in, all_counts = lax.optimization_barrier((first_in, all_counts))
     for there, back in zip(steps[1:], steps[-2::-1]):
         first, first_out = kernel(pair_body, part[0], (first, first_in), 0)
         first_in = cross(first_out, there)

time: 36.1 us -> 36.1 us (level)
  waiting for transfers between devices: 13.9 us -> 12.8 us
  starting transfers between devices: 15.1 us -> 16.1 us
    ppermute x14, waiting for transfers between devices: 13.9 us -> 12.8 us  [send(): lax.ppermute(block, axis, [(i, partner_to(size, i, step)) for i in range(...]
    ppermute x14, starting transfers between devices: 15.1 us -> 16.1 us  [send(): lax.ppermute(block, axis, [(i, partner_to(size, i, step)) for i in range(...]
where the time goes in v14:
time: 36.1 us; the launch traced here: 35.9 us
  starting transfers between devices  16.1 us (45%)
  waiting for transfers between devices  12.8 us (35%)
  Pallas kernels  6.09 us (17%)
  between operations  0.78 us (2%)
    ppermute x14, starting transfers between devices, send(): lax.ppermute(block, axis, [(i, partner_to(size, i, step)) for i in range(...  16.1 us
    ppermute x14, waiting for transfers between devices, send(): lax.ppermute(block, axis, [(i, partner_to(size, i, step)) for i in range(...  12.8 us
    pallas_call x11, Pallas kernels, kernel(): pl.pallas_call(body, out_shape=outs, in_specs=places or [VMEM] * len(oper...  6.09 us
  transfers between devices with their start and end apart: 14, of which 11 were waited for; matrix products, arithmetic and copies ran while one was open for 0% of the time, Pallas kernels for 8%

profile of v14, /device:TPU:0, one launch (start us, length us, event | category | flops | bytes accessed | tf_op | source)
XLA Modules:
  0.0 35.9 jit_solution(10250656293860512489)
XLA Ops:
  0.6 1.2 %shard_map.86 = (bf16[48,640]{1,0:T(8,128)(2,1)S(1)}, bf16[48,640]{1,0:T(8,128)(2,1)S(1)}, bf16[48,640]{1,0:T(8,128)(2,1)S(1)}, bf16[48,640]{1,0:T(8,128)(2,1)S(1)}) custom-call(bf16[128,512]{1,0:T(8,128)(2,1)} %refs_0_.1, s32[1,128]{1,0:T(1,128)} %bitcast.2, s32[1,128]{1,0:T(1,128)} %bitcast.3), custom_call_target="tpu_custom_call" | custom-call | flops 25165824 | tf_op jit(solution)/shard_map/pallas_call | solution.py:237
  1.8 4.0 %collective-permute-start = (bf16[48,640]{1,0:T(8,128)(2,1)S(1)}, bf16[48,640]{1,0:T(8,128)(2,1)S(1)}, u32[]{:S(2)}, u32[]{:S(2)}) collective-permute-start(bf16[48,640]{1,0:T(8,128)(2,1)S(1)} %get-tuple-element.47), channel_id=1, source_target_pairs={{0,24},{8,16},{16,8},{24,0},{1,25},{9,17},{17,9},{25,1},{2,26},{10... | collective-permute-start | bytes 184328 | tf_op jit(solution)/shard_map/ppermute | solution.py:39
  5.8 0.5 %collective-permute-start.1 = (bf16[48,640]{1,0:T(8,128)(2,1)S(1)}, bf16[48,640]{1,0:T(8,128)(2,1)S(1)}, u32[]{:S(2)}, u32[]{:S(2)}) collective-permute-start(bf16[48,640]{1,0:T(8,128)(2,1)S(1)} %get-tuple-element.48), channel_id=1, source_target_pairs={{0,16},{8,24},{16,0},{24,8},{1,17},{9,25},{17,1},{25,9},{2,18},{10... | collective-permute-start | bytes 184328 | tf_op jit(solution)/shard_map/ppermute | solution.py:39
  6.3 0.1 collective-permute-start.2
  6.4 1.2 %shard_map.87 = (bf16[1,512,256]{2,1,0:T(8,128)(2,1)S(1)}, bf16[1,256,512]{2,1,0:T(8,128)(2,1)S(1)}, bf16[512,256]{1,0:T(8,128)(2,1)S(1)}, bf16[512,256]{1,0:T(8,128)(2,1)S(1)}) custom-call(bf16[48,640]{1,0:T(8,128)(2,1)S(1)} %get-tuple-element.46.refs_0_, bf16[1,512,256]{2,1,0:T(8,128)(2,1)} %refs_1_.1, bf16[1,256,512]{2,1,0:T(8,128)(2,1)} %refs_2_.1, ...), custom_call_target="tpu_custom_call" | custom-call | tf_op jit(solution)/shard_map/pallas_call | solution.py:237
  7.7 0.3 collective-permute-done.refs_1_
  8.0 2.0 %collective-permute-done.1.refs_2_ = bf16[48,640]{1,0:T(8,128)(2,1)S(1)} collective-permute-done((bf16[48,640]{1,0:T(8,128)(2,1)S(1)}, bf16[48,640]{1,0:T(8,128)(2,1)S(1)}, u32[]{:S(2)}, u32[]{:S(2)}) %collective-permute-start.1) | collective-permute-done | bytes 61472 | tf_op jit(solution)/shard_map/ppermute | solution.py:39
  10.0 0.5 %collective-permute-done.2.refs_3_ = bf16[48,640]{1,0:T(8,128)(2,1)S(1)} collective-permute-done((bf16[48,640]{1,0:T(8,128)(2,1)S(1)}, bf16[48,640]{1,0:T(8,128)(2,1)S(1)}, u32[]{:S(2)}, u32[]{:S(2)}) %collective-permute-start.2) | collective-permute-done | bytes 61472 | tf_op jit(solution)/shard_map/ppermute | solution.py:39
  10.5 0.7 %shard_map.88 = (f32[192,128]{1,0:T(8,128)S(1)}, f32[1,128]{1,0:T(1,128)S(1)}, bf16[192,256]{1,0:T(8,128)(2,1)S(1)}, f32[192,256]{1,0:T(8,128)S(1)}, f32[112,512...) custom-call(bf16[48,640]{1,0:T(8,128)(2,1)S(1)} %get-tuple-element.4, ...), custom_call_target="tpu_custom_call" | custom-call | flops 201326592 | tf_op jit(solution)/shard_map/pallas_call | solution.py:237
  11.2 1.6 %collective-permute-start.4 = (f16[120,512]{1,0:T(8,128)(2,1)S(1)}, f16[120,512]{1,0:T(8,128)(2,1)S(1)}, u32[]{:S(2)}, u32[]{:S(2)}) collective-permute-start(f16[120,512]{1,0:T(8,128)(2,1)S(1)} %convert_element_type.26), channel_id=1, source_target_pairs={{0,1},{1,0},{2,3},{3,2},{4,5},{5,4},{6,7},{7,6},{8,9},{9,8},{10,11... | collective-permute-start | bytes 368648 | tf_op jit(solution)/shard_map/ppermute | solution.py:39
  12.9 2.7 %collective-permute-start.3 = (f16[88,512]{1,0:T(8,128)(2,1)S(1)}, f16[88,512]{1,0:T(8,128)(2,1)S(1)}, u32[]{:S(2)}, u32[]{:S(2)}) collective-permute-start(f16[88,512]{1,0:T(8,128)(2,1)S(1)} %convert_element_type.24), channel_id=1, source_target_pairs={{0,2},{1,3},{2,0},{3,1},{4,6},{5,7},{6,4},{7,5},{8,10},{9,11},{10,... | collective-permute-start | bytes 270344 | tf_op jit(solution)/shard_map/ppermute | solution.py:39
  15.5 1.4 %collective-permute-done.4 = f16[120,512]{1,0:T(8,128)(2,1)S(1)} collective-permute-done((f16[120,512]{1,0:T(8,128)(2,1)S(1)}, f16[120,512]{1,0:T(8,128)(2,1)S(1)}, u32[]{:S(2)}, u32[]{:S(2)}) %collective-permute-start.4) | collective-permute-done | bytes 122912 | tf_op jit(solution)/shard_map/ppermute | solution.py:39
  17.0 0.2 shard_map.89
  17.2 1.9 %collective-permute-start.7 = (f16[120,512]{1,0:T(8,128)(2,1)S(1)}, f16[120,512]{1,0:T(8,128)(2,1)S(1)}, u32[]{:S(2)}, u32[]{:S(2)}) collective-permute-start(f16[120,512]{1,0:T(8,128)(2,1)S(1)} %convert_element_type.30), channel_id=1, source_target_pairs={{0,2},{1,3},{2,0},{3,1},{4,6},{5,7},{6,4},{7,5},{8,10},{9,11},{10,... | collective-permute-start | bytes 368648 | tf_op jit(solution)/shard_map/ppermute | solution.py:39
  19.1 0.2 collective-permute-done.3
  19.4 0.2 shard_map.90
  19.6 1.4 %collective-permute-start.6 = (f16[88,512]{1,0:T(8,128)(2,1)S(1)}, f16[88,512]{1,0:T(8,128)(2,1)S(1)}, u32[]{:S(2)}, u32[]{:S(2)}) collective-permute-start(f16[88,512]{1,0:T(8,128)(2,1)S(1)} %convert_element_type.28), channel_id=1, source_target_pairs={{0,1},{1,0},{2,3},{3,2},{4,5},{5,4},{6,7},{7,6},{8,9},{9,8},{10,11... | collective-permute-start | bytes 270344 | tf_op jit(solution)/shard_map/ppermute | solution.py:39
  21.0 0.2 collective-permute-start.9
  21.2 0.2 shard_map.92.turned
  21.5 0.8 %collective-permute-done.9.second = bf16[80,512]{1,0:T(8,128)(2,1)S(1)} collective-permute-done((bf16[80,512]{1,0:T(8,128)(2,1)S(1)}, bf16[80,512]{1,0:T(8,128)(2,1)S(1)}, u32[]{:S(2)}, u32[]{:S(2)}) %collective-permute-start.9) | collective-permute-done | bytes 81952 | tf_op jit(solution)/shard_map/ppermute | solution.py:39
  22.3 0.3 shard_map.91
  22.6 3.8 %collective-permute-done.6 = f16[88,512]{1,0:T(8,128)(2,1)S(1)} collective-permute-done((f16[88,512]{1,0:T(8,128)(2,1)S(1)}, f16[88,512]{1,0:T(8,128)(2,1)S(1)}, u32[]{:S(2)}, u32[]{:S(2)}) %collective-permute-start.6) | collective-permute-done | bytes 90144 | tf_op jit(solution)/shard_map/ppermute | solution.py:39
  26.5 0.2 shard_map.93.scaled
  26.8 0.7 %shard_map.94 = (f32[256,256]{1,0:T(8,128)S(1)}, f32[256,256]{1,0:T(8,128)S(1)}) custom-call(bf16[192,512]{1,0:T(8,128)(2,1)S(1)} %shard_map.93.scaled, bf16[256,192]{1,0:T(8,128)(2,1)S(1)} %shard_map.92.turned, bf16[192,256]{1,0:T(8,128)(2,1)S(1)} %get-tuple-element.82.act, f32[192,256]{1,0:T(8,128)S(1)} %get-tuple-element.83.slope, ...), custom_call_target="tpu_custom_call" | custom-call | flops 150994944 | tf_op jit(solution)/shard_map/pallas_call | solution.py:237
  27.4 0.7 %collective-permute-done.10.scaled = bf16[192,512]{1,0:T(8,128)(2,1)S(1)} collective-permute-done((bf16[192,512]{1,0:T(8,128)(2,1)S(1)}, bf16[192,512]{1,0:T(8,128)(2,1)S(1)}, u32[]{:S(2)}, u32[]{:S(2)}) %collective-permute-start.10) | collective-permute-done | bytes 196640 | tf_op jit(solution)/shard_map/ppermute | solution.py:39
  28.2 0.5 %shard_map.95 = (f32[128,256]{1,0:T(8,128)S(1)}, bf16[128,256]{1,0:T(8,128)(2,1)S(1)}, bf16[128,256]{1,0:T(8,128)(2,1)S(1)}, bf16[128,256]{1,0:T(8,128)(2,1)S(1)}) custom-call(bf16[192,512]{1,0:T(8,128)(2,1)S(1)} %collective-permute-done.10.scaled, bf16[256,192]{1,0:T(8,128)(2,1)S(1)} %get-tuple-element.78.turned, ...), custom_call_target="tpu_custom_call" | custom-call | flops 150994944 | tf_op jit(solution)/shard_map/pallas_call | solution.py:237
  28.7 1.6 %collective-permute-start.11 = (bf16[128,256]{1,0:T(8,128)(2,1)S(1)}, bf16[128,256]{1,0:T(8,128)(2,1)S(1)}, u32[]{:S(2)}, u32[]{:S(2)}) collective-permute-start(bf16[128,256]{1,0:T(8,128)(2,1)S(1)} %get-tuple-element.87), channel_id=1, source_target_pairs={{0,24},{8,16},{16,8},{24,0},{1,25},{9,17},{17,9},{25,1},{2,26},{10... | collective-permute-start | bytes 196616 | tf_op jit(solution)/shard_map/ppermute | solution.py:39
  30.2 0.5 %collective-permute-start.12 = (bf16[128,256]{1,0:T(8,128)(2,1)S(1)}, bf16[128,256]{1,0:T(8,128)(2,1)S(1)}, u32[]{:S(2)}, u32[]{:S(2)}) collective-permute-start(bf16[128,256]{1,0:T(8,128)(2,1)S(1)} %get-tuple-element.88), channel_id=1, source_target_pairs={{0,16},{8,24},{16,0},{24,8},{1,17},{9,25},{17,1},{25,9},{2,18},{10... | collective-permute-start | bytes 196616 | tf_op jit(solution)/shard_map/ppermute | solution.py:39
  30.7 1.5 %collective-permute-start.13 = (bf16[128,256]{1,0:T(8,128)(2,1)S(1)}, bf16[128,256]{1,0:T(8,128)(2,1)S(1)}, u32[]{:S(2)}, u32[]{:S(2)}) collective-permute-start(bf16[128,256]{1,0:T(8,128)(2,1)S(1)} %get-tuple-element.89), channel_id=1, source_target_pairs={{0,8},{8,0},{16,24},{24,16},{1,9},{9,1},{17,25},{25,17},{2,10},{10... | collective-permute-start | bytes 196616 | tf_op jit(solution)/shard_map/ppermute | solution.py:39
  32.2 1.8 %collective-permute-done.11.refs_1_ = bf16[128,256]{1,0:T(8,128)(2,1)S(1)} collective-permute-done((bf16[128,256]{1,0:T(8,128)(2,1)S(1)}, bf16[128,256]{1,0:T(8,128)(2,1)S(1)}, u32[]{:S(2)}, u32[]{:S(2)}) %collective-permute-start.11) | collective-permute-done | bytes 65568 | tf_op jit(solution)/shard_map/ppermute | solution.py:39
  34.0 1.2 %collective-permute-done.12.refs_2_ = bf16[128,256]{1,0:T(8,128)(2,1)S(1)} collective-permute-done((bf16[128,256]{1,0:T(8,128)(2,1)S(1)}, bf16[128,256]{1,0:T(8,128)(2,1)S(1)}, u32[]{:S(2)}, u32[]{:S(2)}) %collective-permute-start.12) | collective-permute-done | bytes 65568 | tf_op jit(solution)/shard_map/ppermute | solution.py:39
  35.2 0.7 %shard_map.96 = (f32[64,256]{1,0:T(8,128)}, f32[64,256]{1,0:T(8,128)}) custom-call(f32[128,256]{1,0:T(8,128)S(1)} %get-tuple-element.86.refs_0_, bf16[128,256]{1,0:T(8,128)(2,1)S(1)} %collective-permute-done.11.refs_1_, bf16[128,256]{1,0:T(8,128)(2,1)S(1)} %collective-permute-done.12.refs_2_, bf16[128,256]{1,0:T(8,128)(2,1)S(1)} %collective-permute-done.13.refs_3_), custom_call_target="tpu_custom_call" | custom-call | tf_op jit(solution)/shard_map/pallas_call | solution.py:237
  (15 shorter events, 0.3 us)
Async XLA Ops:
  1.8 6.2 %collective-permute-start = (bf16[48,640]{1,0:T(8,128)(2,1)S(1)}, bf16[48,640]{1,0:T(8,128)(2,1)S(1)}, u32[]{:S(2)}, u32[]{:S(2)}) collective-permute-start(bf16[48,640]{1,0:T(8,128)(2,1)S(1)} %get-tuple-element.47), channel_id=1, source_target_pairs={{0,24},{8,16},{16,8},{24,0},{1,25},{9,17},{17,9},{25,1},{2,26},{10... | collective-permute-start | bytes 184328 | tf_op jit(solution)/shard_map/ppermute | solution.py:39
  5.8 4.2 %collective-permute-start.1 = (bf16[48,640]{1,0:T(8,128)(2,1)S(1)}, bf16[48,640]{1,0:T(8,128)(2,1)S(1)}, u32[]{:S(2)}, u32[]{:S(2)}) collective-permute-start(bf16[48,640]{1,0:T(8,128)(2,1)S(1)} %get-tuple-element.48), channel_id=1, source_target_pairs={{0,16},{8,24},{16,0},{24,8},{1,17},{9,25},{17,1},{25,9},{2,18},{10... | collective-permute-start | bytes 184328 | tf_op jit(solution)/shard_map/ppermute | solution.py:39
  6.3 4.2 %collective-permute-start.2 = (bf16[48,640]{1,0:T(8,128)(2,1)S(1)}, bf16[48,640]{1,0:T(8,128)(2,1)S(1)}, u32[]{:S(2)}, u32[]{:S(2)}) collective-permute-start(bf16[48,640]{1,0:T(8,128)(2,1)S(1)} %get-tuple-element.49), channel_id=1, source_target_pairs={{0,8},{8,0},{16,24},{24,16},{1,9},{9,1},{17,25},{25,17},{2,10},{10... | collective-permute-start | bytes 184328 | tf_op jit(solution)/shard_map/ppermute | solution.py:39
  11.2 5.7 %collective-permute-start.4 = (f16[120,512]{1,0:T(8,128)(2,1)S(1)}, f16[120,512]{1,0:T(8,128)(2,1)S(1)}, u32[]{:S(2)}, u32[]{:S(2)}) collective-permute-start(f16[120,512]{1,0:T(8,128)(2,1)S(1)} %convert_element_type.26), channel_id=1, source_target_pairs={{0,1},{1,0},{2,3},{3,2},{4,5},{5,4},{6,7},{7,6},{8,9},{9,8},{10,11... | collective-permute-start | bytes 368648 | tf_op jit(solution)/shard_map/ppermute | solution.py:39
  12.9 6.5 %collective-permute-start.3 = (f16[88,512]{1,0:T(8,128)(2,1)S(1)}, f16[88,512]{1,0:T(8,128)(2,1)S(1)}, u32[]{:S(2)}, u32[]{:S(2)}) collective-permute-start(f16[88,512]{1,0:T(8,128)(2,1)S(1)} %convert_element_type.24), channel_id=1, source_target_pairs={{0,2},{1,3},{2,0},{3,1},{4,6},{5,7},{6,4},{7,5},{8,10},{9,11},{10,... | collective-permute-start | bytes 270344 | tf_op jit(solution)/shard_map/ppermute | solution.py:39
  15.5 1.4 %collective-permute-start.5 = (f32[1,128]{1,0:T(1,128)S(1)}, f32[1,128]{1,0:T(1,128)S(1)}, u32[]{:S(2)}, u32[]{:S(2)}) collective-permute-start(f32[1,128]{1,0:T(1,128)S(1)} %get-tuple-element.76.refs_5_), channel_id=1, source_target_pairs={{0,4},{4,0},{1,5},{5,1},{2,6},{6,2},{3,7},{7,3},{8,12},{12,8},{9,1... | collective-permute-start | bytes 1544 | tf_op jit(solution)/shard_map/ppermute | solution.py:39
  17.2 9.3 %collective-permute-start.7 = (f16[120,512]{1,0:T(8,128)(2,1)S(1)}, f16[120,512]{1,0:T(8,128)(2,1)S(1)}, u32[]{:S(2)}, u32[]{:S(2)}) collective-permute-start(f16[120,512]{1,0:T(8,128)(2,1)S(1)} %convert_element_type.30), channel_id=1, source_target_pairs={{0,2},{1,3},{2,0},{3,1},{4,6},{5,7},{6,4},{7,5},{8,10},{9,11},{10,... | collective-permute-start | bytes 368648 | tf_op jit(solution)/shard_map/ppermute | solution.py:39
  19.1 3.2 %collective-permute-start.8 = (bf16[112,512]{1,0:T(8,128)(2,1)S(1)}, bf16[112,512]{1,0:T(8,128)(2,1)S(1)}, u32[]{:S(2)}, u32[]{:S(2)}) collective-permute-start(bf16[112,512]{1,0:T(8,128)(2,1)S(1)} %get-tuple-element.66.first), channel_id=1, source_target_pairs={{0,4},{4,0},{1,5},{5,1},{2,6},{6,2},{3,7},{7,3},{8,12},{12,8},{9,1... | collective-permute-start | bytes 344072 | tf_op jit(solution)/shard_map/ppermute | solution.py:39
  19.6 6.8 %collective-permute-start.6 = (f16[88,512]{1,0:T(8,128)(2,1)S(1)}, f16[88,512]{1,0:T(8,128)(2,1)S(1)}, u32[]{:S(2)}, u32[]{:S(2)}) collective-permute-start(f16[88,512]{1,0:T(8,128)(2,1)S(1)} %convert_element_type.28), channel_id=1, source_target_pairs={{0,1},{1,0},{2,3},{3,2},{4,5},{5,4},{6,7},{7,6},{8,9},{9,8},{10,11... | collective-permute-start | bytes 270344 | tf_op jit(solution)/shard_map/ppermute | solution.py:39
  21.0 1.3 %collective-permute-start.9 = (bf16[80,512]{1,0:T(8,128)(2,1)S(1)}, bf16[80,512]{1,0:T(8,128)(2,1)S(1)}, u32[]{:S(2)}, u32[]{:S(2)}) collective-permute-start(bf16[80,512]{1,0:T(8,128)(2,1)S(1)} %get-tuple-element.67.second), channel_id=1, source_target_pairs={{0,4},{4,0},{1,5},{5,1},{2,6},{6,2},{3,7},{7,3},{8,12},{12,8},{9,1... | collective-permute-start | bytes 245768 | tf_op jit(solution)/shard_map/ppermute | solution.py:39
  26.7 1.5 %collective-permute-start.10 = (bf16[192,512]{1,0:T(8,128)(2,1)S(1)}, bf16[192,512]{1,0:T(8,128)(2,1)S(1)}, u32[]{:S(2)}, u32[]{:S(2)}) collective-permute-start(bf16[192,512]{1,0:T(8,128)(2,1)S(1)} %shard_map.93.scaled), channel_id=1, source_target_pairs={{0,4},{4,0},{1,5},{5,1},{2,6},{6,2},{3,7},{7,3},{8,12},{12,8},{9,1... | collective-permute-start | bytes 589832 | tf_op jit(solution)/shard_map/ppermute | solution.py:39
  28.7 5.3 %collective-permute-start.11 = (bf16[128,256]{1,0:T(8,128)(2,1)S(1)}, bf16[128,256]{1,0:T(8,128)(2,1)S(1)}, u32[]{:S(2)}, u32[]{:S(2)}) collective-permute-start(bf16[128,256]{1,0:T(8,128)(2,1)S(1)} %get-tuple-element.87), channel_id=1, source_target_pairs={{0,24},{8,16},{16,8},{24,0},{1,25},{9,17},{17,9},{25,1},{2,26},{10... | collective-permute-start | bytes 196616 | tf_op jit(solution)/shard_map/ppermute | solution.py:39
  30.2 4.9 %collective-permute-start.12 = (bf16[128,256]{1,0:T(8,128)(2,1)S(1)}, bf16[128,256]{1,0:T(8,128)(2,1)S(1)}, u32[]{:S(2)}, u32[]{:S(2)}) collective-permute-start(bf16[128,256]{1,0:T(8,128)(2,1)S(1)} %get-tuple-element.88), channel_id=1, source_target_pairs={{0,16},{8,24},{16,0},{24,8},{1,17},{9,25},{17,1},{25,9},{2,18},{10... | collective-permute-start | bytes 196616 | tf_op jit(solution)/shard_map/ppermute | solution.py:39
  30.7 4.5 %collective-permute-start.13 = (bf16[128,256]{1,0:T(8,128)(2,1)S(1)}, bf16[128,256]{1,0:T(8,128)(2,1)S(1)}, u32[]{:S(2)}, u32[]{:S(2)}) collective-permute-start(bf16[128,256]{1,0:T(8,128)(2,1)S(1)} %get-tuple-element.89), channel_id=1, source_target_pairs={{0,8},{8,0},{16,24},{24,16},{1,9},{9,1},{17,25},{25,17},{2,10},{10... | collective-permute-start | bytes 196616 | tf_op jit(solution)/shard_map/ppermute | solution.py:39

commit v15 on v12

--- a/solution.py
+++ b/solution.py
@@ -114,28 +114,34 @@
         copy.wait()
 
 
+def silu_of(pre):
+    return (pre / (1.0 + jnp.exp(-pre))).astype(jnp.bfloat16)
+
+
 def student(rows, student_up):
     pre = dot(rows, student_up[...])
     sig = 1.0 / (1.0 + jnp.exp(-pre))
-    return (pre * sig).astype(jnp.bfloat16), sig * (1.0 + pre * (1.0 - sig))
-
-
-def forward_body(owners, local, room, *refs):
-    blocks, refs = refs[:owners], refs[owners:]
+    return silu_of(pre), sig * (1.0 + pre * (1.0 - sig))
+
+
+def forward_body(local, room, first, *refs):
+    count = len(refs) - 9 - (not first)
+    blocks, refs = refs[:count], refs[count:]
+    if not first:
+        earlier, refs = refs[0], refs[1:]
     teach_in, teach_out, student_up, student_down = refs[:4]
-    tags_out, counts_out, act_out, slope_out = refs[4:8]
-    halves, rows_halves, (rows_out, error_out) = refs[8:12], refs[12:14], refs[14:]
+    tags_out, counts_out, error_out, packed, rows_out = refs[4:]
     width = rows_out.shape[1]
     full = [block[...] for block in blocks]
-    counts = None
+    counts = None if first else earlier[...]
     for block in full:
         mine = jnp.floor(block[:1, width:].astype(jnp.float32) * 0.5)
         counts = mine if counts is None else counts + mine
     counts_out[...] = counts
     for l in range(local):
-        span = slice(l * owners * room, (l + 1) * owners * room)
+        span = slice(l * count * room, (l + 1) * count * room)
         for k, block in enumerate(full):
-            start = (l * owners + k) * room
+            start = (l * count + k) * room
             rows_out[start : start + room] = block[l * room : (l + 1) * room, :width]
             tag = block[l * room : (l + 1) * room, width:].astype(jnp.float32)
             if l == 0:
@@ -145,16 +151,9 @@
         rows = rows_out[span]
         hidden = dot(rows, teach_in[l])
         hidden = (hidden / (1.0 + jnp.exp(-hidden))).astype(jnp.bfloat16)
-        act, slope = student(rows, student_up)
-        act_out[span] = act
-        slope_out[span] = slope
+        act = silu_of(dot(rows, student_up[...]))
         error_out[span] = dot(act, student_down[...], ((1,), (1,))) - dot(hidden, teach_out[l])
-    height = halves[0].shape[0]
-    for i in range(2):
-        rows_halves[i][...] = rows_out[i * height : (i + 1) * height]
-        value = error_out[i * height : (i + 1) * height]
-        halves[2 * i][...] = value
-        pack(value, halves[2 * i + 1])
+    pack(error_out[...], packed)
 
 
 def chosen_columns(columns, owners, studs):
@@ -172,11 +171,11 @@
     return dot(chosen, value, ((1,), (1,))).astype(jnp.bfloat16)
 
 
-def ahead_body(owners, studs, first, second, student_up, _, turned, *state):
-    rows = jnp.concatenate([first[...], second[...]])
+def ahead_body(owners, studs, *refs):
+    parts, student_up, (turned, act, slope) = refs[:-5], refs[-5], refs[-3:]
+    rows = jnp.concatenate([part[...] for part in parts])
     turned[...] = turn(rows, owners, studs)
-    if state:
-        state[0][...], state[1][...] = student(rows, student_up)
+    act[...], slope[...] = student(rows, student_up)
 
 
 def pair_body(*refs):
@@ -189,18 +188,17 @@
 
 
 def scale_body(*refs):
-    own, tags = (*refs[2:4], *refs[:2]), refs[4]
-    counts, scaled = refs[5:-1], refs[-1]
+    second, first, tags, counts, scaled = refs[:2], refs[2:4], refs[4:6], refs[6:-1], refs[-1]
     all_counts = counts[0][...]
     for piece in counts[1:]:
         all_counts = all_counts + piece[...]
     inverse = jnp.where(all_counts > 0, 2.0 / all_counts, 0.0)
-    weight = jnp.sum(tags[...] * inverse, axis=1, keepdims=True)
-    height = own[0].shape[0]
-    for i in range(2):
-        span = slice(i * height, (i + 1) * height)
-        total = own[2 * i][...] + unpack(own[2 * i + 1])
-        scaled[span] = (total * weight[span]).astype(scaled.dtype)
+    start = 0
+    for (own, arrived), tag in zip((first, second), tags):
+        weight = jnp.sum(tag[...] * inverse, axis=1, keepdims=True)
+        span = slice(start, start + own.shape[0])
+        scaled[span] = ((own[...] + unpack(arrived)) * weight).astype(scaled.dtype)
+        start += own.shape[0]
 
 
 def backward_body(owners, studs, earlier, scaled, turned, act, slope, student_down, *refs):
@@ -287,18 +285,23 @@
         SMALL,
         [VMEM] + [HBM] * 4,
     )
+    def forward(blocks, *earlier):
+        rows = len(blocks) * local * room
+        return kernel(
+            functools.partial(forward_body, local, room, not earlier),
+            [shape(rows, extra, f32), shape(1, extra, f32), half, packed, shape(rows, width, bf16)],
+            (*blocks, *earlier, *weights),
+            0,
+        )
+
+    steps = [1 << i for i in range(parts.bit_length() - 1)]
     blocks = [blocks[0]] + list(arrived.values())
-    tags, counts, act, slope, first, first_out, second, second_out, *rows = kernel(
-        functools.partial(forward_body, owners, local, room),
-        [shape(slots, extra, f32), shape(1, extra, f32), *state]
-        + [half, packed] * 2
-        + [shape(height, width, bf16)] * 2,
-        (*blocks, *weights),
-        4 * slots * width * (hidden + units),
-        [pltpu.VMEM((slots, width), bf16), pltpu.VMEM((slots, actions), f32)],
-    )
-    steps = [1 << i for i in range(parts.bit_length() - 1)]
-    first_in, second_in = cross(first_out, steps[0]), cross(second_out, steps[-1])
+    near, far = blocks[: owners // 2], blocks[owners // 2 :]
+    second_tags, counts, second, second_out, second_rows = forward(near)
+    second_in = cross(second_out, steps[-1])
+    first_tags, counts, first, first_out, first_rows = forward(far, counts)
+    first_in = cross(first_out, steps[0])
+    rows, tags = (first_rows, second_rows), (first_tags, second_tags)
     all_counts, mates = [counts], []
     for k in range(1, studs):
         all_counts.append(send(counts, "stud", k))
@@ -313,17 +316,18 @@
         first_in, second_in = cross(first_out, there), cross(second_out, back)
     ahead = functools.partial(ahead_body, owners, studs)
     turned = shape(width // studs, slots, bf16)
-    (ours,) = kernel(ahead, [turned], (*rows, weights[2], second), 0)
-    known = [kernel(ahead, [turned] + state, (*theirs, weights[2], second), 0) for theirs in mates]
+    ours, *known = [
+        kernel(ahead, [turned] + state, (*group, weights[2], second), 0) for group in (rows, *mates)
+    ]
     sums = (second, second_in, first, first_in)
     sums, all_counts, known, ours = lax.optimization_barrier((sums, all_counts, known, ours))
-    (scaled,) = kernel(scale_body, [shape(slots, actions, bf16)], (*sums, tags, *all_counts), 0)
+    (scaled,) = kernel(scale_body, [shape(slots, actions, bf16)], (*sums, *tags, *all_counts), 0)
     work = 6 * slots * width * units
     grads = [shape(width // studs, units, f32), shape(actions // studs, units, f32)]
     heights = [g.shape[0] // owners for g in grads]
     blocks = [shape(sum(heights), units, f32)] + [shape(sum(heights), units, bf16)] * (owners - 1)
     errors = [scaled] + [send(scaled, "stud", k) for k in range(1, studs)]
-    states = [[ours, act, slope]] + known
+    states = [ours] + known
     sums = []
     for k, (error, state) in enumerate(zip(errors, states)):
         sums = kernel(

time: 35.5 us -> 34.9 us (0.983)
  waiting for transfers between devices: 11.9 us -> 10 us
  starting transfers between devices: 16.6 us -> 17.5 us
  Pallas kernels: 5.91 us -> 6.37 us
    ppermute x14, waiting for transfers between devices: 11.9 us -> 10 us  [send(): lax.ppermute(block, axis, [(i, partner_to(size, i, step)) for i in range(...]
    ppermute x14, starting transfers between devices: 16.6 us -> 17.5 us  [send(): lax.ppermute(block, axis, [(i, partner_to(size, i, step)) for i in range(...]
    pallas_call x10 -> x11, Pallas kernels: 5.91 us -> 6.37 us  [kernel(): pl.pallas_call(body, out_shape=outs, in_specs=places or [VMEM] * len(oper...]
  transfers between devices with their start and end apart: 14 -> 14, of which waited for: 10 -> 9; matrix products, arithmetic and copies ran while one was open for 0% -> 0% of each run, Pallas kernels for 7% -> 10%
where the time goes in v15:
time: 34.9 us; the launch traced here: 34.8 us
  starting transfers between devices  17.5 us (50%)
  waiting for transfers between devices  10 us (29%)
  Pallas kernels  6.37 us (18%)
  between operations  0.79 us (2%)
    ppermute x14, starting transfers between devices, send(): lax.ppermute(block, axis, [(i, partner_to(size, i, step)) for i in range(...  17.5 us
    ppermute x14, waiting for transfers between devices, send(): lax.ppermute(block, axis, [(i, partner_to(size, i, step)) for i in range(...  10 us
    pallas_call x11, Pallas kernels, kernel(): pl.pallas_call(body, out_shape=outs, in_specs=places or [VMEM] * len(oper...  6.37 us
  transfers between devices with their start and end apart: 14, of which 9 were waited for; matrix products, arithmetic and copies ran while one was open for 0% of the time, Pallas kernels for 10%

profile of v15, /device:TPU:0, one launch (start us, length us, event | category | flops | bytes accessed | tf_op | source)
XLA Modules:
  0.0 34.8 jit_solution(5629215940045621425)
XLA Ops:
  0.6 1.2 %shard_map.86 = (bf16[48,640]{1,0:T(8,128)(2,1)S(1)}, bf16[48,640]{1,0:T(8,128)(2,1)S(1)}, bf16[48,640]{1,0:T(8,128)(2,1)S(1)}, bf16[48,640]{1,0:T(8,128)(2,1)S(1)}) custom-call(bf16[128,512]{1,0:T(8,128)(2,1)} %refs_0_.1, s32[1,128]{1,0:T(1,128)} %bitcast.2, s32[1,128]{1,0:T(1,128)} %bitcast.3), custom_call_target="tpu_custom_call" | custom-call | flops 25165824 | tf_op jit(solution)/shard_map/pallas_call | solution.py:238
  1.8 4.0 %collective-permute-start.2 = (bf16[48,640]{1,0:T(8,128)(2,1)S(1)}, bf16[48,640]{1,0:T(8,128)(2,1)S(1)}, u32[]{:S(2)}, u32[]{:S(2)}) collective-permute-start(bf16[48,640]{1,0:T(8,128)(2,1)S(1)} %get-tuple-element.57), channel_id=1, source_target_pairs={{0,24},{8,16},{16,8},{24,0},{1,25},{9,17},{17,9},{25,1},{2,26},{10... | collective-permute-start | bytes 184328 | tf_op jit(solution)/shard_map/ppermute | solution.py:39
  5.8 0.5 %collective-permute-start = (bf16[48,640]{1,0:T(8,128)(2,1)S(1)}, bf16[48,640]{1,0:T(8,128)(2,1)S(1)}, u32[]{:S(2)}, u32[]{:S(2)}) collective-permute-start(bf16[48,640]{1,0:T(8,128)(2,1)S(1)} %get-tuple-element.54), channel_id=1, source_target_pairs={{0,16},{8,24},{16,0},{24,8},{1,17},{9,25},{17,1},{25,9},{2,18},{10... | collective-permute-start | bytes 184328 | tf_op jit(solution)/shard_map/ppermute | solution.py:39
  6.3 0.1 collective-permute-start.1
  6.4 1.2 %shard_map.87 = (bf16[1,512,256]{2,1,0:T(8,128)(2,1)S(1)}, bf16[1,256,512]{2,1,0:T(8,128)(2,1)S(1)}, bf16[512,256]{1,0:T(8,128)(2,1)S(1)}, bf16[512,256]{1,0:T(8,128)(2,1)S(1)}) custom-call(bf16[48,640]{1,0:T(8,128)(2,1)S(1)} %get-tuple-element.56.refs_0_, bf16[1,512,256]{2,1,0:T(8,128)(2,1)} %refs_1_.1, bf16[1,256,512]{2,1,0:T(8,128)(2,1)} %refs_2_.1, ...), custom_call_target="tpu_custom_call" | custom-call | tf_op jit(solution)/shard_map/pallas_call | solution.py:238
  7.7 0.3 collective-permute-done.2.refs_1_
  8.0 0.5 %shard_map.88 = (f32[96,128]{1,0:T(8,128)S(1)}, f32[1,128]{1,0:T(1,128)S(1)}, f32[96,512]{1,0:T(8,128)S(1)}, f32[104,512]{1,0:T(8,128)S(1)}, bf16[96,512]{1,0:T(8,128)(2,1)S(1)}) custom-call(bf16[48,640]{1,0:T(8,128)(2,1)S(1)} %get-tuple-element.56.refs_0_, bf16[48,640]{1,0:T(8,128)(2,1)S(1)} %collective-permute-done.2.refs_1_, ...), custom_call_target="tpu_custom_call" | custom-call | tf_op jit(solution)/shard_map/pallas_call | solution.py:238
  8.6 3.2 %collective-permute-start.4 = (f16[104,512]{1,0:T(8,128)(2,1)S(1)}, f16[104,512]{1,0:T(8,128)(2,1)S(1)}, u32[]{:S(2)}, u32[]{:S(2)}) collective-permute-start(f16[104,512]{1,0:T(8,128)(2,1)S(1)} %convert_element_type.26), channel_id=1, source_target_pairs={{0,2},{1,3},{2,0},{3,1},{4,6},{5,7},{6,4},{7,5},{8,10},{9,11},{10,... | collective-permute-start | bytes 319496 | tf_op jit(solution)/shard_map/ppermute | solution.py:39
  11.8 0.5 %shard_map.89 = (f32[96,128]{1,0:T(8,128)S(1)}, f32[1,128]{1,0:T(1,128)S(1)}, f32[96,512]{1,0:T(8,128)S(1)}, f32[104,512]{1,0:T(8,128)S(1)}, bf16[96,512]{1,0:T(8,128)(2,1)S(1)}) custom-call(bf16[48,640]{1,0:T(8,128)(2,1)S(1)} %collective-permute-done.refs_0_, bf16[48,640]{1,0:T(8,128)(2,1)S(1)} %collective-permute-done.1.refs_1_, ...), custom_call_target="tpu_custom_call" | custom-call | tf_op jit(solution)/shard_map/pallas_call | solution.py:238
  12.3 1.6 %collective-permute-start.3 = (f16[104,512]{1,0:T(8,128)(2,1)S(1)}, f16[104,512]{1,0:T(8,128)(2,1)S(1)}, u32[]{:S(2)}, u32[]{:S(2)}) collective-permute-start(f16[104,512]{1,0:T(8,128)(2,1)S(1)} %convert_element_type.24), channel_id=1, source_target_pairs={{0,1},{1,0},{2,3},{3,2},{4,5},{5,4},{6,7},{7,6},{8,9},{9,8},{10,11... | collective-permute-start | bytes 319496 | tf_op jit(solution)/shard_map/ppermute | solution.py:39
  14.0 0.5 %collective-permute-start.7 = (bf16[96,512]{1,0:T(8,128)(2,1)S(1)}, bf16[96,512]{1,0:T(8,128)(2,1)S(1)}, u32[]{:S(2)}, u32[]{:S(2)}) collective-permute-start(bf16[96,512]{1,0:T(8,128)(2,1)S(1)} %get-tuple-element.68.refs_1_), channel_id=1, source_target_pairs={{0,4},{4,0},{1,5},{5,1},{2,6},{6,2},{3,7},{7,3},{8,12},{12,8},{9,1... | collective-permute-start | bytes 294920 | tf_op jit(solution)/shard_map/ppermute | solution.py:39
  14.5 0.3 collective-permute-done.4
  14.8 2.3 %collective-permute-done.3 = f16[104,512]{1,0:T(8,128)(2,1)S(1)} collective-permute-done((f16[104,512]{1,0:T(8,128)(2,1)S(1)}, f16[104,512]{1,0:T(8,128)(2,1)S(1)}, u32[]{:S(2)}, u32[]{:S(2)}) %collective-permute-start.3) | collective-permute-done | bytes 106528 | tf_op jit(solution)/shard_map/ppermute | solution.py:39
  17.1 0.2 shard_map.90
  17.4 1.4 %collective-permute-start.9 = (f16[104,512]{1,0:T(8,128)(2,1)S(1)}, f16[104,512]{1,0:T(8,128)(2,1)S(1)}, u32[]{:S(2)}, u32[]{:S(2)}) collective-permute-start(f16[104,512]{1,0:T(8,128)(2,1)S(1)} %convert_element_type.30), channel_id=1, source_target_pairs={{0,2},{1,3},{2,0},{3,1},{4,6},{5,7},{6,4},{7,5},{8,10},{9,11},{10,... | collective-permute-start | bytes 319496 | tf_op jit(solution)/shard_map/ppermute | solution.py:39
  18.9 2.5 %collective-permute-start.8 = (f16[104,512]{1,0:T(8,128)(2,1)S(1)}, f16[104,512]{1,0:T(8,128)(2,1)S(1)}, u32[]{:S(2)}, u32[]{:S(2)}) collective-permute-start(f16[104,512]{1,0:T(8,128)(2,1)S(1)} %convert_element_type.28), channel_id=1, source_target_pairs={{0,1},{1,0},{2,3},{3,2},{4,5},{5,4},{6,7},{7,6},{8,9},{9,8},{10,11... | collective-permute-start | bytes 319496 | tf_op jit(solution)/shard_map/ppermute | solution.py:39
  21.3 0.3 shard_map.92
  21.7 0.3 shard_map.91
  22.0 2.4 %collective-permute-done.9 = f16[104,512]{1,0:T(8,128)(2,1)S(1)} collective-permute-done((f16[104,512]{1,0:T(8,128)(2,1)S(1)}, f16[104,512]{1,0:T(8,128)(2,1)S(1)}, u32[]{:S(2)}, u32[]{:S(2)}) %collective-permute-start.9) | collective-permute-done | bytes 106528 | tf_op jit(solution)/shard_map/ppermute | solution.py:39
  24.4 0.1 collective-permute-done.8
  24.5 0.2 shard_map.93.scaled
  24.7 0.1 collective-permute-start.10
  24.7 0.7 %shard_map.94 = (f32[256,256]{1,0:T(8,128)S(1)}, f32[256,256]{1,0:T(8,128)S(1)}) custom-call(bf16[192,512]{1,0:T(8,128)(2,1)S(1)} %shard_map.93.scaled, bf16[256,192]{1,0:T(8,128)(2,1)S(1)} %get-tuple-element.97.turned, bf16[192,256]{1,0:T(8,128)(2,1)S(1)} %get-tuple-element.98.act, f32[192,256]{1,0:T(8,128)S(1)} %get-tuple-element.99.slope, ...), custom_call_target="tpu_custom_call" | custom-call | flops 150994944 | tf_op jit(solution)/shard_map/pallas_call | solution.py:238
  25.4 0.7 %collective-permute-done.10.scaled = bf16[192,512]{1,0:T(8,128)(2,1)S(1)} collective-permute-done((bf16[192,512]{1,0:T(8,128)(2,1)S(1)}, bf16[192,512]{1,0:T(8,128)(2,1)S(1)}, u32[]{:S(2)}, u32[]{:S(2)}) %collective-permute-start.10) | collective-permute-done | bytes 196640 | tf_op jit(solution)/shard_map/ppermute | solution.py:39
  26.2 0.5 %shard_map.95 = (f32[128,256]{1,0:T(8,128)S(1)}, bf16[128,256]{1,0:T(8,128)(2,1)S(1)}, bf16[128,256]{1,0:T(8,128)(2,1)S(1)}, bf16[128,256]{1,0:T(8,128)(2,1)S(1)}) custom-call(bf16[192,512]{1,0:T(8,128)(2,1)S(1)} %collective-permute-done.10.scaled, bf16[256,192]{1,0:T(8,128)(2,1)S(1)} %get-tuple-element.94.turned, ...), custom_call_target="tpu_custom_call" | custom-call | flops 150994944 | tf_op jit(solution)/shard_map/pallas_call | solution.py:238
  26.7 2.5 %collective-permute-start.11 = (bf16[128,256]{1,0:T(8,128)(2,1)S(1)}, bf16[128,256]{1,0:T(8,128)(2,1)S(1)}, u32[]{:S(2)}, u32[]{:S(2)}) collective-permute-start(bf16[128,256]{1,0:T(8,128)(2,1)S(1)} %get-tuple-element.103), channel_id=1, source_target_pairs={{0,24},{8,16},{16,8},{24,0},{1,25},{9,17},{17,9},{25,1},{2,26},{10... | collective-permute-start | bytes 196616 | tf_op jit(solution)/shard_map/ppermute | solution.py:39
  29.1 0.7 %collective-permute-start.12 = (bf16[128,256]{1,0:T(8,128)(2,1)S(1)}, bf16[128,256]{1,0:T(8,128)(2,1)S(1)}, u32[]{:S(2)}, u32[]{:S(2)}) collective-permute-start(bf16[128,256]{1,0:T(8,128)(2,1)S(1)} %get-tuple-element.104), channel_id=1, source_target_pairs={{0,16},{8,24},{16,0},{24,8},{1,17},{9,25},{17,1},{25,9},{2,18},{10... | collective-permute-start | bytes 196616 | tf_op jit(solution)/shard_map/ppermute | solution.py:39
  29.8 0.4 %collective-permute-start.13 = (bf16[128,256]{1,0:T(8,128)(2,1)S(1)}, bf16[128,256]{1,0:T(8,128)(2,1)S(1)}, u32[]{:S(2)}, u32[]{:S(2)}) collective-permute-start(bf16[128,256]{1,0:T(8,128)(2,1)S(1)} %get-tuple-element.105), channel_id=1, source_target_pairs={{0,8},{8,0},{16,24},{24,16},{1,9},{9,1},{17,25},{25,17},{2,10},{10... | collective-permute-start | bytes 196616 | tf_op jit(solution)/shard_map/ppermute | solution.py:39
  30.2 1.7 %collective-permute-done.11.refs_1_ = bf16[128,256]{1,0:T(8,128)(2,1)S(1)} collective-permute-done((bf16[128,256]{1,0:T(8,128)(2,1)S(1)}, bf16[128,256]{1,0:T(8,128)(2,1)S(1)}, u32[]{:S(2)}, u32[]{:S(2)}) %collective-permute-start.11) | collective-permute-done | bytes 65568 | tf_op jit(solution)/shard_map/ppermute | solution.py:39
  31.9 1.5 %collective-permute-done.12.refs_2_ = bf16[128,256]{1,0:T(8,128)(2,1)S(1)} collective-permute-done((bf16[128,256]{1,0:T(8,128)(2,1)S(1)}, bf16[128,256]{1,0:T(8,128)(2,1)S(1)}, u32[]{:S(2)}, u32[]{:S(2)}) %collective-permute-start.12) | collective-permute-done | bytes 65568 | tf_op jit(solution)/shard_map/ppermute | solution.py:39
  33.4 0.7 %collective-permute-done.13.refs_3_ = bf16[128,256]{1,0:T(8,128)(2,1)S(1)} collective-permute-done((bf16[128,256]{1,0:T(8,128)(2,1)S(1)}, bf16[128,256]{1,0:T(8,128)(2,1)S(1)}, u32[]{:S(2)}, u32[]{:S(2)}) %collective-permute-start.13) | collective-permute-done | bytes 65568 | tf_op jit(solution)/shard_map/ppermute | solution.py:39
  34.1 0.7 %shard_map.96 = (f32[64,256]{1,0:T(8,128)}, f32[64,256]{1,0:T(8,128)}) custom-call(f32[128,256]{1,0:T(8,128)S(1)} %get-tuple-element.102.refs_0_, bf16[128,256]{1,0:T(8,128)(2,1)S(1)} %collective-permute-done.11.refs_1_, bf16[128,256]{1,0:T(8,128)(2,1)S(1)} %collective-permute-done.12.refs_2_, bf16[128,256]{1,0:T(8,128)(2,1)S(1)} %collective-permute-done.13.refs_3_), custom_call_target="tpu_custom_call" | custom-call | tf_op jit(solution)/shard_map/pallas_call | solution.py:238
  (15 shorter events, 0.1 us)
Async XLA Ops:
  1.8 6.2 %collective-permute-start.2 = (bf16[48,640]{1,0:T(8,128)(2,1)S(1)}, bf16[48,640]{1,0:T(8,128)(2,1)S(1)}, u32[]{:S(2)}, u32[]{:S(2)}) collective-permute-start(bf16[48,640]{1,0:T(8,128)(2,1)S(1)} %get-tuple-element.57), channel_id=1, source_target_pairs={{0,24},{8,16},{16,8},{24,0},{1,25},{9,17},{17,9},{25,1},{2,26},{10... | collective-permute-start | bytes 184328 | tf_op jit(solution)/shard_map/ppermute | solution.py:39
  5.8 6.0 %collective-permute-start = (bf16[48,640]{1,0:T(8,128)(2,1)S(1)}, bf16[48,640]{1,0:T(8,128)(2,1)S(1)}, u32[]{:S(2)}, u32[]{:S(2)}) collective-permute-start(bf16[48,640]{1,0:T(8,128)(2,1)S(1)} %get-tuple-element.54), channel_id=1, source_target_pairs={{0,16},{8,24},{16,0},{24,8},{1,17},{9,25},{17,1},{25,9},{2,18},{10... | collective-permute-start | bytes 184328 | tf_op jit(solution)/shard_map/ppermute | solution.py:39
  6.3 5.5 %collective-permute-start.1 = (bf16[48,640]{1,0:T(8,128)(2,1)S(1)}, bf16[48,640]{1,0:T(8,128)(2,1)S(1)}, u32[]{:S(2)}, u32[]{:S(2)}) collective-permute-start(bf16[48,640]{1,0:T(8,128)(2,1)S(1)} %get-tuple-element.55), channel_id=1, source_target_pairs={{0,8},{8,0},{16,24},{24,16},{1,9},{9,1},{17,25},{25,17},{2,10},{10... | collective-permute-start | bytes 184328 | tf_op jit(solution)/shard_map/ppermute | solution.py:39
  8.6 6.2 %collective-permute-start.4 = (f16[104,512]{1,0:T(8,128)(2,1)S(1)}, f16[104,512]{1,0:T(8,128)(2,1)S(1)}, u32[]{:S(2)}, u32[]{:S(2)}) collective-permute-start(f16[104,512]{1,0:T(8,128)(2,1)S(1)} %convert_element_type.26), channel_id=1, source_target_pairs={{0,2},{1,3},{2,0},{3,1},{4,6},{5,7},{6,4},{7,5},{8,10},{9,11},{10,... | collective-permute-start | bytes 319496 | tf_op jit(solution)/shard_map/ppermute | solution.py:39
  12.3 4.8 %collective-permute-start.3 = (f16[104,512]{1,0:T(8,128)(2,1)S(1)}, f16[104,512]{1,0:T(8,128)(2,1)S(1)}, u32[]{:S(2)}, u32[]{:S(2)}) collective-permute-start(f16[104,512]{1,0:T(8,128)(2,1)S(1)} %convert_element_type.24), channel_id=1, source_target_pairs={{0,1},{1,0},{2,3},{3,2},{4,5},{5,4},{6,7},{7,6},{8,9},{9,8},{10,11... | collective-permute-start | bytes 319496 | tf_op jit(solution)/shard_map/ppermute | solution.py:39
  14.0 3.2 %collective-permute-start.6 = (bf16[96,512]{1,0:T(8,128)(2,1)S(1)}, bf16[96,512]{1,0:T(8,128)(2,1)S(1)}, u32[]{:S(2)}, u32[]{:S(2)}) collective-permute-start(bf16[96,512]{1,0:T(8,128)(2,1)S(1)} %get-tuple-element.67.refs_0_), channel_id=1, source_target_pairs={{0,4},{4,0},{1,5},{5,1},{2,6},{6,2},{3,7},{7,3},{8,12},{12,8},{9,1... | collective-permute-start | bytes 294920 | tf_op jit(solution)/shard_map/ppermute | solution.py:39
  14.0 3.2 %collective-permute-start.7 = (bf16[96,512]{1,0:T(8,128)(2,1)S(1)}, bf16[96,512]{1,0:T(8,128)(2,1)S(1)}, u32[]{:S(2)}, u32[]{:S(2)}) collective-permute-start(bf16[96,512]{1,0:T(8,128)(2,1)S(1)} %get-tuple-element.68.refs_1_), channel_id=1, source_target_pairs={{0,4},{4,0},{1,5},{5,1},{2,6},{6,2},{3,7},{7,3},{8,12},{12,8},{9,1... | collective-permute-start | bytes 294920 | tf_op jit(solution)/shard_map/ppermute | solution.py:39
  14.5 2.6 %collective-permute-start.5 = (f32[1,128]{1,0:T(1,128)S(1)}, f32[1,128]{1,0:T(1,128)S(1)}, u32[]{:S(2)}, u32[]{:S(2)}) collective-permute-start(f32[1,128]{1,0:T(1,128)S(1)} %get-tuple-element.92.refs_6_), channel_id=1, source_target_pairs={{0,4},{4,0},{1,5},{5,1},{2,6},{6,2},{3,7},{7,3},{8,12},{12,8},{9,1... | collective-permute-start | bytes 1544 | tf_op jit(solution)/shard_map/ppermute | solution.py:39
  17.4 6.9 %collective-permute-start.9 = (f16[104,512]{1,0:T(8,128)(2,1)S(1)}, f16[104,512]{1,0:T(8,128)(2,1)S(1)}, u32[]{:S(2)}, u32[]{:S(2)}) collective-permute-start(f16[104,512]{1,0:T(8,128)(2,1)S(1)} %convert_element_type.30), channel_id=1, source_target_pairs={{0,2},{1,3},{2,0},{3,1},{4,6},{5,7},{6,4},{7,5},{8,10},{9,11},{10,... | collective-permute-start | bytes 319496 | tf_op jit(solution)/shard_map/ppermute | solution.py:39
  18.9 5.6 %collective-permute-start.8 = (f16[104,512]{1,0:T(8,128)(2,1)S(1)}, f16[104,512]{1,0:T(8,128)(2,1)S(1)}, u32[]{:S(2)}, u32[]{:S(2)}) collective-permute-start(f16[104,512]{1,0:T(8,128)(2,1)S(1)} %convert_element_type.28), channel_id=1, source_target_pairs={{0,1},{1,0},{2,3},{3,2},{4,5},{5,4},{6,7},{7,6},{8,9},{9,8},{10,11... | collective-permute-start | bytes 319496 | tf_op jit(solution)/shard_map/ppermute | solution.py:39
  24.7 1.5 %collective-permute-start.10 = (bf16[192,512]{1,0:T(8,128)(2,1)S(1)}, bf16[192,512]{1,0:T(8,128)(2,1)S(1)}, u32[]{:S(2)}, u32[]{:S(2)}) collective-permute-start(bf16[192,512]{1,0:T(8,128)(2,1)S(1)} %shard_map.93.scaled), channel_id=1, source_target_pairs={{0,4},{4,0},{1,5},{5,1},{2,6},{6,2},{3,7},{7,3},{8,12},{12,8},{9,1... | collective-permute-start | bytes 589832 | tf_op jit(solution)/shard_map/ppermute | solution.py:39
  26.7 5.3 %collective-permute-start.11 = (bf16[128,256]{1,0:T(8,128)(2,1)S(1)}, bf16[128,256]{1,0:T(8,128)(2,1)S(1)}, u32[]{:S(2)}, u32[]{:S(2)}) collective-permute-start(bf16[128,256]{1,0:T(8,128)(2,1)S(1)} %get-tuple-element.103), channel_id=1, source_target_pairs={{0,24},{8,16},{16,8},{24,0},{1,25},{9,17},{17,9},{25,1},{2,26},{10... | collective-permute-start | bytes 196616 | tf_op jit(solution)/shard_map/ppermute | solution.py:39
  29.1 4.3 %collective-permute-start.12 = (bf16[128,256]{1,0:T(8,128)(2,1)S(1)}, bf16[128,256]{1,0:T(8,128)(2,1)S(1)}, u32[]{:S(2)}, u32[]{:S(2)}) collective-permute-start(bf16[128,256]{1,0:T(8,128)(2,1)S(1)} %get-tuple-element.104), channel_id=1, source_target_pairs={{0,16},{8,24},{16,0},{24,8},{1,17},{9,25},{17,1},{25,9},{2,18},{10... | collective-permute-start | bytes 196616 | tf_op jit(solution)/shard_map/ppermute | solution.py:39
  29.8 4.3 %collective-permute-start.13 = (bf16[128,256]{1,0:T(8,128)(2,1)S(1)}, bf16[128,256]{1,0:T(8,128)(2,1)S(1)}, u32[]{:S(2)}, u32[]{:S(2)}) collective-permute-start(bf16[128,256]{1,0:T(8,128)(2,1)S(1)} %get-tuple-element.105), channel_id=1, source_target_pairs={{0,8},{8,0},{16,24},{24,16},{1,9},{9,1},{17,25},{25,17},{2,10},{10... | collective-permute-start | bytes 196616 | tf_op jit(solution)/shard_map/ppermute | solution.py:39

commit v16 on v15

--- a/solution.py
+++ b/solution.py
@@ -166,44 +166,42 @@
     return (column == wanted).astype(jnp.float32).astype(jnp.bfloat16)
 
 
-def turn(value, owners, studs):
-    chosen = chosen_columns(value.shape[1], owners, studs)
+def turn(value, chosen):
     return dot(chosen, value, ((1,), (1,))).astype(jnp.bfloat16)
 
 
-def ahead_body(owners, studs, *refs):
-    parts, student_up, (turned, act, slope) = refs[:-5], refs[-5], refs[-3:]
-    rows = jnp.concatenate([part[...] for part in parts])
-    turned[...] = turn(rows, owners, studs)
-    act[...], slope[...] = student(rows, student_up)
-
-
-def pair_body(*refs):
-    for i in range(2):
-        own, arrived = refs[2 * i : 2 * i + 2]
-        total, packed = refs[2 * i + 4 : 2 * i + 6]
-        value = own[...] + unpack(arrived)
-        total[...] = value
-        pack(value, packed)
-
-
-def scale_body(*refs):
-    second, first, tags, counts, scaled = refs[:2], refs[2:4], refs[4:6], refs[6:-1], refs[-1]
+def ahead_body(owners, studs, count, *refs):
+    parts, student_up, outs = refs[:count], refs[count], refs[count + 2 :]
+    chosen = chosen_columns(parts[0].shape[1], owners, studs)
+    for i, part in enumerate(parts):
+        turned, act, slope = outs[3 * i : 3 * i + 3]
+        rows = part[...]
+        turned[...] = turn(rows, chosen)
+        act[...], slope[...] = student(rows, student_up)
+    if len(outs) > 3 * count:
+        outs[-1][...] = chosen_columns(outs[-1].shape[1], owners, studs)
+
+
+def pair_body(own, arrived, *refs):
+    total, packed = refs[-2:]
+    value = own[...] + unpack(arrived)
+    total[...] = value
+    pack(value, packed)
+
+
+def scale_body(own, arrived, tags, *refs):
+    counts, scaled = refs[:-1], refs[-1]
     all_counts = counts[0][...]
     for piece in counts[1:]:
         all_counts = all_counts + piece[...]
     inverse = jnp.where(all_counts > 0, 2.0 / all_counts, 0.0)
-    start = 0
-    for (own, arrived), tag in zip((first, second), tags):
-        weight = jnp.sum(tag[...] * inverse, axis=1, keepdims=True)
-        span = slice(start, start + own.shape[0])
-        scaled[span] = ((own[...] + unpack(arrived)) * weight).astype(scaled.dtype)
-        start += own.shape[0]
-
-
-def backward_body(owners, studs, earlier, scaled, turned, act, slope, student_down, *refs):
+    weight = jnp.sum(tags[...] * inverse, axis=1, keepdims=True)
+    scaled[...] = ((own[...] + unpack(arrived)) * weight).astype(scaled.dtype)
+
+
+def backward_body(owners, earlier, scaled, turned, act, slope, chosen, student_down, *refs):
     error = scaled[...]
-    down = dot(turn(error, owners, studs), act[...])
+    down = dot(turn(error, chosen[...]), act[...])
     pre_grad = (dot(error, student_down[...]) * slope[...]).astype(jnp.bfloat16)
     up = dot(turned[...], pre_grad)
     if earlier:
@@ -263,7 +261,7 @@
 
     height = slots // 2
     half, packed = shape(height, actions, f32), shape(height + PACK_ROWS, actions, f32)
-    state = [shape(slots, units, bf16), shape(slots, units, f32)]
+    state = [shape(width // studs, height, bf16), shape(height, units, bf16), shape(height, units, f32)]
     tokens = [ids.reshape(1, row_count) for ids in (task_ids, student_batch)]
     blocks = kernel(
         functools.partial(dispatch_body, owners, local, room, extra),
@@ -306,36 +304,42 @@
     for k in range(1, studs):
         all_counts.append(send(counts, "stud", k))
         mates.append([send(part, "stud", k) for part in rows])
-    first_in, second_in, all_counts, mates = lax.optimization_barrier(
-        (first_in, second_in, all_counts, mates)
-    )
+    second_in, all_counts, mates = lax.optimization_barrier((second_in, all_counts, mates))
     for there, back in zip(steps[1:], steps[-2::-1]):
-        first, first_out, second, second_out = kernel(
-            pair_body, [half, packed] * 2, (first, first_in, second, second_in), 0
-        )
-        first_in, second_in = cross(first_out, there), cross(second_out, back)
-    ahead = functools.partial(ahead_body, owners, studs)
-    turned = shape(width // studs, slots, bf16)
-    ours, *known = [
-        kernel(ahead, [turned] + state, (*group, weights[2], second), 0) for group in (rows, *mates)
-    ]
-    sums = (second, second_in, first, first_in)
-    sums, all_counts, known, ours = lax.optimization_barrier((sums, all_counts, known, ours))
-    (scaled,) = kernel(scale_body, [shape(slots, actions, bf16)], (*sums, *tags, *all_counts), 0)
-    work = 6 * slots * width * units
+        second, second_out = kernel(pair_body, [half, packed], (second, second_in), 0)
+        second_in = cross(second_out, back)
+        first, first_out = kernel(pair_body, [half, packed], (first, first_in, second), 0)
+        first_in = cross(first_out, there)
+    ahead = functools.partial(ahead_body, owners, studs, 2)
+    *ours, chosen = kernel(
+        ahead, state * 2 + [shape(actions // studs, actions, bf16)], (*rows, weights[2], first), 0
+    )
+    known = [ours] + [kernel(ahead, state * 2, (*theirs, weights[2], first), 0) for theirs in mates]
     grads = [shape(width // studs, units, f32), shape(actions // studs, units, f32)]
     heights = [g.shape[0] // owners for g in grads]
     blocks = [shape(sum(heights), units, f32)] + [shape(sum(heights), units, bf16)] * (owners - 1)
-    errors = [scaled] + [send(scaled, "stud", k) for k in range(1, studs)]
-    states = [ours] + known
-    sums = []
-    for k, (error, state) in enumerate(zip(errors, states)):
-        sums = kernel(
-            functools.partial(backward_body, owners, studs, k > 0),
-            blocks if k == studs - 1 else grads,
-            (error, *state, weights[3], *sums),
-            work,
+
+    def scale(part, own, arrived):
+        (scaled,) = kernel(
+            scale_body, [shape(height, actions, bf16)], (own, arrived, tags[part], *all_counts), 0
         )
+        return [scaled] + [send(scaled, "stud", k) for k in range(1, studs)]
+
+    def backward(k, part, sums, last=False):
+        return kernel(
+            functools.partial(backward_body, owners, len(sums) > 0),
+            blocks if last else grads,
+            (errors[part][k], *known[k][3 * part : 3 * part + 3], chosen, weights[3], *sums),
+            0,
+        )
+
+    errors = {1: scale(1, second, second_in)}
+    sums = backward(0, 1, [])
+    first_in, known, chosen, sums = lax.optimization_barrier((first_in, known, chosen, sums))
+    errors[0] = scale(0, first, first_in)
+    order = [(0, 0)] + [(k, part) for k in range(1, studs) for part in (1, 0)]
+    for k, part in order:
+        sums = backward(k, part, sums, (k, part) == order[-1])
     pieces = [sums[0]] + [send(sums[k], "teach", k) for k in range(owners - 1, 0, -1)]
     outs = [shape(h, units, f32) for h in heights]
     return kernel(

time: 34.9 us -> 35.4 us (1.014)
  waiting for transfers between devices: 10 us -> 8.45 us
  Pallas kernels: 6.37 us -> 7.65 us
  starting transfers between devices: 17.5 us -> 18.2 us
    ppermute x14 -> x15, waiting for transfers between devices: 10 us -> 8.45 us  [send(): lax.ppermute(block, axis, [(i, partner_to(size, i, step)) for i in range(...]
    pallas_call x11 -> x15, Pallas kernels: 6.37 us -> 7.65 us  [kernel(): pl.pallas_call(body, out_shape=outs, in_specs=places or [VMEM] * len(oper...]
    ppermute x14 -> x15, starting transfers between devices: 17.5 us -> 18.2 us  [send(): lax.ppermute(block, axis, [(i, partner_to(size, i, step)) for i in range(...]
  transfers between devices with their start and end apart: 14 -> 15, of which waited for: 9 -> 9; matrix products, arithmetic and copies ran while one was open for 0% -> 0% of each run, Pallas kernels for 10% -> 15%
where the time goes in v16:
time: 35.4 us; the launch traced here: 35.3 us
  starting transfers between devices  18.2 us (51%)
  waiting for transfers between devices  8.45 us (24%)
  Pallas kernels  7.65 us (22%)
  between operations  0.82 us (2%)
    ppermute x15, starting transfers between devices, send(): lax.ppermute(block, axis, [(i, partner_to(size, i, step)) for i in range(...  18.2 us
    ppermute x15, waiting for transfers between devices, send(): lax.ppermute(block, axis, [(i, partner_to(size, i, step)) for i in range(...  8.45 us
    pallas_call x15, Pallas kernels, kernel(): pl.pallas_call(body, out_shape=outs, in_specs=places or [VMEM] * len(oper...  7.65 us
  transfers between devices with their start and end apart: 15, of which 9 were waited for; matrix products, arithmetic and copies ran while one was open for 0% of the time, Pallas kernels for 15%

profile of v16, /device:TPU:0, one launch (start us, length us, event | category | flops | bytes accessed | tf_op | source)
XLA Modules:
  0.0 35.3 jit_solution(9496173986739571276)
XLA Ops:
  0.6 1.2 %shard_map.86 = (bf16[48,640]{1,0:T(8,128)(2,1)S(1)}, bf16[48,640]{1,0:T(8,128)(2,1)S(1)}, bf16[48,640]{1,0:T(8,128)(2,1)S(1)}, bf16[48,640]{1,0:T(8,128)(2,1)S(1)}) custom-call(bf16[128,512]{1,0:T(8,128)(2,1)} %refs_0_.1, s32[1,128]{1,0:T(1,128)} %bitcast.2, s32[1,128]{1,0:T(1,128)} %bitcast.3), custom_call_target="tpu_custom_call" | custom-call | flops 25165824 | tf_op jit(solution)/shard_map/pallas_call | solution.py:236
  1.8 4.0 %collective-permute-start.2 = (bf16[48,640]{1,0:T(8,128)(2,1)S(1)}, bf16[48,640]{1,0:T(8,128)(2,1)S(1)}, u32[]{:S(2)}, u32[]{:S(2)}) collective-permute-start(bf16[48,640]{1,0:T(8,128)(2,1)S(1)} %get-tuple-element.68), channel_id=1, source_target_pairs={{0,24},{8,16},{16,8},{24,0},{1,25},{9,17},{17,9},{25,1},{2,26},{10... | collective-permute-start | bytes 184328 | tf_op jit(solution)/shard_map/ppermute | solution.py:39
  5.8 0.5 %collective-permute-start = (bf16[48,640]{1,0:T(8,128)(2,1)S(1)}, bf16[48,640]{1,0:T(8,128)(2,1)S(1)}, u32[]{:S(2)}, u32[]{:S(2)}) collective-permute-start(bf16[48,640]{1,0:T(8,128)(2,1)S(1)} %get-tuple-element.65), channel_id=1, source_target_pairs={{0,16},{8,24},{16,0},{24,8},{1,17},{9,25},{17,1},{25,9},{2,18},{10... | collective-permute-start | bytes 184328 | tf_op jit(solution)/shard_map/ppermute | solution.py:39
  6.4 1.2 %shard_map.87 = (bf16[1,512,256]{2,1,0:T(8,128)(2,1)S(1)}, bf16[1,256,512]{2,1,0:T(8,128)(2,1)S(1)}, bf16[512,256]{1,0:T(8,128)(2,1)S(1)}, bf16[512,256]{1,0:T(8,128)(2,1)S(1)}) custom-call(bf16[48,640]{1,0:T(8,128)(2,1)S(1)} %get-tuple-element.67.refs_0_, bf16[1,512,256]{2,1,0:T(8,128)(2,1)} %refs_1_.1, bf16[1,256,512]{2,1,0:T(8,128)(2,1)} %refs_2_.1, ...), custom_call_target="tpu_custom_call" | custom-call | tf_op jit(solution)/shard_map/pallas_call | solution.py:236
  7.7 0.3 collective-permute-done.2.refs_1_
  8.0 0.5 %shard_map.88 = (f32[96,128]{1,0:T(8,128)S(1)}, f32[1,128]{1,0:T(1,128)S(1)}, f32[96,512]{1,0:T(8,128)S(1)}, f32[104,512]{1,0:T(8,128)S(1)}, bf16[96,512]{1,0:T(8,128)(2,1)S(1)}) custom-call(bf16[48,640]{1,0:T(8,128)(2,1)S(1)} %get-tuple-element.67.refs_0_, bf16[48,640]{1,0:T(8,128)(2,1)S(1)} %collective-permute-done.2.refs_1_, ...), custom_call_target="tpu_custom_call" | custom-call | tf_op jit(solution)/shard_map/pallas_call | solution.py:236
  8.6 3.2 %collective-permute-start.4 = (f16[104,512]{1,0:T(8,128)(2,1)S(1)}, f16[104,512]{1,0:T(8,128)(2,1)S(1)}, u32[]{:S(2)}, u32[]{:S(2)}) collective-permute-start(f16[104,512]{1,0:T(8,128)(2,1)S(1)} %convert_element_type.26), channel_id=1, source_target_pairs={{0,2},{1,3},{2,0},{3,1},{4,6},{5,7},{6,4},{7,5},{8,10},{9,11},{10,... | collective-permute-start | bytes 319496 | tf_op jit(solution)/shard_map/ppermute | solution.py:39
  11.8 0.5 %shard_map.89 = (f32[96,128]{1,0:T(8,128)S(1)}, f32[1,128]{1,0:T(1,128)S(1)}, f32[96,512]{1,0:T(8,128)S(1)}, f32[104,512]{1,0:T(8,128)S(1)}, bf16[96,512]{1,0:T(8,128)(2,1)S(1)}) custom-call(bf16[48,640]{1,0:T(8,128)(2,1)S(1)} %collective-permute-done.refs_0_, bf16[48,640]{1,0:T(8,128)(2,1)S(1)} %collective-permute-done.1.refs_1_, ...), custom_call_target="tpu_custom_call" | custom-call | tf_op jit(solution)/shard_map/pallas_call | solution.py:236
  12.3 1.6 %collective-permute-start.3 = (f16[104,512]{1,0:T(8,128)(2,1)S(1)}, f16[104,512]{1,0:T(8,128)(2,1)S(1)}, u32[]{:S(2)}, u32[]{:S(2)}) collective-permute-start(f16[104,512]{1,0:T(8,128)(2,1)S(1)} %convert_element_type.24), channel_id=1, source_target_pairs={{0,1},{1,0},{2,3},{3,2},{4,5},{5,4},{6,7},{7,6},{8,9},{9,8},{10,11... | collective-permute-start | bytes 319496 | tf_op jit(solution)/shard_map/ppermute | solution.py:39
  14.0 0.5 %collective-permute-start.7 = (bf16[96,512]{1,0:T(8,128)(2,1)S(1)}, bf16[96,512]{1,0:T(8,128)(2,1)S(1)}, u32[]{:S(2)}, u32[]{:S(2)}) collective-permute-start(bf16[96,512]{1,0:T(8,128)(2,1)S(1)} %get-tuple-element.80.refs_1_), channel_id=1, source_target_pairs={{0,4},{4,0},{1,5},{5,1},{2,6},{6,2},{3,7},{7,3},{8,12},{12,8},{9,1... | collective-permute-start | bytes 294920 | tf_op jit(solution)/shard_map/ppermute | solution.py:39
  14.5 0.3 collective-permute-done.4
  14.8 0.8 %collective-permute-done.5.refs_1_ = f32[1,128]{1,0:T(1,128)S(1)} collective-permute-done((f32[1,128]{1,0:T(1,128)S(1)}, f32[1,128]{1,0:T(1,128)S(1)}, u32[]{:S(2)}, u32[]{:S(2)}) %collective-permute-start.5) | collective-permute-done | bytes 544 | tf_op jit(solution)/shard_map/ppermute | solution.py:39
  15.6 0.2 shard_map.90
  15.8 1.6 %collective-permute-start.9 = (f16[104,512]{1,0:T(8,128)(2,1)S(1)}, f16[104,512]{1,0:T(8,128)(2,1)S(1)}, u32[]{:S(2)}, u32[]{:S(2)}) collective-permute-start(f16[104,512]{1,0:T(8,128)(2,1)S(1)} %convert_element_type.30), channel_id=1, source_target_pairs={{0,1},{1,0},{2,3},{3,2},{4,5},{5,4},{6,7},{7,6},{8,9},{9,8},{10,11... | collective-permute-start | bytes 319496 | tf_op jit(solution)/shard_map/ppermute | solution.py:39
  17.5 0.2 shard_map.91
  17.7 3.0 %collective-permute-start.8 = (f16[104,512]{1,0:T(8,128)(2,1)S(1)}, f16[104,512]{1,0:T(8,128)(2,1)S(1)}, u32[]{:S(2)}, u32[]{:S(2)}) collective-permute-start(f16[104,512]{1,0:T(8,128)(2,1)S(1)} %convert_element_type.28), channel_id=1, source_target_pairs={{0,2},{1,3},{2,0},{3,1},{4,6},{5,7},{6,4},{7,5},{8,10},{9,11},{10,... | collective-permute-start | bytes 319496 | tf_op jit(solution)/shard_map/ppermute | solution.py:39
  20.7 0.4 %shard_map.92 = (bf16[256,96]{1,0:T(8,128)(2,1)S(1)}, bf16[96,256]{1,0:T(8,128)(2,1)S(1)}, f32[96,256]{1,0:T(8,128)S(1)}, bf16[256,96]{1,0:T(8,128)(2,1)S(1)}, b...) custom-call(bf16[96,512]{1,0:T(8,128)(2,1)S(1)} %get-tuple-element.79.refs_0_, ...), custom_call_target="tpu_custom_call" | custom-call | tf_op jit(solution)/shard_map/pallas_call | solution.py:236
  21.1 0.4 %shard_map.93 = (bf16[256,96]{1,0:T(8,128)(2,1)S(1)}, bf16[96,256]{1,0:T(8,128)(2,1)S(1)}, f32[96,256]{1,0:T(8,128)S(1)}, bf16[256,96]{1,0:T(8,128)(2,1)S(1)}, b...) custom-call(bf16[96,512]{1,0:T(8,128)(2,1)S(1)} %collective-permute-done.6.refs_0_, ...), custom_call_target="tpu_custom_call" | custom-call | tf_op jit(solution)/shard_map/pallas_call | solution.py:236
  21.5 0.6 %collective-permute-done.9 = f16[104,512]{1,0:T(8,128)(2,1)S(1)} collective-permute-done((f16[104,512]{1,0:T(8,128)(2,1)S(1)}, f16[104,512]{1,0:T(8,128)(2,1)S(1)}, u32[]{:S(2)}, u32[]{:S(2)}) %collective-permute-start.9) | collective-permute-done | bytes 106528 | tf_op jit(solution)/shard_map/ppermute | solution.py:39
  22.4 0.6 %shard_map.95 = (f32[256,256]{1,0:T(8,128)S(1)}, f32[256,256]{1,0:T(8,128)S(1)}) custom-call(bf16[96,512]{1,0:T(8,128)(2,1)S(1)} %shard_map.94.scaled, bf16[256,96]{1,0:T(8,128)(2,1)S(1)} %get-tuple-element.88.turned, bf16[96,256]{1,0:T(8,128)(2,1)S(1)} %get-tuple-element.89.act, f32[96,256]{1,0:T(8,128)S(1)} %get-tuple-element.90.slope, ...), custom_call_target="tpu_custom_call" | custom-call | tf_op jit(solution)/shard_map/pallas_call | solution.py:236
  23.0 1.9 %collective-permute-done.8 = f16[104,512]{1,0:T(8,128)(2,1)S(1)} collective-permute-done((f16[104,512]{1,0:T(8,128)(2,1)S(1)}, f16[104,512]{1,0:T(8,128)(2,1)S(1)}, u32[]{:S(2)}, u32[]{:S(2)}) %collective-permute-start.8) | collective-permute-done | bytes 106528 | tf_op jit(solution)/shard_map/ppermute | solution.py:39
  25.2 0.4 %shard_map.97 = (f32[256,256]{1,0:T(8,128)S(1)}, f32[256,256]{1,0:T(8,128)S(1)}) custom-call(bf16[96,512]{1,0:T(8,128)(2,1)S(1)} %shard_map.96.scaled, bf16[256,96]{1,0:T(8,128)(2,1)S(1)} %get-tuple-element.115.turned, bf16[96,256]{1,0:T(8,128)(2,1)S(1)} %get-tuple-element.116.act, f32[96,256]{1,0:T(8,128)S(1)} %get-tuple-element.117.slope, ...), custom_call_target="tpu_custom_call" | custom-call | tf_op jit(solution)/shard_map/pallas_call | solution.py:236
  25.6 0.4 %shard_map.98 = (f32[256,256]{1,0:T(8,128)S(1)}, f32[256,256]{1,0:T(8,128)S(1)}) custom-call(bf16[96,512]{1,0:T(8,128)(2,1)S(1)} %collective-permute-done.11.scaled, bf16[256,96]{1,0:T(8,128)(2,1)S(1)} %get-tuple-element.112.turned, bf16[96,256]{1,0:T(8,128)(2,1)S(1)} %get-tuple-element.113.act, f32[96,256]{1,0:T(8,128)S(1)} %get-tuple-element.114.slope, ...), custom_call_target="tpu_custom_call" | custom-call | tf_op jit(solution)/shard_map/pallas_call | solution.py:236
  26.1 0.4 %collective-permute-done.10.scaled = bf16[96,512]{1,0:T(8,128)(2,1)S(1)} collective-permute-done((bf16[96,512]{1,0:T(8,128)(2,1)S(1)}, bf16[96,512]{1,0:T(8,128)(2,1)S(1)}, u32[]{:S(2)}, u32[]{:S(2)}) %collective-permute-start.10) | collective-permute-done | bytes 98336 | tf_op jit(solution)/shard_map/ppermute | solution.py:39
  26.5 0.4 %shard_map.99 = (f32[128,256]{1,0:T(8,128)S(1)}, bf16[128,256]{1,0:T(8,128)(2,1)S(1)}, bf16[128,256]{1,0:T(8,128)(2,1)S(1)}, bf16[128,256]{1,0:T(8,128)(2,1)S(1)}) custom-call(bf16[96,512]{1,0:T(8,128)(2,1)S(1)} %collective-permute-done.10.scaled, bf16[256,96]{1,0:T(8,128)(2,1)S(1)} %get-tuple-element.108.turned, ...), custom_call_target="tpu_custom_call" | custom-call | tf_op jit(solution)/shard_map/pallas_call | solution.py:236
  26.9 2.7 %collective-permute-start.12 = (bf16[128,256]{1,0:T(8,128)(2,1)S(1)}, bf16[128,256]{1,0:T(8,128)(2,1)S(1)}, u32[]{:S(2)}, u32[]{:S(2)}) collective-permute-start(bf16[128,256]{1,0:T(8,128)(2,1)S(1)} %get-tuple-element.125), channel_id=1, source_target_pairs={{0,24},{8,16},{16,8},{24,0},{1,25},{9,17},{17,9},{25,1},{2,26},{10... | collective-permute-start | bytes 196616 | tf_op jit(solution)/shard_map/ppermute | solution.py:39
  29.7 0.7 %collective-permute-start.13 = (bf16[128,256]{1,0:T(8,128)(2,1)S(1)}, bf16[128,256]{1,0:T(8,128)(2,1)S(1)}, u32[]{:S(2)}, u32[]{:S(2)}) collective-permute-start(bf16[128,256]{1,0:T(8,128)(2,1)S(1)} %get-tuple-element.126), channel_id=1, source_target_pairs={{0,16},{8,24},{16,0},{24,8},{1,17},{9,25},{17,1},{25,9},{2,18},{10... | collective-permute-start | bytes 196616 | tf_op jit(solution)/shard_map/ppermute | solution.py:39
  30.3 0.2 collective-permute-start.14
  30.5 1.7 %collective-permute-done.12.refs_1_ = bf16[128,256]{1,0:T(8,128)(2,1)S(1)} collective-permute-done((bf16[128,256]{1,0:T(8,128)(2,1)S(1)}, bf16[128,256]{1,0:T(8,128)(2,1)S(1)}, u32[]{:S(2)}, u32[]{:S(2)}) %collective-permute-start.12) | collective-permute-done | bytes 65568 | tf_op jit(solution)/shard_map/ppermute | solution.py:39
  32.2 1.8 %collective-permute-done.13.refs_2_ = bf16[128,256]{1,0:T(8,128)(2,1)S(1)} collective-permute-done((bf16[128,256]{1,0:T(8,128)(2,1)S(1)}, bf16[128,256]{1,0:T(8,128)(2,1)S(1)}, u32[]{:S(2)}, u32[]{:S(2)}) %collective-permute-start.13) | collective-permute-done | bytes 65568 | tf_op jit(solution)/shard_map/ppermute | solution.py:39
  33.9 0.7 %collective-permute-done.14.refs_3_ = bf16[128,256]{1,0:T(8,128)(2,1)S(1)} collective-permute-done((bf16[128,256]{1,0:T(8,128)(2,1)S(1)}, bf16[128,256]{1,0:T(8,128)(2,1)S(1)}, u32[]{:S(2)}, u32[]{:S(2)}) %collective-permute-start.14) | collective-permute-done | bytes 65568 | tf_op jit(solution)/shard_map/ppermute | solution.py:39
  34.6 0.7 %shard_map.100 = (f32[64,256]{1,0:T(8,128)}, f32[64,256]{1,0:T(8,128)}) custom-call(f32[128,256]{1,0:T(8,128)S(1)} %get-tuple-element.124.refs_0_, bf16[128,256]{1,0:T(8,128)(2,1)S(1)} %collective-permute-done.12.refs_1_, bf16[128,256]{1,0:T(8,128)(2,1)S(1)} %collective-permute-done.13.refs_2_, bf16[128,256]{1,0:T(8,128)(2,1)S(1)} %collective-permute-done.14.refs_3_), custom_call_target="tpu_custom_call" | custom-call | tf_op jit(solution)/shard_map/pallas_call | solution.py:236
  (21 shorter events, 0.7 us)
Async XLA Ops:
  1.8 6.2 %collective-permute-start.2 = (bf16[48,640]{1,0:T(8,128)(2,1)S(1)}, bf16[48,640]{1,0:T(8,128)(2,1)S(1)}, u32[]{:S(2)}, u32[]{:S(2)}) collective-permute-start(bf16[48,640]{1,0:T(8,128)(2,1)S(1)} %get-tuple-element.68), channel_id=1, source_target_pairs={{0,24},{8,16},{16,8},{24,0},{1,25},{9,17},{17,9},{25,1},{2,26},{10... | collective-permute-start | bytes 184328 | tf_op jit(solution)/shard_map/ppermute | solution.py:39
  5.8 6.0 %collective-permute-start = (bf16[48,640]{1,0:T(8,128)(2,1)S(1)}, bf16[48,640]{1,0:T(8,128)(2,1)S(1)}, u32[]{:S(2)}, u32[]{:S(2)}) collective-permute-start(bf16[48,640]{1,0:T(8,128)(2,1)S(1)} %get-tuple-element.65), channel_id=1, source_target_pairs={{0,16},{8,24},{16,0},{24,8},{1,17},{9,25},{17,1},{25,9},{2,18},{10... | collective-permute-start | bytes 184328 | tf_op jit(solution)/shard_map/ppermute | solution.py:39
  6.3 5.5 %collective-permute-start.1 = (bf16[48,640]{1,0:T(8,128)(2,1)S(1)}, bf16[48,640]{1,0:T(8,128)(2,1)S(1)}, u32[]{:S(2)}, u32[]{:S(2)}) collective-permute-start(bf16[48,640]{1,0:T(8,128)(2,1)S(1)} %get-tuple-element.66), channel_id=1, source_target_pairs={{0,8},{8,0},{16,24},{24,16},{1,9},{9,1},{17,25},{25,17},{2,10},{10... | collective-permute-start | bytes 184328 | tf_op jit(solution)/shard_map/ppermute | solution.py:39
  8.6 6.2 %collective-permute-start.4 = (f16[104,512]{1,0:T(8,128)(2,1)S(1)}, f16[104,512]{1,0:T(8,128)(2,1)S(1)}, u32[]{:S(2)}, u32[]{:S(2)}) collective-permute-start(f16[104,512]{1,0:T(8,128)(2,1)S(1)} %convert_element_type.26), channel_id=1, source_target_pairs={{0,2},{1,3},{2,0},{3,1},{4,6},{5,7},{6,4},{7,5},{8,10},{9,11},{10,... | collective-permute-start | bytes 319496 | tf_op jit(solution)/shard_map/ppermute | solution.py:39
  12.3 5.1 %collective-permute-start.3 = (f16[104,512]{1,0:T(8,128)(2,1)S(1)}, f16[104,512]{1,0:T(8,128)(2,1)S(1)}, u32[]{:S(2)}, u32[]{:S(2)}) collective-permute-start(f16[104,512]{1,0:T(8,128)(2,1)S(1)} %convert_element_type.24), channel_id=1, source_target_pairs={{0,1},{1,0},{2,3},{3,2},{4,5},{5,4},{6,7},{7,6},{8,9},{9,8},{10,11... | collective-permute-start | bytes 319496 | tf_op jit(solution)/shard_map/ppermute | solution.py:39
  14.0 1.6 %collective-permute-start.6 = (bf16[96,512]{1,0:T(8,128)(2,1)S(1)}, bf16[96,512]{1,0:T(8,128)(2,1)S(1)}, u32[]{:S(2)}, u32[]{:S(2)}) collective-permute-start(bf16[96,512]{1,0:T(8,128)(2,1)S(1)} %get-tuple-element.79.refs_0_), channel_id=1, source_target_pairs={{0,4},{4,0},{1,5},{5,1},{2,6},{6,2},{3,7},{7,3},{8,12},{12,8},{9,1... | collective-permute-start | bytes 294920 | tf_op jit(solution)/shard_map/ppermute | solution.py:39
  14.0 1.6 %collective-permute-start.7 = (bf16[96,512]{1,0:T(8,128)(2,1)S(1)}, bf16[96,512]{1,0:T(8,128)(2,1)S(1)}, u32[]{:S(2)}, u32[]{:S(2)}) collective-permute-start(bf16[96,512]{1,0:T(8,128)(2,1)S(1)} %get-tuple-element.80.refs_1_), channel_id=1, source_target_pairs={{0,4},{4,0},{1,5},{5,1},{2,6},{6,2},{3,7},{7,3},{8,12},{12,8},{9,1... | collective-permute-start | bytes 294920 | tf_op jit(solution)/shard_map/ppermute | solution.py:39
  14.5 1.1 %collective-permute-start.5 = (f32[1,128]{1,0:T(1,128)S(1)}, f32[1,128]{1,0:T(1,128)S(1)}, u32[]{:S(2)}, u32[]{:S(2)}) collective-permute-start(f32[1,128]{1,0:T(1,128)S(1)} %get-tuple-element.102.refs_0_), channel_id=1, source_target_pairs={{0,4},{4,0},{1,5},{5,1},{2,6},{6,2},{3,7},{7,3},{8,12},{12,8},{9,1... | collective-permute-start | bytes 1544 | tf_op jit(solution)/shard_map/ppermute | solution.py:39
  15.8 6.3 %collective-permute-start.9 = (f16[104,512]{1,0:T(8,128)(2,1)S(1)}, f16[104,512]{1,0:T(8,128)(2,1)S(1)}, u32[]{:S(2)}, u32[]{:S(2)}) collective-permute-start(f16[104,512]{1,0:T(8,128)(2,1)S(1)} %convert_element_type.30), channel_id=1, source_target_pairs={{0,1},{1,0},{2,3},{3,2},{4,5},{5,4},{6,7},{7,6},{8,9},{9,8},{10,11... | collective-permute-start | bytes 319496 | tf_op jit(solution)/shard_map/ppermute | solution.py:39
  17.7 7.2 %collective-permute-start.8 = (f16[104,512]{1,0:T(8,128)(2,1)S(1)}, f16[104,512]{1,0:T(8,128)(2,1)S(1)}, u32[]{:S(2)}, u32[]{:S(2)}) collective-permute-start(f16[104,512]{1,0:T(8,128)(2,1)S(1)} %convert_element_type.28), channel_id=1, source_target_pairs={{0,2},{1,3},{2,0},{3,1},{4,6},{5,7},{6,4},{7,5},{8,10},{9,11},{10,... | collective-permute-start | bytes 319496 | tf_op jit(solution)/shard_map/ppermute | solution.py:39
  22.3 3.3 %collective-permute-start.11 = (bf16[96,512]{1,0:T(8,128)(2,1)S(1)}, bf16[96,512]{1,0:T(8,128)(2,1)S(1)}, u32[]{:S(2)}, u32[]{:S(2)}) collective-permute-start(bf16[96,512]{1,0:T(8,128)(2,1)S(1)} %shard_map.94.scaled), channel_id=1, source_target_pairs={{0,4},{4,0},{1,5},{5,1},{2,6},{6,2},{3,7},{7,3},{8,12},{12,8},{9,1... | collective-permute-start | bytes 294920 | tf_op jit(solution)/shard_map/ppermute | solution.py:39
  25.1 1.4 %collective-permute-start.10 = (bf16[96,512]{1,0:T(8,128)(2,1)S(1)}, bf16[96,512]{1,0:T(8,128)(2,1)S(1)}, u32[]{:S(2)}, u32[]{:S(2)}) collective-permute-start(bf16[96,512]{1,0:T(8,128)(2,1)S(1)} %shard_map.96.scaled), channel_id=1, source_target_pairs={{0,4},{4,0},{1,5},{5,1},{2,6},{6,2},{3,7},{7,3},{8,12},{12,8},{9,1... | collective-permute-start | bytes 294920 | tf_op jit(solution)/shard_map/ppermute | solution.py:39
  26.9 5.2 %collective-permute-start.12 = (bf16[128,256]{1,0:T(8,128)(2,1)S(1)}, bf16[128,256]{1,0:T(8,128)(2,1)S(1)}, u32[]{:S(2)}, u32[]{:S(2)}) collective-permute-start(bf16[128,256]{1,0:T(8,128)(2,1)S(1)} %get-tuple-element.125), channel_id=1, source_target_pairs={{0,24},{8,16},{16,8},{24,0},{1,25},{9,17},{17,9},{25,1},{2,26},{10... | collective-permute-start | bytes 196616 | tf_op jit(solution)/shard_map/ppermute | solution.py:39
  29.7 4.3 %collective-permute-start.13 = (bf16[128,256]{1,0:T(8,128)(2,1)S(1)}, bf16[128,256]{1,0:T(8,128)(2,1)S(1)}, u32[]{:S(2)}, u32[]{:S(2)}) collective-permute-start(bf16[128,256]{1,0:T(8,128)(2,1)S(1)} %get-tuple-element.126), channel_id=1, source_target_pairs={{0,16},{8,24},{16,0},{24,8},{1,17},{9,25},{17,1},{25,9},{2,18},{10... | collective-permute-start | bytes 196616 | tf_op jit(solution)/shard_map/ppermute | solution.py:39
  30.3 4.3 %collective-permute-start.14 = (bf16[128,256]{1,0:T(8,128)(2,1)S(1)}, bf16[128,256]{1,0:T(8,128)(2,1)S(1)}, u32[]{:S(2)}, u32[]{:S(2)}) collective-permute-start(bf16[128,256]{1,0:T(8,128)(2,1)S(1)} %get-tuple-element.127), channel_id=1, source_target_pairs={{0,8},{8,0},{16,24},{24,16},{1,9},{9,1},{17,25},{25,17},{2,10},{10... | collective-permute-start | bytes 196616 | tf_op jit(solution)/shard_map/ppermute | solution.py:39

commit v17 on v16

--- a/solution.py
+++ b/solution.py
@@ -61,15 +61,15 @@
 
 
 def dispatch_body(owners, local, room, extra, *refs):
-    sources, refs = refs[:3], refs[3:]
+    sources, refs = refs[:7], refs[7:]
     outs, refs = refs[:owners], refs[owners:]
-    states, task, batch, sems = refs
+    weights, (states, task, batch, sems) = refs[:4], refs[4:]
     rows, width = states.shape
     copies = [
         pltpu.make_async_copy(source, target, sems.at[i])
-        for i, (source, target) in enumerate(zip(sources, (states, task, batch)))
+        for i, (source, target) in enumerate(zip(sources, (states, task, batch, *weights)))
     ]
-    for i in (1, 2, 0):
+    for i in (1, 2, 0, 3, 4, 5, 6):
         copies[i].start()
     copies[1].wait()
     copies[2].wait()
@@ -100,17 +100,7 @@
         span = slice(k * local * room, (k + 1) * local * room)
         out[:, :width] = moved[span]
         out[:, width:] = tags[span]
-
-
-def weights_body(*refs):
-    sources, outs, sems = refs[1:5], refs[5:9], refs[9]
-    copies = [
-        pltpu.make_async_copy(source, target, sems.at[i])
-        for i, (source, target) in enumerate(zip(sources, outs))
-    ]
-    for copy in copies:
-        copy.start()
-    for copy in copies:
+    for copy in copies[3:]:
         copy.wait()
 
 
@@ -182,11 +172,13 @@
         outs[-1][...] = chosen_columns(outs[-1].shape[1], owners, studs)
 
 
-def pair_body(own, arrived, *refs):
-    total, packed = refs[-2:]
-    value = own[...] + unpack(arrived)
-    total[...] = value
-    pack(value, packed)
+def pair_body(*refs):
+    for i in range(2):
+        own, arrived = refs[2 * i : 2 * i + 2]
+        total, packed = refs[2 * i + 4 : 2 * i + 6]
+        value = own[...] + unpack(arrived)
+        total[...] = value
+        pack(value, packed)
 
 
 def scale_body(own, arrived, tags, *refs):
@@ -263,26 +255,22 @@
     half, packed = shape(height, actions, f32), shape(height + PACK_ROWS, actions, f32)
     state = [shape(width // studs, height, bf16), shape(height, units, bf16), shape(height, units, f32)]
     tokens = [ids.reshape(1, row_count) for ids in (task_ids, student_batch)]
-    blocks = kernel(
+    weights = (teach_in, teach_out, student_up, student_down)
+    results = kernel(
         functools.partial(dispatch_body, owners, local, room, extra),
-        [pltpu.VMEM((local * room, width + extra), bf16)] * owners,
-        (states, *tokens),
-        2 * slots * row_count * width,
-        [pltpu.VMEM(a.shape, a.dtype) for a in (states, *tokens)] + [pltpu.SemaphoreType.DMA((3,))],
+        [pltpu.VMEM((local * room, width + extra), bf16)] * owners
+        + [pltpu.VMEM(w.shape, w.dtype) for w in weights],
+        (states, *tokens, *weights),
+        0,
+        [pltpu.VMEM(a.shape, a.dtype) for a in (states, *tokens)] + [pltpu.SemaphoreType.DMA((7,))],
         LARGE,
-        [HBM] * 3,
-    )
-    arrived = {k: send(blocks[k], "teach", k) for k in range(owners - 1, 0, -1)}
-    weights = (teach_in, teach_out, student_up, student_down)
-    weights = kernel(
-        weights_body,
-        [pltpu.VMEM(w.shape, w.dtype) for w in weights],
-        (blocks[0], *[pltpu.with_memory_space_constraint(w, pltpu.HBM) for w in weights]),
-        0,
-        [pltpu.SemaphoreType.DMA((4,))],
-        SMALL,
-        [VMEM] + [HBM] * 4,
-    )
+        [HBM] * 7,
+    )
+    blocks, weights = results[:owners], results[owners:]
+    middle = owners // 2
+    near = [blocks[0]] + [send(blocks[k], "teach", k) for k in range(1, middle)]
+    far = [send(blocks[k], "teach", k) for k in range(owners - 1, middle - 1, -1)]
+
     def forward(blocks, *earlier):
         rows = len(blocks) * local * room
         return kernel(
@@ -293,8 +281,6 @@
         )
 
     steps = [1 << i for i in range(parts.bit_length() - 1)]
-    blocks = [blocks[0]] + list(arrived.values())
-    near, far = blocks[: owners // 2], blocks[owners // 2 :]
     second_tags, counts, second, second_out, second_rows = forward(near)
     second_in = cross(second_out, steps[-1])
     first_tags, counts, first, first_out, first_rows = forward(far, counts)
@@ -304,12 +290,14 @@
     for k in range(1, studs):
         all_counts.append(send(counts, "stud", k))
         mates.append([send(part, "stud", k) for part in rows])
-    second_in, all_counts, mates = lax.optimization_barrier((second_in, all_counts, mates))
+    first_in, second_in, all_counts, mates = lax.optimization_barrier(
+        (first_in, second_in, all_counts, mates)
+    )
     for there, back in zip(steps[1:], steps[-2::-1]):
-        second, second_out = kernel(pair_body, [half, packed], (second, second_in), 0)
-        second_in = cross(second_out, back)
-        first, first_out = kernel(pair_body, [half, packed], (first, first_in, second), 0)
-        first_in = cross(first_out, there)
+        first, first_out, second, second_out = kernel(
+            pair_body, [half, packed] * 2, (first, first_in, second, second_in), 0
+        )
+        first_in, second_in = cross(first_out, there), cross(second_out, back)
     ahead = functools.partial(ahead_body, owners, studs, 2)
     *ours, chosen = kernel(
         ahead, state * 2 + [shape(actions // studs, actions, bf16)], (*rows, weights[2], first), 0
@@ -333,11 +321,11 @@
             0,
         )
 
-    errors = {1: scale(1, second, second_in)}
-    sums = backward(0, 1, [])
-    first_in, known, chosen, sums = lax.optimization_barrier((first_in, known, chosen, sums))
-    errors[0] = scale(0, first, first_in)
-    order = [(0, 0)] + [(k, part) for k in range(1, studs) for part in (1, 0)]
+    errors = {0: scale(0, first, first_in)}
+    sums = backward(0, 0, [])
+    second_in, known, chosen, sums = lax.optimization_barrier((second_in, known, chosen, sums))
+    errors[1] = scale(1, second, second_in)
+    order = [(0, 1)] + [(k, part) for k in range(1, studs) for part in (0, 1)]
     for k, part in order:
         sums = backward(k, part, sums, (k, part) == order[-1])
     pieces = [sums[0]] + [send(sums[k], "teach", k) for k in range(owners - 1, 0, -1)]

time: 35.4 us -> 35.3 us (level)
  Pallas kernels: 7.65 us -> 6.38 us
  waiting for transfers between devices: 8.45 us -> 9.08 us
  starting transfers between devices: 18.2 us -> 18.7 us
    pallas_call x15 -> x13, Pallas kernels: 7.65 us -> 6.38 us  [kernel(): pl.pallas_call(body, out_shape=outs, in_specs=places or [VMEM] * len(oper...]
    ppermute x15, waiting for transfers between devices: 8.45 us -> 9.08 us  [send(): lax.ppermute(block, axis, [(i, partner_to(size, i, step)) for i in range(...]
    ppermute x15, starting transfers between devices: 18.2 us -> 18.7 us  [send(): lax.ppermute(block, axis, [(i, partner_to(size, i, step)) for i in range(...]
  transfers between devices with their start and end apart: 15 -> 15, of which waited for: 9 -> 7; matrix products, arithmetic and copies ran while one was open for 0% -> 0% of each run, Pallas kernels for 15% -> 10%
where the time goes in v17:
time: 35.3 us; the launch traced here: 35.1 us
  starting transfers between devices  18.7 us (53%)
  waiting for transfers between devices  9.08 us (26%)
  Pallas kernels  6.38 us (18%)
  between operations  0.83 us (2%)
    ppermute x15, starting transfers between devices, send(): lax.ppermute(block, axis, [(i, partner_to(size, i, step)) for i in range(...  18.7 us
    ppermute x15, waiting for transfers between devices, send(): lax.ppermute(block, axis, [(i, partner_to(size, i, step)) for i in range(...  9.08 us
    pallas_call x13, Pallas kernels, kernel(): pl.pallas_call(body, out_shape=outs, in_specs=places or [VMEM] * len(oper...  6.38 us
  transfers between devices with their start and end apart: 15, of which 7 were waited for; matrix products, arithmetic and copies ran while one was open for 0% of the time, Pallas kernels for 10%

profile of v17, /device:TPU:0, one launch (start us, length us, event | category | flops | bytes accessed | tf_op | source)
XLA Modules:
  0.0 35.1 jit_solution(16325813079685085839)
XLA Ops:
  0.6 1.3 %shard_map.86 = (bf16[48,640]{1,0:T(8,128)(2,1)S(1)}, bf16[48,640]{1,0:T(8,128)(2,1)S(1)}, bf16[48,640]{1,0:T(8,128)(2,1)S(1)}, bf16[48,640]{1,0:T(8,128)(2,1)S(...) custom-call(bf16[128,512]{1,0:T(8,128)(2,1)} %refs_0_.1, ...), custom_call_target="tpu_custom_call" | custom-call | tf_op jit(solution)/shard_map/pallas_call | solution.py:228
  2.0 3.0 %collective-permute-start.2 = (bf16[48,640]{1,0:T(8,128)(2,1)S(1)}, bf16[48,640]{1,0:T(8,128)(2,1)S(1)}, u32[]{:S(2)}, u32[]{:S(2)}) collective-permute-start(bf16[48,640]{1,0:T(8,128)(2,1)S(1)} %get-tuple-element.69), channel_id=1, source_target_pairs={{0,8},{8,0},{16,24},{24,16},{1,9},{9,1},{17,25},{25,17},{2,10},{10... | collective-permute-start | bytes 184328 | tf_op jit(solution)/shard_map/ppermute | solution.py:39
  5.0 1.5 %collective-permute-start = (bf16[48,640]{1,0:T(8,128)(2,1)S(1)}, bf16[48,640]{1,0:T(8,128)(2,1)S(1)}, u32[]{:S(2)}, u32[]{:S(2)}) collective-permute-start(bf16[48,640]{1,0:T(8,128)(2,1)S(1)} %get-tuple-element.66), channel_id=1, source_target_pairs={{0,24},{8,16},{16,8},{24,0},{1,25},{9,17},{17,9},{25,1},{2,26},{10... | collective-permute-start | bytes 184328 | tf_op jit(solution)/shard_map/ppermute | solution.py:39
  6.5 0.8 %collective-permute-done.2.refs_1_ = bf16[48,640]{1,0:T(8,128)(2,1)S(1)} collective-permute-done((bf16[48,640]{1,0:T(8,128)(2,1)S(1)}, bf16[48,640]{1,0:T(8,128)(2,1)S(1)}, u32[]{:S(2)}, u32[]{:S(2)}) %collective-permute-start.2) | collective-permute-done | bytes 61472 | tf_op jit(solution)/shard_map/ppermute | solution.py:39
  7.3 0.5 %shard_map.87 = (f32[96,128]{1,0:T(8,128)S(1)}, f32[1,128]{1,0:T(1,128)S(1)}, f32[96,512]{1,0:T(8,128)S(1)}, f32[104,512]{1,0:T(8,128)S(1)}, bf16[96,512]{1,0:T(8,128)(2,1)S(1)}) custom-call(bf16[48,640]{1,0:T(8,128)(2,1)S(1)} %get-tuple-element.68.refs_0_, bf16[48,640]{1,0:T(8,128)(2,1)S(1)} %collective-permute-done.2.refs_1_, ...), custom_call_target="tpu_custom_call" | custom-call | tf_op jit(solution)/shard_map/pallas_call | solution.py:228
  7.9 3.1 %collective-permute-start.4 = (f16[104,512]{1,0:T(8,128)(2,1)S(1)}, f16[104,512]{1,0:T(8,128)(2,1)S(1)}, u32[]{:S(2)}, u32[]{:S(2)}) collective-permute-start(f16[104,512]{1,0:T(8,128)(2,1)S(1)} %convert_element_type.26), channel_id=1, source_target_pairs={{0,2},{1,3},{2,0},{3,1},{4,6},{5,7},{6,4},{7,5},{8,10},{9,11},{10,... | collective-permute-start | bytes 319496 | tf_op jit(solution)/shard_map/ppermute | solution.py:39
  10.9 0.5 %shard_map.88 = (f32[96,128]{1,0:T(8,128)S(1)}, f32[1,128]{1,0:T(1,128)S(1)}, f32[96,512]{1,0:T(8,128)S(1)}, f32[104,512]{1,0:T(8,128)S(1)}, bf16[96,512]{1,0:T(8,128)(2,1)S(1)}) custom-call(bf16[48,640]{1,0:T(8,128)(2,1)S(1)} %collective-permute-done.refs_0_, bf16[48,640]{1,0:T(8,128)(2,1)S(1)} %collective-permute-done.1.refs_1_, ...), custom_call_target="tpu_custom_call" | custom-call | tf_op jit(solution)/shard_map/pallas_call | solution.py:228
  11.5 1.6 %collective-permute-start.3 = (f16[104,512]{1,0:T(8,128)(2,1)S(1)}, f16[104,512]{1,0:T(8,128)(2,1)S(1)}, u32[]{:S(2)}, u32[]{:S(2)}) collective-permute-start(f16[104,512]{1,0:T(8,128)(2,1)S(1)} %convert_element_type.24), channel_id=1, source_target_pairs={{0,1},{1,0},{2,3},{3,2},{4,5},{5,4},{6,7},{7,6},{8,9},{9,8},{10,11... | collective-permute-start | bytes 319496 | tf_op jit(solution)/shard_map/ppermute | solution.py:39
  13.1 0.5 %collective-permute-start.7 = (bf16[96,512]{1,0:T(8,128)(2,1)S(1)}, bf16[96,512]{1,0:T(8,128)(2,1)S(1)}, u32[]{:S(2)}, u32[]{:S(2)}) collective-permute-start(bf16[96,512]{1,0:T(8,128)(2,1)S(1)} %get-tuple-element.80.refs_1_), channel_id=1, source_target_pairs={{0,4},{4,0},{1,5},{5,1},{2,6},{6,2},{3,7},{7,3},{8,12},{12,8},{9,1... | collective-permute-start | bytes 294920 | tf_op jit(solution)/shard_map/ppermute | solution.py:39
  13.7 0.3 collective-permute-done.4
  14.0 2.3 %collective-permute-done.3 = f16[104,512]{1,0:T(8,128)(2,1)S(1)} collective-permute-done((f16[104,512]{1,0:T(8,128)(2,1)S(1)}, f16[104,512]{1,0:T(8,128)(2,1)S(1)}, u32[]{:S(2)}, u32[]{:S(2)}) %collective-permute-start.3) | collective-permute-done | bytes 106528 | tf_op jit(solution)/shard_map/ppermute | solution.py:39
  16.3 0.2 shard_map.89
  16.6 2.5 %collective-permute-start.9 = (f16[104,512]{1,0:T(8,128)(2,1)S(1)}, f16[104,512]{1,0:T(8,128)(2,1)S(1)}, u32[]{:S(2)}, u32[]{:S(2)}) collective-permute-start(f16[104,512]{1,0:T(8,128)(2,1)S(1)} %convert_element_type.30), channel_id=1, source_target_pairs={{0,2},{1,3},{2,0},{3,1},{4,6},{5,7},{6,4},{7,5},{8,10},{9,11},{10,... | collective-permute-start | bytes 319496 | tf_op jit(solution)/shard_map/ppermute | solution.py:39
  19.2 2.2 %collective-permute-start.8 = (f16[104,512]{1,0:T(8,128)(2,1)S(1)}, f16[104,512]{1,0:T(8,128)(2,1)S(1)}, u32[]{:S(2)}, u32[]{:S(2)}) collective-permute-start(f16[104,512]{1,0:T(8,128)(2,1)S(1)} %convert_element_type.28), channel_id=1, source_target_pairs={{0,1},{1,0},{2,3},{3,2},{4,5},{5,4},{6,7},{7,6},{8,9},{9,8},{10,11... | collective-permute-start | bytes 319496 | tf_op jit(solution)/shard_map/ppermute | solution.py:39
  21.4 0.4 %shard_map.90 = (bf16[256,96]{1,0:T(8,128)(2,1)S(1)}, bf16[96,256]{1,0:T(8,128)(2,1)S(1)}, f32[96,256]{1,0:T(8,128)S(1)}, bf16[256,96]{1,0:T(8,128)(2,1)S(1)}, b...) custom-call(bf16[96,512]{1,0:T(8,128)(2,1)S(1)} %get-tuple-element.79.refs_0_, ...), custom_call_target="tpu_custom_call" | custom-call | tf_op jit(solution)/shard_map/pallas_call | solution.py:228
  21.8 0.4 %shard_map.91 = (bf16[256,96]{1,0:T(8,128)(2,1)S(1)}, bf16[96,256]{1,0:T(8,128)(2,1)S(1)}, f32[96,256]{1,0:T(8,128)S(1)}, bf16[256,96]{1,0:T(8,128)(2,1)S(1)}, b...) custom-call(bf16[96,512]{1,0:T(8,128)(2,1)S(1)} %collective-permute-done.6.refs_0_, ...), custom_call_target="tpu_custom_call" | custom-call | tf_op jit(solution)/shard_map/pallas_call | solution.py:228
  22.2 2.0 %collective-permute-done.9 = f16[104,512]{1,0:T(8,128)(2,1)S(1)} collective-permute-done((f16[104,512]{1,0:T(8,128)(2,1)S(1)}, f16[104,512]{1,0:T(8,128)(2,1)S(1)}, u32[]{:S(2)}, u32[]{:S(2)}) %collective-permute-start.9) | collective-permute-done | bytes 106528 | tf_op jit(solution)/shard_map/ppermute | solution.py:39
  24.2 0.1 shard_map.92.scaled
  24.4 0.1 collective-permute-start.11
  24.4 0.6 %shard_map.93 = (f32[256,256]{1,0:T(8,128)S(1)}, f32[256,256]{1,0:T(8,128)S(1)}) custom-call(bf16[96,512]{1,0:T(8,128)(2,1)S(1)} %shard_map.92.scaled, bf16[256,96]{1,0:T(8,128)(2,1)S(1)} %get-tuple-element.87.turned, bf16[96,256]{1,0:T(8,128)(2,1)S(1)} %get-tuple-element.88.act, f32[96,256]{1,0:T(8,128)S(1)} %get-tuple-element.89.slope, ...), custom_call_target="tpu_custom_call" | custom-call | tf_op jit(solution)/shard_map/pallas_call | solution.py:228
  25.1 0.1 shard_map.94.scaled
  25.3 0.6 %collective-permute-start.10 = (bf16[96,512]{1,0:T(8,128)(2,1)S(1)}, bf16[96,512]{1,0:T(8,128)(2,1)S(1)}, u32[]{:S(2)}, u32[]{:S(2)}) collective-permute-start(bf16[96,512]{1,0:T(8,128)(2,1)S(1)} %shard_map.94.scaled), channel_id=1, source_target_pairs={{0,4},{4,0},{1,5},{5,1},{2,6},{6,2},{3,7},{7,3},{8,12},{12,8},{9,1... | collective-permute-start | bytes 294920 | tf_op jit(solution)/shard_map/ppermute | solution.py:39
  25.8 0.4 %shard_map.95 = (f32[256,256]{1,0:T(8,128)S(1)}, f32[256,256]{1,0:T(8,128)S(1)}) custom-call(bf16[96,512]{1,0:T(8,128)(2,1)S(1)} %shard_map.94.scaled, bf16[256,96]{1,0:T(8,128)(2,1)S(1)} %get-tuple-element.117.turned, bf16[96,256]{1,0:T(8,128)(2,1)S(1)} %get-tuple-element.118.act, f32[96,256]{1,0:T(8,128)S(1)} %get-tuple-element.119.slope, ...), custom_call_target="tpu_custom_call" | custom-call | tf_op jit(solution)/shard_map/pallas_call | solution.py:228
  26.3 0.4 %shard_map.96 = (f32[256,256]{1,0:T(8,128)S(1)}, f32[256,256]{1,0:T(8,128)S(1)}) custom-call(bf16[96,512]{1,0:T(8,128)(2,1)S(1)} %collective-permute-done.11.scaled, bf16[256,96]{1,0:T(8,128)(2,1)S(1)} %get-tuple-element.114.turned, bf16[96,256]{1,0:T(8,128)(2,1)S(1)} %get-tuple-element.115.act, f32[96,256]{1,0:T(8,128)S(1)} %get-tuple-element.116.slope, ...), custom_call_target="tpu_custom_call" | custom-call | tf_op jit(solution)/shard_map/pallas_call | solution.py:228
  26.8 0.4 %shard_map.97 = (f32[128,256]{1,0:T(8,128)S(1)}, bf16[128,256]{1,0:T(8,128)(2,1)S(1)}, bf16[128,256]{1,0:T(8,128)(2,1)S(1)}, bf16[128,256]{1,0:T(8,128)(2,1)S(1)}) custom-call(bf16[96,512]{1,0:T(8,128)(2,1)S(1)} %collective-permute-done.10.scaled, bf16[256,96]{1,0:T(8,128)(2,1)S(1)} %get-tuple-element.110.turned, ...), custom_call_target="tpu_custom_call" | custom-call | tf_op jit(solution)/shard_map/pallas_call | solution.py:228
  27.2 2.0 %collective-permute-start.12 = (bf16[128,256]{1,0:T(8,128)(2,1)S(1)}, bf16[128,256]{1,0:T(8,128)(2,1)S(1)}, u32[]{:S(2)}, u32[]{:S(2)}) collective-permute-start(bf16[128,256]{1,0:T(8,128)(2,1)S(1)} %get-tuple-element.127), channel_id=1, source_target_pairs={{0,24},{8,16},{16,8},{24,0},{1,25},{9,17},{17,9},{25,1},{2,26},{10... | collective-permute-start | bytes 196616 | tf_op jit(solution)/shard_map/ppermute | solution.py:39
  29.2 0.9 %collective-permute-start.13 = (bf16[128,256]{1,0:T(8,128)(2,1)S(1)}, bf16[128,256]{1,0:T(8,128)(2,1)S(1)}, u32[]{:S(2)}, u32[]{:S(2)}) collective-permute-start(bf16[128,256]{1,0:T(8,128)(2,1)S(1)} %get-tuple-element.128), channel_id=1, source_target_pairs={{0,16},{8,24},{16,0},{24,8},{1,17},{9,25},{17,1},{25,9},{2,18},{10... | collective-permute-start | bytes 196616 | tf_op jit(solution)/shard_map/ppermute | solution.py:39
  30.2 0.6 %collective-permute-start.14 = (bf16[128,256]{1,0:T(8,128)(2,1)S(1)}, bf16[128,256]{1,0:T(8,128)(2,1)S(1)}, u32[]{:S(2)}, u32[]{:S(2)}) collective-permute-start(bf16[128,256]{1,0:T(8,128)(2,1)S(1)} %get-tuple-element.129), channel_id=1, source_target_pairs={{0,8},{8,0},{16,24},{24,16},{1,9},{9,1},{17,25},{25,17},{2,10},{10... | collective-permute-start | bytes 196616 | tf_op jit(solution)/shard_map/ppermute | solution.py:39
  30.8 1.8 %collective-permute-done.12.refs_1_ = bf16[128,256]{1,0:T(8,128)(2,1)S(1)} collective-permute-done((bf16[128,256]{1,0:T(8,128)(2,1)S(1)}, bf16[128,256]{1,0:T(8,128)(2,1)S(1)}, u32[]{:S(2)}, u32[]{:S(2)}) %collective-permute-start.12) | collective-permute-done | bytes 65568 | tf_op jit(solution)/shard_map/ppermute | solution.py:39
  32.6 1.3 %collective-permute-done.13.refs_2_ = bf16[128,256]{1,0:T(8,128)(2,1)S(1)} collective-permute-done((bf16[128,256]{1,0:T(8,128)(2,1)S(1)}, bf16[128,256]{1,0:T(8,128)(2,1)S(1)}, u32[]{:S(2)}, u32[]{:S(2)}) %collective-permute-start.13) | collective-permute-done | bytes 65568 | tf_op jit(solution)/shard_map/ppermute | solution.py:39
  33.9 0.5 %collective-permute-done.14.refs_3_ = bf16[128,256]{1,0:T(8,128)(2,1)S(1)} collective-permute-done((bf16[128,256]{1,0:T(8,128)(2,1)S(1)}, bf16[128,256]{1,0:T(8,128)(2,1)S(1)}, u32[]{:S(2)}, u32[]{:S(2)}) %collective-permute-start.14) | collective-permute-done | bytes 65568 | tf_op jit(solution)/shard_map/ppermute | solution.py:39
  34.4 0.7 %shard_map.98 = (f32[64,256]{1,0:T(8,128)}, f32[64,256]{1,0:T(8,128)}) custom-call(f32[128,256]{1,0:T(8,128)S(1)} %get-tuple-element.126.refs_0_, bf16[128,256]{1,0:T(8,128)(2,1)S(1)} %collective-permute-done.12.refs_1_, bf16[128,256]{1,0:T(8,128)(2,1)S(1)} %collective-permute-done.13.refs_2_, bf16[128,256]{1,0:T(8,128)(2,1)S(1)} %collective-permute-done.14.refs_3_), custom_call_target="tpu_custom_call" | custom-call | tf_op jit(solution)/shard_map/pallas_call | solution.py:228
  (19 shorter events, 0.2 us)
Async XLA Ops:
  2.0 5.3 %collective-permute-start.2 = (bf16[48,640]{1,0:T(8,128)(2,1)S(1)}, bf16[48,640]{1,0:T(8,128)(2,1)S(1)}, u32[]{:S(2)}, u32[]{:S(2)}) collective-permute-start(bf16[48,640]{1,0:T(8,128)(2,1)S(1)} %get-tuple-element.69), channel_id=1, source_target_pairs={{0,8},{8,0},{16,24},{24,16},{1,9},{9,1},{17,25},{25,17},{2,10},{10... | collective-permute-start | bytes 184328 | tf_op jit(solution)/shard_map/ppermute | solution.py:39
  5.0 6.0 %collective-permute-start = (bf16[48,640]{1,0:T(8,128)(2,1)S(1)}, bf16[48,640]{1,0:T(8,128)(2,1)S(1)}, u32[]{:S(2)}, u32[]{:S(2)}) collective-permute-start(bf16[48,640]{1,0:T(8,128)(2,1)S(1)} %get-tuple-element.66), channel_id=1, source_target_pairs={{0,24},{8,16},{16,8},{24,0},{1,25},{9,17},{17,9},{25,1},{2,26},{10... | collective-permute-start | bytes 184328 | tf_op jit(solution)/shard_map/ppermute | solution.py:39
  6.5 4.5 %collective-permute-start.1 = (bf16[48,640]{1,0:T(8,128)(2,1)S(1)}, bf16[48,640]{1,0:T(8,128)(2,1)S(1)}, u32[]{:S(2)}, u32[]{:S(2)}) collective-permute-start(bf16[48,640]{1,0:T(8,128)(2,1)S(1)} %get-tuple-element.67), channel_id=1, source_target_pairs={{0,16},{8,24},{16,0},{24,8},{1,17},{9,25},{17,1},{25,9},{2,18},{10... | collective-permute-start | bytes 184328 | tf_op jit(solution)/shard_map/ppermute | solution.py:39
  7.9 6.1 %collective-permute-start.4 = (f16[104,512]{1,0:T(8,128)(2,1)S(1)}, f16[104,512]{1,0:T(8,128)(2,1)S(1)}, u32[]{:S(2)}, u32[]{:S(2)}) collective-permute-start(f16[104,512]{1,0:T(8,128)(2,1)S(1)} %convert_element_type.26), channel_id=1, source_target_pairs={{0,2},{1,3},{2,0},{3,1},{4,6},{5,7},{6,4},{7,5},{8,10},{9,11},{10,... | collective-permute-start | bytes 319496 | tf_op jit(solution)/shard_map/ppermute | solution.py:39
  11.5 4.8 %collective-permute-start.3 = (f16[104,512]{1,0:T(8,128)(2,1)S(1)}, f16[104,512]{1,0:T(8,128)(2,1)S(1)}, u32[]{:S(2)}, u32[]{:S(2)}) collective-permute-start(f16[104,512]{1,0:T(8,128)(2,1)S(1)} %convert_element_type.24), channel_id=1, source_target_pairs={{0,1},{1,0},{2,3},{3,2},{4,5},{5,4},{6,7},{7,6},{8,9},{9,8},{10,11... | collective-permute-start | bytes 319496 | tf_op jit(solution)/shard_map/ppermute | solution.py:39
  13.1 3.2 %collective-permute-start.6 = (bf16[96,512]{1,0:T(8,128)(2,1)S(1)}, bf16[96,512]{1,0:T(8,128)(2,1)S(1)}, u32[]{:S(2)}, u32[]{:S(2)}) collective-permute-start(bf16[96,512]{1,0:T(8,128)(2,1)S(1)} %get-tuple-element.79.refs_0_), channel_id=1, source_target_pairs={{0,4},{4,0},{1,5},{5,1},{2,6},{6,2},{3,7},{7,3},{8,12},{12,8},{9,1... | collective-permute-start | bytes 294920 | tf_op jit(solution)/shard_map/ppermute | solution.py:39
  13.1 3.2 %collective-permute-start.7 = (bf16[96,512]{1,0:T(8,128)(2,1)S(1)}, bf16[96,512]{1,0:T(8,128)(2,1)S(1)}, u32[]{:S(2)}, u32[]{:S(2)}) collective-permute-start(bf16[96,512]{1,0:T(8,128)(2,1)S(1)} %get-tuple-element.80.refs_1_), channel_id=1, source_target_pairs={{0,4},{4,0},{1,5},{5,1},{2,6},{6,2},{3,7},{7,3},{8,12},{12,8},{9,1... | collective-permute-start | bytes 294920 | tf_op jit(solution)/shard_map/ppermute | solution.py:39
  13.7 2.6 %collective-permute-start.5 = (f32[1,128]{1,0:T(1,128)S(1)}, f32[1,128]{1,0:T(1,128)S(1)}, u32[]{:S(2)}, u32[]{:S(2)}) collective-permute-start(f32[1,128]{1,0:T(1,128)S(1)} %get-tuple-element.104.refs_0_), channel_id=1, source_target_pairs={{0,4},{4,0},{1,5},{5,1},{2,6},{6,2},{3,7},{7,3},{8,12},{12,8},{9,1... | collective-permute-start | bytes 1544 | tf_op jit(solution)/shard_map/ppermute | solution.py:39
  16.6 7.6 %collective-permute-start.9 = (f16[104,512]{1,0:T(8,128)(2,1)S(1)}, f16[104,512]{1,0:T(8,128)(2,1)S(1)}, u32[]{:S(2)}, u32[]{:S(2)}) collective-permute-start(f16[104,512]{1,0:T(8,128)(2,1)S(1)} %convert_element_type.30), channel_id=1, source_target_pairs={{0,2},{1,3},{2,0},{3,1},{4,6},{5,7},{6,4},{7,5},{8,10},{9,11},{10,... | collective-permute-start | bytes 319496 | tf_op jit(solution)/shard_map/ppermute | solution.py:39
  19.2 5.9 %collective-permute-start.8 = (f16[104,512]{1,0:T(8,128)(2,1)S(1)}, f16[104,512]{1,0:T(8,128)(2,1)S(1)}, u32[]{:S(2)}, u32[]{:S(2)}) collective-permute-start(f16[104,512]{1,0:T(8,128)(2,1)S(1)} %convert_element_type.28), channel_id=1, source_target_pairs={{0,1},{1,0},{2,3},{3,2},{4,5},{5,4},{6,7},{7,6},{8,9},{9,8},{10,11... | collective-permute-start | bytes 319496 | tf_op jit(solution)/shard_map/ppermute | solution.py:39
  24.4 1.9 %collective-permute-start.11 = (bf16[96,512]{1,0:T(8,128)(2,1)S(1)}, bf16[96,512]{1,0:T(8,128)(2,1)S(1)}, u32[]{:S(2)}, u32[]{:S(2)}) collective-permute-start(bf16[96,512]{1,0:T(8,128)(2,1)S(1)} %shard_map.92.scaled), channel_id=1, source_target_pairs={{0,4},{4,0},{1,5},{5,1},{2,6},{6,2},{3,7},{7,3},{8,12},{12,8},{9,1... | collective-permute-start | bytes 294920 | tf_op jit(solution)/shard_map/ppermute | solution.py:39
  25.3 1.5 %collective-permute-start.10 = (bf16[96,512]{1,0:T(8,128)(2,1)S(1)}, bf16[96,512]{1,0:T(8,128)(2,1)S(1)}, u32[]{:S(2)}, u32[]{:S(2)}) collective-permute-start(bf16[96,512]{1,0:T(8,128)(2,1)S(1)} %shard_map.94.scaled), channel_id=1, source_target_pairs={{0,4},{4,0},{1,5},{5,1},{2,6},{6,2},{3,7},{7,3},{8,12},{12,8},{9,1... | collective-permute-start | bytes 294920 | tf_op jit(solution)/shard_map/ppermute | solution.py:39
  27.2 5.4 %collective-permute-start.12 = (bf16[128,256]{1,0:T(8,128)(2,1)S(1)}, bf16[128,256]{1,0:T(8,128)(2,1)S(1)}, u32[]{:S(2)}, u32[]{:S(2)}) collective-permute-start(bf16[128,256]{1,0:T(8,128)(2,1)S(1)} %get-tuple-element.127), channel_id=1, source_target_pairs={{0,24},{8,16},{16,8},{24,0},{1,25},{9,17},{17,9},{25,1},{2,26},{10... | collective-permute-start | bytes 196616 | tf_op jit(solution)/shard_map/ppermute | solution.py:39
  29.2 4.7 %collective-permute-start.13 = (bf16[128,256]{1,0:T(8,128)(2,1)S(1)}, bf16[128,256]{1,0:T(8,128)(2,1)S(1)}, u32[]{:S(2)}, u32[]{:S(2)}) collective-permute-start(bf16[128,256]{1,0:T(8,128)(2,1)S(1)} %get-tuple-element.128), channel_id=1, source_target_pairs={{0,16},{8,24},{16,0},{24,8},{1,17},{9,25},{17,1},{25,9},{2,18},{10... | collective-permute-start | bytes 196616 | tf_op jit(solution)/shard_map/ppermute | solution.py:39
  30.2 4.3 %collective-permute-start.14 = (bf16[128,256]{1,0:T(8,128)(2,1)S(1)}, bf16[128,256]{1,0:T(8,128)(2,1)S(1)}, u32[]{:S(2)}, u32[]{:S(2)}) collective-permute-start(bf16[128,256]{1,0:T(8,128)(2,1)S(1)} %get-tuple-element.129), channel_id=1, source_target_pairs={{0,8},{8,0},{16,24},{24,16},{1,9},{9,1},{17,25},{25,17},{2,10},{10... | collective-permute-start | bytes 196616 | tf_op jit(solution)/shard_map/ppermute | solution.py:39

commit v18 on v17

--- a/solution.py
+++ b/solution.py
@@ -160,16 +160,14 @@
     return dot(chosen, value, ((1,), (1,))).astype(jnp.bfloat16)
 
 
-def ahead_body(owners, studs, count, *refs):
-    parts, student_up, outs = refs[:count], refs[count], refs[count + 2 :]
-    chosen = chosen_columns(parts[0].shape[1], owners, studs)
-    for i, part in enumerate(parts):
-        turned, act, slope = outs[3 * i : 3 * i + 3]
-        rows = part[...]
-        turned[...] = turn(rows, chosen)
-        act[...], slope[...] = student(rows, student_up)
-    if len(outs) > 3 * count:
-        outs[-1][...] = chosen_columns(outs[-1].shape[1], owners, studs)
+def ahead_body(owners, studs, *refs):
+    parts, student_up, outs = refs[:2], refs[2], refs[4:]
+    turned, act, slope = outs[:3]
+    rows = jnp.concatenate([part[...] for part in parts])
+    turned[...] = turn(rows, chosen_columns(rows.shape[1], owners, studs))
+    act[...], slope[...] = student(rows, student_up)
+    if len(outs) > 3:
+        outs[3][...] = chosen_columns(outs[3].shape[1], owners, studs)
 
 
 def pair_body(*refs):
@@ -181,14 +179,18 @@
         pack(value, packed)
 
 
-def scale_body(own, arrived, tags, *refs):
-    counts, scaled = refs[:-1], refs[-1]
+def scale_body(*refs):
+    halves, tags, counts, scaled = (refs[2:4], refs[:2]), refs[4:6], refs[6:-1], refs[-1]
     all_counts = counts[0][...]
     for piece in counts[1:]:
         all_counts = all_counts + piece[...]
     inverse = jnp.where(all_counts > 0, 2.0 / all_counts, 0.0)
-    weight = jnp.sum(tags[...] * inverse, axis=1, keepdims=True)
-    scaled[...] = ((own[...] + unpack(arrived)) * weight).astype(scaled.dtype)
+    start = 0
+    for (own, arrived), tag in zip(halves, tags):
+        weight = jnp.sum(tag[...] * inverse, axis=1, keepdims=True)
+        span = slice(start, start + own.shape[0])
+        scaled[span] = ((own[...] + unpack(arrived)) * weight).astype(scaled.dtype)
+        start += own.shape[0]
 
 
 def backward_body(owners, earlier, scaled, turned, act, slope, chosen, student_down, *refs):
@@ -253,7 +255,7 @@
 
     height = slots // 2
     half, packed = shape(height, actions, f32), shape(height + PACK_ROWS, actions, f32)
-    state = [shape(width // studs, height, bf16), shape(height, units, bf16), shape(height, units, f32)]
+    state = [shape(width // studs, slots, bf16), shape(slots, units, bf16), shape(slots, units, f32)]
     tokens = [ids.reshape(1, row_count) for ids in (task_ids, student_batch)]
     weights = (teach_in, teach_out, student_up, student_down)
     results = kernel(
@@ -298,36 +300,26 @@
             pair_body, [half, packed] * 2, (first, first_in, second, second_in), 0
         )
         first_in, second_in = cross(first_out, there), cross(second_out, back)
-    ahead = functools.partial(ahead_body, owners, studs, 2)
+    ahead = functools.partial(ahead_body, owners, studs)
     *ours, chosen = kernel(
-        ahead, state * 2 + [shape(actions // studs, actions, bf16)], (*rows, weights[2], first), 0
-    )
-    known = [ours] + [kernel(ahead, state * 2, (*theirs, weights[2], first), 0) for theirs in mates]
+        ahead, state + [shape(actions // studs, actions, bf16)], (*rows, weights[2], first), 0
+    )
+    known = [ours] + [kernel(ahead, state, (*theirs, weights[2], first), 0) for theirs in mates]
+    sums = (second, second_in, first, first_in)
+    sums, all_counts, known, chosen = lax.optimization_barrier((sums, all_counts, known, chosen))
+    (scaled,) = kernel(scale_body, [shape(slots, actions, bf16)], (*sums, *tags, *all_counts), 0)
+    errors = [scaled] + [send(scaled, "stud", k) for k in range(1, studs)]
     grads = [shape(width // studs, units, f32), shape(actions // studs, units, f32)]
     heights = [g.shape[0] // owners for g in grads]
     blocks = [shape(sum(heights), units, f32)] + [shape(sum(heights), units, bf16)] * (owners - 1)
-
-    def scale(part, own, arrived):
-        (scaled,) = kernel(
-            scale_body, [shape(height, actions, bf16)], (own, arrived, tags[part], *all_counts), 0
-        )
-        return [scaled] + [send(scaled, "stud", k) for k in range(1, studs)]
-
-    def backward(k, part, sums, last=False):
-        return kernel(
-            functools.partial(backward_body, owners, len(sums) > 0),
-            blocks if last else grads,
-            (errors[part][k], *known[k][3 * part : 3 * part + 3], chosen, weights[3], *sums),
+    sums = []
+    for k, (error, group) in enumerate(zip(errors, known)):
+        sums = kernel(
+            functools.partial(backward_body, owners, k > 0),
+            blocks if k == studs - 1 else grads,
+            (error, *group, chosen, weights[3], *sums),
             0,
         )
-
-    errors = {0: scale(0, first, first_in)}
-    sums = backward(0, 0, [])
-    second_in, known, chosen, sums = lax.optimization_barrier((second_in, known, chosen, sums))
-    errors[1] = scale(1, second, second_in)
-    order = [(0, 1)] + [(k, part) for k in range(1, studs) for part in (0, 1)]
-    for k, part in order:
-        sums = backward(k, part, sums, (k, part) == order[-1])
     pieces = [sums[0]] + [send(sums[k], "teach", k) for k in range(owners - 1, 0, -1)]
     outs = [shape(h, units, f32) for h in heights]
     return kernel(

time: 35.3 us -> 34.8 us (0.986)
  waiting for transfers between devices: 9.08 us -> 10.3 us
  Pallas kernels: 6.38 us -> 5.29 us
  starting transfers between devices: 18.7 us -> 18.1 us
    ppermute x15 -> x14, waiting for transfers between devices: 9.08 us -> 10.3 us  [send(): lax.ppermute(block, axis, [(i, partner_to(size, i, step)) for i in range(...]
    pallas_call x13 -> x10, Pallas kernels: 6.38 us -> 5.29 us  [kernel(): pl.pallas_call(body, out_shape=outs, in_specs=places or [VMEM] * len(oper...]
    ppermute x15 -> x14, starting transfers between devices: 18.7 us -> 18.1 us  [send(): lax.ppermute(block, axis, [(i, partner_to(size, i, step)) for i in range(...]
  transfers between devices with their start and end apart: 15 -> 14, of which waited for: 7 -> 9; matrix products, arithmetic and copies ran while one was open for 0% -> 0% of each run, Pallas kernels for 10% -> 7%
where the time goes in v18:
time: 34.8 us; the launch traced here: 34.7 us
  starting transfers between devices  18.1 us (52%)
  waiting for transfers between devices  10.3 us (30%)
  Pallas kernels  5.29 us (15%)
  between operations  0.78 us (2%)
    ppermute x14, starting transfers between devices, send(): lax.ppermute(block, axis, [(i, partner_to(size, i, step)) for i in range(...  18.1 us
    ppermute x14, waiting for transfers between devices, send(): lax.ppermute(block, axis, [(i, partner_to(size, i, step)) for i in range(...  10.3 us
    pallas_call x10, Pallas kernels, kernel(): pl.pallas_call(body, out_shape=outs, in_specs=places or [VMEM] * len(oper...  5.29 us
  transfers between devices with their start and end apart: 14, of which 9 were waited for; matrix products, arithmetic and copies ran while one was open for 0% of the time, Pallas kernels for 7%

profile of v18, /device:TPU:0, one launch (start us, length us, event | category | flops | bytes accessed | tf_op | source)
XLA Modules:
  0.0 34.7 jit_solution(3000325941025736714)
XLA Ops:
  0.6 1.3 %shard_map.86 = (bf16[48,640]{1,0:T(8,128)(2,1)S(1)}, bf16[48,640]{1,0:T(8,128)(2,1)S(1)}, bf16[48,640]{1,0:T(8,128)(2,1)S(1)}, bf16[48,640]{1,0:T(8,128)(2,1)S(...) custom-call(bf16[128,512]{1,0:T(8,128)(2,1)} %refs_0_.1, ...), custom_call_target="tpu_custom_call" | custom-call | tf_op jit(solution)/shard_map/pallas_call | solution.py:230
  2.0 3.0 %collective-permute-start.2 = (bf16[48,640]{1,0:T(8,128)(2,1)S(1)}, bf16[48,640]{1,0:T(8,128)(2,1)S(1)}, u32[]{:S(2)}, u32[]{:S(2)}) collective-permute-start(bf16[48,640]{1,0:T(8,128)(2,1)S(1)} %get-tuple-element.59), channel_id=1, source_target_pairs={{0,8},{8,0},{16,24},{24,16},{1,9},{9,1},{17,25},{25,17},{2,10},{10... | collective-permute-start | bytes 184328 | tf_op jit(solution)/shard_map/ppermute | solution.py:39
  5.0 1.5 %collective-permute-start = (bf16[48,640]{1,0:T(8,128)(2,1)S(1)}, bf16[48,640]{1,0:T(8,128)(2,1)S(1)}, u32[]{:S(2)}, u32[]{:S(2)}) collective-permute-start(bf16[48,640]{1,0:T(8,128)(2,1)S(1)} %get-tuple-element.56), channel_id=1, source_target_pairs={{0,24},{8,16},{16,8},{24,0},{1,25},{9,17},{17,9},{25,1},{2,26},{10... | collective-permute-start | bytes 184328 | tf_op jit(solution)/shard_map/ppermute | solution.py:39
  6.5 0.1 collective-permute-start.1
  6.5 0.8 %collective-permute-done.2.refs_1_ = bf16[48,640]{1,0:T(8,128)(2,1)S(1)} collective-permute-done((bf16[48,640]{1,0:T(8,128)(2,1)S(1)}, bf16[48,640]{1,0:T(8,128)(2,1)S(1)}, u32[]{:S(2)}, u32[]{:S(2)}) %collective-permute-start.2) | collective-permute-done | bytes 61472 | tf_op jit(solution)/shard_map/ppermute | solution.py:39
  7.3 0.5 %shard_map.87 = (f32[96,128]{1,0:T(8,128)S(1)}, f32[1,128]{1,0:T(1,128)S(1)}, f32[96,512]{1,0:T(8,128)S(1)}, f32[104,512]{1,0:T(8,128)S(1)}, bf16[96,512]{1,0:T(8,128)(2,1)S(1)}) custom-call(bf16[48,640]{1,0:T(8,128)(2,1)S(1)} %get-tuple-element.58.refs_0_, bf16[48,640]{1,0:T(8,128)(2,1)S(1)} %collective-permute-done.2.refs_1_, ...), custom_call_target="tpu_custom_call" | custom-call | tf_op jit(solution)/shard_map/pallas_call | solution.py:230
  7.9 3.1 %collective-permute-start.4 = (f16[104,512]{1,0:T(8,128)(2,1)S(1)}, f16[104,512]{1,0:T(8,128)(2,1)S(1)}, u32[]{:S(2)}, u32[]{:S(2)}) collective-permute-start(f16[104,512]{1,0:T(8,128)(2,1)S(1)} %convert_element_type.26), channel_id=1, source_target_pairs={{0,2},{1,3},{2,0},{3,1},{4,6},{5,7},{6,4},{7,5},{8,10},{9,11},{10,... | collective-permute-start | bytes 319496 | tf_op jit(solution)/shard_map/ppermute | solution.py:39
  10.9 0.5 %shard_map.88 = (f32[96,128]{1,0:T(8,128)S(1)}, f32[1,128]{1,0:T(1,128)S(1)}, f32[96,512]{1,0:T(8,128)S(1)}, f32[104,512]{1,0:T(8,128)S(1)}, bf16[96,512]{1,0:T(8,128)(2,1)S(1)}) custom-call(bf16[48,640]{1,0:T(8,128)(2,1)S(1)} %collective-permute-done.refs_0_, bf16[48,640]{1,0:T(8,128)(2,1)S(1)} %collective-permute-done.1.refs_1_, ...), custom_call_target="tpu_custom_call" | custom-call | tf_op jit(solution)/shard_map/pallas_call | solution.py:230
  11.5 1.6 %collective-permute-start.3 = (f16[104,512]{1,0:T(8,128)(2,1)S(1)}, f16[104,512]{1,0:T(8,128)(2,1)S(1)}, u32[]{:S(2)}, u32[]{:S(2)}) collective-permute-start(f16[104,512]{1,0:T(8,128)(2,1)S(1)} %convert_element_type.24), channel_id=1, source_target_pairs={{0,1},{1,0},{2,3},{3,2},{4,5},{5,4},{6,7},{7,6},{8,9},{9,8},{10,11... | collective-permute-start | bytes 319496 | tf_op jit(solution)/shard_map/ppermute | solution.py:39
  13.1 0.5 %collective-permute-start.7 = (bf16[96,512]{1,0:T(8,128)(2,1)S(1)}, bf16[96,512]{1,0:T(8,128)(2,1)S(1)}, u32[]{:S(2)}, u32[]{:S(2)}) collective-permute-start(bf16[96,512]{1,0:T(8,128)(2,1)S(1)} %get-tuple-element.70.refs_1_), channel_id=1, source_target_pairs={{0,4},{4,0},{1,5},{5,1},{2,6},{6,2},{3,7},{7,3},{8,12},{12,8},{9,1... | collective-permute-start | bytes 294920 | tf_op jit(solution)/shard_map/ppermute | solution.py:39
  13.7 0.0 collective-permute-start.5
  13.7 0.3 collective-permute-done.4
  14.0 2.3 %collective-permute-done.3 = f16[104,512]{1,0:T(8,128)(2,1)S(1)} collective-permute-done((f16[104,512]{1,0:T(8,128)(2,1)S(1)}, f16[104,512]{1,0:T(8,128)(2,1)S(1)}, u32[]{:S(2)}, u32[]{:S(2)}) %collective-permute-start.3) | collective-permute-done | bytes 106528 | tf_op jit(solution)/shard_map/ppermute | solution.py:39
  16.3 0.2 shard_map.89
  16.6 2.5 %collective-permute-start.9 = (f16[104,512]{1,0:T(8,128)(2,1)S(1)}, f16[104,512]{1,0:T(8,128)(2,1)S(1)}, u32[]{:S(2)}, u32[]{:S(2)}) collective-permute-start(f16[104,512]{1,0:T(8,128)(2,1)S(1)} %convert_element_type.30), channel_id=1, source_target_pairs={{0,2},{1,3},{2,0},{3,1},{4,6},{5,7},{6,4},{7,5},{8,10},{9,11},{10,... | collective-permute-start | bytes 319496 | tf_op jit(solution)/shard_map/ppermute | solution.py:39
  19.2 2.2 %collective-permute-start.8 = (f16[104,512]{1,0:T(8,128)(2,1)S(1)}, f16[104,512]{1,0:T(8,128)(2,1)S(1)}, u32[]{:S(2)}, u32[]{:S(2)}) collective-permute-start(f16[104,512]{1,0:T(8,128)(2,1)S(1)} %convert_element_type.28), channel_id=1, source_target_pairs={{0,1},{1,0},{2,3},{3,2},{4,5},{5,4},{6,7},{7,6},{8,9},{9,8},{10,11... | collective-permute-start | bytes 319496 | tf_op jit(solution)/shard_map/ppermute | solution.py:39
  21.4 0.3 shard_map.90
  21.7 0.3 shard_map.91
  22.0 2.2 %collective-permute-done.9 = f16[104,512]{1,0:T(8,128)(2,1)S(1)} collective-permute-done((f16[104,512]{1,0:T(8,128)(2,1)S(1)}, f16[104,512]{1,0:T(8,128)(2,1)S(1)}, u32[]{:S(2)}, u32[]{:S(2)}) %collective-permute-start.9) | collective-permute-done | bytes 106528 | tf_op jit(solution)/shard_map/ppermute | solution.py:39
  24.2 0.5 %collective-permute-done.8 = f16[104,512]{1,0:T(8,128)(2,1)S(1)} collective-permute-done((f16[104,512]{1,0:T(8,128)(2,1)S(1)}, f16[104,512]{1,0:T(8,128)(2,1)S(1)}, u32[]{:S(2)}, u32[]{:S(2)}) %collective-permute-start.8) | collective-permute-done | bytes 106528 | tf_op jit(solution)/shard_map/ppermute | solution.py:39
  24.8 0.2 shard_map.92.scaled
  24.9 0.1 collective-permute-start.10
  25.0 0.7 %shard_map.93 = (f32[256,256]{1,0:T(8,128)S(1)}, f32[256,256]{1,0:T(8,128)S(1)}) custom-call(bf16[192,512]{1,0:T(8,128)(2,1)S(1)} %shard_map.92.scaled, bf16[256,192]{1,0:T(8,128)(2,1)S(1)} %get-tuple-element.101.turned, bf16[192,256]{1,0:T(8,128)(2,1)S(1)} %get-tuple-element.102.act, f32[192,256]{1,0:T(8,128)S(1)} %get-tuple-element.103.slope, ...), custom_call_target="tpu_custom_call" | custom-call | tf_op jit(solution)/shard_map/pallas_call | solution.py:230
  25.7 0.7 %collective-permute-done.10.scaled = bf16[192,512]{1,0:T(8,128)(2,1)S(1)} collective-permute-done((bf16[192,512]{1,0:T(8,128)(2,1)S(1)}, bf16[192,512]{1,0:T(8,128)(2,1)S(1)}, u32[]{:S(2)}, u32[]{:S(2)}) %collective-permute-start.10) | collective-permute-done | bytes 196640 | tf_op jit(solution)/shard_map/ppermute | solution.py:39
  26.5 0.5 %shard_map.94 = (f32[128,256]{1,0:T(8,128)S(1)}, bf16[128,256]{1,0:T(8,128)(2,1)S(1)}, bf16[128,256]{1,0:T(8,128)(2,1)S(1)}, bf16[128,256]{1,0:T(8,128)(2,1)S(1)}) custom-call(bf16[192,512]{1,0:T(8,128)(2,1)S(1)} %collective-permute-done.10.scaled, bf16[256,192]{1,0:T(8,128)(2,1)S(1)} %get-tuple-element.97.turned, ...), custom_call_target="tpu_custom_call" | custom-call | tf_op jit(solution)/shard_map/pallas_call | solution.py:230
  26.9 1.6 %collective-permute-start.11 = (bf16[128,256]{1,0:T(8,128)(2,1)S(1)}, bf16[128,256]{1,0:T(8,128)(2,1)S(1)}, u32[]{:S(2)}, u32[]{:S(2)}) collective-permute-start(bf16[128,256]{1,0:T(8,128)(2,1)S(1)} %get-tuple-element.107), channel_id=1, source_target_pairs={{0,24},{8,16},{16,8},{24,0},{1,25},{9,17},{17,9},{25,1},{2,26},{10... | collective-permute-start | bytes 196616 | tf_op jit(solution)/shard_map/ppermute | solution.py:39
  28.5 1.2 %collective-permute-start.12 = (bf16[128,256]{1,0:T(8,128)(2,1)S(1)}, bf16[128,256]{1,0:T(8,128)(2,1)S(1)}, u32[]{:S(2)}, u32[]{:S(2)}) collective-permute-start(bf16[128,256]{1,0:T(8,128)(2,1)S(1)} %get-tuple-element.108), channel_id=1, source_target_pairs={{0,16},{8,24},{16,0},{24,8},{1,17},{9,25},{17,1},{25,9},{2,18},{10... | collective-permute-start | bytes 196616 | tf_op jit(solution)/shard_map/ppermute | solution.py:39
  29.7 0.8 %collective-permute-start.13 = (bf16[128,256]{1,0:T(8,128)(2,1)S(1)}, bf16[128,256]{1,0:T(8,128)(2,1)S(1)}, u32[]{:S(2)}, u32[]{:S(2)}) collective-permute-start(bf16[128,256]{1,0:T(8,128)(2,1)S(1)} %get-tuple-element.109), channel_id=1, source_target_pairs={{0,8},{8,0},{16,24},{24,16},{1,9},{9,1},{17,25},{25,17},{2,10},{10... | collective-permute-start | bytes 196616 | tf_op jit(solution)/shard_map/ppermute | solution.py:39
  30.5 1.7 %collective-permute-done.11.refs_1_ = bf16[128,256]{1,0:T(8,128)(2,1)S(1)} collective-permute-done((bf16[128,256]{1,0:T(8,128)(2,1)S(1)}, bf16[128,256]{1,0:T(8,128)(2,1)S(1)}, u32[]{:S(2)}, u32[]{:S(2)}) %collective-permute-start.11) | collective-permute-done | bytes 65568 | tf_op jit(solution)/shard_map/ppermute | solution.py:39
  32.2 1.2 %collective-permute-done.12.refs_2_ = bf16[128,256]{1,0:T(8,128)(2,1)S(1)} collective-permute-done((bf16[128,256]{1,0:T(8,128)(2,1)S(1)}, bf16[128,256]{1,0:T(8,128)(2,1)S(1)}, u32[]{:S(2)}, u32[]{:S(2)}) %collective-permute-start.12) | collective-permute-done | bytes 65568 | tf_op jit(solution)/shard_map/ppermute | solution.py:39
  33.4 0.5 %collective-permute-done.13.refs_3_ = bf16[128,256]{1,0:T(8,128)(2,1)S(1)} collective-permute-done((bf16[128,256]{1,0:T(8,128)(2,1)S(1)}, bf16[128,256]{1,0:T(8,128)(2,1)S(1)}, u32[]{:S(2)}, u32[]{:S(2)}) %collective-permute-start.13) | collective-permute-done | bytes 65568 | tf_op jit(solution)/shard_map/ppermute | solution.py:39
  34.0 0.7 %shard_map.95 = (f32[64,256]{1,0:T(8,128)}, f32[64,256]{1,0:T(8,128)}) custom-call(f32[128,256]{1,0:T(8,128)S(1)} %get-tuple-element.106.refs_0_, bf16[128,256]{1,0:T(8,128)(2,1)S(1)} %collective-permute-done.11.refs_1_, bf16[128,256]{1,0:T(8,128)(2,1)S(1)} %collective-permute-done.12.refs_2_, bf16[128,256]{1,0:T(8,128)(2,1)S(1)} %collective-permute-done.13.refs_3_), custom_call_target="tpu_custom_call" | custom-call | tf_op jit(solution)/shard_map/pallas_call | solution.py:230
  (14 shorter events, 0.1 us)
Async XLA Ops:
  2.0 5.3 %collective-permute-start.2 = (bf16[48,640]{1,0:T(8,128)(2,1)S(1)}, bf16[48,640]{1,0:T(8,128)(2,1)S(1)}, u32[]{:S(2)}, u32[]{:S(2)}) collective-permute-start(bf16[48,640]{1,0:T(8,128)(2,1)S(1)} %get-tuple-element.59), channel_id=1, source_target_pairs={{0,8},{8,0},{16,24},{24,16},{1,9},{9,1},{17,25},{25,17},{2,10},{10... | collective-permute-start | bytes 184328 | tf_op jit(solution)/shard_map/ppermute | solution.py:39
  5.0 6.0 %collective-permute-start = (bf16[48,640]{1,0:T(8,128)(2,1)S(1)}, bf16[48,640]{1,0:T(8,128)(2,1)S(1)}, u32[]{:S(2)}, u32[]{:S(2)}) collective-permute-start(bf16[48,640]{1,0:T(8,128)(2,1)S(1)} %get-tuple-element.56), channel_id=1, source_target_pairs={{0,24},{8,16},{16,8},{24,0},{1,25},{9,17},{17,9},{25,1},{2,26},{10... | collective-permute-start | bytes 184328 | tf_op jit(solution)/shard_map/ppermute | solution.py:39
  6.5 4.5 %collective-permute-start.1 = (bf16[48,640]{1,0:T(8,128)(2,1)S(1)}, bf16[48,640]{1,0:T(8,128)(2,1)S(1)}, u32[]{:S(2)}, u32[]{:S(2)}) collective-permute-start(bf16[48,640]{1,0:T(8,128)(2,1)S(1)} %get-tuple-element.57), channel_id=1, source_target_pairs={{0,16},{8,24},{16,0},{24,8},{1,17},{9,25},{17,1},{25,9},{2,18},{10... | collective-permute-start | bytes 184328 | tf_op jit(solution)/shard_map/ppermute | solution.py:39
  7.9 6.1 %collective-permute-start.4 = (f16[104,512]{1,0:T(8,128)(2,1)S(1)}, f16[104,512]{1,0:T(8,128)(2,1)S(1)}, u32[]{:S(2)}, u32[]{:S(2)}) collective-permute-start(f16[104,512]{1,0:T(8,128)(2,1)S(1)} %convert_element_type.26), channel_id=1, source_target_pairs={{0,2},{1,3},{2,0},{3,1},{4,6},{5,7},{6,4},{7,5},{8,10},{9,11},{10,... | collective-permute-start | bytes 319496 | tf_op jit(solution)/shard_map/ppermute | solution.py:39
  11.5 4.8 %collective-permute-start.3 = (f16[104,512]{1,0:T(8,128)(2,1)S(1)}, f16[104,512]{1,0:T(8,128)(2,1)S(1)}, u32[]{:S(2)}, u32[]{:S(2)}) collective-permute-start(f16[104,512]{1,0:T(8,128)(2,1)S(1)} %convert_element_type.24), channel_id=1, source_target_pairs={{0,1},{1,0},{2,3},{3,2},{4,5},{5,4},{6,7},{7,6},{8,9},{9,8},{10,11... | collective-permute-start | bytes 319496 | tf_op jit(solution)/shard_map/ppermute | solution.py:39
  13.1 3.2 %collective-permute-start.6 = (bf16[96,512]{1,0:T(8,128)(2,1)S(1)}, bf16[96,512]{1,0:T(8,128)(2,1)S(1)}, u32[]{:S(2)}, u32[]{:S(2)}) collective-permute-start(bf16[96,512]{1,0:T(8,128)(2,1)S(1)} %get-tuple-element.69.refs_0_), channel_id=1, source_target_pairs={{0,4},{4,0},{1,5},{5,1},{2,6},{6,2},{3,7},{7,3},{8,12},{12,8},{9,1... | collective-permute-start | bytes 294920 | tf_op jit(solution)/shard_map/ppermute | solution.py:39
  13.1 3.2 %collective-permute-start.7 = (bf16[96,512]{1,0:T(8,128)(2,1)S(1)}, bf16[96,512]{1,0:T(8,128)(2,1)S(1)}, u32[]{:S(2)}, u32[]{:S(2)}) collective-permute-start(bf16[96,512]{1,0:T(8,128)(2,1)S(1)} %get-tuple-element.70.refs_1_), channel_id=1, source_target_pairs={{0,4},{4,0},{1,5},{5,1},{2,6},{6,2},{3,7},{7,3},{8,12},{12,8},{9,1... | collective-permute-start | bytes 294920 | tf_op jit(solution)/shard_map/ppermute | solution.py:39
  13.7 2.6 %collective-permute-start.5 = (f32[1,128]{1,0:T(1,128)S(1)}, f32[1,128]{1,0:T(1,128)S(1)}, u32[]{:S(2)}, u32[]{:S(2)}) collective-permute-start(f32[1,128]{1,0:T(1,128)S(1)} %get-tuple-element.95.refs_6_), channel_id=1, source_target_pairs={{0,4},{4,0},{1,5},{5,1},{2,6},{6,2},{3,7},{7,3},{8,12},{12,8},{9,1... | collective-permute-start | bytes 1544 | tf_op jit(solution)/shard_map/ppermute | solution.py:39
  16.6 7.6 %collective-permute-start.9 = (f16[104,512]{1,0:T(8,128)(2,1)S(1)}, f16[104,512]{1,0:T(8,128)(2,1)S(1)}, u32[]{:S(2)}, u32[]{:S(2)}) collective-permute-start(f16[104,512]{1,0:T(8,128)(2,1)S(1)} %convert_element_type.30), channel_id=1, source_target_pairs={{0,2},{1,3},{2,0},{3,1},{4,6},{5,7},{6,4},{7,5},{8,10},{9,11},{10,... | collective-permute-start | bytes 319496 | tf_op jit(solution)/shard_map/ppermute | solution.py:39
  19.2 5.6 %collective-permute-start.8 = (f16[104,512]{1,0:T(8,128)(2,1)S(1)}, f16[104,512]{1,0:T(8,128)(2,1)S(1)}, u32[]{:S(2)}, u32[]{:S(2)}) collective-permute-start(f16[104,512]{1,0:T(8,128)(2,1)S(1)} %convert_element_type.28), channel_id=1, source_target_pairs={{0,1},{1,0},{2,3},{3,2},{4,5},{5,4},{6,7},{7,6},{8,9},{9,8},{10,11... | collective-permute-start | bytes 319496 | tf_op jit(solution)/shard_map/ppermute | solution.py:39
  24.9 1.5 %collective-permute-start.10 = (bf16[192,512]{1,0:T(8,128)(2,1)S(1)}, bf16[192,512]{1,0:T(8,128)(2,1)S(1)}, u32[]{:S(2)}, u32[]{:S(2)}) collective-permute-start(bf16[192,512]{1,0:T(8,128)(2,1)S(1)} %shard_map.92.scaled), channel_id=1, source_target_pairs={{0,4},{4,0},{1,5},{5,1},{2,6},{6,2},{3,7},{7,3},{8,12},{12,8},{9,1... | collective-permute-start | bytes 589832 | tf_op jit(solution)/shard_map/ppermute | solution.py:39
  26.9 5.3 %collective-permute-start.11 = (bf16[128,256]{1,0:T(8,128)(2,1)S(1)}, bf16[128,256]{1,0:T(8,128)(2,1)S(1)}, u32[]{:S(2)}, u32[]{:S(2)}) collective-permute-start(bf16[128,256]{1,0:T(8,128)(2,1)S(1)} %get-tuple-element.107), channel_id=1, source_target_pairs={{0,24},{8,16},{16,8},{24,0},{1,25},{9,17},{17,9},{25,1},{2,26},{10... | collective-permute-start | bytes 196616 | tf_op jit(solution)/shard_map/ppermute | solution.py:39
  28.5 4.9 %collective-permute-start.12 = (bf16[128,256]{1,0:T(8,128)(2,1)S(1)}, bf16[128,256]{1,0:T(8,128)(2,1)S(1)}, u32[]{:S(2)}, u32[]{:S(2)}) collective-permute-start(bf16[128,256]{1,0:T(8,128)(2,1)S(1)} %get-tuple-element.108), channel_id=1, source_target_pairs={{0,16},{8,24},{16,0},{24,8},{1,17},{9,25},{17,1},{25,9},{2,18},{10... | collective-permute-start | bytes 196616 | tf_op jit(solution)/shard_map/ppermute | solution.py:39
  29.7 4.3 %collective-permute-start.13 = (bf16[128,256]{1,0:T(8,128)(2,1)S(1)}, bf16[128,256]{1,0:T(8,128)(2,1)S(1)}, u32[]{:S(2)}, u32[]{:S(2)}) collective-permute-start(bf16[128,256]{1,0:T(8,128)(2,1)S(1)} %get-tuple-element.109), channel_id=1, source_target_pairs={{0,8},{8,0},{16,24},{24,16},{1,9},{9,1},{17,25},{25,17},{2,10},{10... | collective-permute-start | bytes 196616 | tf_op jit(solution)/shard_map/ppermute | solution.py:39

commit v19 on v18

--- a/solution.py
+++ b/solution.py
@@ -9,7 +9,7 @@
 
 LANES = 128
 ROW_TILE = 16
-PACK_ROWS = 8
+POWER_ROWS = 8
 PACK_TOP = 14.0
 TINY = 1e-37
 VMEM = pl.BlockSpec(memory_space=pltpu.VMEM)
@@ -39,21 +39,24 @@
     return lax.ppermute(block, axis, [(i, partner_to(size, i, step)) for i in range(size)])
 
 
-def pack(value, out):
+def pack(value, out, power_out=None):
     height = value.shape[0]
     largest = jnp.max(jnp.max(jnp.abs(value), axis=0, keepdims=True), axis=1, keepdims=True)
     power = jnp.clip(jnp.ceil(jnp.log2(jnp.maximum(largest, TINY))), -100.0, 100.0)
     out[:height] = value * jnp.exp2(PACK_TOP - power)
-    out[height:] = jnp.broadcast_to(power, (PACK_ROWS, value.shape[1]))
-
-
-def unpack(block):
-    height = block.shape[0] - PACK_ROWS
-    return block[:height] * jnp.exp2(block[height : height + 1, :1] - PACK_TOP)
-
-
-def cross(block, step):
-    return send(block.astype(jnp.float16), "mdl", step).astype(jnp.float32)
+    place = out.at[height:] if power_out is None else power_out
+    place[...] = jnp.broadcast_to(power, place.shape)
+
+
+def unpack(block, power=None):
+    height = block.shape[0] - (POWER_ROWS if power is None else 0)
+    power = block[height : height + 1, :1] if power is None else power[:1, :1]
+    return block[:height] * jnp.exp2(power - PACK_TOP)
+
+
+def cross(block, step, power=None):
+    arrived = [send(block.astype(jnp.float16), "mdl", step).astype(jnp.float32)]
+    return arrived if power is None else arrived + [send(power, "mdl", step)]
 
 
 def dot(left, right, contract=((1,), (0,))):
@@ -115,12 +118,12 @@
 
 
 def forward_body(local, room, first, *refs):
-    count = len(refs) - 9 - (not first)
+    count = len(refs) - (9 if first else 11)
     blocks, refs = refs[:count], refs[count:]
     if not first:
         earlier, refs = refs[0], refs[1:]
     teach_in, teach_out, student_up, student_down = refs[:4]
-    tags_out, counts_out, error_out, packed, rows_out = refs[4:]
+    tags_out, counts_out, rows_out, error_out, *message = refs[4:]
     width = rows_out.shape[1]
     full = [block[...] for block in blocks]
     counts = None if first else earlier[...]
@@ -143,7 +146,7 @@
         hidden = (hidden / (1.0 + jnp.exp(-hidden))).astype(jnp.bfloat16)
         act = silu_of(dot(rows, student_up[...]))
         error_out[span] = dot(act, student_down[...], ((1,), (1,))) - dot(hidden, teach_out[l])
-    pack(error_out[...], packed)
+    pack(error_out[...], *message)
 
 
 def chosen_columns(columns, owners, studs):
@@ -170,26 +173,27 @@
         outs[3][...] = chosen_columns(outs[3].shape[1], owners, studs)
 
 
-def pair_body(*refs):
-    for i in range(2):
-        own, arrived = refs[2 * i : 2 * i + 2]
-        total, packed = refs[2 * i + 4 : 2 * i + 6]
-        value = own[...] + unpack(arrived)
+def pair_body(sizes, *refs):
+    refs, outs = refs[:-6], refs[-6:]
+    for i, size in enumerate(sizes):
+        own, arrived, refs = refs[0], refs[1 : 1 + size], refs[1 + size :]
+        total, packed, power = outs[3 * i : 3 * i + 3]
+        value = own[...] + unpack(*arrived)
         total[...] = value
-        pack(value, packed)
+        pack(value, packed, power)
 
 
 def scale_body(*refs):
-    halves, tags, counts, scaled = (refs[2:4], refs[:2]), refs[4:6], refs[6:-1], refs[-1]
+    halves, tags, counts, scaled = (refs[:3], refs[3:6]), refs[6:8], refs[8:-1], refs[-1]
     all_counts = counts[0][...]
     for piece in counts[1:]:
         all_counts = all_counts + piece[...]
     inverse = jnp.where(all_counts > 0, 2.0 / all_counts, 0.0)
     start = 0
-    for (own, arrived), tag in zip(halves, tags):
+    for (own, arrived, power), tag in zip(halves, tags):
         weight = jnp.sum(tag[...] * inverse, axis=1, keepdims=True)
         span = slice(start, start + own.shape[0])
-        scaled[span] = ((own[...] + unpack(arrived)) * weight).astype(scaled.dtype)
+        scaled[span] = ((own[...] + unpack(arrived, power)) * weight).astype(scaled.dtype)
         start += own.shape[0]
 
 
@@ -254,7 +258,8 @@
         return jax.ShapeDtypeStruct((rows, columns), dtype)
 
     height = slots // 2
-    half, packed = shape(height, actions, f32), shape(height + PACK_ROWS, actions, f32)
+    half, power = shape(height, actions, f32), shape(POWER_ROWS, LANES, f32)
+    packed = shape(height + POWER_ROWS, actions, f32)
     state = [shape(width // studs, slots, bf16), shape(slots, units, bf16), shape(slots, units, f32)]
     tokens = [ids.reshape(1, row_count) for ids in (task_ids, student_batch)]
     weights = (teach_in, teach_out, student_up, student_down)
@@ -273,39 +278,43 @@
     near = [blocks[0]] + [send(blocks[k], "teach", k) for k in range(1, middle)]
     far = [send(blocks[k], "teach", k) for k in range(owners - 1, middle - 1, -1)]
 
-    def forward(blocks, *earlier):
+    def forward(blocks, message, *earlier):
         rows = len(blocks) * local * room
         return kernel(
             functools.partial(forward_body, local, room, not earlier),
-            [shape(rows, extra, f32), shape(1, extra, f32), half, packed, shape(rows, width, bf16)],
+            [shape(rows, extra, f32), shape(1, extra, f32), shape(rows, width, bf16), half, *message],
             (*blocks, *earlier, *weights),
             0,
         )
 
     steps = [1 << i for i in range(parts.bit_length() - 1)]
-    second_tags, counts, second, second_out, second_rows = forward(near)
+    second_tags, counts, second_rows, second, second_out = forward(near, [packed])
     second_in = cross(second_out, steps[-1])
-    first_tags, counts, first, first_out, first_rows = forward(far, counts)
-    first_in = cross(first_out, steps[0])
+    first_tags, counts, first_rows, first, first_out, first_power = forward(
+        far, [half, power], counts
+    )
+    first_in = cross(first_out, steps[0], first_power)
     rows, tags = (first_rows, second_rows), (first_tags, second_tags)
     all_counts, mates = [counts], []
     for k in range(1, studs):
         all_counts.append(send(counts, "stud", k))
         mates.append([send(part, "stud", k) for part in rows])
-    first_in, second_in, all_counts, mates = lax.optimization_barrier(
-        (first_in, second_in, all_counts, mates)
-    )
+    first_in, second_in, mates = lax.optimization_barrier((first_in, second_in, mates))
     for there, back in zip(steps[1:], steps[-2::-1]):
-        first, first_out, second, second_out = kernel(
-            pair_body, [half, packed] * 2, (first, first_in, second, second_in), 0
+        first, first_out, first_power, second, second_out, second_power = kernel(
+            functools.partial(pair_body, (len(first_in), len(second_in))),
+            [half, half, power] * 2,
+            (first, *first_in, second, *second_in),
+            0,
         )
-        first_in, second_in = cross(first_out, there), cross(second_out, back)
+        first_in = cross(first_out, there, first_power)
+        second_in = cross(second_out, back, second_power)
     ahead = functools.partial(ahead_body, owners, studs)
     *ours, chosen = kernel(
         ahead, state + [shape(actions // studs, actions, bf16)], (*rows, weights[2], first), 0
     )
     known = [ours] + [kernel(ahead, state, (*theirs, weights[2], first), 0) for theirs in mates]
-    sums = (second, second_in, first, first_in)
+    sums = (first, *first_in, second, *second_in)
     sums, all_counts, known, chosen = lax.optimization_barrier((sums, all_counts, known, chosen))
     (scaled,) = kernel(scale_body, [shape(slots, actions, bf16)], (*sums, *tags, *all_counts), 0)
     errors = [scaled] + [send(scaled, "stud", k) for k in range(1, studs)]

time: 34.8 us -> 36.8 us (1.057)
  waiting for transfers between devices: 10.3 us -> 11.6 us
  starting transfers between devices: 18.1 us -> 18.9 us
    ppermute x14 -> x17, waiting for transfers between devices: 10.3 us -> 11.6 us  [send(): lax.ppermute(block, axis, [(i, partner_to(size, i, step)) for i in range(...]
    ppermute x14 -> x17, starting transfers between devices: 18.1 us -> 18.9 us  [send(): lax.ppermute(block, axis, [(i, partner_to(size, i, step)) for i in range(...]
  transfers between devices with their start and end apart: 14 -> 17, of which waited for: 9 -> 10; matrix products, arithmetic and copies ran while one was open for 0% -> 0% of each run, Pallas kernels for 7% -> 7%
where the time goes in v19:
time: 36.8 us; the launch traced here: 36.6 us
  starting transfers between devices  18.9 us (51%)
  waiting for transfers between devices  11.6 us (32%)
  Pallas kernels  5.22 us (14%)
  between operations  0.78 us (2%)
    ppermute x17, starting transfers between devices, send(): lax.ppermute(block, axis, [(i, partner_to(size, i, step)) for i in range(...  18.9 us
    ppermute x17, waiting for transfers between devices, send(): lax.ppermute(block, axis, [(i, partner_to(size, i, step)) for i in range(...  11.6 us
    pallas_call x10, Pallas kernels, kernel(): pl.pallas_call(body, out_shape=outs, in_specs=places or [VMEM] * len(oper...  5.22 us
  transfers between devices with their start and end apart: 17, of which 10 were waited for; matrix products, arithmetic and copies ran while one was open for 0% of the time, Pallas kernels for 7%

profile of v19, /device:TPU:0, one launch (start us, length us, event | category | flops | bytes accessed | tf_op | source)
XLA Modules:
  0.0 36.6 jit_solution(5988015760390161984)
XLA Ops:
  0.6 1.3 %shard_map.86 = (bf16[48,640]{1,0:T(8,128)(2,1)S(1)}, bf16[48,640]{1,0:T(8,128)(2,1)S(1)}, bf16[48,640]{1,0:T(8,128)(2,1)S(1)}, bf16[48,640]{1,0:T(8,128)(2,1)S(...) custom-call(bf16[128,512]{1,0:T(8,128)(2,1)} %refs_0_.1, ...), custom_call_target="tpu_custom_call" | custom-call | tf_op jit(solution)/shard_map/pallas_call | solution.py:234
  2.0 3.0 %collective-permute-start.2 = (bf16[48,640]{1,0:T(8,128)(2,1)S(1)}, bf16[48,640]{1,0:T(8,128)(2,1)S(1)}, u32[]{:S(2)}, u32[]{:S(2)}) collective-permute-start(bf16[48,640]{1,0:T(8,128)(2,1)S(1)} %get-tuple-element.63), channel_id=1, source_target_pairs={{0,8},{8,0},{16,24},{24,16},{1,9},{9,1},{17,25},{25,17},{2,10},{10... | collective-permute-start | bytes 184328 | tf_op jit(solution)/shard_map/ppermute | solution.py:39
  5.0 1.5 %collective-permute-start = (bf16[48,640]{1,0:T(8,128)(2,1)S(1)}, bf16[48,640]{1,0:T(8,128)(2,1)S(1)}, u32[]{:S(2)}, u32[]{:S(2)}) collective-permute-start(bf16[48,640]{1,0:T(8,128)(2,1)S(1)} %get-tuple-element.60), channel_id=1, source_target_pairs={{0,24},{8,16},{16,8},{24,0},{1,25},{9,17},{17,9},{25,1},{2,26},{10... | collective-permute-start | bytes 184328 | tf_op jit(solution)/shard_map/ppermute | solution.py:39
  6.5 0.8 %collective-permute-done.2.refs_1_ = bf16[48,640]{1,0:T(8,128)(2,1)S(1)} collective-permute-done((bf16[48,640]{1,0:T(8,128)(2,1)S(1)}, bf16[48,640]{1,0:T(8,128)(2,1)S(1)}, u32[]{:S(2)}, u32[]{:S(2)}) %collective-permute-start.2) | collective-permute-done | bytes 61472 | tf_op jit(solution)/shard_map/ppermute | solution.py:39
  7.3 0.5 %shard_map.87 = (f32[96,128]{1,0:T(8,128)S(1)}, f32[1,128]{1,0:T(1,128)S(1)}, bf16[96,512]{1,0:T(8,128)(2,1)S(1)}, f32[96,512]{1,0:T(8,128)S(1)}, f32[104,512]{1,0:T(8,128)S(1)}) custom-call(bf16[48,640]{1,0:T(8,128)(2,1)S(1)} %get-tuple-element.62.refs_0_, bf16[48,640]{1,0:T(8,128)(2,1)S(1)} %collective-permute-done.2.refs_1_, ...), custom_call_target="tpu_custom_call" | custom-call | tf_op jit(solution)/shard_map/pallas_call | solution.py:234
  7.9 3.1 %collective-permute-start.5 = (f16[104,512]{1,0:T(8,128)(2,1)S(1)}, f16[104,512]{1,0:T(8,128)(2,1)S(1)}, u32[]{:S(2)}, u32[]{:S(2)}) collective-permute-start(f16[104,512]{1,0:T(8,128)(2,1)S(1)} %convert_element_type.26), channel_id=1, source_target_pairs={{0,2},{1,3},{2,0},{3,1},{4,6},{5,7},{6,4},{7,5},{8,10},{9,11},{10,... | collective-permute-start | bytes 319496 | tf_op jit(solution)/shard_map/ppermute | solution.py:39
  10.9 0.5 %shard_map.88 = (f32[96,128]{1,0:T(8,128)S(1)}, f32[1,128]{1,0:T(1,128)S(1)}, bf16[96,512]{1,0:T(8,128)(2,1)S(1)}, f32[96,512]{1,0:T(8,128)S(1)}, f32[96,512]{1,0:T(8,128)S(1)}, /*index=5*/f32[8,128]{1,0:T(8,128)S(1)}) custom-call(bf16[48,640]{1,0:T(8,128)(2,1)S(1)} %collective-permute-done.refs_0_, bf16[48,640]{1,0:T(8,128)(2,1)S(1)} %collective-permute-done.1.refs_1_, ...), custom_call_target="tpu_custom_call" | custom-call | tf_op jit(solution)/shard_map/pallas_call | solution.py:234
  11.5 1.6 %collective-permute-start.3 = (f16[96,512]{1,0:T(8,128)(2,1)S(1)}, f16[96,512]{1,0:T(8,128)(2,1)S(1)}, u32[]{:S(2)}, u32[]{:S(2)}) collective-permute-start(f16[96,512]{1,0:T(8,128)(2,1)S(1)} %convert_element_type.24), channel_id=1, source_target_pairs={{0,1},{1,0},{2,3},{3,2},{4,5},{5,4},{6,7},{7,6},{8,9},{9,8},{10,11... | collective-permute-start | bytes 294920 | tf_op jit(solution)/shard_map/ppermute | solution.py:39
  13.1 0.5 %collective-permute-start.7 = (bf16[96,512]{1,0:T(8,128)(2,1)S(1)}, bf16[96,512]{1,0:T(8,128)(2,1)S(1)}, u32[]{:S(2)}, u32[]{:S(2)}) collective-permute-start(bf16[96,512]{1,0:T(8,128)(2,1)S(1)} %get-tuple-element.74.refs_1_), channel_id=1, source_target_pairs={{0,4},{4,0},{1,5},{5,1},{2,6},{6,2},{3,7},{7,3},{8,12},{12,8},{9,1... | collective-permute-start | bytes 294920 | tf_op jit(solution)/shard_map/ppermute | solution.py:39
  13.7 0.4 %collective-permute-start.4 = (f32[8,128]{1,0:T(8,128)S(1)}, f32[8,128]{1,0:T(8,128)S(1)}, u32[]{:S(2)}, u32[]{:S(2)}) collective-permute-start(f32[8,128]{1,0:T(8,128)S(1)} %get-tuple-element.71), channel_id=1, source_target_pairs={{0,1},{1,0},{2,3},{3,2},{4,5},{5,4},{6,7},{7,6},{8,9},{9,8},{10,11... | collective-permute-start | bytes 12296 | tf_op jit(solution)/shard_map/ppermute | solution.py:39
  14.1 2.1 %collective-permute-done.3 = f16[96,512]{1,0:T(8,128)(2,1)S(1)} collective-permute-done((f16[96,512]{1,0:T(8,128)(2,1)S(1)}, f16[96,512]{1,0:T(8,128)(2,1)S(1)}, u32[]{:S(2)}, u32[]{:S(2)}) %collective-permute-start.3) | collective-permute-done | bytes 98336 | tf_op jit(solution)/shard_map/ppermute | solution.py:39
  16.2 1.0 %collective-permute-done.4.refs_2_ = f32[8,128]{1,0:T(8,128)S(1)} collective-permute-done((f32[8,128]{1,0:T(8,128)S(1)}, f32[8,128]{1,0:T(8,128)S(1)}, u32[]{:S(2)}, u32[]{:S(2)}) %collective-permute-start.4) | collective-permute-done | bytes 4128 | tf_op jit(solution)/shard_map/ppermute | solution.py:39
  17.3 0.2 shard_map.89
  17.5 2.5 %collective-permute-start.8 = (f16[96,512]{1,0:T(8,128)(2,1)S(1)}, f16[96,512]{1,0:T(8,128)(2,1)S(1)}, u32[]{:S(2)}, u32[]{:S(2)}) collective-permute-start(f16[96,512]{1,0:T(8,128)(2,1)S(1)} %convert_element_type.28), channel_id=1, source_target_pairs={{0,2},{1,3},{2,0},{3,1},{4,6},{5,7},{6,4},{7,5},{8,10},{9,11},{10,... | collective-permute-start | bytes 294920 | tf_op jit(solution)/shard_map/ppermute | solution.py:39
  20.1 1.2 %collective-permute-start.10 = (f16[96,512]{1,0:T(8,128)(2,1)S(1)}, f16[96,512]{1,0:T(8,128)(2,1)S(1)}, u32[]{:S(2)}, u32[]{:S(2)}) collective-permute-start(f16[96,512]{1,0:T(8,128)(2,1)S(1)} %convert_element_type.30), channel_id=1, source_target_pairs={{0,1},{1,0},{2,3},{3,2},{4,5},{5,4},{6,7},{7,6},{8,9},{9,8},{10,11... | collective-permute-start | bytes 294920 | tf_op jit(solution)/shard_map/ppermute | solution.py:39
  21.2 0.9 %collective-permute-start.11 = (f32[8,128]{1,0:T(8,128)S(1)}, f32[8,128]{1,0:T(8,128)S(1)}, u32[]{:S(2)}, u32[]{:S(2)}) collective-permute-start(f32[8,128]{1,0:T(8,128)S(1)} %get-tuple-element.84), channel_id=1, source_target_pairs={{0,1},{1,0},{2,3},{3,2},{4,5},{5,4},{6,7},{7,6},{8,9},{9,8},{10,11... | collective-permute-start | bytes 12296 | tf_op jit(solution)/shard_map/ppermute | solution.py:39
  22.2 0.5 %collective-permute-start.9 = (f32[8,128]{1,0:T(8,128)S(1)}, f32[8,128]{1,0:T(8,128)S(1)}, u32[]{:S(2)}, u32[]{:S(2)}) collective-permute-start(f32[8,128]{1,0:T(8,128)S(1)} %get-tuple-element.81), channel_id=1, source_target_pairs={{0,2},{1,3},{2,0},{3,1},{4,6},{5,7},{6,4},{7,5},{8,10},{9,11},{10,... | collective-permute-start | bytes 12296 | tf_op jit(solution)/shard_map/ppermute | solution.py:39
  22.6 0.3 shard_map.90
  22.9 0.3 shard_map.91
  23.3 1.1 %collective-permute-done.8 = f16[96,512]{1,0:T(8,128)(2,1)S(1)} collective-permute-done((f16[96,512]{1,0:T(8,128)(2,1)S(1)}, f16[96,512]{1,0:T(8,128)(2,1)S(1)}, u32[]{:S(2)}, u32[]{:S(2)}) %collective-permute-start.8) | collective-permute-done | bytes 98336 | tf_op jit(solution)/shard_map/ppermute | solution.py:39
  24.4 0.7 %collective-permute-done.10 = f16[96,512]{1,0:T(8,128)(2,1)S(1)} collective-permute-done((f16[96,512]{1,0:T(8,128)(2,1)S(1)}, f16[96,512]{1,0:T(8,128)(2,1)S(1)}, u32[]{:S(2)}, u32[]{:S(2)}) %collective-permute-start.10) | collective-permute-done | bytes 98336 | tf_op jit(solution)/shard_map/ppermute | solution.py:39
  25.2 1.5 %collective-permute-done.9.refs_2_ = f32[8,128]{1,0:T(8,128)S(1)} collective-permute-done((f32[8,128]{1,0:T(8,128)S(1)}, f32[8,128]{1,0:T(8,128)S(1)}, u32[]{:S(2)}, u32[]{:S(2)}) %collective-permute-start.9) | collective-permute-done | bytes 4128 | tf_op jit(solution)/shard_map/ppermute | solution.py:39
  26.9 0.7 %shard_map.93 = (f32[256,256]{1,0:T(8,128)S(1)}, f32[256,256]{1,0:T(8,128)S(1)}) custom-call(bf16[192,512]{1,0:T(8,128)(2,1)S(1)} %shard_map.92.scaled, bf16[256,192]{1,0:T(8,128)(2,1)S(1)} %get-tuple-element.109.turned, bf16[192,256]{1,0:T(8,128)(2,1)S(1)} %get-tuple-element.110.act, f32[192,256]{1,0:T(8,128)S(1)} %get-tuple-element.111.slope, ...), custom_call_target="tpu_custom_call" | custom-call | tf_op jit(solution)/shard_map/pallas_call | solution.py:234
  27.6 0.7 %collective-permute-done.13.scaled = bf16[192,512]{1,0:T(8,128)(2,1)S(1)} collective-permute-done((bf16[192,512]{1,0:T(8,128)(2,1)S(1)}, bf16[192,512]{1,0:T(8,128)(2,1)S(1)}, u32[]{:S(2)}, u32[]{:S(2)}) %collective-permute-start.13) | collective-permute-done | bytes 196640 | tf_op jit(solution)/shard_map/ppermute | solution.py:39
  28.3 0.5 %shard_map.94 = (f32[128,256]{1,0:T(8,128)S(1)}, bf16[128,256]{1,0:T(8,128)(2,1)S(1)}, bf16[128,256]{1,0:T(8,128)(2,1)S(1)}, bf16[128,256]{1,0:T(8,128)(2,1)S(1)}) custom-call(bf16[192,512]{1,0:T(8,128)(2,1)S(1)} %collective-permute-done.13.scaled, bf16[256,192]{1,0:T(8,128)(2,1)S(1)} %get-tuple-element.105.turned, ...), custom_call_target="tpu_custom_call" | custom-call | tf_op jit(solution)/shard_map/pallas_call | solution.py:234
  28.8 1.5 %collective-permute-start.14 = (bf16[128,256]{1,0:T(8,128)(2,1)S(1)}, bf16[128,256]{1,0:T(8,128)(2,1)S(1)}, u32[]{:S(2)}, u32[]{:S(2)}) collective-permute-start(bf16[128,256]{1,0:T(8,128)(2,1)S(1)} %get-tuple-element.115), channel_id=1, source_target_pairs={{0,24},{8,16},{16,8},{24,0},{1,25},{9,17},{17,9},{25,1},{2,26},{10... | collective-permute-start | bytes 196616 | tf_op jit(solution)/shard_map/ppermute | solution.py:39
  30.3 1.4 %collective-permute-start.15 = (bf16[128,256]{1,0:T(8,128)(2,1)S(1)}, bf16[128,256]{1,0:T(8,128)(2,1)S(1)}, u32[]{:S(2)}, u32[]{:S(2)}) collective-permute-start(bf16[128,256]{1,0:T(8,128)(2,1)S(1)} %get-tuple-element.116), channel_id=1, source_target_pairs={{0,16},{8,24},{16,0},{24,8},{1,17},{9,25},{17,1},{25,9},{2,18},{10... | collective-permute-start | bytes 196616 | tf_op jit(solution)/shard_map/ppermute | solution.py:39
  31.7 0.7 %collective-permute-start.16 = (bf16[128,256]{1,0:T(8,128)(2,1)S(1)}, bf16[128,256]{1,0:T(8,128)(2,1)S(1)}, u32[]{:S(2)}, u32[]{:S(2)}) collective-permute-start(bf16[128,256]{1,0:T(8,128)(2,1)S(1)} %get-tuple-element.117), channel_id=1, source_target_pairs={{0,8},{8,0},{16,24},{24,16},{1,9},{9,1},{17,25},{25,17},{2,10},{10... | collective-permute-start | bytes 196616 | tf_op jit(solution)/shard_map/ppermute | solution.py:39
  32.3 1.8 %collective-permute-done.14.refs_1_ = bf16[128,256]{1,0:T(8,128)(2,1)S(1)} collective-permute-done((bf16[128,256]{1,0:T(8,128)(2,1)S(1)}, bf16[128,256]{1,0:T(8,128)(2,1)S(1)}, u32[]{:S(2)}, u32[]{:S(2)}) %collective-permute-start.14) | collective-permute-done | bytes 65568 | tf_op jit(solution)/shard_map/ppermute | solution.py:39
  34.1 1.2 %collective-permute-done.15.refs_2_ = bf16[128,256]{1,0:T(8,128)(2,1)S(1)} collective-permute-done((bf16[128,256]{1,0:T(8,128)(2,1)S(1)}, bf16[128,256]{1,0:T(8,128)(2,1)S(1)}, u32[]{:S(2)}, u32[]{:S(2)}) %collective-permute-start.15) | collective-permute-done | bytes 65568 | tf_op jit(solution)/shard_map/ppermute | solution.py:39
  35.3 0.7 %collective-permute-done.16.refs_3_ = bf16[128,256]{1,0:T(8,128)(2,1)S(1)} collective-permute-done((bf16[128,256]{1,0:T(8,128)(2,1)S(1)}, bf16[128,256]{1,0:T(8,128)(2,1)S(1)}, u32[]{:S(2)}, u32[]{:S(2)}) %collective-permute-start.16) | collective-permute-done | bytes 65568 | tf_op jit(solution)/shard_map/ppermute | solution.py:39
  35.9 0.7 %shard_map.95 = (f32[64,256]{1,0:T(8,128)}, f32[64,256]{1,0:T(8,128)}) custom-call(f32[128,256]{1,0:T(8,128)S(1)} %get-tuple-element.114.refs_0_, bf16[128,256]{1,0:T(8,128)(2,1)S(1)} %collective-permute-done.14.refs_1_, bf16[128,256]{1,0:T(8,128)(2,1)S(1)} %collective-permute-done.15.refs_2_, bf16[128,256]{1,0:T(8,128)(2,1)S(1)} %collective-permute-done.16.refs_3_), custom_call_target="tpu_custom_call" | custom-call | tf_op jit(solution)/shard_map/pallas_call | solution.py:234
  (20 shorter events, 0.4 us)
Async XLA Ops:
  2.0 5.3 %collective-permute-start.2 = (bf16[48,640]{1,0:T(8,128)(2,1)S(1)}, bf16[48,640]{1,0:T(8,128)(2,1)S(1)}, u32[]{:S(2)}, u32[]{:S(2)}) collective-permute-start(bf16[48,640]{1,0:T(8,128)(2,1)S(1)} %get-tuple-element.63), channel_id=1, source_target_pairs={{0,8},{8,0},{16,24},{24,16},{1,9},{9,1},{17,25},{25,17},{2,10},{10... | collective-permute-start | bytes 184328 | tf_op jit(solution)/shard_map/ppermute | solution.py:39
  5.0 5.9 %collective-permute-start = (bf16[48,640]{1,0:T(8,128)(2,1)S(1)}, bf16[48,640]{1,0:T(8,128)(2,1)S(1)}, u32[]{:S(2)}, u32[]{:S(2)}) collective-permute-start(bf16[48,640]{1,0:T(8,128)(2,1)S(1)} %get-tuple-element.60), channel_id=1, source_target_pairs={{0,24},{8,16},{16,8},{24,0},{1,25},{9,17},{17,9},{25,1},{2,26},{10... | collective-permute-start | bytes 184328 | tf_op jit(solution)/shard_map/ppermute | solution.py:39
  6.5 4.5 %collective-permute-start.1 = (bf16[48,640]{1,0:T(8,128)(2,1)S(1)}, bf16[48,640]{1,0:T(8,128)(2,1)S(1)}, u32[]{:S(2)}, u32[]{:S(2)}) collective-permute-start(bf16[48,640]{1,0:T(8,128)(2,1)S(1)} %get-tuple-element.61), channel_id=1, source_target_pairs={{0,16},{8,24},{16,0},{24,8},{1,17},{9,25},{17,1},{25,9},{2,18},{10... | collective-permute-start | bytes 184328 | tf_op jit(solution)/shard_map/ppermute | solution.py:39
  7.9 8.3 %collective-permute-start.5 = (f16[104,512]{1,0:T(8,128)(2,1)S(1)}, f16[104,512]{1,0:T(8,128)(2,1)S(1)}, u32[]{:S(2)}, u32[]{:S(2)}) collective-permute-start(f16[104,512]{1,0:T(8,128)(2,1)S(1)} %convert_element_type.26), channel_id=1, source_target_pairs={{0,2},{1,3},{2,0},{3,1},{4,6},{5,7},{6,4},{7,5},{8,10},{9,11},{10,... | collective-permute-start | bytes 319496 | tf_op jit(solution)/shard_map/ppermute | solution.py:39
  11.5 4.7 %collective-permute-start.3 = (f16[96,512]{1,0:T(8,128)(2,1)S(1)}, f16[96,512]{1,0:T(8,128)(2,1)S(1)}, u32[]{:S(2)}, u32[]{:S(2)}) collective-permute-start(f16[96,512]{1,0:T(8,128)(2,1)S(1)} %convert_element_type.24), channel_id=1, source_target_pairs={{0,1},{1,0},{2,3},{3,2},{4,5},{5,4},{6,7},{7,6},{8,9},{9,8},{10,11... | collective-permute-start | bytes 294920 | tf_op jit(solution)/shard_map/ppermute | solution.py:39
  13.1 4.1 %collective-permute-start.6 = (bf16[96,512]{1,0:T(8,128)(2,1)S(1)}, bf16[96,512]{1,0:T(8,128)(2,1)S(1)}, u32[]{:S(2)}, u32[]{:S(2)}) collective-permute-start(bf16[96,512]{1,0:T(8,128)(2,1)S(1)} %get-tuple-element.73.refs_0_), channel_id=1, source_target_pairs={{0,4},{4,0},{1,5},{5,1},{2,6},{6,2},{3,7},{7,3},{8,12},{12,8},{9,1... | collective-permute-start | bytes 294920 | tf_op jit(solution)/shard_map/ppermute | solution.py:39
  13.1 4.1 %collective-permute-start.7 = (bf16[96,512]{1,0:T(8,128)(2,1)S(1)}, bf16[96,512]{1,0:T(8,128)(2,1)S(1)}, u32[]{:S(2)}, u32[]{:S(2)}) collective-permute-start(bf16[96,512]{1,0:T(8,128)(2,1)S(1)} %get-tuple-element.74.refs_1_), channel_id=1, source_target_pairs={{0,4},{4,0},{1,5},{5,1},{2,6},{6,2},{3,7},{7,3},{8,12},{12,8},{9,1... | collective-permute-start | bytes 294920 | tf_op jit(solution)/shard_map/ppermute | solution.py:39
  13.7 3.6 %collective-permute-start.4 = (f32[8,128]{1,0:T(8,128)S(1)}, f32[8,128]{1,0:T(8,128)S(1)}, u32[]{:S(2)}, u32[]{:S(2)}) collective-permute-start(f32[8,128]{1,0:T(8,128)S(1)} %get-tuple-element.71), channel_id=1, source_target_pairs={{0,1},{1,0},{2,3},{3,2},{4,5},{5,4},{6,7},{7,6},{8,9},{9,8},{10,11... | collective-permute-start | bytes 12296 | tf_op jit(solution)/shard_map/ppermute | solution.py:39
  17.5 6.9 %collective-permute-start.8 = (f16[96,512]{1,0:T(8,128)(2,1)S(1)}, f16[96,512]{1,0:T(8,128)(2,1)S(1)}, u32[]{:S(2)}, u32[]{:S(2)}) collective-permute-start(f16[96,512]{1,0:T(8,128)(2,1)S(1)} %convert_element_type.28), channel_id=1, source_target_pairs={{0,2},{1,3},{2,0},{3,1},{4,6},{5,7},{6,4},{7,5},{8,10},{9,11},{10,... | collective-permute-start | bytes 294920 | tf_op jit(solution)/shard_map/ppermute | solution.py:39
  20.1 5.1 %collective-permute-start.10 = (f16[96,512]{1,0:T(8,128)(2,1)S(1)}, f16[96,512]{1,0:T(8,128)(2,1)S(1)}, u32[]{:S(2)}, u32[]{:S(2)}) collective-permute-start(f16[96,512]{1,0:T(8,128)(2,1)S(1)} %convert_element_type.30), channel_id=1, source_target_pairs={{0,1},{1,0},{2,3},{3,2},{4,5},{5,4},{6,7},{7,6},{8,9},{9,8},{10,11... | collective-permute-start | bytes 294920 | tf_op jit(solution)/shard_map/ppermute | solution.py:39
  21.2 3.9 %collective-permute-start.11 = (f32[8,128]{1,0:T(8,128)S(1)}, f32[8,128]{1,0:T(8,128)S(1)}, u32[]{:S(2)}, u32[]{:S(2)}) collective-permute-start(f32[8,128]{1,0:T(8,128)S(1)} %get-tuple-element.84), channel_id=1, source_target_pairs={{0,1},{1,0},{2,3},{3,2},{4,5},{5,4},{6,7},{7,6},{8,9},{9,8},{10,11... | collective-permute-start | bytes 12296 | tf_op jit(solution)/shard_map/ppermute | solution.py:39
  22.2 4.5 %collective-permute-start.9 = (f32[8,128]{1,0:T(8,128)S(1)}, f32[8,128]{1,0:T(8,128)S(1)}, u32[]{:S(2)}, u32[]{:S(2)}) collective-permute-start(f32[8,128]{1,0:T(8,128)S(1)} %get-tuple-element.81), channel_id=1, source_target_pairs={{0,2},{1,3},{2,0},{3,1},{4,6},{5,7},{6,4},{7,5},{8,10},{9,11},{10,... | collective-permute-start | bytes 12296 | tf_op jit(solution)/shard_map/ppermute | solution.py:39
  22.6 2.5 %collective-permute-start.12 = (f32[1,128]{1,0:T(1,128)S(1)}, f32[1,128]{1,0:T(1,128)S(1)}, u32[]{:S(2)}, u32[]{:S(2)}) collective-permute-start(f32[1,128]{1,0:T(1,128)S(1)} %get-tuple-element.103.refs_8_), channel_id=1, source_target_pairs={{0,4},{4,0},{1,5},{5,1},{2,6},{6,2},{3,7},{7,3},{8,12},{12,8},{9,1... | collective-permute-start | bytes 1544 | tf_op jit(solution)/shard_map/ppermute | solution.py:39
  26.8 1.5 %collective-permute-start.13 = (bf16[192,512]{1,0:T(8,128)(2,1)S(1)}, bf16[192,512]{1,0:T(8,128)(2,1)S(1)}, u32[]{:S(2)}, u32[]{:S(2)}) collective-permute-start(bf16[192,512]{1,0:T(8,128)(2,1)S(1)} %shard_map.92.scaled), channel_id=1, source_target_pairs={{0,4},{4,0},{1,5},{5,1},{2,6},{6,2},{3,7},{7,3},{8,12},{12,8},{9,1... | collective-permute-start | bytes 589832 | tf_op jit(solution)/shard_map/ppermute | solution.py:39
  28.8 5.3 %collective-permute-start.14 = (bf16[128,256]{1,0:T(8,128)(2,1)S(1)}, bf16[128,256]{1,0:T(8,128)(2,1)S(1)}, u32[]{:S(2)}, u32[]{:S(2)}) collective-permute-start(bf16[128,256]{1,0:T(8,128)(2,1)S(1)} %get-tuple-element.115), channel_id=1, source_target_pairs={{0,24},{8,16},{16,8},{24,0},{1,25},{9,17},{17,9},{25,1},{2,26},{10... | collective-permute-start | bytes 196616 | tf_op jit(solution)/shard_map/ppermute | solution.py:39
  30.3 5.0 %collective-permute-start.15 = (bf16[128,256]{1,0:T(8,128)(2,1)S(1)}, bf16[128,256]{1,0:T(8,128)(2,1)S(1)}, u32[]{:S(2)}, u32[]{:S(2)}) collective-permute-start(bf16[128,256]{1,0:T(8,128)(2,1)S(1)} %get-tuple-element.116), channel_id=1, source_target_pairs={{0,16},{8,24},{16,0},{24,8},{1,17},{9,25},{17,1},{25,9},{2,18},{10... | collective-permute-start | bytes 196616 | tf_op jit(solution)/shard_map/ppermute | solution.py:39
  31.7 4.3 %collective-permute-start.16 = (bf16[128,256]{1,0:T(8,128)(2,1)S(1)}, bf16[128,256]{1,0:T(8,128)(2,1)S(1)}, u32[]{:S(2)}, u32[]{:S(2)}) collective-permute-start(bf16[128,256]{1,0:T(8,128)(2,1)S(1)} %get-tuple-element.117), channel_id=1, source_target_pairs={{0,8},{8,0},{16,24},{24,16},{1,9},{9,1},{17,25},{25,17},{2,10},{10... | collective-permute-start | bytes 196616 | tf_op jit(solution)/shard_map/ppermute | solution.py:39

commit v20 on v18

--- a/solution.py
+++ b/solution.py
@@ -47,8 +47,7 @@
     out[height:] = jnp.broadcast_to(power, (PACK_ROWS, value.shape[1]))
 
 
-def unpack(block):
-    height = block.shape[0] - PACK_ROWS
+def unpack(block, height):
     return block[:height] * jnp.exp2(block[height : height + 1, :1] - PACK_TOP)
 
 
@@ -170,17 +169,15 @@
         outs[3][...] = chosen_columns(outs[3].shape[1], owners, studs)
 
 
-def pair_body(*refs):
-    for i in range(2):
-        own, arrived = refs[2 * i : 2 * i + 2]
-        total, packed = refs[2 * i + 4 : 2 * i + 6]
-        value = own[...] + unpack(arrived)
-        total[...] = value
-        pack(value, packed)
+def pair_body(own, arrived, *refs):
+    total, packed = refs[-2:]
+    value = own[...] + unpack(arrived, own.shape[0])
+    total[...] = value
+    pack(value, packed)
 
 
 def scale_body(*refs):
-    halves, tags, counts, scaled = (refs[2:4], refs[:2]), refs[4:6], refs[6:-1], refs[-1]
+    halves, tags, counts, scaled = (refs[:2], refs[2:4]), refs[4:6], refs[6:-1], refs[-1]
     all_counts = counts[0][...]
     for piece in counts[1:]:
         all_counts = all_counts + piece[...]
@@ -189,7 +186,7 @@
     for (own, arrived), tag in zip(halves, tags):
         weight = jnp.sum(tag[...] * inverse, axis=1, keepdims=True)
         span = slice(start, start + own.shape[0])
-        scaled[span] = ((own[...] + unpack(arrived)) * weight).astype(scaled.dtype)
+        scaled[span] = ((own[...] + unpack(arrived, own.shape[0])) * weight).astype(scaled.dtype)
         start += own.shape[0]
 
 
@@ -284,28 +281,26 @@
 
     steps = [1 << i for i in range(parts.bit_length() - 1)]
     second_tags, counts, second, second_out, second_rows = forward(near)
-    second_in = cross(second_out, steps[-1])
+    second_in = cross(second_out, steps[0])
     first_tags, counts, first, first_out, first_rows = forward(far, counts)
-    first_in = cross(first_out, steps[0])
+    first_in = cross(first_out, steps[-1])
     rows, tags = (first_rows, second_rows), (first_tags, second_tags)
     all_counts, mates = [counts], []
     for k in range(1, studs):
         all_counts.append(send(counts, "stud", k))
         mates.append([send(part, "stud", k) for part in rows])
-    first_in, second_in, all_counts, mates = lax.optimization_barrier(
-        (first_in, second_in, all_counts, mates)
-    )
+    second_in, all_counts = lax.optimization_barrier((second_in, all_counts))
     for there, back in zip(steps[1:], steps[-2::-1]):
-        first, first_out, second, second_out = kernel(
-            pair_body, [half, packed] * 2, (first, first_in, second, second_in), 0
-        )
-        first_in, second_in = cross(first_out, there), cross(second_out, back)
+        second, second_out = kernel(pair_body, [half, packed], (second, second_in), 0)
+        second_in = cross(second_out, there)
+        first, first_out = kernel(pair_body, [half, packed], (first, first_in, second), 0)
+        first_in = cross(first_out, back)
     ahead = functools.partial(ahead_body, owners, studs)
     *ours, chosen = kernel(
         ahead, state + [shape(actions // studs, actions, bf16)], (*rows, weights[2], first), 0
     )
     known = [ours] + [kernel(ahead, state, (*theirs, weights[2], first), 0) for theirs in mates]
-    sums = (second, second_in, first, first_in)
+    sums = (first, first_in, second, second_in)
     sums, all_counts, known, chosen = lax.optimization_barrier((sums, all_counts, known, chosen))
     (scaled,) = kernel(scale_body, [shape(slots, actions, bf16)], (*sums, *tags, *all_counts), 0)
     errors = [scaled] + [send(scaled, "stud", k) for k in range(1, studs)]

time: 34.8 us -> 35.6 us (1.023)
  waiting for transfers between devices: 10.3 us -> 11.6 us
  starting transfers between devices: 18.1 us -> 17.5 us
    ppermute x14, waiting for transfers between devices: 10.3 us -> 11.6 us  [send(): lax.ppermute(block, axis, [(i, partner_to(size, i, step)) for i in range(...]
    ppermute x14, starting transfers between devices: 18.1 us -> 17.5 us  [send(): lax.ppermute(block, axis, [(i, partner_to(size, i, step)) for i in range(...]
    pallas_call x10 -> x11, Pallas kernels: 5.29 us -> 5.46 us  [kernel(): pl.pallas_call(body, out_shape=outs, in_specs=places or [VMEM] * len(oper...]
  transfers between devices with their start and end apart: 14 -> 14, of which waited for: 9 -> 12; matrix products, arithmetic and copies ran while one was open for 0% -> 0% of each run, Pallas kernels for 7% -> 8%
where the time goes in v20:
time: 35.6 us; the launch traced here: 35.5 us
  starting transfers between devices  17.5 us (49%)
  waiting for transfers between devices  11.6 us (33%)
  Pallas kernels  5.46 us (15%)
  between operations  0.78 us (2%)
    ppermute x14, starting transfers between devices, send(): lax.ppermute(block, axis, [(i, partner_to(size, i, step)) for i in range(...  17.5 us
    ppermute x14, waiting for transfers between devices, send(): lax.ppermute(block, axis, [(i, partner_to(size, i, step)) for i in range(...  11.6 us
    pallas_call x11, Pallas kernels, kernel(): pl.pallas_call(body, out_shape=outs, in_specs=places or [VMEM] * len(oper...  5.46 us
  transfers between devices with their start and end apart: 14, of which 12 were waited for; matrix products, arithmetic and copies ran while one was open for 0% of the time, Pallas kernels for 8%

profile of v20, /device:TPU:0, one launch (start us, length us, event | category | flops | bytes accessed | tf_op | source)
XLA Modules:
  0.0 35.5 jit_solution(8586907482774149179)
XLA Ops:
  0.6 1.3 %shard_map.86 = (bf16[48,640]{1,0:T(8,128)(2,1)S(1)}, bf16[48,640]{1,0:T(8,128)(2,1)S(1)}, bf16[48,640]{1,0:T(8,128)(2,1)S(1)}, bf16[48,640]{1,0:T(8,128)(2,1)S(...) custom-call(bf16[128,512]{1,0:T(8,128)(2,1)} %refs_0_.1, ...), custom_call_target="tpu_custom_call" | custom-call | tf_op jit(solution)/shard_map/pallas_call | solution.py:227
  2.0 3.0 %collective-permute-start.2 = (bf16[48,640]{1,0:T(8,128)(2,1)S(1)}, bf16[48,640]{1,0:T(8,128)(2,1)S(1)}, u32[]{:S(2)}, u32[]{:S(2)}) collective-permute-start(bf16[48,640]{1,0:T(8,128)(2,1)S(1)} %get-tuple-element.56), channel_id=1, source_target_pairs={{0,8},{8,0},{16,24},{24,16},{1,9},{9,1},{17,25},{25,17},{2,10},{10... | collective-permute-start | bytes 184328 | tf_op jit(solution)/shard_map/ppermute | solution.py:39
  5.0 1.5 %collective-permute-start = (bf16[48,640]{1,0:T(8,128)(2,1)S(1)}, bf16[48,640]{1,0:T(8,128)(2,1)S(1)}, u32[]{:S(2)}, u32[]{:S(2)}) collective-permute-start(bf16[48,640]{1,0:T(8,128)(2,1)S(1)} %get-tuple-element.53), channel_id=1, source_target_pairs={{0,24},{8,16},{16,8},{24,0},{1,25},{9,17},{17,9},{25,1},{2,26},{10... | collective-permute-start | bytes 184328 | tf_op jit(solution)/shard_map/ppermute | solution.py:39
  6.5 0.8 %collective-permute-done.2.refs_1_ = bf16[48,640]{1,0:T(8,128)(2,1)S(1)} collective-permute-done((bf16[48,640]{1,0:T(8,128)(2,1)S(1)}, bf16[48,640]{1,0:T(8,128)(2,1)S(1)}, u32[]{:S(2)}, u32[]{:S(2)}) %collective-permute-start.2) | collective-permute-done | bytes 61472 | tf_op jit(solution)/shard_map/ppermute | solution.py:39
  7.3 0.5 %shard_map.87 = (f32[96,128]{1,0:T(8,128)S(1)}, f32[1,128]{1,0:T(1,128)S(1)}, f32[96,512]{1,0:T(8,128)S(1)}, f32[104,512]{1,0:T(8,128)S(1)}, bf16[96,512]{1,0:T(8,128)(2,1)S(1)}) custom-call(bf16[48,640]{1,0:T(8,128)(2,1)S(1)} %get-tuple-element.55.refs_0_, bf16[48,640]{1,0:T(8,128)(2,1)S(1)} %collective-permute-done.2.refs_1_, ...), custom_call_target="tpu_custom_call" | custom-call | tf_op jit(solution)/shard_map/pallas_call | solution.py:227
  7.9 2.1 %collective-permute-start.4 = (f16[104,512]{1,0:T(8,128)(2,1)S(1)}, f16[104,512]{1,0:T(8,128)(2,1)S(1)}, u32[]{:S(2)}, u32[]{:S(2)}) collective-permute-start(f16[104,512]{1,0:T(8,128)(2,1)S(1)} %convert_element_type.26), channel_id=1, source_target_pairs={{0,1},{1,0},{2,3},{3,2},{4,5},{5,4},{6,7},{7,6},{8,9},{9,8},{10,11... | collective-permute-start | bytes 319496 | tf_op jit(solution)/shard_map/ppermute | solution.py:39
  9.9 0.2 collective-permute-done.refs_0_
  10.2 0.7 %collective-permute-done.1.refs_1_ = bf16[48,640]{1,0:T(8,128)(2,1)S(1)} collective-permute-done((bf16[48,640]{1,0:T(8,128)(2,1)S(1)}, bf16[48,640]{1,0:T(8,128)(2,1)S(1)}, u32[]{:S(2)}, u32[]{:S(2)}) %collective-permute-start.1) | collective-permute-done | bytes 61472 | tf_op jit(solution)/shard_map/ppermute | solution.py:39
  10.8 0.5 %shard_map.88 = (f32[96,128]{1,0:T(8,128)S(1)}, f32[1,128]{1,0:T(1,128)S(1)}, f32[96,512]{1,0:T(8,128)S(1)}, f32[104,512]{1,0:T(8,128)S(1)}, bf16[96,512]{1,0:T(8,128)(2,1)S(1)}) custom-call(bf16[48,640]{1,0:T(8,128)(2,1)S(1)} %collective-permute-done.refs_0_, bf16[48,640]{1,0:T(8,128)(2,1)S(1)} %collective-permute-done.1.refs_1_, ...), custom_call_target="tpu_custom_call" | custom-call | tf_op jit(solution)/shard_map/pallas_call | solution.py:227
  11.4 2.7 %collective-permute-start.3 = (f16[104,512]{1,0:T(8,128)(2,1)S(1)}, f16[104,512]{1,0:T(8,128)(2,1)S(1)}, u32[]{:S(2)}, u32[]{:S(2)}) collective-permute-start(f16[104,512]{1,0:T(8,128)(2,1)S(1)} %convert_element_type.24), channel_id=1, source_target_pairs={{0,2},{1,3},{2,0},{3,1},{4,6},{5,7},{6,4},{7,5},{8,10},{9,11},{10,... | collective-permute-start | bytes 319496 | tf_op jit(solution)/shard_map/ppermute | solution.py:39
  14.1 1.1 %collective-permute-done.5.refs_7_ = f32[1,128]{1,0:T(1,128)S(1)} collective-permute-done((f32[1,128]{1,0:T(1,128)S(1)}, f32[1,128]{1,0:T(1,128)S(1)}, u32[]{:S(2)}, u32[]{:S(2)}) %collective-permute-start.5) | collective-permute-done | bytes 544 | tf_op jit(solution)/shard_map/ppermute | solution.py:39
  15.2 0.2 shard_map.89
  15.4 0.6 %collective-permute-start.7 = (f16[104,512]{1,0:T(8,128)(2,1)S(1)}, f16[104,512]{1,0:T(8,128)(2,1)S(1)}, u32[]{:S(2)}, u32[]{:S(2)}) collective-permute-start(f16[104,512]{1,0:T(8,128)(2,1)S(1)} %convert_element_type.30), channel_id=1, source_target_pairs={{0,2},{1,3},{2,0},{3,1},{4,6},{5,7},{6,4},{7,5},{8,10},{9,11},{10,... | collective-permute-start | bytes 319496 | tf_op jit(solution)/shard_map/ppermute | solution.py:39
  16.0 2.9 %collective-permute-done.3 = f16[104,512]{1,0:T(8,128)(2,1)S(1)} collective-permute-done((f16[104,512]{1,0:T(8,128)(2,1)S(1)}, f16[104,512]{1,0:T(8,128)(2,1)S(1)}, u32[]{:S(2)}, u32[]{:S(2)}) %collective-permute-start.3) | collective-permute-done | bytes 106528 | tf_op jit(solution)/shard_map/ppermute | solution.py:39
  18.9 0.2 shard_map.90
  19.2 3.5 %collective-permute-start.6 = (f16[104,512]{1,0:T(8,128)(2,1)S(1)}, f16[104,512]{1,0:T(8,128)(2,1)S(1)}, u32[]{:S(2)}, u32[]{:S(2)}) collective-permute-start(f16[104,512]{1,0:T(8,128)(2,1)S(1)} %convert_element_type.28), channel_id=1, source_target_pairs={{0,1},{1,0},{2,3},{3,2},{4,5},{5,4},{6,7},{7,6},{8,9},{9,8},{10,11... | collective-permute-start | bytes 319496 | tf_op jit(solution)/shard_map/ppermute | solution.py:39
  22.7 0.5 %collective-permute-start.9 = (bf16[96,512]{1,0:T(8,128)(2,1)S(1)}, bf16[96,512]{1,0:T(8,128)(2,1)S(1)}, u32[]{:S(2)}, u32[]{:S(2)}) collective-permute-start(bf16[96,512]{1,0:T(8,128)(2,1)S(1)} %get-tuple-element.75.refs_1_), channel_id=1, source_target_pairs={{0,4},{4,0},{1,5},{5,1},{2,6},{6,2},{3,7},{7,3},{8,12},{12,8},{9,1... | collective-permute-start | bytes 294920 | tf_op jit(solution)/shard_map/ppermute | solution.py:39
  23.2 0.3 shard_map.91
  23.5 0.5 %collective-permute-done.8.refs_0_ = bf16[96,512]{1,0:T(8,128)(2,1)S(1)} collective-permute-done((bf16[96,512]{1,0:T(8,128)(2,1)S(1)}, bf16[96,512]{1,0:T(8,128)(2,1)S(1)}, u32[]{:S(2)}, u32[]{:S(2)}) %collective-permute-start.8) | collective-permute-done | bytes 98336 | tf_op jit(solution)/shard_map/ppermute | solution.py:39
  24.1 0.3 shard_map.92
  24.5 1.5 %collective-permute-done.6 = f16[104,512]{1,0:T(8,128)(2,1)S(1)} collective-permute-done((f16[104,512]{1,0:T(8,128)(2,1)S(1)}, f16[104,512]{1,0:T(8,128)(2,1)S(1)}, u32[]{:S(2)}, u32[]{:S(2)}) %collective-permute-start.6) | collective-permute-done | bytes 106528 | tf_op jit(solution)/shard_map/ppermute | solution.py:39
  26.0 0.2 shard_map.93.scaled
  26.3 0.7 %shard_map.94 = (f32[256,256]{1,0:T(8,128)S(1)}, f32[256,256]{1,0:T(8,128)S(1)}) custom-call(bf16[192,512]{1,0:T(8,128)(2,1)S(1)} %shard_map.93.scaled, bf16[256,192]{1,0:T(8,128)(2,1)S(1)} %get-tuple-element.95.turned, bf16[192,256]{1,0:T(8,128)(2,1)S(1)} %get-tuple-element.96.act, f32[192,256]{1,0:T(8,128)S(1)} %get-tuple-element.97.slope, ...), custom_call_target="tpu_custom_call" | custom-call | tf_op jit(solution)/shard_map/pallas_call | solution.py:227
  27.0 0.7 %collective-permute-done.10.scaled = bf16[192,512]{1,0:T(8,128)(2,1)S(1)} collective-permute-done((bf16[192,512]{1,0:T(8,128)(2,1)S(1)}, bf16[192,512]{1,0:T(8,128)(2,1)S(1)}, u32[]{:S(2)}, u32[]{:S(2)}) %collective-permute-start.10) | collective-permute-done | bytes 196640 | tf_op jit(solution)/shard_map/ppermute | solution.py:39
  27.7 0.5 %shard_map.95 = (f32[128,256]{1,0:T(8,128)S(1)}, bf16[128,256]{1,0:T(8,128)(2,1)S(1)}, bf16[128,256]{1,0:T(8,128)(2,1)S(1)}, bf16[128,256]{1,0:T(8,128)(2,1)S(1)}) custom-call(bf16[192,512]{1,0:T(8,128)(2,1)S(1)} %collective-permute-done.10.scaled, bf16[256,192]{1,0:T(8,128)(2,1)S(1)} %get-tuple-element.91.turned, ...), custom_call_target="tpu_custom_call" | custom-call | tf_op jit(solution)/shard_map/pallas_call | solution.py:227
  28.2 0.8 %collective-permute-start.11 = (bf16[128,256]{1,0:T(8,128)(2,1)S(1)}, bf16[128,256]{1,0:T(8,128)(2,1)S(1)}, u32[]{:S(2)}, u32[]{:S(2)}) collective-permute-start(bf16[128,256]{1,0:T(8,128)(2,1)S(1)} %get-tuple-element.101), channel_id=1, source_target_pairs={{0,24},{8,16},{16,8},{24,0},{1,25},{9,17},{17,9},{25,1},{2,26},{10... | collective-permute-start | bytes 196616 | tf_op jit(solution)/shard_map/ppermute | solution.py:39
  29.0 1.5 %collective-permute-start.12 = (bf16[128,256]{1,0:T(8,128)(2,1)S(1)}, bf16[128,256]{1,0:T(8,128)(2,1)S(1)}, u32[]{:S(2)}, u32[]{:S(2)}) collective-permute-start(bf16[128,256]{1,0:T(8,128)(2,1)S(1)} %get-tuple-element.102), channel_id=1, source_target_pairs={{0,16},{8,24},{16,0},{24,8},{1,17},{9,25},{17,1},{25,9},{2,18},{10... | collective-permute-start | bytes 196616 | tf_op jit(solution)/shard_map/ppermute | solution.py:39
  30.5 1.2 %collective-permute-start.13 = (bf16[128,256]{1,0:T(8,128)(2,1)S(1)}, bf16[128,256]{1,0:T(8,128)(2,1)S(1)}, u32[]{:S(2)}, u32[]{:S(2)}) collective-permute-start(bf16[128,256]{1,0:T(8,128)(2,1)S(1)} %get-tuple-element.103), channel_id=1, source_target_pairs={{0,8},{8,0},{16,24},{24,16},{1,9},{9,1},{17,25},{25,17},{2,10},{10... | collective-permute-start | bytes 196616 | tf_op jit(solution)/shard_map/ppermute | solution.py:39
  31.8 2.3 %collective-permute-done.11.refs_1_ = bf16[128,256]{1,0:T(8,128)(2,1)S(1)} collective-permute-done((bf16[128,256]{1,0:T(8,128)(2,1)S(1)}, bf16[128,256]{1,0:T(8,128)(2,1)S(1)}, u32[]{:S(2)}, u32[]{:S(2)}) %collective-permute-start.11) | collective-permute-done | bytes 65568 | tf_op jit(solution)/shard_map/ppermute | solution.py:39
  34.1 0.2 collective-permute-done.12.refs_2_
  34.3 0.5 %collective-permute-done.13.refs_3_ = bf16[128,256]{1,0:T(8,128)(2,1)S(1)} collective-permute-done((bf16[128,256]{1,0:T(8,128)(2,1)S(1)}, bf16[128,256]{1,0:T(8,128)(2,1)S(1)}, u32[]{:S(2)}, u32[]{:S(2)}) %collective-permute-start.13) | collective-permute-done | bytes 65568 | tf_op jit(solution)/shard_map/ppermute | solution.py:39
  34.8 0.7 %shard_map.96 = (f32[64,256]{1,0:T(8,128)}, f32[64,256]{1,0:T(8,128)}) custom-call(f32[128,256]{1,0:T(8,128)S(1)} %get-tuple-element.100.refs_0_, bf16[128,256]{1,0:T(8,128)(2,1)S(1)} %collective-permute-done.11.refs_1_, bf16[128,256]{1,0:T(8,128)(2,1)S(1)} %collective-permute-done.12.refs_2_, bf16[128,256]{1,0:T(8,128)(2,1)S(1)} %collective-permute-done.13.refs_3_), custom_call_target="tpu_custom_call" | custom-call | tf_op jit(solution)/shard_map/pallas_call | solution.py:227
  (15 shorter events, 0.4 us)
Async XLA Ops:
  2.0 5.3 %collective-permute-start.2 = (bf16[48,640]{1,0:T(8,128)(2,1)S(1)}, bf16[48,640]{1,0:T(8,128)(2,1)S(1)}, u32[]{:S(2)}, u32[]{:S(2)}) collective-permute-start(bf16[48,640]{1,0:T(8,128)(2,1)S(1)} %get-tuple-element.56), channel_id=1, source_target_pairs={{0,8},{8,0},{16,24},{24,16},{1,9},{9,1},{17,25},{25,17},{2,10},{10... | collective-permute-start | bytes 184328 | tf_op jit(solution)/shard_map/ppermute | solution.py:39
  5.0 5.2 %collective-permute-start = (bf16[48,640]{1,0:T(8,128)(2,1)S(1)}, bf16[48,640]{1,0:T(8,128)(2,1)S(1)}, u32[]{:S(2)}, u32[]{:S(2)}) collective-permute-start(bf16[48,640]{1,0:T(8,128)(2,1)S(1)} %get-tuple-element.53), channel_id=1, source_target_pairs={{0,24},{8,16},{16,8},{24,0},{1,25},{9,17},{17,9},{25,1},{2,26},{10... | collective-permute-start | bytes 184328 | tf_op jit(solution)/shard_map/ppermute | solution.py:39
  6.5 4.3 %collective-permute-start.1 = (bf16[48,640]{1,0:T(8,128)(2,1)S(1)}, bf16[48,640]{1,0:T(8,128)(2,1)S(1)}, u32[]{:S(2)}, u32[]{:S(2)}) collective-permute-start(bf16[48,640]{1,0:T(8,128)(2,1)S(1)} %get-tuple-element.54), channel_id=1, source_target_pairs={{0,16},{8,24},{16,0},{24,8},{1,17},{9,25},{17,1},{25,9},{2,18},{10... | collective-permute-start | bytes 184328 | tf_op jit(solution)/shard_map/ppermute | solution.py:39
  7.9 6.2 %collective-permute-start.4 = (f16[104,512]{1,0:T(8,128)(2,1)S(1)}, f16[104,512]{1,0:T(8,128)(2,1)S(1)}, u32[]{:S(2)}, u32[]{:S(2)}) collective-permute-start(f16[104,512]{1,0:T(8,128)(2,1)S(1)} %convert_element_type.26), channel_id=1, source_target_pairs={{0,1},{1,0},{2,3},{3,2},{4,5},{5,4},{6,7},{7,6},{8,9},{9,8},{10,11... | collective-permute-start | bytes 319496 | tf_op jit(solution)/shard_map/ppermute | solution.py:39
  11.4 7.5 %collective-permute-start.3 = (f16[104,512]{1,0:T(8,128)(2,1)S(1)}, f16[104,512]{1,0:T(8,128)(2,1)S(1)}, u32[]{:S(2)}, u32[]{:S(2)}) collective-permute-start(f16[104,512]{1,0:T(8,128)(2,1)S(1)} %convert_element_type.24), channel_id=1, source_target_pairs={{0,2},{1,3},{2,0},{3,1},{4,6},{5,7},{6,4},{7,5},{8,10},{9,11},{10,... | collective-permute-start | bytes 319496 | tf_op jit(solution)/shard_map/ppermute | solution.py:39
  14.0 1.1 %collective-permute-start.5 = (f32[1,128]{1,0:T(1,128)S(1)}, f32[1,128]{1,0:T(1,128)S(1)}, u32[]{:S(2)}, u32[]{:S(2)}) collective-permute-start(f32[1,128]{1,0:T(1,128)S(1)} %get-tuple-element.89.refs_6_), channel_id=1, source_target_pairs={{0,4},{4,0},{1,5},{5,1},{2,6},{6,2},{3,7},{7,3},{8,12},{12,8},{9,1... | collective-permute-start | bytes 1544 | tf_op jit(solution)/shard_map/ppermute | solution.py:39
  15.4 9.1 %collective-permute-start.7 = (f16[104,512]{1,0:T(8,128)(2,1)S(1)}, f16[104,512]{1,0:T(8,128)(2,1)S(1)}, u32[]{:S(2)}, u32[]{:S(2)}) collective-permute-start(f16[104,512]{1,0:T(8,128)(2,1)S(1)} %convert_element_type.30), channel_id=1, source_target_pairs={{0,2},{1,3},{2,0},{3,1},{4,6},{5,7},{6,4},{7,5},{8,10},{9,11},{10,... | collective-permute-start | bytes 319496 | tf_op jit(solution)/shard_map/ppermute | solution.py:39
  19.2 6.8 %collective-permute-start.6 = (f16[104,512]{1,0:T(8,128)(2,1)S(1)}, f16[104,512]{1,0:T(8,128)(2,1)S(1)}, u32[]{:S(2)}, u32[]{:S(2)}) collective-permute-start(f16[104,512]{1,0:T(8,128)(2,1)S(1)} %convert_element_type.28), channel_id=1, source_target_pairs={{0,1},{1,0},{2,3},{3,2},{4,5},{5,4},{6,7},{7,6},{8,9},{9,8},{10,11... | collective-permute-start | bytes 319496 | tf_op jit(solution)/shard_map/ppermute | solution.py:39
  22.7 1.3 %collective-permute-start.8 = (bf16[96,512]{1,0:T(8,128)(2,1)S(1)}, bf16[96,512]{1,0:T(8,128)(2,1)S(1)}, u32[]{:S(2)}, u32[]{:S(2)}) collective-permute-start(bf16[96,512]{1,0:T(8,128)(2,1)S(1)} %get-tuple-element.74.refs_0_), channel_id=1, source_target_pairs={{0,4},{4,0},{1,5},{5,1},{2,6},{6,2},{3,7},{7,3},{8,12},{12,8},{9,1... | collective-permute-start | bytes 294920 | tf_op jit(solution)/shard_map/ppermute | solution.py:39
  22.7 1.5 %collective-permute-start.9 = (bf16[96,512]{1,0:T(8,128)(2,1)S(1)}, bf16[96,512]{1,0:T(8,128)(2,1)S(1)}, u32[]{:S(2)}, u32[]{:S(2)}) collective-permute-start(bf16[96,512]{1,0:T(8,128)(2,1)S(1)} %get-tuple-element.75.refs_1_), channel_id=1, source_target_pairs={{0,4},{4,0},{1,5},{5,1},{2,6},{6,2},{3,7},{7,3},{8,12},{12,8},{9,1... | collective-permute-start | bytes 294920 | tf_op jit(solution)/shard_map/ppermute | solution.py:39
  26.2 1.5 %collective-permute-start.10 = (bf16[192,512]{1,0:T(8,128)(2,1)S(1)}, bf16[192,512]{1,0:T(8,128)(2,1)S(1)}, u32[]{:S(2)}, u32[]{:S(2)}) collective-permute-start(bf16[192,512]{1,0:T(8,128)(2,1)S(1)} %shard_map.93.scaled), channel_id=1, source_target_pairs={{0,4},{4,0},{1,5},{5,1},{2,6},{6,2},{3,7},{7,3},{8,12},{12,8},{9,1... | collective-permute-start | bytes 589832 | tf_op jit(solution)/shard_map/ppermute | solution.py:39
  28.2 5.9 %collective-permute-start.11 = (bf16[128,256]{1,0:T(8,128)(2,1)S(1)}, bf16[128,256]{1,0:T(8,128)(2,1)S(1)}, u32[]{:S(2)}, u32[]{:S(2)}) collective-permute-start(bf16[128,256]{1,0:T(8,128)(2,1)S(1)} %get-tuple-element.101), channel_id=1, source_target_pairs={{0,24},{8,16},{16,8},{24,0},{1,25},{9,17},{17,9},{25,1},{2,26},{10... | collective-permute-start | bytes 196616 | tf_op jit(solution)/shard_map/ppermute | solution.py:39
  29.0 5.3 %collective-permute-start.12 = (bf16[128,256]{1,0:T(8,128)(2,1)S(1)}, bf16[128,256]{1,0:T(8,128)(2,1)S(1)}, u32[]{:S(2)}, u32[]{:S(2)}) collective-permute-start(bf16[128,256]{1,0:T(8,128)(2,1)S(1)} %get-tuple-element.102), channel_id=1, source_target_pairs={{0,16},{8,24},{16,0},{24,8},{1,17},{9,25},{17,1},{25,9},{2,18},{10... | collective-permute-start | bytes 196616 | tf_op jit(solution)/shard_map/ppermute | solution.py:39
  30.5 4.3 %collective-permute-start.13 = (bf16[128,256]{1,0:T(8,128)(2,1)S(1)}, bf16[128,256]{1,0:T(8,128)(2,1)S(1)}, u32[]{:S(2)}, u32[]{:S(2)}) collective-permute-start(bf16[128,256]{1,0:T(8,128)(2,1)S(1)} %get-tuple-element.103), channel_id=1, source_target_pairs={{0,8},{8,0},{16,24},{24,16},{1,9},{9,1},{17,25},{25,17},{2,10},{10... | collective-permute-start | bytes 196616 | tf_op jit(solution)/shard_map/ppermute | solution.py:39

commit v21 on v20

--- a/solution.py
+++ b/solution.py
@@ -34,9 +34,10 @@
     return me ^ step if is_power(size) else (me + size - step) % size
 
 
-def send(block, axis, step):
+def send(block, axis, step, parity=None):
     size = lax.axis_size(axis)
-    return lax.ppermute(block, axis, [(i, partner_to(size, i, step)) for i in range(size)])
+    sources = [i for i in range(size) if parity is None or i & 1 == parity]
+    return lax.ppermute(block, axis, [(i, partner_to(size, i, step)) for i in sources])
 
 
 def pack(value, out):
@@ -47,12 +48,13 @@
     out[height:] = jnp.broadcast_to(power, (PACK_ROWS, value.shape[1]))
 
 
-def unpack(block, height):
+def unpack(block):
+    height = block.shape[0] - PACK_ROWS
     return block[:height] * jnp.exp2(block[height : height + 1, :1] - PACK_TOP)
 
 
-def cross(block, step):
-    return send(block.astype(jnp.float16), "mdl", step).astype(jnp.float32)
+def cross(block, step, parity=None):
+    return send(block.astype(jnp.float16), "mdl", step, parity).astype(jnp.float32)
 
 
 def dot(left, right, contract=((1,), (0,))):
@@ -171,22 +173,25 @@
 
 def pair_body(own, arrived, *refs):
     total, packed = refs[-2:]
-    value = own[...] + unpack(arrived, own.shape[0])
+    value = own[...] + unpack(arrived)
     total[...] = value
     pack(value, packed)
 
 
 def scale_body(*refs):
-    halves, tags, counts, scaled = (refs[:2], refs[2:4]), refs[4:6], refs[6:-1], refs[-1]
+    halves, tags, counts, scaled = ((refs[0], refs[1], refs[4]), refs[2:4]), refs[5:7], refs[7:-1], refs[-1]
     all_counts = counts[0][...]
     for piece in counts[1:]:
         all_counts = all_counts + piece[...]
     inverse = jnp.where(all_counts > 0, 2.0 / all_counts, 0.0)
     start = 0
-    for (own, arrived), tag in zip(halves, tags):
+    for (own, *arrived), tag in zip(halves, tags):
         weight = jnp.sum(tag[...] * inverse, axis=1, keepdims=True)
         span = slice(start, start + own.shape[0])
-        scaled[span] = ((own[...] + unpack(arrived, own.shape[0])) * weight).astype(scaled.dtype)
+        message = arrived[0][...]
+        for piece in arrived[1:]:
+            message = message + piece[...]
+        scaled[span] = ((own[...] + unpack(message)) * weight).astype(scaled.dtype)
         start += own.shape[0]
 
 
@@ -281,26 +286,27 @@
 
     steps = [1 << i for i in range(parts.bit_length() - 1)]
     second_tags, counts, second, second_out, second_rows = forward(near)
-    second_in = cross(second_out, steps[0])
+    second_in = cross(second_out, steps[-1])
     first_tags, counts, first, first_out, first_rows = forward(far, counts)
-    first_in = cross(first_out, steps[-1])
+    first_in = cross(first_out, steps[0])
     rows, tags = (first_rows, second_rows), (first_tags, second_tags)
     all_counts, mates = [counts], []
     for k in range(1, studs):
         all_counts.append(send(counts, "stud", k))
         mates.append([send(part, "stud", k) for part in rows])
-    second_in, all_counts = lax.optimization_barrier((second_in, all_counts))
+    second_in, all_counts, mates = lax.optimization_barrier((second_in, all_counts, mates))
     for there, back in zip(steps[1:], steps[-2::-1]):
         second, second_out = kernel(pair_body, [half, packed], (second, second_in), 0)
-        second_in = cross(second_out, there)
         first, first_out = kernel(pair_body, [half, packed], (first, first_in, second), 0)
-        first_in = cross(first_out, back)
+        first_out, second_out = lax.optimization_barrier((first_out, second_out))
+        first_in = [cross(first_out, there, parity) for parity in (0, 1)]
+        second_in = cross(second_out, back)
     ahead = functools.partial(ahead_body, owners, studs)
     *ours, chosen = kernel(
         ahead, state + [shape(actions // studs, actions, bf16)], (*rows, weights[2], first), 0
     )
     known = [ours] + [kernel(ahead, state, (*theirs, weights[2], first), 0) for theirs in mates]
-    sums = (first, first_in, second, second_in)
+    sums = (first, first_in[0], second, second_in, first_in[1])
     sums, all_counts, known, chosen = lax.optimization_barrier((sums, all_counts, known, chosen))
     (scaled,) = kernel(scale_body, [shape(slots, actions, bf16)], (*sums, *tags, *all_counts), 0)
     errors = [scaled] + [send(scaled, "stud", k) for k in range(1, studs)]

time: 35.6 us -> 37.7 us (1.059)
  the two profiles are of different devices: /device:TPU:0 before, /device:TPU:8 now
where the time goes in v21:
time: 37.7 us; the launch traced here: 37.5 us
  starting transfers between devices  18 us (48%)
  waiting for transfers between devices  13 us (34%)
  Pallas kernels  5.43 us (14%)
  between operations  0.82 us (2%)
    ppermute x15, starting transfers between devices, send(): lax.ppermute(block, axis, [(i, partner_to(size, i, step)) for i in sources])  18 us
    ppermute x15, waiting for transfers between devices, send(): lax.ppermute(block, axis, [(i, partner_to(size, i, step)) for i in sources])  13 us
    pallas_call x11, Pallas kernels, kernel(): pl.pallas_call(body, out_shape=outs, in_specs=places or [VMEM] * len(oper...  5.43 us
  transfers between devices with their start and end apart: 15, of which 9 were waited for; matrix products, arithmetic and copies ran while one was open for 0% of the time, Pallas kernels for 7%

profile of v21, /device:TPU:8, one launch (start us, length us, event | category | flops | bytes accessed | tf_op | source)
XLA Modules:
  0.0 37.5 jit_solution(14597019320618484403)
XLA Ops:
  0.6 1.3 %shard_map.86 = (bf16[48,640]{1,0:T(8,128)(2,1)S(1)}, bf16[48,640]{1,0:T(8,128)(2,1)S(1)}, bf16[48,640]{1,0:T(8,128)(2,1)S(1)}, bf16[48,640]{1,0:T(8,128)(2,1)S(...) custom-call(bf16[128,512]{1,0:T(8,128)(2,1)} %refs_0_.1, ...), custom_call_target="tpu_custom_call" | custom-call | tf_op jit(solution)/shard_map/pallas_call | solution.py:232
  2.0 1.6 %collective-permute-start.2 = (bf16[48,640]{1,0:T(8,128)(2,1)S(1)}, bf16[48,640]{1,0:T(8,128)(2,1)S(1)}, u32[]{:S(2)}, u32[]{:S(2)}) collective-permute-start(bf16[48,640]{1,0:T(8,128)(2,1)S(1)} %get-tuple-element.61), channel_id=1, source_target_pairs={{0,8},{8,0},{16,24},{24,16},{1,9},{9,1},{17,25},{25,17},{2,10},{10... | collective-permute-start | bytes 184328 | tf_op jit(solution)/shard_map/ppermute | solution.py:40
  3.5 1.5 %collective-permute-start = (bf16[48,640]{1,0:T(8,128)(2,1)S(1)}, bf16[48,640]{1,0:T(8,128)(2,1)S(1)}, u32[]{:S(2)}, u32[]{:S(2)}) collective-permute-start(bf16[48,640]{1,0:T(8,128)(2,1)S(1)} %get-tuple-element.58), channel_id=1, source_target_pairs={{0,24},{8,16},{16,8},{24,0},{1,25},{9,17},{17,9},{25,1},{2,26},{10... | collective-permute-start | bytes 184328 | tf_op jit(solution)/shard_map/ppermute | solution.py:40
  5.0 0.5 %collective-permute-start.1 = (bf16[48,640]{1,0:T(8,128)(2,1)S(1)}, bf16[48,640]{1,0:T(8,128)(2,1)S(1)}, u32[]{:S(2)}, u32[]{:S(2)}) collective-permute-start(bf16[48,640]{1,0:T(8,128)(2,1)S(1)} %get-tuple-element.59), channel_id=1, source_target_pairs={{0,16},{8,24},{16,0},{24,8},{1,17},{9,25},{17,1},{25,9},{2,18},{10... | collective-permute-start | bytes 184328 | tf_op jit(solution)/shard_map/ppermute | solution.py:40
  5.5 0.7 %collective-permute-done.2.refs_1_ = bf16[48,640]{1,0:T(8,128)(2,1)S(1)} collective-permute-done((bf16[48,640]{1,0:T(8,128)(2,1)S(1)}, bf16[48,640]{1,0:T(8,128)(2,1)S(1)}, u32[]{:S(2)}, u32[]{:S(2)}) %collective-permute-start.2) | collective-permute-done | bytes 61472 | tf_op jit(solution)/shard_map/ppermute | solution.py:40
  6.3 0.5 %shard_map.87 = (f32[96,128]{1,0:T(8,128)S(1)}, f32[1,128]{1,0:T(1,128)S(1)}, f32[96,512]{1,0:T(8,128)S(1)}, f32[104,512]{1,0:T(8,128)S(1)}, bf16[96,512]{1,0:T(8,128)(2,1)S(1)}) custom-call(bf16[48,640]{1,0:T(8,128)(2,1)S(1)} %get-tuple-element.60.refs_0_, bf16[48,640]{1,0:T(8,128)(2,1)S(1)} %collective-permute-done.2.refs_1_, ...), custom_call_target="tpu_custom_call" | custom-call | tf_op jit(solution)/shard_map/pallas_call | solution.py:232
  6.8 2.6 %collective-permute-start.4 = (f16[104,512]{1,0:T(8,128)(2,1)S(1)}, f16[104,512]{1,0:T(8,128)(2,1)S(1)}, u32[]{:S(2)}, u32[]{:S(2)}) collective-permute-start(f16[104,512]{1,0:T(8,128)(2,1)S(1)} %convert_element_type.30), channel_id=1, source_target_pairs={{0,2},{1,3},{2,0},{3,1},{4,6},{5,7},{6,4},{7,5},{8,10},{9,11},{10,... | collective-permute-start | bytes 319496 | tf_op jit(solution)/shard_map/ppermute | solution.py:40
  9.5 0.5 %shard_map.88 = (f32[96,128]{1,0:T(8,128)S(1)}, f32[1,128]{1,0:T(1,128)S(1)}, f32[96,512]{1,0:T(8,128)S(1)}, f32[104,512]{1,0:T(8,128)S(1)}, bf16[96,512]{1,0:T(8,128)(2,1)S(1)}) custom-call(bf16[48,640]{1,0:T(8,128)(2,1)S(1)} %collective-permute-done.refs_0_, bf16[48,640]{1,0:T(8,128)(2,1)S(1)} %collective-permute-done.1.refs_1_, ...), custom_call_target="tpu_custom_call" | custom-call | tf_op jit(solution)/shard_map/pallas_call | solution.py:232
  10.1 0.5 %collective-permute-start.3 = (f16[104,512]{1,0:T(8,128)(2,1)S(1)}, f16[104,512]{1,0:T(8,128)(2,1)S(1)}, u32[]{:S(2)}, u32[]{:S(2)}) collective-permute-start(f16[104,512]{1,0:T(8,128)(2,1)S(1)} %convert_element_type.28), channel_id=1, source_target_pairs={{0,1},{1,0},{2,3},{3,2},{4,5},{5,4},{6,7},{7,6},{8,9},{9,8},{10,11... | collective-permute-start | bytes 319496 | tf_op jit(solution)/shard_map/ppermute | solution.py:40
  10.6 0.5 %collective-permute-start.7 = (bf16[96,512]{1,0:T(8,128)(2,1)S(1)}, bf16[96,512]{1,0:T(8,128)(2,1)S(1)}, u32[]{:S(2)}, u32[]{:S(2)}) collective-permute-start(bf16[96,512]{1,0:T(8,128)(2,1)S(1)} %get-tuple-element.73.refs_1_), channel_id=1, source_target_pairs={{0,4},{4,0},{1,5},{5,1},{2,6},{6,2},{3,7},{7,3},{8,12},{12,8},{9,1... | collective-permute-start | bytes 294920 | tf_op jit(solution)/shard_map/ppermute | solution.py:40
  11.1 1.7 %collective-permute-done.4 = f16[104,512]{1,0:T(8,128)(2,1)S(1)} collective-permute-done((f16[104,512]{1,0:T(8,128)(2,1)S(1)}, f16[104,512]{1,0:T(8,128)(2,1)S(1)}, u32[]{:S(2)}, u32[]{:S(2)}) %collective-permute-start.4) | collective-permute-done | bytes 106528 | tf_op jit(solution)/shard_map/ppermute | solution.py:40
  12.8 0.2 shard_map.89
  13.0 1.9 %collective-permute-done.3 = f16[104,512]{1,0:T(8,128)(2,1)S(1)} collective-permute-done((f16[104,512]{1,0:T(8,128)(2,1)S(1)}, f16[104,512]{1,0:T(8,128)(2,1)S(1)}, u32[]{:S(2)}, u32[]{:S(2)}) %collective-permute-start.3) | collective-permute-done | bytes 106528 | tf_op jit(solution)/shard_map/ppermute | solution.py:40
  14.9 0.2 shard_map.90
  15.2 0.7 %collective-permute-start.8 = (f16[104,512]{1,0:T(8,128)(2,1)S(1)}, f16[104,512]{1,0:T(8,128)(2,1)S(1)}, u32[]{:S(2)}, u32[]{:S(2)}) collective-permute-start(f16[104,512]{1,0:T(8,128)(2,1)S(1)} %convert_element_type.32), channel_id=1, source_target_pairs={{0,2},{2,0},{4,6},{6,4},{8,10},{10,8},{12,14},{14,12},{16,18},{18,... | collective-permute-start | bytes 319496 | tf_op jit(solution)/shard_map/ppermute | solution.py:40
  15.9 4.2 %collective-permute-start.9 = (f16[104,512]{1,0:T(8,128)(2,1)S(1)}, f16[104,512]{1,0:T(8,128)(2,1)S(1)}, u32[]{:S(2)}, u32[]{:S(2)}) collective-permute-start(f16[104,512]{1,0:T(8,128)(2,1)S(1)} %convert_element_type.34), channel_id=1, source_target_pairs={{0,1},{1,0},{2,3},{3,2},{4,5},{5,4},{6,7},{7,6},{8,9},{9,8},{10,11... | collective-permute-start | bytes 319496 | tf_op jit(solution)/shard_map/ppermute | solution.py:40
  20.0 2.4 %collective-permute-start.10 = (f16[104,512]{1,0:T(8,128)(2,1)S(1)}, f16[104,512]{1,0:T(8,128)(2,1)S(1)}, u32[]{:S(2)}, u32[]{:S(2)}) collective-permute-start(f16[104,512]{1,0:T(8,128)(2,1)S(1)} %convert_element_type.32), channel_id=1, source_target_pairs={{1,3},{3,1},{5,7},{7,5},{9,11},{11,9},{13,15},{15,13},{17,19},{19,... | collective-permute-start | bytes 319496 | tf_op jit(solution)/shard_map/ppermute | solution.py:40
  22.4 0.3 shard_map.91
  22.7 0.3 shard_map.92
  23.1 1.0 %collective-permute-done.9 = f16[104,512]{1,0:T(8,128)(2,1)S(1)} collective-permute-done((f16[104,512]{1,0:T(8,128)(2,1)S(1)}, f16[104,512]{1,0:T(8,128)(2,1)S(1)}, u32[]{:S(2)}, u32[]{:S(2)}) %collective-permute-start.9) | collective-permute-done | bytes 106528 | tf_op jit(solution)/shard_map/ppermute | solution.py:40
  24.1 3.4 %collective-permute-done.10 = f16[104,512]{1,0:T(8,128)(2,1)S(1)} collective-permute-done((f16[104,512]{1,0:T(8,128)(2,1)S(1)}, f16[104,512]{1,0:T(8,128)(2,1)S(1)}, u32[]{:S(2)}, u32[]{:S(2)}) %collective-permute-start.10) | collective-permute-done | bytes 106528 | tf_op jit(solution)/shard_map/ppermute | solution.py:40
  27.5 0.1 shard_map.93.scaled
  27.7 0.7 %shard_map.94 = (f32[256,256]{1,0:T(8,128)S(1)}, f32[256,256]{1,0:T(8,128)S(1)}) custom-call(bf16[192,512]{1,0:T(8,128)(2,1)S(1)} %shard_map.93.scaled, bf16[256,192]{1,0:T(8,128)(2,1)S(1)} %get-tuple-element.105.turned, bf16[192,256]{1,0:T(8,128)(2,1)S(1)} %get-tuple-element.106.act, f32[192,256]{1,0:T(8,128)S(1)} %get-tuple-element.107.slope, ...), custom_call_target="tpu_custom_call" | custom-call | tf_op jit(solution)/shard_map/pallas_call | solution.py:232
  28.4 0.7 %collective-permute-done.11.scaled = bf16[192,512]{1,0:T(8,128)(2,1)S(1)} collective-permute-done((bf16[192,512]{1,0:T(8,128)(2,1)S(1)}, bf16[192,512]{1,0:T(8,128)(2,1)S(1)}, u32[]{:S(2)}, u32[]{:S(2)}) %collective-permute-start.11) | collective-permute-done | bytes 196640 | tf_op jit(solution)/shard_map/ppermute | solution.py:40
  29.2 0.5 %shard_map.95 = (f32[128,256]{1,0:T(8,128)S(1)}, bf16[128,256]{1,0:T(8,128)(2,1)S(1)}, bf16[128,256]{1,0:T(8,128)(2,1)S(1)}, bf16[128,256]{1,0:T(8,128)(2,1)S(1)}) custom-call(bf16[192,512]{1,0:T(8,128)(2,1)S(1)} %collective-permute-done.11.scaled, bf16[256,192]{1,0:T(8,128)(2,1)S(1)} %get-tuple-element.101.turned, ...), custom_call_target="tpu_custom_call" | custom-call | tf_op jit(solution)/shard_map/pallas_call | solution.py:232
  29.6 1.8 %collective-permute-start.12 = (bf16[128,256]{1,0:T(8,128)(2,1)S(1)}, bf16[128,256]{1,0:T(8,128)(2,1)S(1)}, u32[]{:S(2)}, u32[]{:S(2)}) collective-permute-start(bf16[128,256]{1,0:T(8,128)(2,1)S(1)} %get-tuple-element.111), channel_id=1, source_target_pairs={{0,24},{8,16},{16,8},{24,0},{1,25},{9,17},{17,9},{25,1},{2,26},{10... | collective-permute-start | bytes 196616 | tf_op jit(solution)/shard_map/ppermute | solution.py:40
  31.4 1.1 %collective-permute-start.13 = (bf16[128,256]{1,0:T(8,128)(2,1)S(1)}, bf16[128,256]{1,0:T(8,128)(2,1)S(1)}, u32[]{:S(2)}, u32[]{:S(2)}) collective-permute-start(bf16[128,256]{1,0:T(8,128)(2,1)S(1)} %get-tuple-element.112), channel_id=1, source_target_pairs={{0,16},{8,24},{16,0},{24,8},{1,17},{9,25},{17,1},{25,9},{2,18},{10... | collective-permute-start | bytes 196616 | tf_op jit(solution)/shard_map/ppermute | solution.py:40
  32.5 0.7 %collective-permute-start.14 = (bf16[128,256]{1,0:T(8,128)(2,1)S(1)}, bf16[128,256]{1,0:T(8,128)(2,1)S(1)}, u32[]{:S(2)}, u32[]{:S(2)}) collective-permute-start(bf16[128,256]{1,0:T(8,128)(2,1)S(1)} %get-tuple-element.113), channel_id=1, source_target_pairs={{0,8},{8,0},{16,24},{24,16},{1,9},{9,1},{17,25},{25,17},{2,10},{10... | collective-permute-start | bytes 196616 | tf_op jit(solution)/shard_map/ppermute | solution.py:40
  33.2 1.7 %collective-permute-done.12.refs_1_ = bf16[128,256]{1,0:T(8,128)(2,1)S(1)} collective-permute-done((bf16[128,256]{1,0:T(8,128)(2,1)S(1)}, bf16[128,256]{1,0:T(8,128)(2,1)S(1)}, u32[]{:S(2)}, u32[]{:S(2)}) %collective-permute-start.12) | collective-permute-done | bytes 65568 | tf_op jit(solution)/shard_map/ppermute | solution.py:40
  34.9 1.2 %collective-permute-done.13.refs_2_ = bf16[128,256]{1,0:T(8,128)(2,1)S(1)} collective-permute-done((bf16[128,256]{1,0:T(8,128)(2,1)S(1)}, bf16[128,256]{1,0:T(8,128)(2,1)S(1)}, u32[]{:S(2)}, u32[]{:S(2)}) %collective-permute-start.13) | collective-permute-done | bytes 65568 | tf_op jit(solution)/shard_map/ppermute | solution.py:40
  36.1 0.7 %collective-permute-done.14.refs_3_ = bf16[128,256]{1,0:T(8,128)(2,1)S(1)} collective-permute-done((bf16[128,256]{1,0:T(8,128)(2,1)S(1)}, bf16[128,256]{1,0:T(8,128)(2,1)S(1)}, u32[]{:S(2)}, u32[]{:S(2)}) %collective-permute-start.14) | collective-permute-done | bytes 65568 | tf_op jit(solution)/shard_map/ppermute | solution.py:40
  36.8 0.7 %shard_map.96 = (f32[64,256]{1,0:T(8,128)}, f32[64,256]{1,0:T(8,128)}) custom-call(f32[128,256]{1,0:T(8,128)S(1)} %get-tuple-element.110.refs_0_, bf16[128,256]{1,0:T(8,128)(2,1)S(1)} %collective-permute-done.12.refs_1_, bf16[128,256]{1,0:T(8,128)(2,1)S(1)} %collective-permute-done.13.refs_2_, bf16[128,256]{1,0:T(8,128)(2,1)S(1)} %collective-permute-done.14.refs_3_), custom_call_target="tpu_custom_call" | custom-call | tf_op jit(solution)/shard_map/pallas_call | solution.py:232
  (18 shorter events, 0.2 us)
Async XLA Ops:
  2.0 4.3 %collective-permute-start.2 = (bf16[48,640]{1,0:T(8,128)(2,1)S(1)}, bf16[48,640]{1,0:T(8,128)(2,1)S(1)}, u32[]{:S(2)}, u32[]{:S(2)}) collective-permute-start(bf16[48,640]{1,0:T(8,128)(2,1)S(1)} %get-tuple-element.61), channel_id=1, source_target_pairs={{0,8},{8,0},{16,24},{24,16},{1,9},{9,1},{17,25},{25,17},{2,10},{10... | collective-permute-start | bytes 184328 | tf_op jit(solution)/shard_map/ppermute | solution.py:40
  3.5 5.9 %collective-permute-start = (bf16[48,640]{1,0:T(8,128)(2,1)S(1)}, bf16[48,640]{1,0:T(8,128)(2,1)S(1)}, u32[]{:S(2)}, u32[]{:S(2)}) collective-permute-start(bf16[48,640]{1,0:T(8,128)(2,1)S(1)} %get-tuple-element.58), channel_id=1, source_target_pairs={{0,24},{8,16},{16,8},{24,0},{1,25},{9,17},{17,9},{25,1},{2,26},{10... | collective-permute-start | bytes 184328 | tf_op jit(solution)/shard_map/ppermute | solution.py:40
  5.0 4.5 %collective-permute-start.1 = (bf16[48,640]{1,0:T(8,128)(2,1)S(1)}, bf16[48,640]{1,0:T(8,128)(2,1)S(1)}, u32[]{:S(2)}, u32[]{:S(2)}) collective-permute-start(bf16[48,640]{1,0:T(8,128)(2,1)S(1)} %get-tuple-element.59), channel_id=1, source_target_pairs={{0,16},{8,24},{16,0},{24,8},{1,17},{9,25},{17,1},{25,9},{2,18},{10... | collective-permute-start | bytes 184328 | tf_op jit(solution)/shard_map/ppermute | solution.py:40
  6.8 5.9 %collective-permute-start.4 = (f16[104,512]{1,0:T(8,128)(2,1)S(1)}, f16[104,512]{1,0:T(8,128)(2,1)S(1)}, u32[]{:S(2)}, u32[]{:S(2)}) collective-permute-start(f16[104,512]{1,0:T(8,128)(2,1)S(1)} %convert_element_type.30), channel_id=1, source_target_pairs={{0,2},{1,3},{2,0},{3,1},{4,6},{5,7},{6,4},{7,5},{8,10},{9,11},{10,... | collective-permute-start | bytes 319496 | tf_op jit(solution)/shard_map/ppermute | solution.py:40
  10.1 4.8 %collective-permute-start.3 = (f16[104,512]{1,0:T(8,128)(2,1)S(1)}, f16[104,512]{1,0:T(8,128)(2,1)S(1)}, u32[]{:S(2)}, u32[]{:S(2)}) collective-permute-start(f16[104,512]{1,0:T(8,128)(2,1)S(1)} %convert_element_type.28), channel_id=1, source_target_pairs={{0,1},{1,0},{2,3},{3,2},{4,5},{5,4},{6,7},{7,6},{8,9},{9,8},{10,11... | collective-permute-start | bytes 319496 | tf_op jit(solution)/shard_map/ppermute | solution.py:40
  10.6 2.2 %collective-permute-start.6 = (bf16[96,512]{1,0:T(8,128)(2,1)S(1)}, bf16[96,512]{1,0:T(8,128)(2,1)S(1)}, u32[]{:S(2)}, u32[]{:S(2)}) collective-permute-start(bf16[96,512]{1,0:T(8,128)(2,1)S(1)} %get-tuple-element.72.refs_0_), channel_id=1, source_target_pairs={{0,4},{4,0},{1,5},{5,1},{2,6},{6,2},{3,7},{7,3},{8,12},{12,8},{9,1... | collective-permute-start | bytes 294920 | tf_op jit(solution)/shard_map/ppermute | solution.py:40
  10.6 2.2 %collective-permute-start.7 = (bf16[96,512]{1,0:T(8,128)(2,1)S(1)}, bf16[96,512]{1,0:T(8,128)(2,1)S(1)}, u32[]{:S(2)}, u32[]{:S(2)}) collective-permute-start(bf16[96,512]{1,0:T(8,128)(2,1)S(1)} %get-tuple-element.73.refs_1_), channel_id=1, source_target_pairs={{0,4},{4,0},{1,5},{5,1},{2,6},{6,2},{3,7},{7,3},{8,12},{12,8},{9,1... | collective-permute-start | bytes 294920 | tf_op jit(solution)/shard_map/ppermute | solution.py:40
  11.1 1.7 %collective-permute-start.5 = (f32[1,128]{1,0:T(1,128)S(1)}, f32[1,128]{1,0:T(1,128)S(1)}, u32[]{:S(2)}, u32[]{:S(2)}) collective-permute-start(f32[1,128]{1,0:T(1,128)S(1)} %get-tuple-element.99.refs_7_), channel_id=1, source_target_pairs={{0,4},{4,0},{1,5},{5,1},{2,6},{6,2},{3,7},{7,3},{8,12},{12,8},{9,1... | collective-permute-start | bytes 1544 | tf_op jit(solution)/shard_map/ppermute | solution.py:40
  15.2 7.9 %collective-permute-start.8 = (f16[104,512]{1,0:T(8,128)(2,1)S(1)}, f16[104,512]{1,0:T(8,128)(2,1)S(1)}, u32[]{:S(2)}, u32[]{:S(2)}) collective-permute-start(f16[104,512]{1,0:T(8,128)(2,1)S(1)} %convert_element_type.32), channel_id=1, source_target_pairs={{0,2},{2,0},{4,6},{6,4},{8,10},{10,8},{12,14},{14,12},{16,18},{18,... | collective-permute-start | bytes 319496 | tf_op jit(solution)/shard_map/ppermute | solution.py:40
  15.9 8.2 %collective-permute-start.9 = (f16[104,512]{1,0:T(8,128)(2,1)S(1)}, f16[104,512]{1,0:T(8,128)(2,1)S(1)}, u32[]{:S(2)}, u32[]{:S(2)}) collective-permute-start(f16[104,512]{1,0:T(8,128)(2,1)S(1)} %convert_element_type.34), channel_id=1, source_target_pairs={{0,1},{1,0},{2,3},{3,2},{4,5},{5,4},{6,7},{7,6},{8,9},{9,8},{10,11... | collective-permute-start | bytes 319496 | tf_op jit(solution)/shard_map/ppermute | solution.py:40
  20.0 7.5 %collective-permute-start.10 = (f16[104,512]{1,0:T(8,128)(2,1)S(1)}, f16[104,512]{1,0:T(8,128)(2,1)S(1)}, u32[]{:S(2)}, u32[]{:S(2)}) collective-permute-start(f16[104,512]{1,0:T(8,128)(2,1)S(1)} %convert_element_type.32), channel_id=1, source_target_pairs={{1,3},{3,1},{5,7},{7,5},{9,11},{11,9},{13,15},{15,13},{17,19},{19,... | collective-permute-start | bytes 319496 | tf_op jit(solution)/shard_map/ppermute | solution.py:40
  27.6 1.5 %collective-permute-start.11 = (bf16[192,512]{1,0:T(8,128)(2,1)S(1)}, bf16[192,512]{1,0:T(8,128)(2,1)S(1)}, u32[]{:S(2)}, u32[]{:S(2)}) collective-permute-start(bf16[192,512]{1,0:T(8,128)(2,1)S(1)} %shard_map.93.scaled), channel_id=1, source_target_pairs={{0,4},{4,0},{1,5},{5,1},{2,6},{6,2},{3,7},{7,3},{8,12},{12,8},{9,1... | collective-permute-start | bytes 589832 | tf_op jit(solution)/shard_map/ppermute | solution.py:40
  29.6 5.3 %collective-permute-start.12 = (bf16[128,256]{1,0:T(8,128)(2,1)S(1)}, bf16[128,256]{1,0:T(8,128)(2,1)S(1)}, u32[]{:S(2)}, u32[]{:S(2)}) collective-permute-start(bf16[128,256]{1,0:T(8,128)(2,1)S(1)} %get-tuple-element.111), channel_id=1, source_target_pairs={{0,24},{8,16},{16,8},{24,0},{1,25},{9,17},{17,9},{25,1},{2,26},{10... | collective-permute-start | bytes 196616 | tf_op jit(solution)/shard_map/ppermute | solution.py:40
  31.4 4.7 %collective-permute-start.13 = (bf16[128,256]{1,0:T(8,128)(2,1)S(1)}, bf16[128,256]{1,0:T(8,128)(2,1)S(1)}, u32[]{:S(2)}, u32[]{:S(2)}) collective-permute-start(bf16[128,256]{1,0:T(8,128)(2,1)S(1)} %get-tuple-element.112), channel_id=1, source_target_pairs={{0,16},{8,24},{16,0},{24,8},{1,17},{9,25},{17,1},{25,9},{2,18},{10... | collective-permute-start | bytes 196616 | tf_op jit(solution)/shard_map/ppermute | solution.py:40
  32.5 4.3 %collective-permute-start.14 = (bf16[128,256]{1,0:T(8,128)(2,1)S(1)}, bf16[128,256]{1,0:T(8,128)(2,1)S(1)}, u32[]{:S(2)}, u32[]{:S(2)}) collective-permute-start(bf16[128,256]{1,0:T(8,128)(2,1)S(1)} %get-tuple-element.113), channel_id=1, source_target_pairs={{0,8},{8,0},{16,24},{24,16},{1,9},{9,1},{17,25},{25,17},{2,10},{10... | collective-permute-start | bytes 196616 | tf_op jit(solution)/shard_map/ppermute | solution.py:40

commit v22 on v20

--- a/solution.py
+++ b/solution.py
@@ -47,7 +47,8 @@
     out[height:] = jnp.broadcast_to(power, (PACK_ROWS, value.shape[1]))
 
 
-def unpack(block, height):
+def unpack(block):
+    height = block.shape[0] - PACK_ROWS
     return block[:height] * jnp.exp2(block[height : height + 1, :1] - PACK_TOP)
 
 
@@ -171,13 +172,13 @@
 
 def pair_body(own, arrived, *refs):
     total, packed = refs[-2:]
-    value = own[...] + unpack(arrived, own.shape[0])
+    value = own[...] + unpack(arrived)
     total[...] = value
     pack(value, packed)
 
 
 def scale_body(*refs):
-    halves, tags, counts, scaled = (refs[:2], refs[2:4]), refs[4:6], refs[6:-1], refs[-1]
+    halves, tags, counts, scaled = (refs[2:4], refs[:2]), refs[4:6], refs[6:-1], refs[-1]
     all_counts = counts[0][...]
     for piece in counts[1:]:
         all_counts = all_counts + piece[...]
@@ -186,7 +187,7 @@
     for (own, arrived), tag in zip(halves, tags):
         weight = jnp.sum(tag[...] * inverse, axis=1, keepdims=True)
         span = slice(start, start + own.shape[0])
-        scaled[span] = ((own[...] + unpack(arrived, own.shape[0])) * weight).astype(scaled.dtype)
+        scaled[span] = ((own[...] + unpack(arrived)) * weight).astype(scaled.dtype)
         start += own.shape[0]
 
 
@@ -281,26 +282,26 @@
 
     steps = [1 << i for i in range(parts.bit_length() - 1)]
     second_tags, counts, second, second_out, second_rows = forward(near)
-    second_in = cross(second_out, steps[0])
+    second_in = cross(second_out, steps[-1])
     first_tags, counts, first, first_out, first_rows = forward(far, counts)
-    first_in = cross(first_out, steps[-1])
+    first_in = cross(first_out, steps[0])
     rows, tags = (first_rows, second_rows), (first_tags, second_tags)
     all_counts, mates = [counts], []
     for k in range(1, studs):
         all_counts.append(send(counts, "stud", k))
         mates.append([send(part, "stud", k) for part in rows])
-    second_in, all_counts = lax.optimization_barrier((second_in, all_counts))
+    second_in, all_counts, mates = lax.optimization_barrier((second_in, all_counts, mates))
     for there, back in zip(steps[1:], steps[-2::-1]):
         second, second_out = kernel(pair_body, [half, packed], (second, second_in), 0)
-        second_in = cross(second_out, there)
         first, first_out = kernel(pair_body, [half, packed], (first, first_in, second), 0)
-        first_in = cross(first_out, back)
+        first_out, second_out = lax.optimization_barrier((first_out, second_out))
+        first_in, second_in = cross(first_out, there), cross(second_out, back)
     ahead = functools.partial(ahead_body, owners, studs)
     *ours, chosen = kernel(
         ahead, state + [shape(actions // studs, actions, bf16)], (*rows, weights[2], first), 0
     )
     known = [ours] + [kernel(ahead, state, (*theirs, weights[2], first), 0) for theirs in mates]
-    sums = (first, first_in, second, second_in)
+    sums = (second, second_in, first, first_in)
     sums, all_counts, known, chosen = lax.optimization_barrier((sums, all_counts, known, chosen))
     (scaled,) = kernel(scale_body, [shape(slots, actions, bf16)], (*sums, *tags, *all_counts), 0)
     errors = [scaled] + [send(scaled, "stud", k) for k in range(1, studs)]

time: 35.6 us -> 35.1 us (0.986)
  waiting for transfers between devices: 11.6 us -> 10.5 us
  starting transfers between devices: 17.5 us -> 18.1 us
    ppermute x14, waiting for transfers between devices: 11.6 us -> 10.5 us  [send(): lax.ppermute(block, axis, [(i, partner_to(size, i, step)) for i in range(...]
    ppermute x14, starting transfers between devices: 17.5 us -> 18.1 us  [send(): lax.ppermute(block, axis, [(i, partner_to(size, i, step)) for i in range(...]
  transfers between devices with their start and end apart: 14 -> 14, of which waited for: 12 -> 10; matrix products, arithmetic and copies ran while one was open for 0% -> 0% of each run, Pallas kernels for 8% -> 7%
where the time goes in v22:
time: 35.1 us; the launch traced here: 35 us
  starting transfers between devices  18.1 us (52%)
  waiting for transfers between devices  10.5 us (30%)
  Pallas kernels  5.47 us (16%)
  between operations  0.77 us (2%)
    ppermute x14, starting transfers between devices, send(): lax.ppermute(block, axis, [(i, partner_to(size, i, step)) for i in range(...  18.1 us
    ppermute x14, waiting for transfers between devices, send(): lax.ppermute(block, axis, [(i, partner_to(size, i, step)) for i in range(...  10.5 us
    pallas_call x11, Pallas kernels, kernel(): pl.pallas_call(body, out_shape=outs, in_specs=places or [VMEM] * len(oper...  5.47 us
  transfers between devices with their start and end apart: 14, of which 10 were waited for; matrix products, arithmetic and copies ran while one was open for 0% of the time, Pallas kernels for 7%

profile of v22, /device:TPU:0, one launch (start us, length us, event | category | flops | bytes accessed | tf_op | source)
XLA Modules:
  0.0 35.0 jit_solution(18044814532734085372)
XLA Ops:
  0.6 1.3 %shard_map.86 = (bf16[48,640]{1,0:T(8,128)(2,1)S(1)}, bf16[48,640]{1,0:T(8,128)(2,1)S(1)}, bf16[48,640]{1,0:T(8,128)(2,1)S(1)}, bf16[48,640]{1,0:T(8,128)(2,1)S(...) custom-call(bf16[128,512]{1,0:T(8,128)(2,1)} %refs_0_.1, ...), custom_call_target="tpu_custom_call" | custom-call | tf_op jit(solution)/shard_map/pallas_call | solution.py:228
  2.0 3.0 %collective-permute-start = (bf16[48,640]{1,0:T(8,128)(2,1)S(1)}, bf16[48,640]{1,0:T(8,128)(2,1)S(1)}, u32[]{:S(2)}, u32[]{:S(2)}) collective-permute-start(bf16[48,640]{1,0:T(8,128)(2,1)S(1)} %get-tuple-element.58), channel_id=1, source_target_pairs={{0,8},{8,0},{16,24},{24,16},{1,9},{9,1},{17,25},{25,17},{2,10},{10... | collective-permute-start | bytes 184328 | tf_op jit(solution)/shard_map/ppermute | solution.py:39
  5.0 1.5 %collective-permute-start.2 = (bf16[48,640]{1,0:T(8,128)(2,1)S(1)}, bf16[48,640]{1,0:T(8,128)(2,1)S(1)}, u32[]{:S(2)}, u32[]{:S(2)}) collective-permute-start(bf16[48,640]{1,0:T(8,128)(2,1)S(1)} %get-tuple-element.65), channel_id=1, source_target_pairs={{0,24},{8,16},{16,8},{24,0},{1,25},{9,17},{17,9},{25,1},{2,26},{10... | collective-permute-start | bytes 184328 | tf_op jit(solution)/shard_map/ppermute | solution.py:39
  6.5 0.8 %collective-permute-done.refs_1_ = bf16[48,640]{1,0:T(8,128)(2,1)S(1)} collective-permute-done((bf16[48,640]{1,0:T(8,128)(2,1)S(1)}, bf16[48,640]{1,0:T(8,128)(2,1)S(1)}, u32[]{:S(2)}, u32[]{:S(2)}) %collective-permute-start) | collective-permute-done | bytes 61472 | tf_op jit(solution)/shard_map/ppermute | solution.py:39
  7.3 0.5 %shard_map.87 = (f32[96,128]{1,0:T(8,128)S(1)}, f32[1,128]{1,0:T(1,128)S(1)}, f32[96,512]{1,0:T(8,128)S(1)}, f32[104,512]{1,0:T(8,128)S(1)}, bf16[96,512]{1,0:T(8,128)(2,1)S(1)}) custom-call(bf16[48,640]{1,0:T(8,128)(2,1)S(1)} %get-tuple-element.57.refs_0_, bf16[48,640]{1,0:T(8,128)(2,1)S(1)} %collective-permute-done.refs_1_, ...), custom_call_target="tpu_custom_call" | custom-call | tf_op jit(solution)/shard_map/pallas_call | solution.py:228
  7.9 3.1 %collective-permute-start.1 = (f16[104,512]{1,0:T(8,128)(2,1)S(1)}, f16[104,512]{1,0:T(8,128)(2,1)S(1)}, u32[]{:S(2)}, u32[]{:S(2)}) collective-permute-start(f16[104,512]{1,0:T(8,128)(2,1)S(1)} %convert_element_type.24), channel_id=1, source_target_pairs={{0,2},{1,3},{2,0},{3,1},{4,6},{5,7},{6,4},{7,5},{8,10},{9,11},{10,... | collective-permute-start | bytes 319496 | tf_op jit(solution)/shard_map/ppermute | solution.py:39
  10.9 0.5 %shard_map.88 = (f32[96,128]{1,0:T(8,128)S(1)}, f32[1,128]{1,0:T(1,128)S(1)}, f32[96,512]{1,0:T(8,128)S(1)}, f32[104,512]{1,0:T(8,128)S(1)}, bf16[96,512]{1,0:T(8,128)(2,1)S(1)}) custom-call(bf16[48,640]{1,0:T(8,128)(2,1)S(1)} %collective-permute-done.2.refs_0_, bf16[48,640]{1,0:T(8,128)(2,1)S(1)} %collective-permute-done.3.refs_1_, ...), custom_call_target="tpu_custom_call" | custom-call | tf_op jit(solution)/shard_map/pallas_call | solution.py:228
  11.5 1.6 %collective-permute-start.7 = (f16[104,512]{1,0:T(8,128)(2,1)S(1)}, f16[104,512]{1,0:T(8,128)(2,1)S(1)}, u32[]{:S(2)}, u32[]{:S(2)}) collective-permute-start(f16[104,512]{1,0:T(8,128)(2,1)S(1)} %convert_element_type.26), channel_id=1, source_target_pairs={{0,1},{1,0},{2,3},{3,2},{4,5},{5,4},{6,7},{7,6},{8,9},{9,8},{10,11... | collective-permute-start | bytes 319496 | tf_op jit(solution)/shard_map/ppermute | solution.py:39
  13.1 0.5 %collective-permute-start.6 = (bf16[96,512]{1,0:T(8,128)(2,1)S(1)}, bf16[96,512]{1,0:T(8,128)(2,1)S(1)}, u32[]{:S(2)}, u32[]{:S(2)}) collective-permute-start(bf16[96,512]{1,0:T(8,128)(2,1)S(1)} %get-tuple-element.70.refs_1_), channel_id=1, source_target_pairs={{0,4},{4,0},{1,5},{5,1},{2,6},{6,2},{3,7},{7,3},{8,12},{12,8},{9,1... | collective-permute-start | bytes 294920 | tf_op jit(solution)/shard_map/ppermute | solution.py:39
  13.7 0.3 collective-permute-done.1
  14.0 0.8 %collective-permute-done.4.refs_7_ = f32[1,128]{1,0:T(1,128)S(1)} collective-permute-done((f32[1,128]{1,0:T(1,128)S(1)}, f32[1,128]{1,0:T(1,128)S(1)}, u32[]{:S(2)}, u32[]{:S(2)}) %collective-permute-start.4) | collective-permute-done | bytes 544 | tf_op jit(solution)/shard_map/ppermute | solution.py:39
  14.8 0.2 shard_map.89
  15.0 1.3 %collective-permute-done.7 = f16[104,512]{1,0:T(8,128)(2,1)S(1)} collective-permute-done((f16[104,512]{1,0:T(8,128)(2,1)S(1)}, f16[104,512]{1,0:T(8,128)(2,1)S(1)}, u32[]{:S(2)}, u32[]{:S(2)}) %collective-permute-start.7) | collective-permute-done | bytes 106528 | tf_op jit(solution)/shard_map/ppermute | solution.py:39
  16.3 0.2 shard_map.90
  16.5 2.5 %collective-permute-start.9 = (f16[104,512]{1,0:T(8,128)(2,1)S(1)}, f16[104,512]{1,0:T(8,128)(2,1)S(1)}, u32[]{:S(2)}, u32[]{:S(2)}) collective-permute-start(f16[104,512]{1,0:T(8,128)(2,1)S(1)} %convert_element_type.30), channel_id=1, source_target_pairs={{0,2},{1,3},{2,0},{3,1},{4,6},{5,7},{6,4},{7,5},{8,10},{9,11},{10,... | collective-permute-start | bytes 319496 | tf_op jit(solution)/shard_map/ppermute | solution.py:39
  19.1 2.2 %collective-permute-start.8 = (f16[104,512]{1,0:T(8,128)(2,1)S(1)}, f16[104,512]{1,0:T(8,128)(2,1)S(1)}, u32[]{:S(2)}, u32[]{:S(2)}) collective-permute-start(f16[104,512]{1,0:T(8,128)(2,1)S(1)} %convert_element_type.28), channel_id=1, source_target_pairs={{0,1},{1,0},{2,3},{3,2},{4,5},{5,4},{6,7},{7,6},{8,9},{9,8},{10,11... | collective-permute-start | bytes 319496 | tf_op jit(solution)/shard_map/ppermute | solution.py:39
  21.3 0.3 shard_map.91
  21.6 0.3 shard_map.92
  21.9 2.2 %collective-permute-done.9 = f16[104,512]{1,0:T(8,128)(2,1)S(1)} collective-permute-done((f16[104,512]{1,0:T(8,128)(2,1)S(1)}, f16[104,512]{1,0:T(8,128)(2,1)S(1)}, u32[]{:S(2)}, u32[]{:S(2)}) %collective-permute-start.9) | collective-permute-done | bytes 106528 | tf_op jit(solution)/shard_map/ppermute | solution.py:39
  24.2 0.5 %collective-permute-done.8 = f16[104,512]{1,0:T(8,128)(2,1)S(1)} collective-permute-done((f16[104,512]{1,0:T(8,128)(2,1)S(1)}, f16[104,512]{1,0:T(8,128)(2,1)S(1)}, u32[]{:S(2)}, u32[]{:S(2)}) %collective-permute-start.8) | collective-permute-done | bytes 106528 | tf_op jit(solution)/shard_map/ppermute | solution.py:39
  24.7 0.2 shard_map.93.scaled
  24.9 0.1 collective-permute-start.10
  25.0 0.7 %shard_map.94 = (f32[256,256]{1,0:T(8,128)S(1)}, f32[256,256]{1,0:T(8,128)S(1)}) custom-call(bf16[192,512]{1,0:T(8,128)(2,1)S(1)} %shard_map.93.scaled, bf16[256,192]{1,0:T(8,128)(2,1)S(1)} %get-tuple-element.103.turned, bf16[192,256]{1,0:T(8,128)(2,1)S(1)} %get-tuple-element.104.act, f32[192,256]{1,0:T(8,128)S(1)} %get-tuple-element.105.slope, ...), custom_call_target="tpu_custom_call" | custom-call | tf_op jit(solution)/shard_map/pallas_call | solution.py:228
  25.6 0.7 %collective-permute-done.10.scaled = bf16[192,512]{1,0:T(8,128)(2,1)S(1)} collective-permute-done((bf16[192,512]{1,0:T(8,128)(2,1)S(1)}, bf16[192,512]{1,0:T(8,128)(2,1)S(1)}, u32[]{:S(2)}, u32[]{:S(2)}) %collective-permute-start.10) | collective-permute-done | bytes 196640 | tf_op jit(solution)/shard_map/ppermute | solution.py:39
  26.4 0.5 %shard_map.95 = (f32[128,256]{1,0:T(8,128)S(1)}, bf16[128,256]{1,0:T(8,128)(2,1)S(1)}, bf16[128,256]{1,0:T(8,128)(2,1)S(1)}, bf16[128,256]{1,0:T(8,128)(2,1)S(1)}) custom-call(bf16[192,512]{1,0:T(8,128)(2,1)S(1)} %collective-permute-done.10.scaled, bf16[256,192]{1,0:T(8,128)(2,1)S(1)} %get-tuple-element.99.turned, ...), custom_call_target="tpu_custom_call" | custom-call | tf_op jit(solution)/shard_map/pallas_call | solution.py:228
  26.9 1.9 %collective-permute-start.11 = (bf16[128,256]{1,0:T(8,128)(2,1)S(1)}, bf16[128,256]{1,0:T(8,128)(2,1)S(1)}, u32[]{:S(2)}, u32[]{:S(2)}) collective-permute-start(bf16[128,256]{1,0:T(8,128)(2,1)S(1)} %get-tuple-element.109), channel_id=1, source_target_pairs={{0,24},{8,16},{16,8},{24,0},{1,25},{9,17},{17,9},{25,1},{2,26},{10... | collective-permute-start | bytes 196616 | tf_op jit(solution)/shard_map/ppermute | solution.py:39
  28.8 1.2 %collective-permute-start.12 = (bf16[128,256]{1,0:T(8,128)(2,1)S(1)}, bf16[128,256]{1,0:T(8,128)(2,1)S(1)}, u32[]{:S(2)}, u32[]{:S(2)}) collective-permute-start(bf16[128,256]{1,0:T(8,128)(2,1)S(1)} %get-tuple-element.110), channel_id=1, source_target_pairs={{0,16},{8,24},{16,0},{24,8},{1,17},{9,25},{17,1},{25,9},{2,18},{10... | collective-permute-start | bytes 196616 | tf_op jit(solution)/shard_map/ppermute | solution.py:39
  30.0 0.4 %collective-permute-start.13 = (bf16[128,256]{1,0:T(8,128)(2,1)S(1)}, bf16[128,256]{1,0:T(8,128)(2,1)S(1)}, u32[]{:S(2)}, u32[]{:S(2)}) collective-permute-start(bf16[128,256]{1,0:T(8,128)(2,1)S(1)} %get-tuple-element.111), channel_id=1, source_target_pairs={{0,8},{8,0},{16,24},{24,16},{1,9},{9,1},{17,25},{25,17},{2,10},{10... | collective-permute-start | bytes 196616 | tf_op jit(solution)/shard_map/ppermute | solution.py:39
  30.4 1.7 %collective-permute-done.11.refs_1_ = bf16[128,256]{1,0:T(8,128)(2,1)S(1)} collective-permute-done((bf16[128,256]{1,0:T(8,128)(2,1)S(1)}, bf16[128,256]{1,0:T(8,128)(2,1)S(1)}, u32[]{:S(2)}, u32[]{:S(2)}) %collective-permute-start.11) | collective-permute-done | bytes 65568 | tf_op jit(solution)/shard_map/ppermute | solution.py:39
  32.2 1.2 %collective-permute-done.12.refs_2_ = bf16[128,256]{1,0:T(8,128)(2,1)S(1)} collective-permute-done((bf16[128,256]{1,0:T(8,128)(2,1)S(1)}, bf16[128,256]{1,0:T(8,128)(2,1)S(1)}, u32[]{:S(2)}, u32[]{:S(2)}) %collective-permute-start.12) | collective-permute-done | bytes 65568 | tf_op jit(solution)/shard_map/ppermute | solution.py:39
  33.4 0.9 %collective-permute-done.13.refs_3_ = bf16[128,256]{1,0:T(8,128)(2,1)S(1)} collective-permute-done((bf16[128,256]{1,0:T(8,128)(2,1)S(1)}, bf16[128,256]{1,0:T(8,128)(2,1)S(1)}, u32[]{:S(2)}, u32[]{:S(2)}) %collective-permute-start.13) | collective-permute-done | bytes 65568 | tf_op jit(solution)/shard_map/ppermute | solution.py:39
  34.3 0.7 %shard_map.96 = (f32[64,256]{1,0:T(8,128)}, f32[64,256]{1,0:T(8,128)}) custom-call(f32[128,256]{1,0:T(8,128)S(1)} %get-tuple-element.108.refs_0_, bf16[128,256]{1,0:T(8,128)(2,1)S(1)} %collective-permute-done.11.refs_1_, bf16[128,256]{1,0:T(8,128)(2,1)S(1)} %collective-permute-done.12.refs_2_, bf16[128,256]{1,0:T(8,128)(2,1)S(1)} %collective-permute-done.13.refs_3_), custom_call_target="tpu_custom_call" | custom-call | tf_op jit(solution)/shard_map/pallas_call | solution.py:228
  (15 shorter events, 0.2 us)
Async XLA Ops:
  2.0 5.3 %collective-permute-start = (bf16[48,640]{1,0:T(8,128)(2,1)S(1)}, bf16[48,640]{1,0:T(8,128)(2,1)S(1)}, u32[]{:S(2)}, u32[]{:S(2)}) collective-permute-start(bf16[48,640]{1,0:T(8,128)(2,1)S(1)} %get-tuple-element.58), channel_id=1, source_target_pairs={{0,8},{8,0},{16,24},{24,16},{1,9},{9,1},{17,25},{25,17},{2,10},{10... | collective-permute-start | bytes 184328 | tf_op jit(solution)/shard_map/ppermute | solution.py:39
  5.0 6.0 %collective-permute-start.2 = (bf16[48,640]{1,0:T(8,128)(2,1)S(1)}, bf16[48,640]{1,0:T(8,128)(2,1)S(1)}, u32[]{:S(2)}, u32[]{:S(2)}) collective-permute-start(bf16[48,640]{1,0:T(8,128)(2,1)S(1)} %get-tuple-element.65), channel_id=1, source_target_pairs={{0,24},{8,16},{16,8},{24,0},{1,25},{9,17},{17,9},{25,1},{2,26},{10... | collective-permute-start | bytes 184328 | tf_op jit(solution)/shard_map/ppermute | solution.py:39
  6.5 4.5 %collective-permute-start.3 = (bf16[48,640]{1,0:T(8,128)(2,1)S(1)}, bf16[48,640]{1,0:T(8,128)(2,1)S(1)}, u32[]{:S(2)}, u32[]{:S(2)}) collective-permute-start(bf16[48,640]{1,0:T(8,128)(2,1)S(1)} %get-tuple-element.66), channel_id=1, source_target_pairs={{0,16},{8,24},{16,0},{24,8},{1,17},{9,25},{17,1},{25,9},{2,18},{10... | collective-permute-start | bytes 184328 | tf_op jit(solution)/shard_map/ppermute | solution.py:39
  7.9 6.1 %collective-permute-start.1 = (f16[104,512]{1,0:T(8,128)(2,1)S(1)}, f16[104,512]{1,0:T(8,128)(2,1)S(1)}, u32[]{:S(2)}, u32[]{:S(2)}) collective-permute-start(f16[104,512]{1,0:T(8,128)(2,1)S(1)} %convert_element_type.24), channel_id=1, source_target_pairs={{0,2},{1,3},{2,0},{3,1},{4,6},{5,7},{6,4},{7,5},{8,10},{9,11},{10,... | collective-permute-start | bytes 319496 | tf_op jit(solution)/shard_map/ppermute | solution.py:39
  11.5 4.8 %collective-permute-start.7 = (f16[104,512]{1,0:T(8,128)(2,1)S(1)}, f16[104,512]{1,0:T(8,128)(2,1)S(1)}, u32[]{:S(2)}, u32[]{:S(2)}) collective-permute-start(f16[104,512]{1,0:T(8,128)(2,1)S(1)} %convert_element_type.26), channel_id=1, source_target_pairs={{0,1},{1,0},{2,3},{3,2},{4,5},{5,4},{6,7},{7,6},{8,9},{9,8},{10,11... | collective-permute-start | bytes 319496 | tf_op jit(solution)/shard_map/ppermute | solution.py:39
  13.1 1.6 %collective-permute-start.5 = (bf16[96,512]{1,0:T(8,128)(2,1)S(1)}, bf16[96,512]{1,0:T(8,128)(2,1)S(1)}, u32[]{:S(2)}, u32[]{:S(2)}) collective-permute-start(bf16[96,512]{1,0:T(8,128)(2,1)S(1)} %get-tuple-element.69.refs_0_), channel_id=1, source_target_pairs={{0,4},{4,0},{1,5},{5,1},{2,6},{6,2},{3,7},{7,3},{8,12},{12,8},{9,1... | collective-permute-start | bytes 294920 | tf_op jit(solution)/shard_map/ppermute | solution.py:39
  13.1 1.6 %collective-permute-start.6 = (bf16[96,512]{1,0:T(8,128)(2,1)S(1)}, bf16[96,512]{1,0:T(8,128)(2,1)S(1)}, u32[]{:S(2)}, u32[]{:S(2)}) collective-permute-start(bf16[96,512]{1,0:T(8,128)(2,1)S(1)} %get-tuple-element.70.refs_1_), channel_id=1, source_target_pairs={{0,4},{4,0},{1,5},{5,1},{2,6},{6,2},{3,7},{7,3},{8,12},{12,8},{9,1... | collective-permute-start | bytes 294920 | tf_op jit(solution)/shard_map/ppermute | solution.py:39
  13.7 1.1 %collective-permute-start.4 = (f32[1,128]{1,0:T(1,128)S(1)}, f32[1,128]{1,0:T(1,128)S(1)}, u32[]{:S(2)}, u32[]{:S(2)}) collective-permute-start(f32[1,128]{1,0:T(1,128)S(1)} %get-tuple-element.97.refs_6_), channel_id=1, source_target_pairs={{0,4},{4,0},{1,5},{5,1},{2,6},{6,2},{3,7},{7,3},{8,12},{12,8},{9,1... | collective-permute-start | bytes 1544 | tf_op jit(solution)/shard_map/ppermute | solution.py:39
  16.5 7.6 %collective-permute-start.9 = (f16[104,512]{1,0:T(8,128)(2,1)S(1)}, f16[104,512]{1,0:T(8,128)(2,1)S(1)}, u32[]{:S(2)}, u32[]{:S(2)}) collective-permute-start(f16[104,512]{1,0:T(8,128)(2,1)S(1)} %convert_element_type.30), channel_id=1, source_target_pairs={{0,2},{1,3},{2,0},{3,1},{4,6},{5,7},{6,4},{7,5},{8,10},{9,11},{10,... | collective-permute-start | bytes 319496 | tf_op jit(solution)/shard_map/ppermute | solution.py:39
  19.1 5.6 %collective-permute-start.8 = (f16[104,512]{1,0:T(8,128)(2,1)S(1)}, f16[104,512]{1,0:T(8,128)(2,1)S(1)}, u32[]{:S(2)}, u32[]{:S(2)}) collective-permute-start(f16[104,512]{1,0:T(8,128)(2,1)S(1)} %convert_element_type.28), channel_id=1, source_target_pairs={{0,1},{1,0},{2,3},{3,2},{4,5},{5,4},{6,7},{7,6},{8,9},{9,8},{10,11... | collective-permute-start | bytes 319496 | tf_op jit(solution)/shard_map/ppermute | solution.py:39
  24.9 1.5 %collective-permute-start.10 = (bf16[192,512]{1,0:T(8,128)(2,1)S(1)}, bf16[192,512]{1,0:T(8,128)(2,1)S(1)}, u32[]{:S(2)}, u32[]{:S(2)}) collective-permute-start(bf16[192,512]{1,0:T(8,128)(2,1)S(1)} %shard_map.93.scaled), channel_id=1, source_target_pairs={{0,4},{4,0},{1,5},{5,1},{2,6},{6,2},{3,7},{7,3},{8,12},{12,8},{9,1... | collective-permute-start | bytes 589832 | tf_op jit(solution)/shard_map/ppermute | solution.py:39
  26.9 5.3 %collective-permute-start.11 = (bf16[128,256]{1,0:T(8,128)(2,1)S(1)}, bf16[128,256]{1,0:T(8,128)(2,1)S(1)}, u32[]{:S(2)}, u32[]{:S(2)}) collective-permute-start(bf16[128,256]{1,0:T(8,128)(2,1)S(1)} %get-tuple-element.109), channel_id=1, source_target_pairs={{0,24},{8,16},{16,8},{24,0},{1,25},{9,17},{17,9},{25,1},{2,26},{10... | collective-permute-start | bytes 196616 | tf_op jit(solution)/shard_map/ppermute | solution.py:39
  28.8 4.6 %collective-permute-start.12 = (bf16[128,256]{1,0:T(8,128)(2,1)S(1)}, bf16[128,256]{1,0:T(8,128)(2,1)S(1)}, u32[]{:S(2)}, u32[]{:S(2)}) collective-permute-start(bf16[128,256]{1,0:T(8,128)(2,1)S(1)} %get-tuple-element.110), channel_id=1, source_target_pairs={{0,16},{8,24},{16,0},{24,8},{1,17},{9,25},{17,1},{25,9},{2,18},{10... | collective-permute-start | bytes 196616 | tf_op jit(solution)/shard_map/ppermute | solution.py:39
  30.0 4.3 %collective-permute-start.13 = (bf16[128,256]{1,0:T(8,128)(2,1)S(1)}, bf16[128,256]{1,0:T(8,128)(2,1)S(1)}, u32[]{:S(2)}, u32[]{:S(2)}) collective-permute-start(bf16[128,256]{1,0:T(8,128)(2,1)S(1)} %get-tuple-element.111), channel_id=1, source_target_pairs={{0,8},{8,0},{16,24},{24,16},{1,9},{9,1},{17,25},{25,17},{2,10},{10... | collective-permute-start | bytes 196616 | tf_op jit(solution)/shard_map/ppermute | solution.py:39

commit v23 on v22

--- a/solution.py
+++ b/solution.py
@@ -268,8 +268,8 @@
     )
     blocks, weights = results[:owners], results[owners:]
     middle = owners // 2
-    near = [blocks[0]] + [send(blocks[k], "teach", k) for k in range(1, middle)]
-    far = [send(blocks[k], "teach", k) for k in range(owners - 1, middle - 1, -1)]
+    near = [blocks[0]] + [send(blocks[k], "teach", k) for k in range(owners - 1, middle, -1)]
+    far = [send(blocks[k], "teach", k) for k in range(middle, 0, -1)]
 
     def forward(blocks, *earlier):
         rows = len(blocks) * local * room

time: 35.1 us -> 35.1 us (level)
  starting transfers between devices: 18.1 us -> 17.5 us
  waiting for transfers between devices: 10.5 us -> 11.1 us
    ppermute x14, waiting for transfers between devices: 10.5 us -> 11.1 us  [send(): lax.ppermute(block, axis, [(i, partner_to(size, i, step)) for i in range(...]
    ppermute x14, starting transfers between devices: 18.1 us -> 17.5 us  [send(): lax.ppermute(block, axis, [(i, partner_to(size, i, step)) for i in range(...]
where the time goes in v23:
time: 35.1 us; the launch traced here: 35 us
  starting transfers between devices  17.5 us (50%)
  waiting for transfers between devices  11.1 us (32%)
  Pallas kernels  5.47 us (16%)
  between operations  0.77 us (2%)
    ppermute x14, starting transfers between devices, send(): lax.ppermute(block, axis, [(i, partner_to(size, i, step)) for i in range(...  17.5 us
    ppermute x14, waiting for transfers between devices, send(): lax.ppermute(block, axis, [(i, partner_to(size, i, step)) for i in range(...  11.1 us
    pallas_call x11, Pallas kernels, kernel(): pl.pallas_call(body, out_shape=outs, in_specs=places or [VMEM] * len(oper...  5.47 us
  transfers between devices with their start and end apart: 14, of which 10 were waited for; matrix products, arithmetic and copies ran while one was open for 0% of the time, Pallas kernels for 7%

profile of v23, /device:TPU:0, one launch (start us, length us, event | category | flops | bytes accessed | tf_op | source)
XLA Modules:
  0.0 35.0 jit_solution(15024162899038832924)
XLA Ops:
  0.6 1.3 %shard_map.86 = (bf16[48,640]{1,0:T(8,128)(2,1)S(1)}, bf16[48,640]{1,0:T(8,128)(2,1)S(1)}, bf16[48,640]{1,0:T(8,128)(2,1)S(1)}, bf16[48,640]{1,0:T(8,128)(2,1)S(...) custom-call(bf16[128,512]{1,0:T(8,128)(2,1)} %refs_0_.1, ...), custom_call_target="tpu_custom_call" | custom-call | tf_op jit(solution)/shard_map/pallas_call | solution.py:228
  2.0 4.0 %collective-permute-start = (bf16[48,640]{1,0:T(8,128)(2,1)S(1)}, bf16[48,640]{1,0:T(8,128)(2,1)S(1)}, u32[]{:S(2)}, u32[]{:S(2)}) collective-permute-start(bf16[48,640]{1,0:T(8,128)(2,1)S(1)} %get-tuple-element.58), channel_id=1, source_target_pairs={{0,24},{8,16},{16,8},{24,0},{1,25},{9,17},{17,9},{25,1},{2,26},{10... | collective-permute-start | bytes 184328 | tf_op jit(solution)/shard_map/ppermute | solution.py:39
  5.9 0.5 %collective-permute-start.2 = (bf16[48,640]{1,0:T(8,128)(2,1)S(1)}, bf16[48,640]{1,0:T(8,128)(2,1)S(1)}, u32[]{:S(2)}, u32[]{:S(2)}) collective-permute-start(bf16[48,640]{1,0:T(8,128)(2,1)S(1)} %get-tuple-element.65), channel_id=1, source_target_pairs={{0,16},{8,24},{16,0},{24,8},{1,17},{9,25},{17,1},{25,9},{2,18},{10... | collective-permute-start | bytes 184328 | tf_op jit(solution)/shard_map/ppermute | solution.py:39
  6.5 0.1 collective-permute-start.3
  6.6 1.6 %collective-permute-done.refs_1_ = bf16[48,640]{1,0:T(8,128)(2,1)S(1)} collective-permute-done((bf16[48,640]{1,0:T(8,128)(2,1)S(1)}, bf16[48,640]{1,0:T(8,128)(2,1)S(1)}, u32[]{:S(2)}, u32[]{:S(2)}) %collective-permute-start) | collective-permute-done | bytes 61472 | tf_op jit(solution)/shard_map/ppermute | solution.py:39
  8.1 0.5 %shard_map.87 = (f32[96,128]{1,0:T(8,128)S(1)}, f32[1,128]{1,0:T(1,128)S(1)}, f32[96,512]{1,0:T(8,128)S(1)}, f32[104,512]{1,0:T(8,128)S(1)}, bf16[96,512]{1,0:T(8,128)(2,1)S(1)}) custom-call(bf16[48,640]{1,0:T(8,128)(2,1)S(1)} %get-tuple-element.57.refs_0_, bf16[48,640]{1,0:T(8,128)(2,1)S(1)} %collective-permute-done.refs_1_, ...), custom_call_target="tpu_custom_call" | custom-call | tf_op jit(solution)/shard_map/pallas_call | solution.py:228
  8.7 3.2 %collective-permute-start.1 = (f16[104,512]{1,0:T(8,128)(2,1)S(1)}, f16[104,512]{1,0:T(8,128)(2,1)S(1)}, u32[]{:S(2)}, u32[]{:S(2)}) collective-permute-start(f16[104,512]{1,0:T(8,128)(2,1)S(1)} %convert_element_type.24), channel_id=1, source_target_pairs={{0,2},{1,3},{2,0},{3,1},{4,6},{5,7},{6,4},{7,5},{8,10},{9,11},{10,... | collective-permute-start | bytes 319496 | tf_op jit(solution)/shard_map/ppermute | solution.py:39
  11.9 0.5 %shard_map.88 = (f32[96,128]{1,0:T(8,128)S(1)}, f32[1,128]{1,0:T(1,128)S(1)}, f32[96,512]{1,0:T(8,128)S(1)}, f32[104,512]{1,0:T(8,128)S(1)}, bf16[96,512]{1,0:T(8,128)(2,1)S(1)}) custom-call(bf16[48,640]{1,0:T(8,128)(2,1)S(1)} %collective-permute-done.2.refs_0_, bf16[48,640]{1,0:T(8,128)(2,1)S(1)} %collective-permute-done.3.refs_1_, ...), custom_call_target="tpu_custom_call" | custom-call | tf_op jit(solution)/shard_map/pallas_call | solution.py:228
  12.5 1.6 %collective-permute-start.7 = (f16[104,512]{1,0:T(8,128)(2,1)S(1)}, f16[104,512]{1,0:T(8,128)(2,1)S(1)}, u32[]{:S(2)}, u32[]{:S(2)}) collective-permute-start(f16[104,512]{1,0:T(8,128)(2,1)S(1)} %convert_element_type.26), channel_id=1, source_target_pairs={{0,1},{1,0},{2,3},{3,2},{4,5},{5,4},{6,7},{7,6},{8,9},{9,8},{10,11... | collective-permute-start | bytes 319496 | tf_op jit(solution)/shard_map/ppermute | solution.py:39
  14.1 0.5 %collective-permute-start.6 = (bf16[96,512]{1,0:T(8,128)(2,1)S(1)}, bf16[96,512]{1,0:T(8,128)(2,1)S(1)}, u32[]{:S(2)}, u32[]{:S(2)}) collective-permute-start(bf16[96,512]{1,0:T(8,128)(2,1)S(1)} %get-tuple-element.70.refs_1_), channel_id=1, source_target_pairs={{0,4},{4,0},{1,5},{5,1},{2,6},{6,2},{3,7},{7,3},{8,12},{12,8},{9,1... | collective-permute-start | bytes 294920 | tf_op jit(solution)/shard_map/ppermute | solution.py:39
  14.6 0.3 collective-permute-done.1
  14.9 0.8 %collective-permute-done.4.refs_7_ = f32[1,128]{1,0:T(1,128)S(1)} collective-permute-done((f32[1,128]{1,0:T(1,128)S(1)}, f32[1,128]{1,0:T(1,128)S(1)}, u32[]{:S(2)}, u32[]{:S(2)}) %collective-permute-start.4) | collective-permute-done | bytes 544 | tf_op jit(solution)/shard_map/ppermute | solution.py:39
  15.7 0.2 shard_map.89
  16.0 1.3 %collective-permute-done.7 = f16[104,512]{1,0:T(8,128)(2,1)S(1)} collective-permute-done((f16[104,512]{1,0:T(8,128)(2,1)S(1)}, f16[104,512]{1,0:T(8,128)(2,1)S(1)}, u32[]{:S(2)}, u32[]{:S(2)}) %collective-permute-start.7) | collective-permute-done | bytes 106528 | tf_op jit(solution)/shard_map/ppermute | solution.py:39
  17.3 0.2 shard_map.90
  17.5 1.4 %collective-permute-start.9 = (f16[104,512]{1,0:T(8,128)(2,1)S(1)}, f16[104,512]{1,0:T(8,128)(2,1)S(1)}, u32[]{:S(2)}, u32[]{:S(2)}) collective-permute-start(f16[104,512]{1,0:T(8,128)(2,1)S(1)} %convert_element_type.30), channel_id=1, source_target_pairs={{0,2},{1,3},{2,0},{3,1},{4,6},{5,7},{6,4},{7,5},{8,10},{9,11},{10,... | collective-permute-start | bytes 319496 | tf_op jit(solution)/shard_map/ppermute | solution.py:39
  19.0 2.5 %collective-permute-start.8 = (f16[104,512]{1,0:T(8,128)(2,1)S(1)}, f16[104,512]{1,0:T(8,128)(2,1)S(1)}, u32[]{:S(2)}, u32[]{:S(2)}) collective-permute-start(f16[104,512]{1,0:T(8,128)(2,1)S(1)} %convert_element_type.28), channel_id=1, source_target_pairs={{0,1},{1,0},{2,3},{3,2},{4,5},{5,4},{6,7},{7,6},{8,9},{9,8},{10,11... | collective-permute-start | bytes 319496 | tf_op jit(solution)/shard_map/ppermute | solution.py:39
  21.4 0.3 shard_map.91
  21.8 0.3 shard_map.92
  22.1 2.6 %collective-permute-done.9 = f16[104,512]{1,0:T(8,128)(2,1)S(1)} collective-permute-done((f16[104,512]{1,0:T(8,128)(2,1)S(1)}, f16[104,512]{1,0:T(8,128)(2,1)S(1)}, u32[]{:S(2)}, u32[]{:S(2)}) %collective-permute-start.9) | collective-permute-done | bytes 106528 | tf_op jit(solution)/shard_map/ppermute | solution.py:39
  24.7 0.1 collective-permute-done.8
  24.9 0.2 shard_map.93.scaled
  25.1 0.7 %shard_map.94 = (f32[256,256]{1,0:T(8,128)S(1)}, f32[256,256]{1,0:T(8,128)S(1)}) custom-call(bf16[192,512]{1,0:T(8,128)(2,1)S(1)} %shard_map.93.scaled, bf16[256,192]{1,0:T(8,128)(2,1)S(1)} %get-tuple-element.103.turned, bf16[192,256]{1,0:T(8,128)(2,1)S(1)} %get-tuple-element.104.act, f32[192,256]{1,0:T(8,128)S(1)} %get-tuple-element.105.slope, ...), custom_call_target="tpu_custom_call" | custom-call | tf_op jit(solution)/shard_map/pallas_call | solution.py:228
  25.8 0.7 %collective-permute-done.10.scaled = bf16[192,512]{1,0:T(8,128)(2,1)S(1)} collective-permute-done((bf16[192,512]{1,0:T(8,128)(2,1)S(1)}, bf16[192,512]{1,0:T(8,128)(2,1)S(1)}, u32[]{:S(2)}, u32[]{:S(2)}) %collective-permute-start.10) | collective-permute-done | bytes 196640 | tf_op jit(solution)/shard_map/ppermute | solution.py:39
  26.5 0.5 %shard_map.95 = (f32[128,256]{1,0:T(8,128)S(1)}, bf16[128,256]{1,0:T(8,128)(2,1)S(1)}, bf16[128,256]{1,0:T(8,128)(2,1)S(1)}, bf16[128,256]{1,0:T(8,128)(2,1)S(1)}) custom-call(bf16[192,512]{1,0:T(8,128)(2,1)S(1)} %collective-permute-done.10.scaled, bf16[256,192]{1,0:T(8,128)(2,1)S(1)} %get-tuple-element.99.turned, ...), custom_call_target="tpu_custom_call" | custom-call | tf_op jit(solution)/shard_map/pallas_call | solution.py:228
  27.0 2.3 %collective-permute-start.11 = (bf16[128,256]{1,0:T(8,128)(2,1)S(1)}, bf16[128,256]{1,0:T(8,128)(2,1)S(1)}, u32[]{:S(2)}, u32[]{:S(2)}) collective-permute-start(bf16[128,256]{1,0:T(8,128)(2,1)S(1)} %get-tuple-element.109), channel_id=1, source_target_pairs={{0,24},{8,16},{16,8},{24,0},{1,25},{9,17},{17,9},{25,1},{2,26},{10... | collective-permute-start | bytes 196616 | tf_op jit(solution)/shard_map/ppermute | solution.py:39
  29.4 0.7 %collective-permute-start.12 = (bf16[128,256]{1,0:T(8,128)(2,1)S(1)}, bf16[128,256]{1,0:T(8,128)(2,1)S(1)}, u32[]{:S(2)}, u32[]{:S(2)}) collective-permute-start(bf16[128,256]{1,0:T(8,128)(2,1)S(1)} %get-tuple-element.110), channel_id=1, source_target_pairs={{0,16},{8,24},{16,0},{24,8},{1,17},{9,25},{17,1},{25,9},{2,18},{10... | collective-permute-start | bytes 196616 | tf_op jit(solution)/shard_map/ppermute | solution.py:39
  30.0 0.5 %collective-permute-start.13 = (bf16[128,256]{1,0:T(8,128)(2,1)S(1)}, bf16[128,256]{1,0:T(8,128)(2,1)S(1)}, u32[]{:S(2)}, u32[]{:S(2)}) collective-permute-start(bf16[128,256]{1,0:T(8,128)(2,1)S(1)} %get-tuple-element.111), channel_id=1, source_target_pairs={{0,8},{8,0},{16,24},{24,16},{1,9},{9,1},{17,25},{25,17},{2,10},{10... | collective-permute-start | bytes 196616 | tf_op jit(solution)/shard_map/ppermute | solution.py:39
  30.6 1.7 %collective-permute-done.11.refs_1_ = bf16[128,256]{1,0:T(8,128)(2,1)S(1)} collective-permute-done((bf16[128,256]{1,0:T(8,128)(2,1)S(1)}, bf16[128,256]{1,0:T(8,128)(2,1)S(1)}, u32[]{:S(2)}, u32[]{:S(2)}) %collective-permute-start.11) | collective-permute-done | bytes 65568 | tf_op jit(solution)/shard_map/ppermute | solution.py:39
  32.3 1.4 %collective-permute-done.12.refs_2_ = bf16[128,256]{1,0:T(8,128)(2,1)S(1)} collective-permute-done((bf16[128,256]{1,0:T(8,128)(2,1)S(1)}, bf16[128,256]{1,0:T(8,128)(2,1)S(1)}, u32[]{:S(2)}, u32[]{:S(2)}) %collective-permute-start.12) | collective-permute-done | bytes 65568 | tf_op jit(solution)/shard_map/ppermute | solution.py:39
  33.7 0.6 %collective-permute-done.13.refs_3_ = bf16[128,256]{1,0:T(8,128)(2,1)S(1)} collective-permute-done((bf16[128,256]{1,0:T(8,128)(2,1)S(1)}, bf16[128,256]{1,0:T(8,128)(2,1)S(1)}, u32[]{:S(2)}, u32[]{:S(2)}) %collective-permute-start.13) | collective-permute-done | bytes 65568 | tf_op jit(solution)/shard_map/ppermute | solution.py:39
  34.3 0.7 %shard_map.96 = (f32[64,256]{1,0:T(8,128)}, f32[64,256]{1,0:T(8,128)}) custom-call(f32[128,256]{1,0:T(8,128)S(1)} %get-tuple-element.108.refs_0_, bf16[128,256]{1,0:T(8,128)(2,1)S(1)} %collective-permute-done.11.refs_1_, bf16[128,256]{1,0:T(8,128)(2,1)S(1)} %collective-permute-done.12.refs_2_, bf16[128,256]{1,0:T(8,128)(2,1)S(1)} %collective-permute-done.13.refs_3_), custom_call_target="tpu_custom_call" | custom-call | tf_op jit(solution)/shard_map/pallas_call | solution.py:228
  (15 shorter events, 0.2 us)
Async XLA Ops:
  2.0 6.2 %collective-permute-start = (bf16[48,640]{1,0:T(8,128)(2,1)S(1)}, bf16[48,640]{1,0:T(8,128)(2,1)S(1)}, u32[]{:S(2)}, u32[]{:S(2)}) collective-permute-start(bf16[48,640]{1,0:T(8,128)(2,1)S(1)} %get-tuple-element.58), channel_id=1, source_target_pairs={{0,24},{8,16},{16,8},{24,0},{1,25},{9,17},{17,9},{25,1},{2,26},{10... | collective-permute-start | bytes 184328 | tf_op jit(solution)/shard_map/ppermute | solution.py:39
  5.9 5.9 %collective-permute-start.2 = (bf16[48,640]{1,0:T(8,128)(2,1)S(1)}, bf16[48,640]{1,0:T(8,128)(2,1)S(1)}, u32[]{:S(2)}, u32[]{:S(2)}) collective-permute-start(bf16[48,640]{1,0:T(8,128)(2,1)S(1)} %get-tuple-element.65), channel_id=1, source_target_pairs={{0,16},{8,24},{16,0},{24,8},{1,17},{9,25},{17,1},{25,9},{2,18},{10... | collective-permute-start | bytes 184328 | tf_op jit(solution)/shard_map/ppermute | solution.py:39
  6.5 5.4 %collective-permute-start.3 = (bf16[48,640]{1,0:T(8,128)(2,1)S(1)}, bf16[48,640]{1,0:T(8,128)(2,1)S(1)}, u32[]{:S(2)}, u32[]{:S(2)}) collective-permute-start(bf16[48,640]{1,0:T(8,128)(2,1)S(1)} %get-tuple-element.66), channel_id=1, source_target_pairs={{0,8},{8,0},{16,24},{24,16},{1,9},{9,1},{17,25},{25,17},{2,10},{10... | collective-permute-start | bytes 184328 | tf_op jit(solution)/shard_map/ppermute | solution.py:39
  8.7 6.2 %collective-permute-start.1 = (f16[104,512]{1,0:T(8,128)(2,1)S(1)}, f16[104,512]{1,0:T(8,128)(2,1)S(1)}, u32[]{:S(2)}, u32[]{:S(2)}) collective-permute-start(f16[104,512]{1,0:T(8,128)(2,1)S(1)} %convert_element_type.24), channel_id=1, source_target_pairs={{0,2},{1,3},{2,0},{3,1},{4,6},{5,7},{6,4},{7,5},{8,10},{9,11},{10,... | collective-permute-start | bytes 319496 | tf_op jit(solution)/shard_map/ppermute | solution.py:39
  12.5 4.8 %collective-permute-start.7 = (f16[104,512]{1,0:T(8,128)(2,1)S(1)}, f16[104,512]{1,0:T(8,128)(2,1)S(1)}, u32[]{:S(2)}, u32[]{:S(2)}) collective-permute-start(f16[104,512]{1,0:T(8,128)(2,1)S(1)} %convert_element_type.26), channel_id=1, source_target_pairs={{0,1},{1,0},{2,3},{3,2},{4,5},{5,4},{6,7},{7,6},{8,9},{9,8},{10,11... | collective-permute-start | bytes 319496 | tf_op jit(solution)/shard_map/ppermute | solution.py:39
  14.1 1.6 %collective-permute-start.5 = (bf16[96,512]{1,0:T(8,128)(2,1)S(1)}, bf16[96,512]{1,0:T(8,128)(2,1)S(1)}, u32[]{:S(2)}, u32[]{:S(2)}) collective-permute-start(bf16[96,512]{1,0:T(8,128)(2,1)S(1)} %get-tuple-element.69.refs_0_), channel_id=1, source_target_pairs={{0,4},{4,0},{1,5},{5,1},{2,6},{6,2},{3,7},{7,3},{8,12},{12,8},{9,1... | collective-permute-start | bytes 294920 | tf_op jit(solution)/shard_map/ppermute | solution.py:39
  14.1 1.6 %collective-permute-start.6 = (bf16[96,512]{1,0:T(8,128)(2,1)S(1)}, bf16[96,512]{1,0:T(8,128)(2,1)S(1)}, u32[]{:S(2)}, u32[]{:S(2)}) collective-permute-start(bf16[96,512]{1,0:T(8,128)(2,1)S(1)} %get-tuple-element.70.refs_1_), channel_id=1, source_target_pairs={{0,4},{4,0},{1,5},{5,1},{2,6},{6,2},{3,7},{7,3},{8,12},{12,8},{9,1... | collective-permute-start | bytes 294920 | tf_op jit(solution)/shard_map/ppermute | solution.py:39
  14.6 1.1 %collective-permute-start.4 = (f32[1,128]{1,0:T(1,128)S(1)}, f32[1,128]{1,0:T(1,128)S(1)}, u32[]{:S(2)}, u32[]{:S(2)}) collective-permute-start(f32[1,128]{1,0:T(1,128)S(1)} %get-tuple-element.97.refs_6_), channel_id=1, source_target_pairs={{0,4},{4,0},{1,5},{5,1},{2,6},{6,2},{3,7},{7,3},{8,12},{12,8},{9,1... | collective-permute-start | bytes 1544 | tf_op jit(solution)/shard_map/ppermute | solution.py:39
  17.5 7.2 %collective-permute-start.9 = (f16[104,512]{1,0:T(8,128)(2,1)S(1)}, f16[104,512]{1,0:T(8,128)(2,1)S(1)}, u32[]{:S(2)}, u32[]{:S(2)}) collective-permute-start(f16[104,512]{1,0:T(8,128)(2,1)S(1)} %convert_element_type.30), channel_id=1, source_target_pairs={{0,2},{1,3},{2,0},{3,1},{4,6},{5,7},{6,4},{7,5},{8,10},{9,11},{10,... | collective-permute-start | bytes 319496 | tf_op jit(solution)/shard_map/ppermute | solution.py:39
  19.0 5.9 %collective-permute-start.8 = (f16[104,512]{1,0:T(8,128)(2,1)S(1)}, f16[104,512]{1,0:T(8,128)(2,1)S(1)}, u32[]{:S(2)}, u32[]{:S(2)}) collective-permute-start(f16[104,512]{1,0:T(8,128)(2,1)S(1)} %convert_element_type.28), channel_id=1, source_target_pairs={{0,1},{1,0},{2,3},{3,2},{4,5},{5,4},{6,7},{7,6},{8,9},{9,8},{10,11... | collective-permute-start | bytes 319496 | tf_op jit(solution)/shard_map/ppermute | solution.py:39
  25.0 1.5 %collective-permute-start.10 = (bf16[192,512]{1,0:T(8,128)(2,1)S(1)}, bf16[192,512]{1,0:T(8,128)(2,1)S(1)}, u32[]{:S(2)}, u32[]{:S(2)}) collective-permute-start(bf16[192,512]{1,0:T(8,128)(2,1)S(1)} %shard_map.93.scaled), channel_id=1, source_target_pairs={{0,4},{4,0},{1,5},{5,1},{2,6},{6,2},{3,7},{7,3},{8,12},{12,8},{9,1... | collective-permute-start | bytes 589832 | tf_op jit(solution)/shard_map/ppermute | solution.py:39
  27.0 5.3 %collective-permute-start.11 = (bf16[128,256]{1,0:T(8,128)(2,1)S(1)}, bf16[128,256]{1,0:T(8,128)(2,1)S(1)}, u32[]{:S(2)}, u32[]{:S(2)}) collective-permute-start(bf16[128,256]{1,0:T(8,128)(2,1)S(1)} %get-tuple-element.109), channel_id=1, source_target_pairs={{0,24},{8,16},{16,8},{24,0},{1,25},{9,17},{17,9},{25,1},{2,26},{10... | collective-permute-start | bytes 196616 | tf_op jit(solution)/shard_map/ppermute | solution.py:39
  29.4 4.3 %collective-permute-start.12 = (bf16[128,256]{1,0:T(8,128)(2,1)S(1)}, bf16[128,256]{1,0:T(8,128)(2,1)S(1)}, u32[]{:S(2)}, u32[]{:S(2)}) collective-permute-start(bf16[128,256]{1,0:T(8,128)(2,1)S(1)} %get-tuple-element.110), channel_id=1, source_target_pairs={{0,16},{8,24},{16,0},{24,8},{1,17},{9,25},{17,1},{25,9},{2,18},{10... | collective-permute-start | bytes 196616 | tf_op jit(solution)/shard_map/ppermute | solution.py:39
  30.0 4.3 %collective-permute-start.13 = (bf16[128,256]{1,0:T(8,128)(2,1)S(1)}, bf16[128,256]{1,0:T(8,128)(2,1)S(1)}, u32[]{:S(2)}, u32[]{:S(2)}) collective-permute-start(bf16[128,256]{1,0:T(8,128)(2,1)S(1)} %get-tuple-element.111), channel_id=1, source_target_pairs={{0,8},{8,0},{16,24},{24,16},{1,9},{9,1},{17,25},{25,17},{2,10},{10... | collective-permute-start | bytes 196616 | tf_op jit(solution)/shard_map/ppermute | solution.py:39

commit v24 on v18

--- a/solution.py
+++ b/solution.py
@@ -292,9 +292,7 @@
     for k in range(1, studs):
         all_counts.append(send(counts, "stud", k))
         mates.append([send(part, "stud", k) for part in rows])
-    first_in, second_in, all_counts, mates = lax.optimization_barrier(
-        (first_in, second_in, all_counts, mates)
-    )
+    first_in, second_in, all_counts = lax.optimization_barrier((first_in, second_in, all_counts))
     for there, back in zip(steps[1:], steps[-2::-1]):
         first, first_out, second, second_out = kernel(
             pair_body, [half, packed] * 2, (first, first_in, second, second_in), 0

time: 34.8 us -> 34.5 us (level)
  transfers between devices with their start and end apart: 14 -> 14, of which waited for: 9 -> 11; matrix products, arithmetic and copies ran while one was open for 0% -> 0% of each run, Pallas kernels for 7% -> 7%
where the time goes in v24:
time: 34.5 us; the launch traced here: 34.3 us
  starting transfers between devices  18.1 us (52%)
  waiting for transfers between devices  10 us (29%)
  Pallas kernels  5.29 us (15%)
  between operations  0.77 us (2%)
    ppermute x14, starting transfers between devices, send(): lax.ppermute(block, axis, [(i, partner_to(size, i, step)) for i in range(...  18.1 us
    ppermute x14, waiting for transfers between devices, send(): lax.ppermute(block, axis, [(i, partner_to(size, i, step)) for i in range(...  10 us
    pallas_call x10, Pallas kernels, kernel(): pl.pallas_call(body, out_shape=outs, in_specs=places or [VMEM] * len(oper...  5.29 us
  transfers between devices with their start and end apart: 14, of which 11 were waited for; matrix products, arithmetic and copies ran while one was open for 0% of the time, Pallas kernels for 7%

profile of v24, /device:TPU:0, one launch (start us, length us, event | category | flops | bytes accessed | tf_op | source)
XLA Modules:
  0.0 34.3 jit_solution(902264722647583895)
XLA Ops:
  0.6 1.3 %shard_map.86 = (bf16[48,640]{1,0:T(8,128)(2,1)S(1)}, bf16[48,640]{1,0:T(8,128)(2,1)S(1)}, bf16[48,640]{1,0:T(8,128)(2,1)S(1)}, bf16[48,640]{1,0:T(8,128)(2,1)S(...) custom-call(bf16[128,512]{1,0:T(8,128)(2,1)} %refs_0_.1, ...), custom_call_target="tpu_custom_call" | custom-call | tf_op jit(solution)/shard_map/pallas_call | solution.py:230
  2.0 3.0 %collective-permute-start.2 = (bf16[48,640]{1,0:T(8,128)(2,1)S(1)}, bf16[48,640]{1,0:T(8,128)(2,1)S(1)}, u32[]{:S(2)}, u32[]{:S(2)}) collective-permute-start(bf16[48,640]{1,0:T(8,128)(2,1)S(1)} %get-tuple-element.57), channel_id=1, source_target_pairs={{0,8},{8,0},{16,24},{24,16},{1,9},{9,1},{17,25},{25,17},{2,10},{10... | collective-permute-start | bytes 184328 | tf_op jit(solution)/shard_map/ppermute | solution.py:39
  5.0 1.5 %collective-permute-start = (bf16[48,640]{1,0:T(8,128)(2,1)S(1)}, bf16[48,640]{1,0:T(8,128)(2,1)S(1)}, u32[]{:S(2)}, u32[]{:S(2)}) collective-permute-start(bf16[48,640]{1,0:T(8,128)(2,1)S(1)} %get-tuple-element.54), channel_id=1, source_target_pairs={{0,24},{8,16},{16,8},{24,0},{1,25},{9,17},{17,9},{25,1},{2,26},{10... | collective-permute-start | bytes 184328 | tf_op jit(solution)/shard_map/ppermute | solution.py:39
  6.5 0.8 %collective-permute-done.2.refs_1_ = bf16[48,640]{1,0:T(8,128)(2,1)S(1)} collective-permute-done((bf16[48,640]{1,0:T(8,128)(2,1)S(1)}, bf16[48,640]{1,0:T(8,128)(2,1)S(1)}, u32[]{:S(2)}, u32[]{:S(2)}) %collective-permute-start.2) | collective-permute-done | bytes 61472 | tf_op jit(solution)/shard_map/ppermute | solution.py:39
  7.3 0.5 %shard_map.87 = (f32[96,128]{1,0:T(8,128)S(1)}, f32[1,128]{1,0:T(1,128)S(1)}, f32[96,512]{1,0:T(8,128)S(1)}, f32[104,512]{1,0:T(8,128)S(1)}, bf16[96,512]{1,0:T(8,128)(2,1)S(1)}) custom-call(bf16[48,640]{1,0:T(8,128)(2,1)S(1)} %get-tuple-element.56.refs_0_, bf16[48,640]{1,0:T(8,128)(2,1)S(1)} %collective-permute-done.2.refs_1_, ...), custom_call_target="tpu_custom_call" | custom-call | tf_op jit(solution)/shard_map/pallas_call | solution.py:230
  7.9 3.1 %collective-permute-start.4 = (f16[104,512]{1,0:T(8,128)(2,1)S(1)}, f16[104,512]{1,0:T(8,128)(2,1)S(1)}, u32[]{:S(2)}, u32[]{:S(2)}) collective-permute-start(f16[104,512]{1,0:T(8,128)(2,1)S(1)} %convert_element_type.26), channel_id=1, source_target_pairs={{0,2},{1,3},{2,0},{3,1},{4,6},{5,7},{6,4},{7,5},{8,10},{9,11},{10,... | collective-permute-start | bytes 319496 | tf_op jit(solution)/shard_map/ppermute | solution.py:39
  10.9 0.5 %shard_map.88 = (f32[96,128]{1,0:T(8,128)S(1)}, f32[1,128]{1,0:T(1,128)S(1)}, f32[96,512]{1,0:T(8,128)S(1)}, f32[104,512]{1,0:T(8,128)S(1)}, bf16[96,512]{1,0:T(8,128)(2,1)S(1)}) custom-call(bf16[48,640]{1,0:T(8,128)(2,1)S(1)} %collective-permute-done.refs_0_, bf16[48,640]{1,0:T(8,128)(2,1)S(1)} %collective-permute-done.1.refs_1_, ...), custom_call_target="tpu_custom_call" | custom-call | tf_op jit(solution)/shard_map/pallas_call | solution.py:230
  11.5 1.6 %collective-permute-start.3 = (f16[104,512]{1,0:T(8,128)(2,1)S(1)}, f16[104,512]{1,0:T(8,128)(2,1)S(1)}, u32[]{:S(2)}, u32[]{:S(2)}) collective-permute-start(f16[104,512]{1,0:T(8,128)(2,1)S(1)} %convert_element_type.24), channel_id=1, source_target_pairs={{0,1},{1,0},{2,3},{3,2},{4,5},{5,4},{6,7},{7,6},{8,9},{9,8},{10,11... | collective-permute-start | bytes 319496 | tf_op jit(solution)/shard_map/ppermute | solution.py:39
  13.1 0.8 %collective-permute-done.4 = f16[104,512]{1,0:T(8,128)(2,1)S(1)} collective-permute-done((f16[104,512]{1,0:T(8,128)(2,1)S(1)}, f16[104,512]{1,0:T(8,128)(2,1)S(1)}, u32[]{:S(2)}, u32[]{:S(2)}) %collective-permute-start.4) | collective-permute-done | bytes 106528 | tf_op jit(solution)/shard_map/ppermute | solution.py:39
  14.0 2.3 %collective-permute-done.3 = f16[104,512]{1,0:T(8,128)(2,1)S(1)} collective-permute-done((f16[104,512]{1,0:T(8,128)(2,1)S(1)}, f16[104,512]{1,0:T(8,128)(2,1)S(1)}, u32[]{:S(2)}, u32[]{:S(2)}) %collective-permute-start.3) | collective-permute-done | bytes 106528 | tf_op jit(solution)/shard_map/ppermute | solution.py:39
  16.3 0.2 shard_map.89
  16.6 2.5 %collective-permute-start.7 = (f16[104,512]{1,0:T(8,128)(2,1)S(1)}, f16[104,512]{1,0:T(8,128)(2,1)S(1)}, u32[]{:S(2)}, u32[]{:S(2)}) collective-permute-start(f16[104,512]{1,0:T(8,128)(2,1)S(1)} %convert_element_type.30), channel_id=1, source_target_pairs={{0,2},{1,3},{2,0},{3,1},{4,6},{5,7},{6,4},{7,5},{8,10},{9,11},{10,... | collective-permute-start | bytes 319496 | tf_op jit(solution)/shard_map/ppermute | solution.py:39
  19.1 2.2 %collective-permute-start.6 = (f16[104,512]{1,0:T(8,128)(2,1)S(1)}, f16[104,512]{1,0:T(8,128)(2,1)S(1)}, u32[]{:S(2)}, u32[]{:S(2)}) collective-permute-start(f16[104,512]{1,0:T(8,128)(2,1)S(1)} %convert_element_type.28), channel_id=1, source_target_pairs={{0,1},{1,0},{2,3},{3,2},{4,5},{5,4},{6,7},{7,6},{8,9},{9,8},{10,11... | collective-permute-start | bytes 319496 | tf_op jit(solution)/shard_map/ppermute | solution.py:39
  21.3 0.5 %collective-permute-start.9 = (bf16[96,512]{1,0:T(8,128)(2,1)S(1)}, bf16[96,512]{1,0:T(8,128)(2,1)S(1)}, u32[]{:S(2)}, u32[]{:S(2)}) collective-permute-start(bf16[96,512]{1,0:T(8,128)(2,1)S(1)} %get-tuple-element.77.refs_1_), channel_id=1, source_target_pairs={{0,4},{4,0},{1,5},{5,1},{2,6},{6,2},{3,7},{7,3},{8,12},{12,8},{9,1... | collective-permute-start | bytes 294920 | tf_op jit(solution)/shard_map/ppermute | solution.py:39
  21.8 0.3 shard_map.90
  22.2 0.5 %collective-permute-done.8.refs_0_ = bf16[96,512]{1,0:T(8,128)(2,1)S(1)} collective-permute-done((bf16[96,512]{1,0:T(8,128)(2,1)S(1)}, bf16[96,512]{1,0:T(8,128)(2,1)S(1)}, u32[]{:S(2)}, u32[]{:S(2)}) %collective-permute-start.8) | collective-permute-done | bytes 98336 | tf_op jit(solution)/shard_map/ppermute | solution.py:39
  22.6 0.2 collective-permute-done.9.refs_1_
  22.8 0.3 shard_map.91
  23.1 1.1 %collective-permute-done.7 = f16[104,512]{1,0:T(8,128)(2,1)S(1)} collective-permute-done((f16[104,512]{1,0:T(8,128)(2,1)S(1)}, f16[104,512]{1,0:T(8,128)(2,1)S(1)}, u32[]{:S(2)}, u32[]{:S(2)}) %collective-permute-start.7) | collective-permute-done | bytes 106528 | tf_op jit(solution)/shard_map/ppermute | solution.py:39
  24.2 0.5 %collective-permute-done.6 = f16[104,512]{1,0:T(8,128)(2,1)S(1)} collective-permute-done((f16[104,512]{1,0:T(8,128)(2,1)S(1)}, f16[104,512]{1,0:T(8,128)(2,1)S(1)}, u32[]{:S(2)}, u32[]{:S(2)}) %collective-permute-start.6) | collective-permute-done | bytes 106528 | tf_op jit(solution)/shard_map/ppermute | solution.py:39
  24.7 0.2 shard_map.92.scaled
  24.9 0.1 collective-permute-start.10
  25.0 0.7 %shard_map.93 = (f32[256,256]{1,0:T(8,128)S(1)}, f32[256,256]{1,0:T(8,128)S(1)}) custom-call(bf16[192,512]{1,0:T(8,128)(2,1)S(1)} %shard_map.92.scaled, bf16[256,192]{1,0:T(8,128)(2,1)S(1)} %get-tuple-element.97.turned, bf16[192,256]{1,0:T(8,128)(2,1)S(1)} %get-tuple-element.98.act, f32[192,256]{1,0:T(8,128)S(1)} %get-tuple-element.99.slope, ...), custom_call_target="tpu_custom_call" | custom-call | tf_op jit(solution)/shard_map/pallas_call | solution.py:230
  25.7 0.7 %collective-permute-done.10.scaled = bf16[192,512]{1,0:T(8,128)(2,1)S(1)} collective-permute-done((bf16[192,512]{1,0:T(8,128)(2,1)S(1)}, bf16[192,512]{1,0:T(8,128)(2,1)S(1)}, u32[]{:S(2)}, u32[]{:S(2)}) %collective-permute-start.10) | collective-permute-done | bytes 196640 | tf_op jit(solution)/shard_map/ppermute | solution.py:39
  26.4 0.5 %shard_map.94 = (f32[128,256]{1,0:T(8,128)S(1)}, bf16[128,256]{1,0:T(8,128)(2,1)S(1)}, bf16[128,256]{1,0:T(8,128)(2,1)S(1)}, bf16[128,256]{1,0:T(8,128)(2,1)S(1)}) custom-call(bf16[192,512]{1,0:T(8,128)(2,1)S(1)} %collective-permute-done.10.scaled, bf16[256,192]{1,0:T(8,128)(2,1)S(1)} %get-tuple-element.93.turned, ...), custom_call_target="tpu_custom_call" | custom-call | tf_op jit(solution)/shard_map/pallas_call | solution.py:230
  26.9 1.4 %collective-permute-start.11 = (bf16[128,256]{1,0:T(8,128)(2,1)S(1)}, bf16[128,256]{1,0:T(8,128)(2,1)S(1)}, u32[]{:S(2)}, u32[]{:S(2)}) collective-permute-start(bf16[128,256]{1,0:T(8,128)(2,1)S(1)} %get-tuple-element.103), channel_id=1, source_target_pairs={{0,24},{8,16},{16,8},{24,0},{1,25},{9,17},{17,9},{25,1},{2,26},{10... | collective-permute-start | bytes 196616 | tf_op jit(solution)/shard_map/ppermute | solution.py:39
  28.3 1.1 %collective-permute-start.12 = (bf16[128,256]{1,0:T(8,128)(2,1)S(1)}, bf16[128,256]{1,0:T(8,128)(2,1)S(1)}, u32[]{:S(2)}, u32[]{:S(2)}) collective-permute-start(bf16[128,256]{1,0:T(8,128)(2,1)S(1)} %get-tuple-element.104), channel_id=1, source_target_pairs={{0,16},{8,24},{16,0},{24,8},{1,17},{9,25},{17,1},{25,9},{2,18},{10... | collective-permute-start | bytes 196616 | tf_op jit(solution)/shard_map/ppermute | solution.py:39
  29.4 1.1 %collective-permute-start.13 = (bf16[128,256]{1,0:T(8,128)(2,1)S(1)}, bf16[128,256]{1,0:T(8,128)(2,1)S(1)}, u32[]{:S(2)}, u32[]{:S(2)}) collective-permute-start(bf16[128,256]{1,0:T(8,128)(2,1)S(1)} %get-tuple-element.105), channel_id=1, source_target_pairs={{0,8},{8,0},{16,24},{24,16},{1,9},{9,1},{17,25},{25,17},{2,10},{10... | collective-permute-start | bytes 196616 | tf_op jit(solution)/shard_map/ppermute | solution.py:39
  30.5 1.9 %collective-permute-done.11.refs_1_ = bf16[128,256]{1,0:T(8,128)(2,1)S(1)} collective-permute-done((bf16[128,256]{1,0:T(8,128)(2,1)S(1)}, bf16[128,256]{1,0:T(8,128)(2,1)S(1)}, u32[]{:S(2)}, u32[]{:S(2)}) %collective-permute-start.11) | collective-permute-done | bytes 65568 | tf_op jit(solution)/shard_map/ppermute | solution.py:39
  32.4 1.0 %collective-permute-done.12.refs_2_ = bf16[128,256]{1,0:T(8,128)(2,1)S(1)} collective-permute-done((bf16[128,256]{1,0:T(8,128)(2,1)S(1)}, bf16[128,256]{1,0:T(8,128)(2,1)S(1)}, u32[]{:S(2)}, u32[]{:S(2)}) %collective-permute-start.12) | collective-permute-done | bytes 65568 | tf_op jit(solution)/shard_map/ppermute | solution.py:39
  33.4 0.2 collective-permute-done.13.refs_3_
  33.6 0.7 %shard_map.95 = (f32[64,256]{1,0:T(8,128)}, f32[64,256]{1,0:T(8,128)}) custom-call(f32[128,256]{1,0:T(8,128)S(1)} %get-tuple-element.102.refs_0_, bf16[128,256]{1,0:T(8,128)(2,1)S(1)} %collective-permute-done.11.refs_1_, bf16[128,256]{1,0:T(8,128)(2,1)S(1)} %collective-permute-done.12.refs_2_, bf16[128,256]{1,0:T(8,128)(2,1)S(1)} %collective-permute-done.13.refs_3_), custom_call_target="tpu_custom_call" | custom-call | tf_op jit(solution)/shard_map/pallas_call | solution.py:230
  (14 shorter events, 0.2 us)
Async XLA Ops:
  2.0 5.3 %collective-permute-start.2 = (bf16[48,640]{1,0:T(8,128)(2,1)S(1)}, bf16[48,640]{1,0:T(8,128)(2,1)S(1)}, u32[]{:S(2)}, u32[]{:S(2)}) collective-permute-start(bf16[48,640]{1,0:T(8,128)(2,1)S(1)} %get-tuple-element.57), channel_id=1, source_target_pairs={{0,8},{8,0},{16,24},{24,16},{1,9},{9,1},{17,25},{25,17},{2,10},{10... | collective-permute-start | bytes 184328 | tf_op jit(solution)/shard_map/ppermute | solution.py:39
  5.0 6.0 %collective-permute-start = (bf16[48,640]{1,0:T(8,128)(2,1)S(1)}, bf16[48,640]{1,0:T(8,128)(2,1)S(1)}, u32[]{:S(2)}, u32[]{:S(2)}) collective-permute-start(bf16[48,640]{1,0:T(8,128)(2,1)S(1)} %get-tuple-element.54), channel_id=1, source_target_pairs={{0,24},{8,16},{16,8},{24,0},{1,25},{9,17},{17,9},{25,1},{2,26},{10... | collective-permute-start | bytes 184328 | tf_op jit(solution)/shard_map/ppermute | solution.py:39
  6.5 4.5 %collective-permute-start.1 = (bf16[48,640]{1,0:T(8,128)(2,1)S(1)}, bf16[48,640]{1,0:T(8,128)(2,1)S(1)}, u32[]{:S(2)}, u32[]{:S(2)}) collective-permute-start(bf16[48,640]{1,0:T(8,128)(2,1)S(1)} %get-tuple-element.55), channel_id=1, source_target_pairs={{0,16},{8,24},{16,0},{24,8},{1,17},{9,25},{17,1},{25,9},{2,18},{10... | collective-permute-start | bytes 184328 | tf_op jit(solution)/shard_map/ppermute | solution.py:39
  7.9 6.1 %collective-permute-start.4 = (f16[104,512]{1,0:T(8,128)(2,1)S(1)}, f16[104,512]{1,0:T(8,128)(2,1)S(1)}, u32[]{:S(2)}, u32[]{:S(2)}) collective-permute-start(f16[104,512]{1,0:T(8,128)(2,1)S(1)} %convert_element_type.26), channel_id=1, source_target_pairs={{0,2},{1,3},{2,0},{3,1},{4,6},{5,7},{6,4},{7,5},{8,10},{9,11},{10,... | collective-permute-start | bytes 319496 | tf_op jit(solution)/shard_map/ppermute | solution.py:39
  11.5 4.8 %collective-permute-start.3 = (f16[104,512]{1,0:T(8,128)(2,1)S(1)}, f16[104,512]{1,0:T(8,128)(2,1)S(1)}, u32[]{:S(2)}, u32[]{:S(2)}) collective-permute-start(f16[104,512]{1,0:T(8,128)(2,1)S(1)} %convert_element_type.24), channel_id=1, source_target_pairs={{0,1},{1,0},{2,3},{3,2},{4,5},{5,4},{6,7},{7,6},{8,9},{9,8},{10,11... | collective-permute-start | bytes 319496 | tf_op jit(solution)/shard_map/ppermute | solution.py:39
  13.1 3.2 %collective-permute-start.5 = (f32[1,128]{1,0:T(1,128)S(1)}, f32[1,128]{1,0:T(1,128)S(1)}, u32[]{:S(2)}, u32[]{:S(2)}) collective-permute-start(f32[1,128]{1,0:T(1,128)S(1)} %get-tuple-element.91.refs_6_), channel_id=1, source_target_pairs={{0,4},{4,0},{1,5},{5,1},{2,6},{6,2},{3,7},{7,3},{8,12},{12,8},{9,1... | collective-permute-start | bytes 1544 | tf_op jit(solution)/shard_map/ppermute | solution.py:39
  16.6 7.6 %collective-permute-start.7 = (f16[104,512]{1,0:T(8,128)(2,1)S(1)}, f16[104,512]{1,0:T(8,128)(2,1)S(1)}, u32[]{:S(2)}, u32[]{:S(2)}) collective-permute-start(f16[104,512]{1,0:T(8,128)(2,1)S(1)} %convert_element_type.30), channel_id=1, source_target_pairs={{0,2},{1,3},{2,0},{3,1},{4,6},{5,7},{6,4},{7,5},{8,10},{9,11},{10,... | collective-permute-start | bytes 319496 | tf_op jit(solution)/shard_map/ppermute | solution.py:39
  19.1 5.6 %collective-permute-start.6 = (f16[104,512]{1,0:T(8,128)(2,1)S(1)}, f16[104,512]{1,0:T(8,128)(2,1)S(1)}, u32[]{:S(2)}, u32[]{:S(2)}) collective-permute-start(f16[104,512]{1,0:T(8,128)(2,1)S(1)} %convert_element_type.28), channel_id=1, source_target_pairs={{0,1},{1,0},{2,3},{3,2},{4,5},{5,4},{6,7},{7,6},{8,9},{9,8},{10,11... | collective-permute-start | bytes 319496 | tf_op jit(solution)/shard_map/ppermute | solution.py:39
  21.3 1.3 %collective-permute-start.8 = (bf16[96,512]{1,0:T(8,128)(2,1)S(1)}, bf16[96,512]{1,0:T(8,128)(2,1)S(1)}, u32[]{:S(2)}, u32[]{:S(2)}) collective-permute-start(bf16[96,512]{1,0:T(8,128)(2,1)S(1)} %get-tuple-element.76.refs_0_), channel_id=1, source_target_pairs={{0,4},{4,0},{1,5},{5,1},{2,6},{6,2},{3,7},{7,3},{8,12},{12,8},{9,1... | collective-permute-start | bytes 294920 | tf_op jit(solution)/shard_map/ppermute | solution.py:39
  21.3 1.5 %collective-permute-start.9 = (bf16[96,512]{1,0:T(8,128)(2,1)S(1)}, bf16[96,512]{1,0:T(8,128)(2,1)S(1)}, u32[]{:S(2)}, u32[]{:S(2)}) collective-permute-start(bf16[96,512]{1,0:T(8,128)(2,1)S(1)} %get-tuple-element.77.refs_1_), channel_id=1, source_target_pairs={{0,4},{4,0},{1,5},{5,1},{2,6},{6,2},{3,7},{7,3},{8,12},{12,8},{9,1... | collective-permute-start | bytes 294920 | tf_op jit(solution)/shard_map/ppermute | solution.py:39
  24.9 1.5 %collective-permute-start.10 = (bf16[192,512]{1,0:T(8,128)(2,1)S(1)}, bf16[192,512]{1,0:T(8,128)(2,1)S(1)}, u32[]{:S(2)}, u32[]{:S(2)}) collective-permute-start(bf16[192,512]{1,0:T(8,128)(2,1)S(1)} %shard_map.92.scaled), channel_id=1, source_target_pairs={{0,4},{4,0},{1,5},{5,1},{2,6},{6,2},{3,7},{7,3},{8,12},{12,8},{9,1... | collective-permute-start | bytes 589832 | tf_op jit(solution)/shard_map/ppermute | solution.py:39
  26.9 5.5 %collective-permute-start.11 = (bf16[128,256]{1,0:T(8,128)(2,1)S(1)}, bf16[128,256]{1,0:T(8,128)(2,1)S(1)}, u32[]{:S(2)}, u32[]{:S(2)}) collective-permute-start(bf16[128,256]{1,0:T(8,128)(2,1)S(1)} %get-tuple-element.103), channel_id=1, source_target_pairs={{0,24},{8,16},{16,8},{24,0},{1,25},{9,17},{17,9},{25,1},{2,26},{10... | collective-permute-start | bytes 196616 | tf_op jit(solution)/shard_map/ppermute | solution.py:39
  28.3 5.1 %collective-permute-start.12 = (bf16[128,256]{1,0:T(8,128)(2,1)S(1)}, bf16[128,256]{1,0:T(8,128)(2,1)S(1)}, u32[]{:S(2)}, u32[]{:S(2)}) collective-permute-start(bf16[128,256]{1,0:T(8,128)(2,1)S(1)} %get-tuple-element.104), channel_id=1, source_target_pairs={{0,16},{8,24},{16,0},{24,8},{1,17},{9,25},{17,1},{25,9},{2,18},{10... | collective-permute-start | bytes 196616 | tf_op jit(solution)/shard_map/ppermute | solution.py:39
  29.4 4.3 %collective-permute-start.13 = (bf16[128,256]{1,0:T(8,128)(2,1)S(1)}, bf16[128,256]{1,0:T(8,128)(2,1)S(1)}, u32[]{:S(2)}, u32[]{:S(2)}) collective-permute-start(bf16[128,256]{1,0:T(8,128)(2,1)S(1)} %get-tuple-element.105), channel_id=1, source_target_pairs={{0,8},{8,0},{16,24},{24,16},{1,9},{9,1},{17,25},{25,17},{2,10},{10... | collective-permute-start | bytes 196616 | tf_op jit(solution)/shard_map/ppermute | solution.py:39

commit v25 on v22

--- a/solution.py
+++ b/solution.py
@@ -290,7 +290,7 @@
     for k in range(1, studs):
         all_counts.append(send(counts, "stud", k))
         mates.append([send(part, "stud", k) for part in rows])
-    second_in, all_counts, mates = lax.optimization_barrier((second_in, all_counts, mates))
+    second_in, all_counts = lax.optimization_barrier((second_in, all_counts))
     for there, back in zip(steps[1:], steps[-2::-1]):
         second, second_out = kernel(pair_body, [half, packed], (second, second_in), 0)
         first, first_out = kernel(pair_body, [half, packed], (first, first_in, second), 0)

time: 35.1 us -> 34.5 us (0.983)
  waiting for transfers between devices: 10.5 us -> 9.87 us
    ppermute x14, waiting for transfers between devices: 10.5 us -> 9.87 us  [send(): lax.ppermute(block, axis, [(i, partner_to(size, i, step)) for i in range(...]
  transfers between devices with their start and end apart: 14 -> 14, of which waited for: 10 -> 12; matrix products, arithmetic and copies ran while one was open for 0% -> 0% of each run, Pallas kernels for 7% -> 8%
where the time goes in v25:
time: 34.5 us; the launch traced here: 34.4 us
  starting transfers between devices  18.1 us (52%)
  waiting for transfers between devices  9.87 us (29%)
  Pallas kernels  5.47 us (16%)
  between operations  0.77 us (2%)
    ppermute x14, starting transfers between devices, send(): lax.ppermute(block, axis, [(i, partner_to(size, i, step)) for i in range(...  18.1 us
    ppermute x14, waiting for transfers between devices, send(): lax.ppermute(block, axis, [(i, partner_to(size, i, step)) for i in range(...  9.87 us
    pallas_call x11, Pallas kernels, kernel(): pl.pallas_call(body, out_shape=outs, in_specs=places or [VMEM] * len(oper...  5.47 us
  transfers between devices with their start and end apart: 14, of which 12 were waited for; matrix products, arithmetic and copies ran while one was open for 0% of the time, Pallas kernels for 8%

profile of v25, /device:TPU:0, one launch (start us, length us, event | category | flops | bytes accessed | tf_op | source)
XLA Modules:
  0.0 34.4 jit_solution(15347507072191257224)
XLA Ops:
  0.6 1.3 %shard_map.86 = (bf16[48,640]{1,0:T(8,128)(2,1)S(1)}, bf16[48,640]{1,0:T(8,128)(2,1)S(1)}, bf16[48,640]{1,0:T(8,128)(2,1)S(1)}, bf16[48,640]{1,0:T(8,128)(2,1)S(...) custom-call(bf16[128,512]{1,0:T(8,128)(2,1)} %refs_0_.1, ...), custom_call_target="tpu_custom_call" | custom-call | tf_op jit(solution)/shard_map/pallas_call | solution.py:228
  2.0 3.0 %collective-permute-start = (bf16[48,640]{1,0:T(8,128)(2,1)S(1)}, bf16[48,640]{1,0:T(8,128)(2,1)S(1)}, u32[]{:S(2)}, u32[]{:S(2)}) collective-permute-start(bf16[48,640]{1,0:T(8,128)(2,1)S(1)} %get-tuple-element.56), channel_id=1, source_target_pairs={{0,8},{8,0},{16,24},{24,16},{1,9},{9,1},{17,25},{25,17},{2,10},{10... | collective-permute-start | bytes 184328 | tf_op jit(solution)/shard_map/ppermute | solution.py:39
  5.0 1.5 %collective-permute-start.2 = (bf16[48,640]{1,0:T(8,128)(2,1)S(1)}, bf16[48,640]{1,0:T(8,128)(2,1)S(1)}, u32[]{:S(2)}, u32[]{:S(2)}) collective-permute-start(bf16[48,640]{1,0:T(8,128)(2,1)S(1)} %get-tuple-element.63), channel_id=1, source_target_pairs={{0,24},{8,16},{16,8},{24,0},{1,25},{9,17},{17,9},{25,1},{2,26},{10... | collective-permute-start | bytes 184328 | tf_op jit(solution)/shard_map/ppermute | solution.py:39
  6.5 0.8 %collective-permute-done.refs_1_ = bf16[48,640]{1,0:T(8,128)(2,1)S(1)} collective-permute-done((bf16[48,640]{1,0:T(8,128)(2,1)S(1)}, bf16[48,640]{1,0:T(8,128)(2,1)S(1)}, u32[]{:S(2)}, u32[]{:S(2)}) %collective-permute-start) | collective-permute-done | bytes 61472 | tf_op jit(solution)/shard_map/ppermute | solution.py:39
  7.3 0.5 %shard_map.87 = (f32[96,128]{1,0:T(8,128)S(1)}, f32[1,128]{1,0:T(1,128)S(1)}, f32[96,512]{1,0:T(8,128)S(1)}, f32[104,512]{1,0:T(8,128)S(1)}, bf16[96,512]{1,0:T(8,128)(2,1)S(1)}) custom-call(bf16[48,640]{1,0:T(8,128)(2,1)S(1)} %get-tuple-element.55.refs_0_, bf16[48,640]{1,0:T(8,128)(2,1)S(1)} %collective-permute-done.refs_1_, ...), custom_call_target="tpu_custom_call" | custom-call | tf_op jit(solution)/shard_map/pallas_call | solution.py:228
  7.9 3.1 %collective-permute-start.1 = (f16[104,512]{1,0:T(8,128)(2,1)S(1)}, f16[104,512]{1,0:T(8,128)(2,1)S(1)}, u32[]{:S(2)}, u32[]{:S(2)}) collective-permute-start(f16[104,512]{1,0:T(8,128)(2,1)S(1)} %convert_element_type.24), channel_id=1, source_target_pairs={{0,2},{1,3},{2,0},{3,1},{4,6},{5,7},{6,4},{7,5},{8,10},{9,11},{10,... | collective-permute-start | bytes 319496 | tf_op jit(solution)/shard_map/ppermute | solution.py:39
  10.9 0.5 %shard_map.88 = (f32[96,128]{1,0:T(8,128)S(1)}, f32[1,128]{1,0:T(1,128)S(1)}, f32[96,512]{1,0:T(8,128)S(1)}, f32[104,512]{1,0:T(8,128)S(1)}, bf16[96,512]{1,0:T(8,128)(2,1)S(1)}) custom-call(bf16[48,640]{1,0:T(8,128)(2,1)S(1)} %collective-permute-done.2.refs_0_, bf16[48,640]{1,0:T(8,128)(2,1)S(1)} %collective-permute-done.3.refs_1_, ...), custom_call_target="tpu_custom_call" | custom-call | tf_op jit(solution)/shard_map/pallas_call | solution.py:228
  11.5 1.6 %collective-permute-start.5 = (f16[104,512]{1,0:T(8,128)(2,1)S(1)}, f16[104,512]{1,0:T(8,128)(2,1)S(1)}, u32[]{:S(2)}, u32[]{:S(2)}) collective-permute-start(f16[104,512]{1,0:T(8,128)(2,1)S(1)} %convert_element_type.26), channel_id=1, source_target_pairs={{0,1},{1,0},{2,3},{3,2},{4,5},{5,4},{6,7},{7,6},{8,9},{9,8},{10,11... | collective-permute-start | bytes 319496 | tf_op jit(solution)/shard_map/ppermute | solution.py:39
  13.1 0.8 %collective-permute-done.1 = f16[104,512]{1,0:T(8,128)(2,1)S(1)} collective-permute-done((f16[104,512]{1,0:T(8,128)(2,1)S(1)}, f16[104,512]{1,0:T(8,128)(2,1)S(1)}, u32[]{:S(2)}, u32[]{:S(2)}) %collective-permute-start.1) | collective-permute-done | bytes 106528 | tf_op jit(solution)/shard_map/ppermute | solution.py:39
  14.0 0.3 collective-permute-done.4.refs_7_
  14.3 0.2 shard_map.89
  14.5 1.8 %collective-permute-done.5 = f16[104,512]{1,0:T(8,128)(2,1)S(1)} collective-permute-done((f16[104,512]{1,0:T(8,128)(2,1)S(1)}, f16[104,512]{1,0:T(8,128)(2,1)S(1)}, u32[]{:S(2)}, u32[]{:S(2)}) %collective-permute-start.5) | collective-permute-done | bytes 106528 | tf_op jit(solution)/shard_map/ppermute | solution.py:39
  16.3 0.2 shard_map.90
  16.5 2.5 %collective-permute-start.7 = (f16[104,512]{1,0:T(8,128)(2,1)S(1)}, f16[104,512]{1,0:T(8,128)(2,1)S(1)}, u32[]{:S(2)}, u32[]{:S(2)}) collective-permute-start(f16[104,512]{1,0:T(8,128)(2,1)S(1)} %convert_element_type.30), channel_id=1, source_target_pairs={{0,2},{1,3},{2,0},{3,1},{4,6},{5,7},{6,4},{7,5},{8,10},{9,11},{10,... | collective-permute-start | bytes 319496 | tf_op jit(solution)/shard_map/ppermute | solution.py:39
  19.1 2.2 %collective-permute-start.6 = (f16[104,512]{1,0:T(8,128)(2,1)S(1)}, f16[104,512]{1,0:T(8,128)(2,1)S(1)}, u32[]{:S(2)}, u32[]{:S(2)}) collective-permute-start(f16[104,512]{1,0:T(8,128)(2,1)S(1)} %convert_element_type.28), channel_id=1, source_target_pairs={{0,1},{1,0},{2,3},{3,2},{4,5},{5,4},{6,7},{7,6},{8,9},{9,8},{10,11... | collective-permute-start | bytes 319496 | tf_op jit(solution)/shard_map/ppermute | solution.py:39
  21.3 0.5 %collective-permute-start.9 = (bf16[96,512]{1,0:T(8,128)(2,1)S(1)}, bf16[96,512]{1,0:T(8,128)(2,1)S(1)}, u32[]{:S(2)}, u32[]{:S(2)}) collective-permute-start(bf16[96,512]{1,0:T(8,128)(2,1)S(1)} %get-tuple-element.79.refs_1_), channel_id=1, source_target_pairs={{0,4},{4,0},{1,5},{5,1},{2,6},{6,2},{3,7},{7,3},{8,12},{12,8},{9,1... | collective-permute-start | bytes 294920 | tf_op jit(solution)/shard_map/ppermute | solution.py:39
  21.8 0.3 shard_map.91
  22.1 0.5 %collective-permute-done.8.refs_0_ = bf16[96,512]{1,0:T(8,128)(2,1)S(1)} collective-permute-done((bf16[96,512]{1,0:T(8,128)(2,1)S(1)}, bf16[96,512]{1,0:T(8,128)(2,1)S(1)}, u32[]{:S(2)}, u32[]{:S(2)}) %collective-permute-start.8) | collective-permute-done | bytes 98336 | tf_op jit(solution)/shard_map/ppermute | solution.py:39
  22.8 0.3 shard_map.92
  23.1 1.1 %collective-permute-done.7 = f16[104,512]{1,0:T(8,128)(2,1)S(1)} collective-permute-done((f16[104,512]{1,0:T(8,128)(2,1)S(1)}, f16[104,512]{1,0:T(8,128)(2,1)S(1)}, u32[]{:S(2)}, u32[]{:S(2)}) %collective-permute-start.7) | collective-permute-done | bytes 106528 | tf_op jit(solution)/shard_map/ppermute | solution.py:39
  24.2 0.5 %collective-permute-done.6 = f16[104,512]{1,0:T(8,128)(2,1)S(1)} collective-permute-done((f16[104,512]{1,0:T(8,128)(2,1)S(1)}, f16[104,512]{1,0:T(8,128)(2,1)S(1)}, u32[]{:S(2)}, u32[]{:S(2)}) %collective-permute-start.6) | collective-permute-done | bytes 106528 | tf_op jit(solution)/shard_map/ppermute | solution.py:39
  24.7 0.2 shard_map.93.scaled
  25.0 0.7 %shard_map.94 = (f32[256,256]{1,0:T(8,128)S(1)}, f32[256,256]{1,0:T(8,128)S(1)}) custom-call(bf16[192,512]{1,0:T(8,128)(2,1)S(1)} %shard_map.93.scaled, bf16[256,192]{1,0:T(8,128)(2,1)S(1)} %get-tuple-element.99.turned, bf16[192,256]{1,0:T(8,128)(2,1)S(1)} %get-tuple-element.100.act, f32[192,256]{1,0:T(8,128)S(1)} %get-tuple-element.101.slope, ...), custom_call_target="tpu_custom_call" | custom-call | tf_op jit(solution)/shard_map/pallas_call | solution.py:228
  25.6 0.7 %collective-permute-done.10.scaled = bf16[192,512]{1,0:T(8,128)(2,1)S(1)} collective-permute-done((bf16[192,512]{1,0:T(8,128)(2,1)S(1)}, bf16[192,512]{1,0:T(8,128)(2,1)S(1)}, u32[]{:S(2)}, u32[]{:S(2)}) %collective-permute-start.10) | collective-permute-done | bytes 196640 | tf_op jit(solution)/shard_map/ppermute | solution.py:39
  26.4 0.5 %shard_map.95 = (f32[128,256]{1,0:T(8,128)S(1)}, bf16[128,256]{1,0:T(8,128)(2,1)S(1)}, bf16[128,256]{1,0:T(8,128)(2,1)S(1)}, bf16[128,256]{1,0:T(8,128)(2,1)S(1)}) custom-call(bf16[192,512]{1,0:T(8,128)(2,1)S(1)} %collective-permute-done.10.scaled, bf16[256,192]{1,0:T(8,128)(2,1)S(1)} %get-tuple-element.95.turned, ...), custom_call_target="tpu_custom_call" | custom-call | tf_op jit(solution)/shard_map/pallas_call | solution.py:228
  26.9 1.4 %collective-permute-start.11 = (bf16[128,256]{1,0:T(8,128)(2,1)S(1)}, bf16[128,256]{1,0:T(8,128)(2,1)S(1)}, u32[]{:S(2)}, u32[]{:S(2)}) collective-permute-start(bf16[128,256]{1,0:T(8,128)(2,1)S(1)} %get-tuple-element.105), channel_id=1, source_target_pairs={{0,24},{8,16},{16,8},{24,0},{1,25},{9,17},{17,9},{25,1},{2,26},{10... | collective-permute-start | bytes 196616 | tf_op jit(solution)/shard_map/ppermute | solution.py:39
  28.3 1.1 %collective-permute-start.12 = (bf16[128,256]{1,0:T(8,128)(2,1)S(1)}, bf16[128,256]{1,0:T(8,128)(2,1)S(1)}, u32[]{:S(2)}, u32[]{:S(2)}) collective-permute-start(bf16[128,256]{1,0:T(8,128)(2,1)S(1)} %get-tuple-element.106), channel_id=1, source_target_pairs={{0,16},{8,24},{16,0},{24,8},{1,17},{9,25},{17,1},{25,9},{2,18},{10... | collective-permute-start | bytes 196616 | tf_op jit(solution)/shard_map/ppermute | solution.py:39
  29.4 1.0 %collective-permute-start.13 = (bf16[128,256]{1,0:T(8,128)(2,1)S(1)}, bf16[128,256]{1,0:T(8,128)(2,1)S(1)}, u32[]{:S(2)}, u32[]{:S(2)}) collective-permute-start(bf16[128,256]{1,0:T(8,128)(2,1)S(1)} %get-tuple-element.107), channel_id=1, source_target_pairs={{0,8},{8,0},{16,24},{24,16},{1,9},{9,1},{17,25},{25,17},{2,10},{10... | collective-permute-start | bytes 196616 | tf_op jit(solution)/shard_map/ppermute | solution.py:39
  30.4 1.9 %collective-permute-done.11.refs_1_ = bf16[128,256]{1,0:T(8,128)(2,1)S(1)} collective-permute-done((bf16[128,256]{1,0:T(8,128)(2,1)S(1)}, bf16[128,256]{1,0:T(8,128)(2,1)S(1)}, u32[]{:S(2)}, u32[]{:S(2)}) %collective-permute-start.11) | collective-permute-done | bytes 65568 | tf_op jit(solution)/shard_map/ppermute | solution.py:39
  32.4 1.0 %collective-permute-done.12.refs_2_ = bf16[128,256]{1,0:T(8,128)(2,1)S(1)} collective-permute-done((bf16[128,256]{1,0:T(8,128)(2,1)S(1)}, bf16[128,256]{1,0:T(8,128)(2,1)S(1)}, u32[]{:S(2)}, u32[]{:S(2)}) %collective-permute-start.12) | collective-permute-done | bytes 65568 | tf_op jit(solution)/shard_map/ppermute | solution.py:39
  33.4 0.3 collective-permute-done.13.refs_3_
  33.7 0.7 %shard_map.96 = (f32[64,256]{1,0:T(8,128)}, f32[64,256]{1,0:T(8,128)}) custom-call(f32[128,256]{1,0:T(8,128)S(1)} %get-tuple-element.104.refs_0_, bf16[128,256]{1,0:T(8,128)(2,1)S(1)} %collective-permute-done.11.refs_1_, bf16[128,256]{1,0:T(8,128)(2,1)S(1)} %collective-permute-done.12.refs_2_, bf16[128,256]{1,0:T(8,128)(2,1)S(1)} %collective-permute-done.13.refs_3_), custom_call_target="tpu_custom_call" | custom-call | tf_op jit(solution)/shard_map/pallas_call | solution.py:228
  (15 shorter events, 0.4 us)
Async XLA Ops:
  2.0 5.3 %collective-permute-start = (bf16[48,640]{1,0:T(8,128)(2,1)S(1)}, bf16[48,640]{1,0:T(8,128)(2,1)S(1)}, u32[]{:S(2)}, u32[]{:S(2)}) collective-permute-start(bf16[48,640]{1,0:T(8,128)(2,1)S(1)} %get-tuple-element.56), channel_id=1, source_target_pairs={{0,8},{8,0},{16,24},{24,16},{1,9},{9,1},{17,25},{25,17},{2,10},{10... | collective-permute-start | bytes 184328 | tf_op jit(solution)/shard_map/ppermute | solution.py:39
  5.0 6.0 %collective-permute-start.2 = (bf16[48,640]{1,0:T(8,128)(2,1)S(1)}, bf16[48,640]{1,0:T(8,128)(2,1)S(1)}, u32[]{:S(2)}, u32[]{:S(2)}) collective-permute-start(bf16[48,640]{1,0:T(8,128)(2,1)S(1)} %get-tuple-element.63), channel_id=1, source_target_pairs={{0,24},{8,16},{16,8},{24,0},{1,25},{9,17},{17,9},{25,1},{2,26},{10... | collective-permute-start | bytes 184328 | tf_op jit(solution)/shard_map/ppermute | solution.py:39
  6.5 4.5 %collective-permute-start.3 = (bf16[48,640]{1,0:T(8,128)(2,1)S(1)}, bf16[48,640]{1,0:T(8,128)(2,1)S(1)}, u32[]{:S(2)}, u32[]{:S(2)}) collective-permute-start(bf16[48,640]{1,0:T(8,128)(2,1)S(1)} %get-tuple-element.64), channel_id=1, source_target_pairs={{0,16},{8,24},{16,0},{24,8},{1,17},{9,25},{17,1},{25,9},{2,18},{10... | collective-permute-start | bytes 184328 | tf_op jit(solution)/shard_map/ppermute | solution.py:39
  7.9 6.1 %collective-permute-start.1 = (f16[104,512]{1,0:T(8,128)(2,1)S(1)}, f16[104,512]{1,0:T(8,128)(2,1)S(1)}, u32[]{:S(2)}, u32[]{:S(2)}) collective-permute-start(f16[104,512]{1,0:T(8,128)(2,1)S(1)} %convert_element_type.24), channel_id=1, source_target_pairs={{0,2},{1,3},{2,0},{3,1},{4,6},{5,7},{6,4},{7,5},{8,10},{9,11},{10,... | collective-permute-start | bytes 319496 | tf_op jit(solution)/shard_map/ppermute | solution.py:39
  11.5 4.8 %collective-permute-start.5 = (f16[104,512]{1,0:T(8,128)(2,1)S(1)}, f16[104,512]{1,0:T(8,128)(2,1)S(1)}, u32[]{:S(2)}, u32[]{:S(2)}) collective-permute-start(f16[104,512]{1,0:T(8,128)(2,1)S(1)} %convert_element_type.26), channel_id=1, source_target_pairs={{0,1},{1,0},{2,3},{3,2},{4,5},{5,4},{6,7},{7,6},{8,9},{9,8},{10,11... | collective-permute-start | bytes 319496 | tf_op jit(solution)/shard_map/ppermute | solution.py:39
  13.1 1.1 %collective-permute-start.4 = (f32[1,128]{1,0:T(1,128)S(1)}, f32[1,128]{1,0:T(1,128)S(1)}, u32[]{:S(2)}, u32[]{:S(2)}) collective-permute-start(f32[1,128]{1,0:T(1,128)S(1)} %get-tuple-element.93.refs_6_), channel_id=1, source_target_pairs={{0,4},{4,0},{1,5},{5,1},{2,6},{6,2},{3,7},{7,3},{8,12},{12,8},{9,1... | collective-permute-start | bytes 1544 | tf_op jit(solution)/shard_map/ppermute | solution.py:39
  16.5 7.6 %collective-permute-start.7 = (f16[104,512]{1,0:T(8,128)(2,1)S(1)}, f16[104,512]{1,0:T(8,128)(2,1)S(1)}, u32[]{:S(2)}, u32[]{:S(2)}) collective-permute-start(f16[104,512]{1,0:T(8,128)(2,1)S(1)} %convert_element_type.30), channel_id=1, source_target_pairs={{0,2},{1,3},{2,0},{3,1},{4,6},{5,7},{6,4},{7,5},{8,10},{9,11},{10,... | collective-permute-start | bytes 319496 | tf_op jit(solution)/shard_map/ppermute | solution.py:39
  19.1 5.6 %collective-permute-start.6 = (f16[104,512]{1,0:T(8,128)(2,1)S(1)}, f16[104,512]{1,0:T(8,128)(2,1)S(1)}, u32[]{:S(2)}, u32[]{:S(2)}) collective-permute-start(f16[104,512]{1,0:T(8,128)(2,1)S(1)} %convert_element_type.28), channel_id=1, source_target_pairs={{0,1},{1,0},{2,3},{3,2},{4,5},{5,4},{6,7},{7,6},{8,9},{9,8},{10,11... | collective-permute-start | bytes 319496 | tf_op jit(solution)/shard_map/ppermute | solution.py:39
  21.3 1.3 %collective-permute-start.8 = (bf16[96,512]{1,0:T(8,128)(2,1)S(1)}, bf16[96,512]{1,0:T(8,128)(2,1)S(1)}, u32[]{:S(2)}, u32[]{:S(2)}) collective-permute-start(bf16[96,512]{1,0:T(8,128)(2,1)S(1)} %get-tuple-element.78.refs_0_), channel_id=1, source_target_pairs={{0,4},{4,0},{1,5},{5,1},{2,6},{6,2},{3,7},{7,3},{8,12},{12,8},{9,1... | collective-permute-start | bytes 294920 | tf_op jit(solution)/shard_map/ppermute | solution.py:39
  21.3 1.5 %collective-permute-start.9 = (bf16[96,512]{1,0:T(8,128)(2,1)S(1)}, bf16[96,512]{1,0:T(8,128)(2,1)S(1)}, u32[]{:S(2)}, u32[]{:S(2)}) collective-permute-start(bf16[96,512]{1,0:T(8,128)(2,1)S(1)} %get-tuple-element.79.refs_1_), channel_id=1, source_target_pairs={{0,4},{4,0},{1,5},{5,1},{2,6},{6,2},{3,7},{7,3},{8,12},{12,8},{9,1... | collective-permute-start | bytes 294920 | tf_op jit(solution)/shard_map/ppermute | solution.py:39
  24.9 1.5 %collective-permute-start.10 = (bf16[192,512]{1,0:T(8,128)(2,1)S(1)}, bf16[192,512]{1,0:T(8,128)(2,1)S(1)}, u32[]{:S(2)}, u32[]{:S(2)}) collective-permute-start(bf16[192,512]{1,0:T(8,128)(2,1)S(1)} %shard_map.93.scaled), channel_id=1, source_target_pairs={{0,4},{4,0},{1,5},{5,1},{2,6},{6,2},{3,7},{7,3},{8,12},{12,8},{9,1... | collective-permute-start | bytes 589832 | tf_op jit(solution)/shard_map/ppermute | solution.py:39
  26.9 5.5 %collective-permute-start.11 = (bf16[128,256]{1,0:T(8,128)(2,1)S(1)}, bf16[128,256]{1,0:T(8,128)(2,1)S(1)}, u32[]{:S(2)}, u32[]{:S(2)}) collective-permute-start(bf16[128,256]{1,0:T(8,128)(2,1)S(1)} %get-tuple-element.105), channel_id=1, source_target_pairs={{0,24},{8,16},{16,8},{24,0},{1,25},{9,17},{17,9},{25,1},{2,26},{10... | collective-permute-start | bytes 196616 | tf_op jit(solution)/shard_map/ppermute | solution.py:39
  28.3 5.1 %collective-permute-start.12 = (bf16[128,256]{1,0:T(8,128)(2,1)S(1)}, bf16[128,256]{1,0:T(8,128)(2,1)S(1)}, u32[]{:S(2)}, u32[]{:S(2)}) collective-permute-start(bf16[128,256]{1,0:T(8,128)(2,1)S(1)} %get-tuple-element.106), channel_id=1, source_target_pairs={{0,16},{8,24},{16,0},{24,8},{1,17},{9,25},{17,1},{25,9},{2,18},{10... | collective-permute-start | bytes 196616 | tf_op jit(solution)/shard_map/ppermute | solution.py:39
  29.4 4.3 %collective-permute-start.13 = (bf16[128,256]{1,0:T(8,128)(2,1)S(1)}, bf16[128,256]{1,0:T(8,128)(2,1)S(1)}, u32[]{:S(2)}, u32[]{:S(2)}) collective-permute-start(bf16[128,256]{1,0:T(8,128)(2,1)S(1)} %get-tuple-element.107), channel_id=1, source_target_pairs={{0,8},{8,0},{16,24},{24,16},{1,9},{9,1},{17,25},{25,17},{2,10},{10... | collective-permute-start | bytes 196616 | tf_op jit(solution)/shard_map/ppermute | solution.py:39
